TPU v7x, 256 devices: a whole 4x4x8 slice. The times are simulated.
256 devices in a mesh: dp: 16 (over z_lo, y, core), tensor: 16 (over x, z_hi).
Axes of the slice: x: 4, y: 4, z: 8 (z_hi: 4, z_lo: 2; z = z_hi * 2 + z_lo), core: 2. Of those that a mesh axis runs over, the one named last changes fastest.
Arguments:
- tokens: bfloat16 [4096, 6144], P(('dp', 'tensor')), parts along dimension 0, may hold values from -6 to 6
- norm_gain: float32 [6144], replicated, may hold values from 0.1 to 1.9
- gate_weight: bfloat16 [6144, 14336], P(None, 'tensor'), may hold values from -0.078125 to 0.078125
- up_weight: bfloat16 [6144, 14336], P(None, 'tensor'), may hold values from -0.078125 to 0.078125
- down_weight: bfloat16 [14336, 6144], P('tensor'), may hold values from -0.046875 to 0.046875
Outputs:
- block_out: bfloat16 [4096, 6144], P(('dp', 'tensor')), parts along dimension 0
There are 16 independent parts, one for each index of `dp`. A program takes and returns all parts, laid end to end along the dimension named above; an argument that names none is the same for every part. Nothing has to cross between parts.
All inputs are finite; a program needn't handle non-finite values.
Results may differ from a plain program's by a relative error of at most 0.0051.
Values may be sent and summed in bfloat16 or wider, within the bound.
No kernel may reach another device: no remote copies, remote signals or barrier semaphores. Data moves between devices by JAX's collectives and lax.ppermute only.
A program may use at most 128 MiB of HBM per device.

v0:
```python
import jax
import jax.numpy as jnp
from jax import lax
from jax.sharding import PartitionSpec as P


def rms_normed(rows_in, norm_gain):
    rows = rows_in.astype(jnp.float32)
    scale = lax.rsqrt(jnp.mean(rows * rows, axis=1, keepdims=True) + 1e-05)
    return (rows * scale * norm_gain).astype(jnp.bfloat16)


def block_terms(normed, gate_weight, up_weight, down_weight):
    gate = jnp.dot(normed, gate_weight, preferred_element_type=jnp.float32)
    up = jnp.dot(normed, up_weight, preferred_element_type=jnp.float32)
    hidden = (jax.nn.silu(gate) * up).astype(jnp.bfloat16)
    return jnp.dot(hidden, down_weight, preferred_element_type=jnp.float32)


def on_device(tokens, norm_gain, gate_weight, up_weight, down_weight):
    gathered = rms_normed(lax.all_gather(tokens, "tensor", axis=0, tiled=True), norm_gain)
    terms = block_terms(gathered, gate_weight, up_weight, down_weight)
    mine = lax.psum_scatter(terms, "tensor", scatter_dimension=0, tiled=True)
    return (tokens.astype(jnp.float32) + mine).astype(jnp.bfloat16)


def solution(mesh):
    return jax.shard_map(
        on_device,
        mesh=mesh,
        in_specs=(
            P(("dp", "tensor"), None),
            P(),
            P(None, "tensor"),
            P(None, "tensor"),
            P("tensor", None),
        ),
        out_specs=P(("dp", "tensor"), None),
        check_vma=False,
    )
```

profile of v0, /device:TPU:8, one launch (start us, length us, event | category | flops | bytes accessed | tf_op | source)
XLA Modules:
  0.0 225.7 jit_solution(3171563518563648820)
XLA Ops:
  6.5 0.0 all-gather.2.cloned.1.call-start
  6.5 0.7 all-gather.2.cloned.1.call-update
  7.3 0.0 reduce-scatter.2.cloned.1.call-start
  7.3 73.1 %all-gather.2.cloned.1.call-done = bf16[256,6144]{1,0:T(8,128)(2,1)} async-done(((bf16[16,6144]{1,0:T(8,128)(2,1)}), bf16[256,6144]{1,0:T(8,128)(2,1)}) %all-gather.2.cloned.1.call-update) | async-done | bytes 3145744 | tf_op jit(solution)/shard_map/all_gather | solution.py:21
  80.4 2.6 %fusion = f32[256]{0:T(256)S(1)} fusion(bf16[256,6144]{1,0:T(8,128)(2,1)} %all-gather.2.cloned.1.call-done), kind=kLoop, calls=%fused_computation.2 | loop fusion | flops 4718336 | bytes 3146752 | tf_op jit(solution)/shard_map/reduce_sum | solution.py:9
  83.0 0.0 copy-start
  83.0 0.0 copy-start.2
  83.0 9.7 %fusion.5 = f32[256,896]{1,0:T(8,128)} fusion(bf16[6144,896]{1,0:T(8,128)(2,1)} %param.7, bf16[256,6144]{1,0:T(8,128)(2,1)} %all-gather.2.cloned.1.call-done, f32[6144]{0:T(1024)} %param.6, f32[256]{0:T(256)S(1)} %add_rsqrt_fusion), kind=kOutput, calls=%fused_computation.7 | convolution fusion | flops 2824863744 | bytes 15098880 | tf_op jit(solution)/shard_map/dot_general | solution.py:14
  92.7 0.0 copy-done
  92.7 0.0 copy-done.2
  92.7 17.0 %fusion.8 = f32[256,6144]{1,0:T(8,128)} fusion(bf16[896,6144]{1,0:T(8,128)(2,1)} %param.9, bf16[6144,896]{1,0:T(8,128)(2,1)} %param.8, f32[256,896]{1,0:T(8,128)} %fusion.5, bf16[256,6144]{1,0:T(8,128)(2,1)S(1)} %copy-done, f32[6144]{0:T(1024)S(1)} %copy-done.2, f32[256]{0:T(256)S(1)} %add_rsqrt_fusion), kind=kOutput, calls=%fused_computation.9 | convolution fusion | flops 5644812288 | bytes 32400384 | tf_op jit(solution)/shard_map/dot_general | solution.py:17
  109.7 0.0 copy-start.1
  109.7 0.0 reduce-scatter.2.cloned.1.call-update
  109.7 107.5 %reduce-scatter.2.cloned.1.call-done = f32[16,6144]{1,0:T(8,128)} async-done(((f32[256,6144]{1,0:T(8,128)}), f32[16,6144]{1,0:T(8,128)}) %reduce-scatter.2.cloned.1.call-update) | async-done | bytes 393232 | tf_op jit(solution)/shard_map/reduce_scatter | solution.py:23
  217.2 0.0 copy-done.1
  217.2 1.7 add_convert_fusion
  (1 shorter events, 0.0 us)
Async XLA Ops:
  6.5 73.9 %all-gather.2.cloned.1.call-start = ((), (), s32[]{:S(2)}) async-start(), calls=%async_computation.1 | async-start | bytes 3342336 | tf_op jit(solution)/shard_map/all_gather | solution.py:21
  7.3 209.9 %reduce-scatter.2.cloned.1.call-start = ((), (), s32[]{:S(2)}) async-start(), calls=%async_computation.2 | async-start | bytes 6684672 | tf_op jit(solution)/shard_map/reduce_scatter | solution.py:23
  83.0 9.7 %copy-start = (bf16[256,6144]{1,0:T(8,128)(2,1)S(1)}, bf16[256,6144]{1,0:T(8,128)(2,1)}, u32[]{:S(2)}) copy-start(bf16[256,6144]{1,0:T(8,128)(2,1)} %all-gather.2.cloned.1.call-done) | copy-start | bytes 9437188
  83.0 9.7 %copy-start.2 = (f32[6144]{0:T(1024)S(1)}, f32[6144]{0:T(1024)}, u32[]{:S(2)}) copy-start(f32[6144]{0:T(1024)} %param.6) | copy-start | bytes 73732
  109.7 107.5 %copy-start.1 = (bf16[16,6144]{1,0:T(8,128)(2,1)S(1)}, bf16[16,6144]{1,0:T(8,128)(2,1)}, u32[]{:S(2)}) copy-start(bf16[16,6144]{1,0:T(8,128)(2,1)} %param.5) | copy-start | bytes 589828
Sparse Core Ops, SparseCore 0:
  9.8 70.5 all-gather.1
  109.9 107.2 reduce-scatter.1
where the time goes:
time: 226 us
  waiting for transfers between devices  181 us (80%)
  matrix products  26.7 us (12%)
  between operations  13.4 us (6%)
  other arithmetic  4.31 us (2%)
    reduce_scatter x1, waiting for transfers between devices, on_device(): mine = lax.psum_scatter(terms, 'tensor', scatter_dimension=0, tiled=True)  107 us
    all_gather x1, waiting for transfers between devices, on_device(): lax.all_gather(tokens, 'tensor', axis=0, tiled=True)  73.1 us
    dot_general x1, matrix products, block_terms(): return jnp.dot(hidden, down_weight, preferred_element_type=jnp.float32)  17 us
    dot_general x1, matrix products, block_terms(): gate = jnp.dot(normed, gate_weight, preferred_element_type=jnp.float32)  9.67 us
  transfers between devices with their start and end apart: 2, of which 2 were waited for; matrix products, arithmetic and copies ran while one was open for 0% of the time, Pallas kernels for 0%

commit v1 on v0

--- a/solution.py
+++ b/solution.py
@@ -2,6 +2,17 @@
 import jax.numpy as jnp
 from jax import lax
 from jax.sharding import PartitionSpec as P
+
+SIDE = 4
+
+
+def shift(block, dx, dz):
+    pairs = [
+        (x * SIDE + z, (x + dx) % SIDE * SIDE + (z + dz) % SIDE)
+        for x in range(SIDE)
+        for z in range(SIDE)
+    ]
+    return lax.ppermute(block, "tensor", pairs)
 
 
 def rms_normed(rows_in, norm_gain):
@@ -17,10 +28,32 @@
     return jnp.dot(hidden, down_weight, preferred_element_type=jnp.float32)
 
 
+HOPS = (1, -1, 2)
+
+
 def on_device(tokens, norm_gain, gate_weight, up_weight, down_weight):
-    gathered = rms_normed(lax.all_gather(tokens, "tensor", axis=0, tiled=True), norm_gain)
-    terms = block_terms(gathered, gate_weight, up_weight, down_weight)
-    mine = lax.psum_scatter(terms, "tensor", scatter_dimension=0, tiled=True)
+    n = tokens.shape[0]
+    own = rms_normed(tokens, norm_gain)
+    z_near = jnp.concatenate([shift(own, 0, 1), shift(own, 0, -1)], 0)
+    z_far = shift(own, 0, 2)
+    sets = []
+    for held in (own, z_near, z_far):
+        sets.append([held] + [shift(held, d, 0) for d in HOPS])
+    rows = [jnp.concatenate(s, 0) for s in sets]
+    terms = block_terms(jnp.concatenate(rows, 0), gate_weight, up_weight, down_weight)
+    t_own, t_near, t_far = terms[: 4 * n], terms[4 * n : 12 * n], terms[12 * n :]
+
+    def back(t, k):
+        total = t[:k]
+        for i, d in enumerate(HOPS):
+            total = total + shift(t[(i + 1) * k : (i + 2) * k].astype(jnp.bfloat16), -d, 0).astype(jnp.float32)
+        return total
+
+    near = back(t_near, 2 * n).astype(jnp.bfloat16)
+    far = back(t_far, n).astype(jnp.bfloat16)
+    mine = back(t_own, n)
+    for part in (shift(near[:n], 0, -1), shift(near[n:], 0, 1), shift(far, 0, -2)):
+        mine = mine + part.astype(jnp.float32)
     return (tokens.astype(jnp.float32) + mine).astype(jnp.bfloat16)
 
 

time: 226 us -> 142 us (0.63)
  the two profiles are of different devices: /device:TPU:8 before, /device:TPU:39 now
where the time goes in v1:
time: 142 us
  waiting for transfers between devices  72.3 us (51%)
  starting transfers between devices  36 us (25%)
  matrix products  24.9 us (18%)
  other arithmetic  6.41 us (5%)
  local copies, waits for them, and re-layouts  2.12 us (1%)
    ppermute x24, waiting for transfers between devices, shift(): return lax.ppermute(block, 'tensor', pairs)  72.3 us
    ppermute x24, starting transfers between devices, shift(): return lax.ppermute(block, 'tensor', pairs)  36 us
    dot_general x1, matrix products, block_terms(): return jnp.dot(hidden, down_weight, preferred_element_type=jnp.float32)  17.8 us
    dot_general x1, matrix products, block_terms(): gate = jnp.dot(normed, gate_weight, preferred_element_type=jnp.float32)  7.12 us
  transfers between devices with their start and end apart: 24, of which 13 were waited for; matrix products, arithmetic and copies ran while one was open for 2% of the time, Pallas kernels for 0%

profile of v1, /device:TPU:39, one launch (start us, length us, event | category | flops | bytes accessed | tf_op | source)
XLA Modules:
  0.0 141.8 jit_solution(5359749532725747434)
XLA Ops:
  0.0 1.1 fusion.5
  1.1 1.1 constant_dynamic-update-slice_fusion.14
  2.2 0.3 collective-permute-start
  2.4 5.1 %collective-permute-start.4 = (bf16[16,6144]{1,0:T(8,128)(2,1)S(1)}, bf16[16,6144]{1,0:T(8,128)(2,1)S(1)}, u32[]{:S(2)}, u32[]{:S(2)}) collective-permute-start(bf16[16,6144]{1,0:T(8,128)(2,1)S(1)} %get-tuple-element.6), channel_id=1, source_target_pairs={{0,3},{1,0},{2,1},{3,2},{4,7},{5,4},{6,5},{7,6},{8,11},{9,8},{10,9... | collective-permute-start | bytes 589832 | tf_op jit(solution)/shard_map/ppermute | solution.py:15
  7.6 0.0 collective-permute-start.3
  7.6 2.1 %collective-permute-start.2 = (bf16[16,6144]{1,0:T(8,128)(2,1)S(1)}, bf16[16,6144]{1,0:T(8,128)(2,1)S(1)}, u32[]{:S(2)}, u32[]{:S(2)}) collective-permute-start(bf16[16,6144]{1,0:T(8,128)(2,1)S(1)} %get-tuple-element.6), channel_id=1, source_target_pairs={{0,8},{1,9},{2,10},{3,11},{4,12},{5,13},{6,14},{7,15},{8,0},{9,1},... | collective-permute-start | bytes 589832 | tf_op jit(solution)/shard_map/ppermute | solution.py:15
  9.7 0.0 collective-permute-start.1
  9.7 0.0 collective-permute-done
  9.7 9.7 %collective-permute-done.1 = bf16[16,6144]{1,0:T(8,128)(2,1)S(1)} collective-permute-done((bf16[16,6144]{1,0:T(8,128)(2,1)S(1)}, bf16[16,6144]{1,0:T(8,128)(2,1)S(1)}, u32[]{:S(2)}, u32[]{:S(2)}) %collective-permute-start.1) | collective-permute-done | bytes 196640 | tf_op jit(solution)/shard_map/ppermute | solution.py:15
  19.5 0.0 collective-permute-done.2
  19.5 0.4 collective-permute-done.3
  19.9 0.0 collective-permute-done.4
  20.0 1.3 collective-permute-start.5
  21.3 1.5 %collective-permute-start.8 = (bf16[16,6144]{1,0:T(8,128)(2,1)S(1)}, bf16[16,6144]{1,0:T(8,128)(2,1)S(1)}, u32[]{:S(2)}, u32[]{:S(2)}) collective-permute-start(bf16[16,6144]{1,0:T(8,128)(2,1)S(1)} %get-tuple-element.6), channel_id=1, source_target_pairs={{0,2},{1,3},{2,0},{3,1},{4,6},{5,7},{6,4},{7,5},{8,10},{9,11},{10,... | collective-permute-start | bytes 589832 | tf_op jit(solution)/shard_map/ppermute | solution.py:15
  22.8 1.7 %collective-permute-start.7 = (bf16[32,6144]{1,0:T(8,128)(2,1)S(1)}, bf16[32,6144]{1,0:T(8,128)(2,1)S(1)}, u32[]{:S(2)}, u32[]{:S(2)}) collective-permute-start(bf16[32,6144]{1,0:T(8,128)(2,1)S(1)} %get-tuple-element.18), channel_id=1, source_target_pairs={{0,8},{1,9},{2,10},{3,11},{4,12},{5,13},{6,14},{7,15},{8,0},{9,1},... | collective-permute-start | bytes 1179656 | tf_op jit(solution)/shard_map/ppermute | solution.py:15
  24.4 0.8 collective-permute-start.6
  25.2 9.9 %collective-permute-done.8 = bf16[16,6144]{1,0:T(8,128)(2,1)S(1)} collective-permute-done((bf16[16,6144]{1,0:T(8,128)(2,1)S(1)}, bf16[16,6144]{1,0:T(8,128)(2,1)S(1)}, u32[]{:S(2)}, u32[]{:S(2)}) %collective-permute-start.8) | collective-permute-done | bytes 196640 | tf_op jit(solution)/shard_map/ppermute | solution.py:15
  35.1 1.3 collective-permute-start.11
  36.4 1.6 %collective-permute-start.10 = (bf16[16,6144]{1,0:T(8,128)(2,1)S(1)}, bf16[16,6144]{1,0:T(8,128)(2,1)S(1)}, u32[]{:S(2)}, u32[]{:S(2)}) collective-permute-start(bf16[16,6144]{1,0:T(8,128)(2,1)S(1)} %collective-permute-done.8), channel_id=1, source_target_pairs={{0,12},{1,13},{2,14},{3,15},{4,0},{5,1},{6,2},{7,3},{8,4},{9,5},{1... | collective-permute-start | bytes 589832 | tf_op jit(solution)/shard_map/ppermute | solution.py:15
  38.0 1.1 collective-permute-start.9
  39.1 6.7 %collective-permute-done.6 = bf16[32,6144]{1,0:T(8,128)(2,1)S(1)} collective-permute-done((bf16[32,6144]{1,0:T(8,128)(2,1)S(1)}, bf16[32,6144]{1,0:T(8,128)(2,1)S(1)}, u32[]{:S(2)}, u32[]{:S(2)}) %collective-permute-start.6) | collective-permute-done | bytes 393248 | tf_op jit(solution)/shard_map/ppermute | solution.py:15
  45.9 1.6 %collective-permute-done.9 = bf16[16,6144]{1,0:T(8,128)(2,1)S(1)} collective-permute-done((bf16[16,6144]{1,0:T(8,128)(2,1)S(1)}, bf16[16,6144]{1,0:T(8,128)(2,1)S(1)}, u32[]{:S(2)}, u32[]{:S(2)}) %collective-permute-start.9) | collective-permute-done | bytes 196640 | tf_op jit(solution)/shard_map/ppermute | solution.py:15
  47.5 4.6 %collective-permute-done.10 = bf16[16,6144]{1,0:T(8,128)(2,1)S(1)} collective-permute-done((bf16[16,6144]{1,0:T(8,128)(2,1)S(1)}, bf16[16,6144]{1,0:T(8,128)(2,1)S(1)}, u32[]{:S(2)}, u32[]{:S(2)}) %collective-permute-start.10) | collective-permute-done | bytes 196640 | tf_op jit(solution)/shard_map/ppermute | solution.py:15
  52.2 0.0 collective-permute-done.11
  52.2 1.7 %copy-done.1 = bf16[256,6144]{1,0:T(8,128)(2,1)} copy-done((bf16[256,6144]{1,0:T(8,128)(2,1)}, bf16[256,6144]{1,0:T(8,128)(2,1)S(1)}, u32[]{:S(2)}) %copy-start.1) | copy-done | bytes 3145752
  53.9 7.1 %fusion.25 = f32[256,896]{1,0:T(8,128)} fusion(bf16[256,6144]{1,0:T(8,128)(2,1)S(1)} %constant_dynamic-update-slice_fusion.2, bf16[6144,896]{1,0:T(8,128)(2,1)} %param.7), kind=kOutput, calls=%fused_computation.46 | convolution fusion | flops 2818572288 | bytes 15073280 | tf_op jit(solution)/shard_map/dot_general | solution.py:25
  61.0 17.8 %fusion.22 = (bf16[256,6144]{1,0:T(8,128)(2,1)S(1)}, f32[256,6144]{1,0:T(8,128)}) fusion(bf16[896,6144]{1,0:T(8,128)(2,1)} %param.9, f32[256,896]{1,0:T(8,128)} %fusion.25, bf16[256,6144]{1,0:T(8,128)(2,1)} %copy-done.1, bf16[6144,896]{1,0:T(8,128)(2,1)} %param.8), kind=kOutput, calls=%fused_computation.44 | convolution fusion | flops 5640093696 | bytes 35520512 | tf_op jit(solution)/shard_map/dot_general | solution.py:28
  78.8 0.1 fusion.19
  78.9 1.4 collective-permute-start.22
  80.2 1.5 %collective-permute-start.20 = (bf16[16,6144]{1,0:T(8,128)(2,1)S(1)}, bf16[16,6144]{1,0:T(8,128)(2,1)S(1)}, u32[]{:S(2)}, u32[]{:S(2)}) collective-permute-start(bf16[16,6144]{1,0:T(8,128)(2,1)S(1)} %get-tuple-element.10), channel_id=1, source_target_pairs={{0,12},{1,13},{2,14},{3,15},{4,0},{5,1},{6,2},{7,3},{8,4},{9,5},{1... | collective-permute-start | bytes 589832 | tf_op jit(solution)/shard_map/ppermute | solution.py:15
  81.7 0.1 fusion.20
  81.8 0.1 collective-permute-start.12
  81.9 2.4 %collective-permute-start.14 = (bf16[16,6144]{1,0:T(8,128)(2,1)S(1)}, bf16[16,6144]{1,0:T(8,128)(2,1)S(1)}, u32[]{:S(2)}, u32[]{:S(2)}) collective-permute-start(bf16[16,6144]{1,0:T(8,128)(2,1)S(1)} %get-tuple-element.11), channel_id=1, source_target_pairs={{0,8},{1,9},{2,10},{3,11},{4,12},{5,13},{6,14},{7,15},{8,0},{9,1},... | collective-permute-start | bytes 589832 | tf_op jit(solution)/shard_map/ppermute | solution.py:15
  84.3 2.2 %collective-permute-done.22 = bf16[16,6144]{1,0:T(8,128)(2,1)S(1)} collective-permute-done((bf16[16,6144]{1,0:T(8,128)(2,1)S(1)}, bf16[16,6144]{1,0:T(8,128)(2,1)S(1)}, u32[]{:S(2)}, u32[]{:S(2)}) %collective-permute-start.22) | collective-permute-done | bytes 196640 | tf_op jit(solution)/shard_map/ppermute | solution.py:15
  86.5 0.6 collective-permute-done.21
  87.1 4.6 %collective-permute-start.17 = (bf16[32,6144]{1,0:T(8,128)(2,1)S(1)}, bf16[32,6144]{1,0:T(8,128)(2,1)S(1)}, u32[]{:S(2)}, u32[]{:S(2)}) collective-permute-start(bf16[32,6144]{1,0:T(8,128)(2,1)S(1)} %get-tuple-element.14), channel_id=1, source_target_pairs={{0,8},{1,9},{2,10},{3,11},{4,12},{5,13},{6,14},{7,15},{8,0},{9,1},... | collective-permute-start | bytes 1179656 | tf_op jit(solution)/shard_map/ppermute | solution.py:15
  91.7 3.1 %collective-permute-start.16 = (bf16[32,6144]{1,0:T(8,128)(2,1)S(1)}, bf16[32,6144]{1,0:T(8,128)(2,1)S(1)}, u32[]{:S(2)}, u32[]{:S(2)}) collective-permute-start(bf16[32,6144]{1,0:T(8,128)(2,1)S(1)} %get-tuple-element.15), channel_id=1, source_target_pairs={{0,4},{1,5},{2,6},{3,7},{4,8},{5,9},{6,10},{7,11},{8,12},{9,13},{1... | collective-permute-start | bytes 1179656 | tf_op jit(solution)/shard_map/ppermute | solution.py:15
  94.8 1.1 fusion.11
  95.9 12.8 %collective-permute-done.15 = bf16[32,6144]{1,0:T(8,128)(2,1)S(1)} collective-permute-done((bf16[32,6144]{1,0:T(8,128)(2,1)S(1)}, bf16[32,6144]{1,0:T(8,128)(2,1)S(1)}, u32[]{:S(2)}, u32[]{:S(2)}) %collective-permute-start.15) | collective-permute-done | bytes 393248 | tf_op jit(solution)/shard_map/ppermute | solution.py:15
  108.7 7.4 %collective-permute-done.17 = bf16[32,6144]{1,0:T(8,128)(2,1)S(1)} collective-permute-done((bf16[32,6144]{1,0:T(8,128)(2,1)S(1)}, bf16[32,6144]{1,0:T(8,128)(2,1)S(1)}, u32[]{:S(2)}, u32[]{:S(2)}) %collective-permute-start.17) | collective-permute-done | bytes 393248 | tf_op jit(solution)/shard_map/ppermute | solution.py:15
  116.0 3.9 %collective-permute-start.23 = (bf16[16,6144]{1,0:T(8,128)(2,1)S(1)}, bf16[16,6144]{1,0:T(8,128)(2,1)S(1)}, u32[]{:S(2)}, u32[]{:S(2)}) collective-permute-start(bf16[16,6144]{1,0:T(8,128)(2,1)S(1)} %fusion.11), channel_id=1, source_target_pairs={{0,2},{1,3},{2,0},{3,1},{4,6},{5,7},{6,4},{7,5},{8,10},{9,11},{10,... | collective-permute-start | bytes 589832 | tf_op jit(solution)/shard_map/ppermute | solution.py:15
  119.9 1.3 fusion.2
  121.3 1.9 %collective-permute-start.18 = (bf16[16,6144]{1,0:T(8,128)(2,1)S(1)}, bf16[16,6144]{1,0:T(8,128)(2,1)S(1)}, u32[]{:S(2)}, u32[]{:S(2)}) collective-permute-start(bf16[16,6144]{1,0:T(8,128)(2,1)S(1)} %get-tuple-element.16), channel_id=1, source_target_pairs={{0,3},{1,0},{2,1},{3,2},{4,7},{5,4},{6,5},{7,6},{8,11},{9,8},{10,9... | collective-permute-start | bytes 589832 | tf_op jit(solution)/shard_map/ppermute | solution.py:15
  123.2 0.6 collective-permute-start.19
  123.7 3.8 %collective-permute-done.23 = bf16[16,6144]{1,0:T(8,128)(2,1)S(1)} collective-permute-done((bf16[16,6144]{1,0:T(8,128)(2,1)S(1)}, bf16[16,6144]{1,0:T(8,128)(2,1)S(1)}, u32[]{:S(2)}, u32[]{:S(2)}) %collective-permute-start.23) | collective-permute-done | bytes 196640 | tf_op jit(solution)/shard_map/ppermute | solution.py:15
  127.6 4.5 %collective-permute-done.18 = bf16[16,6144]{1,0:T(8,128)(2,1)S(1)} collective-permute-done((bf16[16,6144]{1,0:T(8,128)(2,1)S(1)}, bf16[16,6144]{1,0:T(8,128)(2,1)S(1)}, u32[]{:S(2)}, u32[]{:S(2)}) %collective-permute-start.18) | collective-permute-done | bytes 196640 | tf_op jit(solution)/shard_map/ppermute | solution.py:15
  132.1 7.9 %collective-permute-done.19 = bf16[16,6144]{1,0:T(8,128)(2,1)S(1)} collective-permute-done((bf16[16,6144]{1,0:T(8,128)(2,1)S(1)}, bf16[16,6144]{1,0:T(8,128)(2,1)S(1)}, u32[]{:S(2)}, u32[]{:S(2)}) %collective-permute-start.19) | collective-permute-done | bytes 196640 | tf_op jit(solution)/shard_map/ppermute | solution.py:15
  140.0 1.9 %fusion.8 = bf16[16,6144]{1,0:T(8,128)(2,1)} fusion(bf16[16,6144]{1,0:T(8,128)(2,1)S(1)} %copy-done, f32[256,6144]{1,0:T(8,128)} %get-tuple-element.23, bf16[16,6144]{1,0:T(8,128)(2,1)S(1)} %collective-permute-done.23, bf16[16,6144]{1,0:T(8,128)(2,1)S(1)} %collective-permute-done.19, bf16[16,6144]{1,0:T(8,128)(2,1)S(1)} %collective-permute-done.18, ...), kind=kLoop, calls=%fused_computation.13 | loop fusion | flops 1474560 | bytes 1966080 | tf_op jit(solution)/shard_map/convert_element_type | solution.py:57
  (27 shorter events, 0.3 us)
Async XLA Ops:
  2.2 7.5 %collective-permute-start = (bf16[16,6144]{1,0:T(8,128)(2,1)S(1)}, bf16[16,6144]{1,0:T(8,128)(2,1)S(1)}, u32[]{:S(2)}, u32[]{:S(2)}) collective-permute-start(bf16[16,6144]{1,0:T(8,128)(2,1)S(1)} %get-tuple-element.6), channel_id=1, source_target_pairs={{0,4},{1,5},{2,6},{3,7},{4,8},{5,9},{6,10},{7,11},{8,12},{9,13},{1... | collective-permute-start | bytes 589832 | tf_op jit(solution)/shard_map/ppermute | solution.py:15
  2.4 17.5 %collective-permute-start.4 = (bf16[16,6144]{1,0:T(8,128)(2,1)S(1)}, bf16[16,6144]{1,0:T(8,128)(2,1)S(1)}, u32[]{:S(2)}, u32[]{:S(2)}) collective-permute-start(bf16[16,6144]{1,0:T(8,128)(2,1)S(1)} %get-tuple-element.6), channel_id=1, source_target_pairs={{0,3},{1,0},{2,1},{3,2},{4,7},{5,4},{6,5},{7,6},{8,11},{9,8},{10,9... | collective-permute-start | bytes 589832 | tf_op jit(solution)/shard_map/ppermute | solution.py:15
  7.6 12.3 %collective-permute-start.3 = (bf16[16,6144]{1,0:T(8,128)(2,1)S(1)}, bf16[16,6144]{1,0:T(8,128)(2,1)S(1)}, u32[]{:S(2)}, u32[]{:S(2)}) collective-permute-start(bf16[16,6144]{1,0:T(8,128)(2,1)S(1)} %get-tuple-element.6), channel_id=1, source_target_pairs={{0,1},{1,2},{2,3},{3,0},{4,5},{5,6},{6,7},{7,4},{8,9},{9,10},{10,1... | collective-permute-start | bytes 589832 | tf_op jit(solution)/shard_map/ppermute | solution.py:15
  7.6 11.9 %collective-permute-start.2 = (bf16[16,6144]{1,0:T(8,128)(2,1)S(1)}, bf16[16,6144]{1,0:T(8,128)(2,1)S(1)}, u32[]{:S(2)}, u32[]{:S(2)}) collective-permute-start(bf16[16,6144]{1,0:T(8,128)(2,1)S(1)} %get-tuple-element.6), channel_id=1, source_target_pairs={{0,8},{1,9},{2,10},{3,11},{4,12},{5,13},{6,14},{7,15},{8,0},{9,1},... | collective-permute-start | bytes 589832 | tf_op jit(solution)/shard_map/ppermute | solution.py:15
  9.7 9.7 %collective-permute-start.1 = (bf16[16,6144]{1,0:T(8,128)(2,1)S(1)}, bf16[16,6144]{1,0:T(8,128)(2,1)S(1)}, u32[]{:S(2)}, u32[]{:S(2)}) collective-permute-start(bf16[16,6144]{1,0:T(8,128)(2,1)S(1)} %get-tuple-element.6), channel_id=1, source_target_pairs={{0,12},{1,13},{2,14},{3,15},{4,0},{5,1},{6,2},{7,3},{8,4},{9,5},{1... | collective-permute-start | bytes 589832 | tf_op jit(solution)/shard_map/ppermute | solution.py:15
  20.0 18.0 %collective-permute-start.5 = (bf16[32,6144]{1,0:T(8,128)(2,1)S(1)}, bf16[32,6144]{1,0:T(8,128)(2,1)S(1)}, u32[]{:S(2)}, u32[]{:S(2)}) collective-permute-start(bf16[32,6144]{1,0:T(8,128)(2,1)S(1)} %get-tuple-element.18), channel_id=1, source_target_pairs={{0,4},{1,5},{2,6},{3,7},{4,8},{5,9},{6,10},{7,11},{8,12},{9,13},{1... | collective-permute-start | bytes 1179656 | tf_op jit(solution)/shard_map/ppermute | solution.py:15
  21.3 13.8 %collective-permute-start.8 = (bf16[16,6144]{1,0:T(8,128)(2,1)S(1)}, bf16[16,6144]{1,0:T(8,128)(2,1)S(1)}, u32[]{:S(2)}, u32[]{:S(2)}) collective-permute-start(bf16[16,6144]{1,0:T(8,128)(2,1)S(1)} %get-tuple-element.6), channel_id=1, source_target_pairs={{0,2},{1,3},{2,0},{3,1},{4,6},{5,7},{6,4},{7,5},{8,10},{9,11},{10,... | collective-permute-start | bytes 589832 | tf_op jit(solution)/shard_map/ppermute | solution.py:15
  22.8 23.1 %collective-permute-start.7 = (bf16[32,6144]{1,0:T(8,128)(2,1)S(1)}, bf16[32,6144]{1,0:T(8,128)(2,1)S(1)}, u32[]{:S(2)}, u32[]{:S(2)}) collective-permute-start(bf16[32,6144]{1,0:T(8,128)(2,1)S(1)} %get-tuple-element.18), channel_id=1, source_target_pairs={{0,8},{1,9},{2,10},{3,11},{4,12},{5,13},{6,14},{7,15},{8,0},{9,1},... | collective-permute-start | bytes 1179656 | tf_op jit(solution)/shard_map/ppermute | solution.py:15
  24.4 21.4 %collective-permute-start.6 = (bf16[32,6144]{1,0:T(8,128)(2,1)S(1)}, bf16[32,6144]{1,0:T(8,128)(2,1)S(1)}, u32[]{:S(2)}, u32[]{:S(2)}) collective-permute-start(bf16[32,6144]{1,0:T(8,128)(2,1)S(1)} %get-tuple-element.18), channel_id=1, source_target_pairs={{0,12},{1,13},{2,14},{3,15},{4,0},{5,1},{6,2},{7,3},{8,4},{9,5},{1... | collective-permute-start | bytes 1179656 | tf_op jit(solution)/shard_map/ppermute | solution.py:15
  35.1 17.1 %collective-permute-start.11 = (bf16[16,6144]{1,0:T(8,128)(2,1)S(1)}, bf16[16,6144]{1,0:T(8,128)(2,1)S(1)}, u32[]{:S(2)}, u32[]{:S(2)}) collective-permute-start(bf16[16,6144]{1,0:T(8,128)(2,1)S(1)} %collective-permute-done.8), channel_id=1, source_target_pairs={{0,8},{1,9},{2,10},{3,11},{4,12},{5,13},{6,14},{7,15},{8,0},{9,1},... | collective-permute-start | bytes 589832 | tf_op jit(solution)/shard_map/ppermute | solution.py:15
  36.4 15.7 %collective-permute-start.10 = (bf16[16,6144]{1,0:T(8,128)(2,1)S(1)}, bf16[16,6144]{1,0:T(8,128)(2,1)S(1)}, u32[]{:S(2)}, u32[]{:S(2)}) collective-permute-start(bf16[16,6144]{1,0:T(8,128)(2,1)S(1)} %collective-permute-done.8), channel_id=1, source_target_pairs={{0,12},{1,13},{2,14},{3,15},{4,0},{5,1},{6,2},{7,3},{8,4},{9,5},{1... | collective-permute-start | bytes 589832 | tf_op jit(solution)/shard_map/ppermute | solution.py:15
  38.0 9.5 %collective-permute-start.9 = (bf16[16,6144]{1,0:T(8,128)(2,1)S(1)}, bf16[16,6144]{1,0:T(8,128)(2,1)S(1)}, u32[]{:S(2)}, u32[]{:S(2)}) collective-permute-start(bf16[16,6144]{1,0:T(8,128)(2,1)S(1)} %collective-permute-done.8), channel_id=1, source_target_pairs={{0,4},{1,5},{2,6},{3,7},{4,8},{5,9},{6,10},{7,11},{8,12},{9,13},{1... | collective-permute-start | bytes 589832 | tf_op jit(solution)/shard_map/ppermute | solution.py:15
  52.2 1.7 %copy-start.1 = (bf16[256,6144]{1,0:T(8,128)(2,1)}, bf16[256,6144]{1,0:T(8,128)(2,1)S(1)}, u32[]{:S(2)}) copy-start(bf16[256,6144]{1,0:T(8,128)(2,1)S(1)} %constant_dynamic-update-slice_fusion.2) | copy-start | bytes 9437188
  78.9 7.6 %collective-permute-start.22 = (bf16[16,6144]{1,0:T(8,128)(2,1)S(1)}, bf16[16,6144]{1,0:T(8,128)(2,1)S(1)}, u32[]{:S(2)}, u32[]{:S(2)}) collective-permute-start(bf16[16,6144]{1,0:T(8,128)(2,1)S(1)} %get-tuple-element.8), channel_id=1, source_target_pairs={{0,8},{1,9},{2,10},{3,11},{4,12},{5,13},{6,14},{7,15},{8,0},{9,1},... | collective-permute-start | bytes 589832 | tf_op jit(solution)/shard_map/ppermute | solution.py:15
  80.2 6.9 %collective-permute-start.21 = (bf16[16,6144]{1,0:T(8,128)(2,1)S(1)}, bf16[16,6144]{1,0:T(8,128)(2,1)S(1)}, u32[]{:S(2)}, u32[]{:S(2)}) collective-permute-start(bf16[16,6144]{1,0:T(8,128)(2,1)S(1)} %get-tuple-element.9), channel_id=1, source_target_pairs={{0,4},{1,5},{2,6},{3,7},{4,8},{5,9},{6,10},{7,11},{8,12},{9,13},{1... | collective-permute-start | bytes 589832 | tf_op jit(solution)/shard_map/ppermute | solution.py:15
  80.2 59.7 %copy-start = (bf16[16,6144]{1,0:T(8,128)(2,1)S(1)}, bf16[16,6144]{1,0:T(8,128)(2,1)}, u32[]{:S(2)}) copy-start(bf16[16,6144]{1,0:T(8,128)(2,1)} %param.5) | copy-start | bytes 589828
  80.2 11.5 %collective-permute-start.20 = (bf16[16,6144]{1,0:T(8,128)(2,1)S(1)}, bf16[16,6144]{1,0:T(8,128)(2,1)S(1)}, u32[]{:S(2)}, u32[]{:S(2)}) collective-permute-start(bf16[16,6144]{1,0:T(8,128)(2,1)S(1)} %get-tuple-element.10), channel_id=1, source_target_pairs={{0,12},{1,13},{2,14},{3,15},{4,0},{5,1},{6,2},{7,3},{8,4},{9,5},{1... | collective-permute-start | bytes 589832 | tf_op jit(solution)/shard_map/ppermute | solution.py:15
  81.8 41.4 %collective-permute-start.12 = (bf16[16,6144]{1,0:T(8,128)(2,1)S(1)}, bf16[16,6144]{1,0:T(8,128)(2,1)S(1)}, u32[]{:S(2)}, u32[]{:S(2)}) collective-permute-start(bf16[16,6144]{1,0:T(8,128)(2,1)S(1)} %get-tuple-element.7), channel_id=1, source_target_pairs={{0,12},{1,13},{2,14},{3,15},{4,0},{5,1},{6,2},{7,3},{8,4},{9,5},{1... | collective-permute-start | bytes 589832 | tf_op jit(solution)/shard_map/ppermute | solution.py:15
  81.9 41.8 %collective-permute-start.14 = (bf16[16,6144]{1,0:T(8,128)(2,1)S(1)}, bf16[16,6144]{1,0:T(8,128)(2,1)S(1)}, u32[]{:S(2)}, u32[]{:S(2)}) collective-permute-start(bf16[16,6144]{1,0:T(8,128)(2,1)S(1)} %get-tuple-element.11), channel_id=1, source_target_pairs={{0,8},{1,9},{2,10},{3,11},{4,12},{5,13},{6,14},{7,15},{8,0},{9,1},... | collective-permute-start | bytes 589832 | tf_op jit(solution)/shard_map/ppermute | solution.py:15
  86.5 22.2 %collective-permute-start.15 = (bf16[32,6144]{1,0:T(8,128)(2,1)S(1)}, bf16[32,6144]{1,0:T(8,128)(2,1)S(1)}, u32[]{:S(2)}, u32[]{:S(2)}) collective-permute-start(bf16[32,6144]{1,0:T(8,128)(2,1)S(1)} %get-tuple-element.13), channel_id=1, source_target_pairs={{0,12},{1,13},{2,14},{3,15},{4,0},{5,1},{6,2},{7,3},{8,4},{9,5},{1... | collective-permute-start | bytes 1179656 | tf_op jit(solution)/shard_map/ppermute | solution.py:15
  87.1 28.9 %collective-permute-start.17 = (bf16[32,6144]{1,0:T(8,128)(2,1)S(1)}, bf16[32,6144]{1,0:T(8,128)(2,1)S(1)}, u32[]{:S(2)}, u32[]{:S(2)}) collective-permute-start(bf16[32,6144]{1,0:T(8,128)(2,1)S(1)} %get-tuple-element.14), channel_id=1, source_target_pairs={{0,8},{1,9},{2,10},{3,11},{4,12},{5,13},{6,14},{7,15},{8,0},{9,1},... | collective-permute-start | bytes 1179656 | tf_op jit(solution)/shard_map/ppermute | solution.py:15
  91.7 28.2 %collective-permute-start.16 = (bf16[32,6144]{1,0:T(8,128)(2,1)S(1)}, bf16[32,6144]{1,0:T(8,128)(2,1)S(1)}, u32[]{:S(2)}, u32[]{:S(2)}) collective-permute-start(bf16[32,6144]{1,0:T(8,128)(2,1)S(1)} %get-tuple-element.15), channel_id=1, source_target_pairs={{0,4},{1,5},{2,6},{3,7},{4,8},{5,9},{6,10},{7,11},{8,12},{9,13},{1... | collective-permute-start | bytes 1179656 | tf_op jit(solution)/shard_map/ppermute | solution.py:15
  108.7 15.1 %collective-permute-start.13 = (bf16[16,6144]{1,0:T(8,128)(2,1)S(1)}, bf16[16,6144]{1,0:T(8,128)(2,1)S(1)}, u32[]{:S(2)}, u32[]{:S(2)}) collective-permute-start(bf16[16,6144]{1,0:T(8,128)(2,1)S(1)} %get-tuple-element.12), channel_id=1, source_target_pairs={{0,4},{1,5},{2,6},{3,7},{4,8},{5,9},{6,10},{7,11},{8,12},{9,13},{1... | collective-permute-start | bytes 589832 | tf_op jit(solution)/shard_map/ppermute | solution.py:15
  116.0 11.5 %collective-permute-start.23 = (bf16[16,6144]{1,0:T(8,128)(2,1)S(1)}, bf16[16,6144]{1,0:T(8,128)(2,1)S(1)}, u32[]{:S(2)}, u32[]{:S(2)}) collective-permute-start(bf16[16,6144]{1,0:T(8,128)(2,1)S(1)} %fusion.11), channel_id=1, source_target_pairs={{0,2},{1,3},{2,0},{3,1},{4,6},{5,7},{6,4},{7,5},{8,10},{9,11},{10,... | collective-permute-start | bytes 589832 | tf_op jit(solution)/shard_map/ppermute | solution.py:15
  121.3 10.8 %collective-permute-start.18 = (bf16[16,6144]{1,0:T(8,128)(2,1)S(1)}, bf16[16,6144]{1,0:T(8,128)(2,1)S(1)}, u32[]{:S(2)}, u32[]{:S(2)}) collective-permute-start(bf16[16,6144]{1,0:T(8,128)(2,1)S(1)} %get-tuple-element.16), channel_id=1, source_target_pairs={{0,3},{1,0},{2,1},{3,2},{4,7},{5,4},{6,5},{7,6},{8,11},{9,8},{10,9... | collective-permute-start | bytes 589832 | tf_op jit(solution)/shard_map/ppermute | solution.py:15
  123.2 16.8 %collective-permute-start.19 = (bf16[16,6144]{1,0:T(8,128)(2,1)S(1)}, bf16[16,6144]{1,0:T(8,128)(2,1)S(1)}, u32[]{:S(2)}, u32[]{:S(2)}) collective-permute-start(bf16[16,6144]{1,0:T(8,128)(2,1)S(1)} %get-tuple-element.17), channel_id=1, source_target_pairs={{0,1},{1,2},{2,3},{3,0},{4,5},{5,6},{6,7},{7,4},{8,9},{9,10},{10,1... | collective-permute-start | bytes 589832 | tf_op jit(solution)/shard_map/ppermute | solution.py:15

commit v2 on v0

v2 whole, which is shorter than its diff:
```python
import jax
import jax.numpy as jnp
from jax import lax
from jax.experimental import pallas as pl
from jax.experimental.pallas import tpu as pltpu
from jax.sharding import PartitionSpec as P

SIDE = 4


def shift(block, dx, dz):
    pairs = [
        (x * SIDE + z, (x + dx) % SIDE * SIDE + (z + dz) % SIDE)
        for x in range(SIDE)
        for z in range(SIDE)
    ]
    return lax.ppermute(block, "tensor", pairs)


def b16(v):
    return v.astype(jnp.bfloat16)


def f32(v):
    return v.astype(jnp.float32)


def rms_normed(rows_in, norm_gain):
    rows = f32(rows_in)
    scale = lax.rsqrt(jnp.mean(rows * rows, axis=1, keepdims=True) + 1e-05)
    return b16(rows * scale * norm_gain)


def swiglu(n, *refs):
    ins, (gate_w, up_w, down_w), outs, (rows, hidden) = refs[:15], refs[15:18], refs[18:-2], refs[-2:]
    plain, (two_up, two_down, below_2, above_2, far_2up, far_2down) = ins[:9], ins[9:]
    own_here, own_left, own_right, near_here, near_left, near_right, far_here, far_left, far_right = outs[:9]
    out_up, out_down = outs[9:]
    d = rows.shape[1]
    half = d // 2
    for ref, at in zip(plain, (0, 1, 2, 4, 5, 6, 8, 13, 14), strict=True):
        rows[at * n : at * n + ref.shape[0], :] = ref[...]
    rows[3 * n : 4 * n, :half] = two_up[:, d:]
    rows[3 * n : 4 * n, half:] = two_down[:, d:]
    rows[10 * n : 11 * n, :] = two_up[:, :d]
    rows[11 * n : 12 * n, :] = two_down[:, :d]
    rows[12 * n : 13 * n, :half] = below_2[...]
    rows[12 * n : 13 * n, half:] = above_2[...]
    rows[15 * n :, :half] = far_2up[...]
    rows[15 * n :, half:] = far_2down[...]

    def units(start, size):
        cut = pl.ds(start, size)
        gate = jnp.dot(rows[...], gate_w[:, cut], preferred_element_type=jnp.float32)
        up = jnp.dot(rows[...], up_w[:, cut], preferred_element_type=jnp.float32)
        hidden[:, cut] = b16(gate / (1.0 + jnp.exp(-gate)) * up)

    step = 1024
    units(0, gate_w.shape[1])

    def columns(start, second):
        cut = pl.ds(start, step)
        terms = jnp.dot(hidden[...], down_w[:, cut], preferred_element_type=jnp.float32)

        def part(i, k=1):
            return terms[i * n : (i + k) * n]

        own_here[:, cut] = part(0)
        near_here[:, cut] = part(4, 2)
        far_here[:, cut] = part(12)
        near_left[:, cut] = part(6, 2)
        near_right[:, cut] = part(8, 2)
        own_left[:, cut] = part(1)
        own_right[:, cut] = part(2)
        far_left[:, cut] = part(13)
        far_right[:, cut] = part(14)
        out_up[:, cut] = b16(part(10))
        out_down[:, cut] = b16(part(11))
        if second:
            out_down[:, pl.ds(start + half, step)] = b16(part(3))
            out_down[:, pl.ds(start + d, step)] = b16(part(15))
        else:
            out_up[:, pl.ds(start + d, step)] = b16(part(3))
            out_up[:, pl.ds(start + d + half, step)] = b16(part(15))

    for second in (False, True):

        @pl.loop(0, half // step)
        def _(i):
            columns(pl.multiple_of(i * step, step) + second * half, second)


def block_terms(blocks):
    n, d = blocks[0].shape
    ff = blocks[-1].shape[0]
    b, f, h = jnp.bfloat16, jnp.float32, d // 2
    shapes = [
        (n, d, f), (n, d, f), (n, d, f), (2 * n, d, f), (2 * n, d, f), (2 * n, d, f),
        (n, d, f), (n, d, f), (n, d, f), (n, 2 * d, b), (n, 2 * d, b),
    ]
    vmem = pl.BlockSpec(memory_space=pltpu.VMEM)
    return pl.pallas_call(
        lambda *refs: swiglu(n, *refs),
        out_shape=[jax.ShapeDtypeStruct(s[:2], s[2]) for s in shapes],
        in_specs=[vmem] * len(blocks),
        out_specs=[vmem] * len(shapes),
        scratch_shapes=[pltpu.VMEM((16 * n, d), b), pltpu.VMEM((16 * n, ff), b)],
        compiler_params=pltpu.CompilerParams(vmem_limit_bytes=14 * 1024 * 1024),
        cost_estimate=pl.CostEstimate(flops=6 * 16 * n * d * ff, bytes_accessed=6 * d * ff, transcendentals=16 * n * ff),
    )(*[pltpu.with_memory_space_constraint(b, pltpu.VMEM) for b in blocks])


def fetched(weight):
    def kernel(source, target, done):
        copy = pltpu.make_async_copy(source, target, done)
        copy.start()
        copy.wait()

    return pl.pallas_call(
        kernel,
        out_shape=pltpu.VMEM(weight.shape, weight.dtype),
        in_specs=[pl.BlockSpec(memory_space=pltpu.HBM)],
        out_specs=pl.BlockSpec(memory_space=pltpu.VMEM),
        scratch_shapes=[pltpu.SemaphoreType.DMA],
        compiler_params=pltpu.CompilerParams(vmem_limit_bytes=1024 * 1024),
        cost_estimate=pl.CostEstimate(flops=0, bytes_accessed=2 * weight.size, transcendentals=0),
    )(pltpu.with_memory_space_constraint(weight, pltpu.HBM))


def gathered(own, gate_weight, up_weight, down_weight):
    n, d = own.shape
    h = d // 2
    below, above = shift(own, 0, 1), shift(own, 0, -1)
    own_l, own_r = shift(own, 1, 0), shift(own, -1, 0)
    gate_weight = fetched(gate_weight)
    near, own_l, own_r, gate_weight = lax.optimization_barrier((jnp.concatenate([below, above], 0), own_l, own_r, gate_weight))
    below_2, above_2 = shift(below[:, :h], 0, 1), shift(above[:, h:], 0, -1)
    near_l, near_r = shift(near, 1, 0), shift(near, -1, 0)
    up_weight = fetched(up_weight)
    far, up_weight = lax.optimization_barrier((jnp.concatenate([below_2, above_2], 1), up_weight))
    far_l, far_r = shift(far, 1, 0), shift(far, -1, 0)
    two_up = shift(jnp.concatenate([near_l[:n], own_l[:, :h]], 1), 1, 0)
    two_down = shift(jnp.concatenate([near_r[n:], own_r[:, h:]], 1), -1, 0)
    far_2up, far_2down = shift(far_l[:, :h], 1, 0), shift(far_r[:, h:], -1, 0)
    return [
        own, own_l, own_r, below, above, near_l, near_r, far_l, far_r,
        two_up, two_down, below_2, above_2, far_2up, far_2down, gate_weight, up_weight, fetched(down_weight),
    ]


def returned(own_here, own_left, own_right, near_here, near_left, near_right, far_here, far_left, far_right, two_up, two_down):
    n, d = own_here.shape
    h = d // 2
    two_up, two_down = shift(two_up, 1, 0), shift(two_down, -1, 0)
    far_up, far_down = two_up[:, d + h :], two_down[:, d + h :]
    far_right = jnp.concatenate([b16(far_right[:, :h] + f32(far_up)), b16(far_right[:, h:])], 1)
    far_left = jnp.concatenate([b16(far_left[:, :h]), b16(far_left[:, h:] + f32(far_down))], 1)
    far_p, far_m = shift(far_right, 1, 0), shift(far_left, -1, 0)
    near_right = jnp.concatenate([b16(near_right[:n] + f32(two_up[:, :d])), b16(near_right[n:])], 0)
    near_left = jnp.concatenate([b16(near_left[:n]), b16(near_left[n:] + f32(two_down[:, :d]))], 0)
    near_p, near_m = shift(near_right, 1, 0), shift(near_left, -1, 0)
    own_right = jnp.concatenate([b16(own_right[:, :h] + f32(two_up[:, d : d + h])), b16(own_right[:, h:])], 1)
    own_left = jnp.concatenate([b16(own_left[:, :h]), b16(own_left[:, h:] + f32(two_down[:, d : d + h]))], 1)
    own_right, own_left, far_p, far_m = lax.optimization_barrier((own_right, own_left, far_p, far_m))
    own_p, own_m = shift(own_right, 1, 0), shift(own_left, -1, 0)
    far_sum = b16(far_here + f32(far_p) + f32(far_m))
    by_above, by_below = shift(far_sum[:, :h], 0, 1), shift(far_sum[:, h:], 0, -1)
    near_sum = near_here + f32(near_p) + f32(near_m)
    below_sum, above_sum = near_sum[:n], near_sum[n:]
    above_sum = jnp.concatenate([b16(above_sum[:, :h] + f32(by_above)), b16(above_sum[:, h:])], 1)
    below_sum = jnp.concatenate([b16(below_sum[:, :h]), b16(below_sum[:, h:] + f32(by_below))], 1)
    from_below, from_above = shift(above_sum, 0, 1), shift(below_sum, 0, -1)
    return own_here + f32(own_p) + f32(own_m) + f32(from_below) + f32(from_above)


def on_device(tokens, norm_gain, gate_weight, up_weight, down_weight):
    own = rms_normed(tokens, norm_gain)
    terms = block_terms(gathered(own, gate_weight, up_weight, down_weight))
    return b16(f32(tokens) + returned(*terms))


def solution(mesh):
    return jax.shard_map(
        on_device,
        mesh=mesh,
        in_specs=(
            P(("dp", "tensor"), None),
            P(),
            P(None, "tensor"),
            P(None, "tensor"),
            P("tensor", None),
        ),
        out_specs=P(("dp", "tensor"), None),
        check_vma=False,
    )
```

time: 226 us -> 106 us (0.47)
  waiting for transfers between devices: 181 us -> 28 us
  starting transfers between devices: 0.04 us -> 50.4 us
  matrix products: 26.7 us -> 0 us
  Pallas kernels: 0 us -> 23.4 us
  between operations: 13.4 us -> 0.38 us
    reduce_scatter x1 -> x0, waiting for transfers between devices: 107 us -> none  [on_device(): mine = lax.psum_scatter(terms, 'tensor', scatter_dimension=0, tiled=True)]
    all_gather x1 -> x0, waiting for transfers between devices: 73.1 us -> none  [on_device(): lax.all_gather(tokens, 'tensor', axis=0, tiled=True)]
    ppermute x0 -> x26, starting transfers between devices: none -> 50.4 us  [shift(): return lax.ppermute(block, 'tensor', pairs)]
    ppermute x0 -> x26, waiting for transfers between devices: none -> 28 us  [shift(): return lax.ppermute(block, 'tensor', pairs)]
    dot_general x2 -> x0, matrix products: 26.7 us -> none  [the longest x1 17 us: block_terms(): return jnp.dot(hidden, down_weight, preferred_element_type=jnp.float32)]
    pallas_call x0 -> x4, Pallas kernels: none -> 23.4 us  [the longest x3 12.4 us: fetched(): pl.pallas_call(kernel, out_shape=pltpu.VMEM(weight.shape, weight.dtype),...]
  transfers between devices with their start and end apart: 2 -> 26, of which waited for: 2 -> 10; matrix products, arithmetic and copies ran while one was open for 0% -> 1% of each run, Pallas kernels for 0% -> 12%
where the time goes in v2:
time: 106 us
  starting transfers between devices  50.4 us (48%)
  waiting for transfers between devices  28 us (26%)
  Pallas kernels  23.4 us (22%)
  other arithmetic  3.56 us (3%)
    ppermute x26, starting transfers between devices, shift(): return lax.ppermute(block, 'tensor', pairs)  50.4 us
    ppermute x26, waiting for transfers between devices, shift(): return lax.ppermute(block, 'tensor', pairs)  28 us
    pallas_call x3, Pallas kernels, fetched(): pl.pallas_call(kernel, out_shape=pltpu.VMEM(weight.shape, weight.dtype),...  12.4 us
    pallas_call x1, Pallas kernels, block_terms(): pl.pallas_call(lambda *refs: swiglu(n, *refs), out_shape=[jax.ShapeDtypeS...  11 us
  transfers between devices with their start and end apart: 26, of which 10 were waited for; matrix products, arithmetic and copies ran while one was open for 1% of the time, Pallas kernels for 12%

profile of v2, /device:TPU:8, one launch (start us, length us, event | category | flops | bytes accessed | tf_op | source)
XLA Modules:
  0.0 105.9 jit_solution(8028643160044219705)
XLA Ops:
  0.0 1.1 %fusion = f32[16]{0:T(128)S(1)} fusion(bf16[16,6144]{1,0:T(8,128)(2,1)} %param.5), kind=kLoop, calls=%fused_computation.4 | loop fusion | flops 294896 | bytes 196672 | tf_op jit(solution)/shard_map/reduce_sum | solution.py:30
  1.1 1.1 fusion.2.refs_0_
  2.2 6.4 %collective-permute-start.1 = (bf16[16,6144]{1,0:T(8,128)(2,1)S(1)}, bf16[16,6144]{1,0:T(8,128)(2,1)S(1)}, u32[]{:S(2)}, u32[]{:S(2)}) collective-permute-start(bf16[16,6144]{1,0:T(8,128)(2,1)S(1)} %fusion.2.refs_0_), channel_id=1, source_target_pairs={{0,3},{1,0},{2,1},{3,2},{4,7},{5,4},{6,5},{7,6},{8,11},{9,8},{10,9... | collective-permute-start | bytes 589832 | tf_op jit(solution)/shard_map/ppermute | solution.py:17
  8.5 0.0 collective-permute-start
  8.5 2.8 %collective-permute-start.3 = (bf16[16,6144]{1,0:T(8,128)(2,1)S(1)}, bf16[16,6144]{1,0:T(8,128)(2,1)S(1)}, u32[]{:S(2)}, u32[]{:S(2)}) collective-permute-start(bf16[16,6144]{1,0:T(8,128)(2,1)S(1)} %fusion.2.refs_0_), channel_id=1, source_target_pairs={{0,12},{1,13},{2,14},{3,15},{4,0},{5,1},{6,2},{7,3},{8,4},{9,5},{1... | collective-permute-start | bytes 589832 | tf_op jit(solution)/shard_map/ppermute | solution.py:17
  11.3 4.1 %shard_map.55.refs_15_ = bf16[6144,896]{1,0:T(8,128)(2,1)S(1)} custom-call(bf16[6144,896]{1,0:T(8,128)(2,1)} %source.3), custom_call_target="tpu_custom_call" | custom-call | bytes 11010048 | tf_op jit(solution)/shard_map/pallas_call | solution.py:119
  15.4 4.1 %shard_map.56.refs_16_ = bf16[6144,896]{1,0:T(8,128)(2,1)S(1)} custom-call(bf16[6144,896]{1,0:T(8,128)(2,1)} %source.4), custom_call_target="tpu_custom_call" | custom-call | bytes 11010048 | tf_op jit(solution)/shard_map/pallas_call | solution.py:119
  19.6 0.0 collective-permute-done.1.refs_4_
  19.6 4.2 %collective-permute-start.7 = (bf16[16,3072]{1,0:T(8,128)(2,1)S(1)}, bf16[16,3072]{1,0:T(8,128)(2,1)S(1)}, u32[]{:S(2)}, u32[]{:S(2)}) collective-permute-start(bf16[16,3072]{1,0:T(8,128)(2,1)S(1)} %slice.143), channel_id=1, source_target_pairs={{0,3},{1,0},{2,1},{3,2},{4,7},{5,4},{6,5},{7,6},{8,11},{9,8},{10,9... | collective-permute-start | bytes 294920 | tf_op jit(solution)/shard_map/ppermute | solution.py:17
  23.8 0.0 collective-permute-done.refs_3_
  23.8 0.1 collective-permute-start.6
  24.0 0.0 collective-permute-done.3.refs_2_
  24.0 0.0 collective-permute-done.2.refs_1_
  24.0 3.3 %collective-permute-start.5 = (bf16[32,6144]{1,0:T(8,128)(2,1)S(1)}, bf16[32,6144]{1,0:T(8,128)(2,1)S(1)}, u32[]{:S(2)}, u32[]{:S(2)}) collective-permute-start(bf16[32,6144]{1,0:T(8,128)(2,1)S(1)} %pad_maximum_fusion), channel_id=1, source_target_pairs={{0,12},{1,13},{2,14},{3,15},{4,0},{5,1},{6,2},{7,3},{8,4},{9,5},{1... | collective-permute-start | bytes 1179656 | tf_op jit(solution)/shard_map/ppermute | solution.py:17
  27.3 0.0 collective-permute-start.4
  27.3 0.4 collective-permute-done.7.refs_12_
  27.8 2.9 %collective-permute-done.6.refs_11_ = bf16[16,3072]{1,0:T(8,128)(2,1)S(1)} collective-permute-done((bf16[16,3072]{1,0:T(8,128)(2,1)S(1)}, bf16[16,3072]{1,0:T(8,128)(2,1)S(1)}, u32[]{:S(2)}, u32[]{:S(2)}) %collective-permute-start.6) | collective-permute-done | bytes 98336 | tf_op jit(solution)/shard_map/ppermute | solution.py:17
  30.7 3.3 %collective-permute-start.9 = (bf16[16,6144]{1,0:T(8,128)(2,1)S(1)}, bf16[16,6144]{1,0:T(8,128)(2,1)S(1)}, u32[]{:S(2)}, u32[]{:S(2)}) collective-permute-start(bf16[16,6144]{1,0:T(8,128)(2,1)S(1)} %pad_maximum_fusion.5), channel_id=1, source_target_pairs={{0,12},{1,13},{2,14},{3,15},{4,0},{5,1},{6,2},{7,3},{8,4},{9,5},{1... | collective-permute-start | bytes 589832 | tf_op jit(solution)/shard_map/ppermute | solution.py:17
  34.0 2.0 %collective-permute-done.5.refs_6_ = bf16[32,6144]{1,0:T(8,128)(2,1)S(1)} collective-permute-done((bf16[32,6144]{1,0:T(8,128)(2,1)S(1)}, bf16[32,6144]{1,0:T(8,128)(2,1)S(1)}, u32[]{:S(2)}, u32[]{:S(2)}) %collective-permute-start.5) | collective-permute-done | bytes 393248 | tf_op jit(solution)/shard_map/ppermute | solution.py:17
  36.1 3.8 %collective-permute-start.11 = (bf16[16,9216]{1,0:T(8,128)(2,1)S(1)}, bf16[16,9216]{1,0:T(8,128)(2,1)S(1)}, u32[]{:S(2)}, u32[]{:S(2)}) collective-permute-start(bf16[16,9216]{1,0:T(8,128)(2,1)S(1)} %pad_maximum_fusion.4), channel_id=1, source_target_pairs={{0,12},{1,13},{2,14},{3,15},{4,0},{5,1},{6,2},{7,3},{8,4},{9,5},{1... | collective-permute-start | bytes 884744 | tf_op jit(solution)/shard_map/ppermute | solution.py:17
  39.9 0.1 collective-permute-start.10
  40.0 0.3 collective-permute-done.9.refs_8_
  40.2 3.8 %collective-permute-start.13 = (bf16[16,3072]{1,0:T(8,128)(2,1)S(1)}, bf16[16,3072]{1,0:T(8,128)(2,1)S(1)}, u32[]{:S(2)}, u32[]{:S(2)}) collective-permute-start(bf16[16,3072]{1,0:T(8,128)(2,1)S(1)} %slice.147), channel_id=1, source_target_pairs={{0,12},{1,13},{2,14},{3,15},{4,0},{5,1},{6,2},{7,3},{8,4},{9,5},{1... | collective-permute-start | bytes 294920 | tf_op jit(solution)/shard_map/ppermute | solution.py:17
  44.0 0.3 collective-permute-start.12
  44.3 4.1 %shard_map.57.refs_17_ = bf16[896,6144]{1,0:T(8,128)(2,1)S(1)} custom-call(bf16[896,6144]{1,0:T(8,128)(2,1)} %source.5), custom_call_target="tpu_custom_call" | custom-call | bytes 11010048 | tf_op jit(solution)/shard_map/pallas_call | solution.py:119
  48.4 1.9 %collective-permute-done.12.refs_13_ = bf16[16,3072]{1,0:T(8,128)(2,1)S(1)} collective-permute-done((bf16[16,3072]{1,0:T(8,128)(2,1)S(1)}, bf16[16,3072]{1,0:T(8,128)(2,1)S(1)}, u32[]{:S(2)}, u32[]{:S(2)}) %collective-permute-start.12) | collective-permute-done | bytes 98336 | tf_op jit(solution)/shard_map/ppermute | solution.py:17
  50.3 11.0 %shard_map.58 = (f32[16,6144]{1,0:T(8,128)S(1)}, f32[16,6144]{1,0:T(8,128)S(1)}, f32[16,6144]{1,0:T(8,128)S(1)}, f32[32,6144]{1,0:T(8,128)S(1)}, f32[32,6144]{1,...) custom-call(bf16[16,6144]{1,0:T(8,128)(2,1)S(1)} %fusion.2.refs_0_, ...), custom_call_target="tpu_custom_call" | custom-call | flops 8455716864 | bytes 33030144 | tf_op jit(solution)/shard_map/pallas_call | solution.py:102
  61.3 0.0 copy-start
  61.3 0.1 collective-permute-start.14
  61.5 3.3 %collective-permute-start.15 = (bf16[16,12288]{1,0:T(8,128)(2,1)S(1)}, bf16[16,12288]{1,0:T(8,128)(2,1)S(1)}, u32[]{:S(2)}, u32[]{:S(2)}) collective-permute-start(bf16[16,12288]{1,0:T(8,128)(2,1)S(1)} %get-tuple-element.36), channel_id=1, source_target_pairs={{0,12},{1,13},{2,14},{3,15},{4,0},{5,1},{6,2},{7,3},{8,4},{9,5},{1... | collective-permute-start | bytes 1179656 | tf_op jit(solution)/shard_map/ppermute | solution.py:17
  64.8 6.0 %collective-permute-done.14 = bf16[16,12288]{1,0:T(8,128)(2,1)S(1)} collective-permute-done((bf16[16,12288]{1,0:T(8,128)(2,1)S(1)}, bf16[16,12288]{1,0:T(8,128)(2,1)S(1)}, u32[]{:S(2)}, u32[]{:S(2)}) %collective-permute-start.14) | collective-permute-done | bytes 393248 | tf_op jit(solution)/shard_map/ppermute | solution.py:17
  70.9 0.1 collective-permute-start.16
  71.1 0.1 collective-permute-start.20
  71.2 3.3 %collective-permute-start.17 = (bf16[16,6144]{1,0:T(8,128)(2,1)S(1)}, bf16[16,6144]{1,0:T(8,128)(2,1)S(1)}, u32[]{:S(2)}, u32[]{:S(2)}) collective-permute-start(bf16[16,6144]{1,0:T(8,128)(2,1)S(1)} %pad_maximum_fusion.9), channel_id=1, source_target_pairs={{0,12},{1,13},{2,14},{3,15},{4,0},{5,1},{6,2},{7,3},{8,4},{9,5},{1... | collective-permute-start | bytes 589832 | tf_op jit(solution)/shard_map/ppermute | solution.py:17
  74.6 2.1 %collective-permute-start.21 = (bf16[32,6144]{1,0:T(8,128)(2,1)S(1)}, bf16[32,6144]{1,0:T(8,128)(2,1)S(1)}, u32[]{:S(2)}, u32[]{:S(2)}) collective-permute-start(bf16[32,6144]{1,0:T(8,128)(2,1)S(1)} %pad_maximum_fusion.2), channel_id=1, source_target_pairs={{0,12},{1,13},{2,14},{3,15},{4,0},{5,1},{6,2},{7,3},{8,4},{9,5},{1... | collective-permute-start | bytes 1179656 | tf_op jit(solution)/shard_map/ppermute | solution.py:17
  76.7 2.8 %collective-permute-done.16 = bf16[16,6144]{1,0:T(8,128)(2,1)S(1)} collective-permute-done((bf16[16,6144]{1,0:T(8,128)(2,1)S(1)}, bf16[16,6144]{1,0:T(8,128)(2,1)S(1)}, u32[]{:S(2)}, u32[]{:S(2)}) %collective-permute-start.16) | collective-permute-done | bytes 196640 | tf_op jit(solution)/shard_map/ppermute | solution.py:17
  79.5 0.1 add_convert_fusion
  79.6 2.8 %collective-permute-start.22 = (bf16[16,3072]{1,0:T(8,128)(2,1)S(1)}, bf16[16,3072]{1,0:T(8,128)(2,1)S(1)}, u32[]{:S(2)}, u32[]{:S(2)}) collective-permute-start(bf16[16,3072]{1,0:T(8,128)(2,1)S(1)} %get-tuple-element.57), channel_id=1, source_target_pairs={{0,1},{1,2},{2,3},{3,0},{4,5},{5,6},{6,7},{7,4},{8,9},{9,10},{10,1... | collective-permute-start | bytes 294920 | tf_op jit(solution)/shard_map/ppermute | solution.py:17
  82.4 4.0 %collective-permute-start.24 = (bf16[16,3072]{1,0:T(8,128)(2,1)S(1)}, bf16[16,3072]{1,0:T(8,128)(2,1)S(1)}, u32[]{:S(2)}, u32[]{:S(2)}) collective-permute-start(bf16[16,3072]{1,0:T(8,128)(2,1)S(1)} %get-tuple-element.58), channel_id=1, source_target_pairs={{0,3},{1,0},{2,1},{3,2},{4,7},{5,4},{6,5},{7,6},{8,11},{9,8},{10,9... | collective-permute-start | bytes 294920 | tf_op jit(solution)/shard_map/ppermute | solution.py:17
  86.4 2.5 %collective-permute-start.18 = (bf16[16,6144]{1,0:T(8,128)(2,1)S(1)}, bf16[16,6144]{1,0:T(8,128)(2,1)S(1)}, u32[]{:S(2)}, u32[]{:S(2)}) collective-permute-start(bf16[16,6144]{1,0:T(8,128)(2,1)S(1)} %get-tuple-element.39), channel_id=1, source_target_pairs={{0,4},{1,5},{2,6},{3,7},{4,8},{5,9},{6,10},{7,11},{8,12},{9,13},{1... | collective-permute-start | bytes 589832 | tf_op jit(solution)/shard_map/ppermute | solution.py:17
  88.9 0.8 collective-permute-start.19
  89.7 0.1 fusion.6
  89.8 1.9 %collective-permute-done.22 = bf16[16,3072]{1,0:T(8,128)(2,1)S(1)} collective-permute-done((bf16[16,3072]{1,0:T(8,128)(2,1)S(1)}, bf16[16,3072]{1,0:T(8,128)(2,1)S(1)}, u32[]{:S(2)}, u32[]{:S(2)}) %collective-permute-start.22) | collective-permute-done | bytes 98336 | tf_op jit(solution)/shard_map/ppermute | solution.py:17
  91.8 3.4 %collective-permute-start.25 = (bf16[16,6144]{1,0:T(8,128)(2,1)S(1)}, bf16[16,6144]{1,0:T(8,128)(2,1)S(1)}, u32[]{:S(2)}, u32[]{:S(2)}) collective-permute-start(bf16[16,6144]{1,0:T(8,128)(2,1)S(1)} %pad_maximum_fusion.11), channel_id=1, source_target_pairs={{0,3},{1,0},{2,1},{3,2},{4,7},{5,4},{6,5},{7,6},{8,11},{9,8},{10,9... | collective-permute-start | bytes 589832 | tf_op jit(solution)/shard_map/ppermute | solution.py:17
  95.2 0.1 collective-permute-start.23
  95.3 5.2 %collective-permute-done.25 = bf16[16,6144]{1,0:T(8,128)(2,1)S(1)} collective-permute-done((bf16[16,6144]{1,0:T(8,128)(2,1)S(1)}, bf16[16,6144]{1,0:T(8,128)(2,1)S(1)}, u32[]{:S(2)}, u32[]{:S(2)}) %collective-permute-start.25) | collective-permute-done | bytes 196640 | tf_op jit(solution)/shard_map/ppermute | solution.py:17
  100.5 4.6 %collective-permute-done.23 = bf16[16,6144]{1,0:T(8,128)(2,1)S(1)} collective-permute-done((bf16[16,6144]{1,0:T(8,128)(2,1)S(1)}, bf16[16,6144]{1,0:T(8,128)(2,1)S(1)}, u32[]{:S(2)}, u32[]{:S(2)}) %collective-permute-start.23) | collective-permute-done | bytes 196640 | tf_op jit(solution)/shard_map/ppermute | solution.py:17
  105.1 0.8 fusion.3
  (48 shorter events, 0.7 us)
Async XLA Ops:
  2.2 17.4 %collective-permute-start.1 = (bf16[16,6144]{1,0:T(8,128)(2,1)S(1)}, bf16[16,6144]{1,0:T(8,128)(2,1)S(1)}, u32[]{:S(2)}, u32[]{:S(2)}) collective-permute-start(bf16[16,6144]{1,0:T(8,128)(2,1)S(1)} %fusion.2.refs_0_), channel_id=1, source_target_pairs={{0,3},{1,0},{2,1},{3,2},{4,7},{5,4},{6,5},{7,6},{8,11},{9,8},{10,9... | collective-permute-start | bytes 589832 | tf_op jit(solution)/shard_map/ppermute | solution.py:17
  8.5 15.3 %collective-permute-start = (bf16[16,6144]{1,0:T(8,128)(2,1)S(1)}, bf16[16,6144]{1,0:T(8,128)(2,1)S(1)}, u32[]{:S(2)}, u32[]{:S(2)}) collective-permute-start(bf16[16,6144]{1,0:T(8,128)(2,1)S(1)} %fusion.2.refs_0_), channel_id=1, source_target_pairs={{0,1},{1,2},{2,3},{3,0},{4,5},{5,6},{6,7},{7,4},{8,9},{9,10},{10,1... | collective-permute-start | bytes 589832 | tf_op jit(solution)/shard_map/ppermute | solution.py:17
  8.5 15.4 %collective-permute-start.3 = (bf16[16,6144]{1,0:T(8,128)(2,1)S(1)}, bf16[16,6144]{1,0:T(8,128)(2,1)S(1)}, u32[]{:S(2)}, u32[]{:S(2)}) collective-permute-start(bf16[16,6144]{1,0:T(8,128)(2,1)S(1)} %fusion.2.refs_0_), channel_id=1, source_target_pairs={{0,12},{1,13},{2,14},{3,15},{4,0},{5,1},{6,2},{7,3},{8,4},{9,5},{1... | collective-permute-start | bytes 589832 | tf_op jit(solution)/shard_map/ppermute | solution.py:17
  11.3 12.7 %collective-permute-start.2 = (bf16[16,6144]{1,0:T(8,128)(2,1)S(1)}, bf16[16,6144]{1,0:T(8,128)(2,1)S(1)}, u32[]{:S(2)}, u32[]{:S(2)}) collective-permute-start(bf16[16,6144]{1,0:T(8,128)(2,1)S(1)} %fusion.2.refs_0_), channel_id=1, source_target_pairs={{0,4},{1,5},{2,6},{3,7},{4,8},{5,9},{6,10},{7,11},{8,12},{9,13},{1... | collective-permute-start | bytes 589832 | tf_op jit(solution)/shard_map/ppermute | solution.py:17
  19.6 8.2 %collective-permute-start.7 = (bf16[16,3072]{1,0:T(8,128)(2,1)S(1)}, bf16[16,3072]{1,0:T(8,128)(2,1)S(1)}, u32[]{:S(2)}, u32[]{:S(2)}) collective-permute-start(bf16[16,3072]{1,0:T(8,128)(2,1)S(1)} %slice.143), channel_id=1, source_target_pairs={{0,3},{1,0},{2,1},{3,2},{4,7},{5,4},{6,5},{7,6},{8,11},{9,8},{10,9... | collective-permute-start | bytes 294920 | tf_op jit(solution)/shard_map/ppermute | solution.py:17
  23.8 6.9 %collective-permute-start.6 = (bf16[16,3072]{1,0:T(8,128)(2,1)S(1)}, bf16[16,3072]{1,0:T(8,128)(2,1)S(1)}, u32[]{:S(2)}, u32[]{:S(2)}) collective-permute-start(bf16[16,3072]{1,0:T(8,128)(2,1)S(1)} %slice.142), channel_id=1, source_target_pairs={{0,1},{1,2},{2,3},{3,0},{4,5},{5,6},{6,7},{7,4},{8,9},{9,10},{10,1... | collective-permute-start | bytes 294920 | tf_op jit(solution)/shard_map/ppermute | solution.py:17
  24.0 12.0 %collective-permute-start.5 = (bf16[32,6144]{1,0:T(8,128)(2,1)S(1)}, bf16[32,6144]{1,0:T(8,128)(2,1)S(1)}, u32[]{:S(2)}, u32[]{:S(2)}) collective-permute-start(bf16[32,6144]{1,0:T(8,128)(2,1)S(1)} %pad_maximum_fusion), channel_id=1, source_target_pairs={{0,12},{1,13},{2,14},{3,15},{4,0},{5,1},{6,2},{7,3},{8,4},{9,5},{1... | collective-permute-start | bytes 1179656 | tf_op jit(solution)/shard_map/ppermute | solution.py:17
  27.3 12.5 %collective-permute-start.4 = (bf16[32,6144]{1,0:T(8,128)(2,1)S(1)}, bf16[32,6144]{1,0:T(8,128)(2,1)S(1)}, u32[]{:S(2)}, u32[]{:S(2)}) collective-permute-start(bf16[32,6144]{1,0:T(8,128)(2,1)S(1)} %pad_maximum_fusion), channel_id=1, source_target_pairs={{0,4},{1,5},{2,6},{3,7},{4,8},{5,9},{6,10},{7,11},{8,12},{9,13},{1... | collective-permute-start | bytes 1179656 | tf_op jit(solution)/shard_map/ppermute | solution.py:17
  30.7 9.5 %collective-permute-start.9 = (bf16[16,6144]{1,0:T(8,128)(2,1)S(1)}, bf16[16,6144]{1,0:T(8,128)(2,1)S(1)}, u32[]{:S(2)}, u32[]{:S(2)}) collective-permute-start(bf16[16,6144]{1,0:T(8,128)(2,1)S(1)} %pad_maximum_fusion.5), channel_id=1, source_target_pairs={{0,12},{1,13},{2,14},{3,15},{4,0},{5,1},{6,2},{7,3},{8,4},{9,5},{1... | collective-permute-start | bytes 589832 | tf_op jit(solution)/shard_map/ppermute | solution.py:17
  34.0 10.0 %collective-permute-start.8 = (bf16[16,6144]{1,0:T(8,128)(2,1)S(1)}, bf16[16,6144]{1,0:T(8,128)(2,1)S(1)}, u32[]{:S(2)}, u32[]{:S(2)}) collective-permute-start(bf16[16,6144]{1,0:T(8,128)(2,1)S(1)} %pad_maximum_fusion.5), channel_id=1, source_target_pairs={{0,4},{1,5},{2,6},{3,7},{4,8},{5,9},{6,10},{7,11},{8,12},{9,13},{1... | collective-permute-start | bytes 589832 | tf_op jit(solution)/shard_map/ppermute | solution.py:17
  36.1 14.3 %collective-permute-start.11 = (bf16[16,9216]{1,0:T(8,128)(2,1)S(1)}, bf16[16,9216]{1,0:T(8,128)(2,1)S(1)}, u32[]{:S(2)}, u32[]{:S(2)}) collective-permute-start(bf16[16,9216]{1,0:T(8,128)(2,1)S(1)} %pad_maximum_fusion.4), channel_id=1, source_target_pairs={{0,12},{1,13},{2,14},{3,15},{4,0},{5,1},{6,2},{7,3},{8,4},{9,5},{1... | collective-permute-start | bytes 884744 | tf_op jit(solution)/shard_map/ppermute | solution.py:17
  39.9 10.5 %collective-permute-start.10 = (bf16[16,9216]{1,0:T(8,128)(2,1)S(1)}, bf16[16,9216]{1,0:T(8,128)(2,1)S(1)}, u32[]{:S(2)}, u32[]{:S(2)}) collective-permute-start(bf16[16,9216]{1,0:T(8,128)(2,1)S(1)} %pad_maximum_fusion.3), channel_id=1, source_target_pairs={{0,4},{1,5},{2,6},{3,7},{4,8},{5,9},{6,10},{7,11},{8,12},{9,13},{1... | collective-permute-start | bytes 884744 | tf_op jit(solution)/shard_map/ppermute | solution.py:17
  40.2 8.2 %collective-permute-start.13 = (bf16[16,3072]{1,0:T(8,128)(2,1)S(1)}, bf16[16,3072]{1,0:T(8,128)(2,1)S(1)}, u32[]{:S(2)}, u32[]{:S(2)}) collective-permute-start(bf16[16,3072]{1,0:T(8,128)(2,1)S(1)} %slice.147), channel_id=1, source_target_pairs={{0,12},{1,13},{2,14},{3,15},{4,0},{5,1},{6,2},{7,3},{8,4},{9,5},{1... | collective-permute-start | bytes 294920 | tf_op jit(solution)/shard_map/ppermute | solution.py:17
  44.0 6.3 %collective-permute-start.12 = (bf16[16,3072]{1,0:T(8,128)(2,1)S(1)}, bf16[16,3072]{1,0:T(8,128)(2,1)S(1)}, u32[]{:S(2)}, u32[]{:S(2)}) collective-permute-start(bf16[16,3072]{1,0:T(8,128)(2,1)S(1)} %slice.146), channel_id=1, source_target_pairs={{0,4},{1,5},{2,6},{3,7},{4,8},{5,9},{6,10},{7,11},{8,12},{9,13},{1... | collective-permute-start | bytes 294920 | tf_op jit(solution)/shard_map/ppermute | solution.py:17
  61.3 43.8 %copy-start = (bf16[16,6144]{1,0:T(8,128)(2,1)S(1)}, bf16[16,6144]{1,0:T(8,128)(2,1)}, u32[]{:S(2)}) copy-start(bf16[16,6144]{1,0:T(8,128)(2,1)} %param.5) | copy-start | bytes 589828
  61.3 9.5 %collective-permute-start.14 = (bf16[16,12288]{1,0:T(8,128)(2,1)S(1)}, bf16[16,12288]{1,0:T(8,128)(2,1)S(1)}, u32[]{:S(2)}, u32[]{:S(2)}) collective-permute-start(bf16[16,12288]{1,0:T(8,128)(2,1)S(1)} %get-tuple-element.34), channel_id=1, source_target_pairs={{0,4},{1,5},{2,6},{3,7},{4,8},{5,9},{6,10},{7,11},{8,12},{9,13},{1... | collective-permute-start | bytes 1179656 | tf_op jit(solution)/shard_map/ppermute | solution.py:17
  61.5 9.6 %collective-permute-start.15 = (bf16[16,12288]{1,0:T(8,128)(2,1)S(1)}, bf16[16,12288]{1,0:T(8,128)(2,1)S(1)}, u32[]{:S(2)}, u32[]{:S(2)}) collective-permute-start(bf16[16,12288]{1,0:T(8,128)(2,1)S(1)} %get-tuple-element.36), channel_id=1, source_target_pairs={{0,12},{1,13},{2,14},{3,15},{4,0},{5,1},{6,2},{7,3},{8,4},{9,5},{1... | collective-permute-start | bytes 1179656 | tf_op jit(solution)/shard_map/ppermute | solution.py:17
  70.9 8.6 %collective-permute-start.16 = (bf16[16,6144]{1,0:T(8,128)(2,1)S(1)}, bf16[16,6144]{1,0:T(8,128)(2,1)S(1)}, u32[]{:S(2)}, u32[]{:S(2)}) collective-permute-start(bf16[16,6144]{1,0:T(8,128)(2,1)S(1)} %pad_maximum_fusion.8), channel_id=1, source_target_pairs={{0,4},{1,5},{2,6},{3,7},{4,8},{5,9},{6,10},{7,11},{8,12},{9,13},{1... | collective-permute-start | bytes 589832 | tf_op jit(solution)/shard_map/ppermute | solution.py:17
  71.1 17.8 %collective-permute-start.20 = (bf16[32,6144]{1,0:T(8,128)(2,1)S(1)}, bf16[32,6144]{1,0:T(8,128)(2,1)S(1)}, u32[]{:S(2)}, u32[]{:S(2)}) collective-permute-start(bf16[32,6144]{1,0:T(8,128)(2,1)S(1)} %pad_maximum_fusion.1), channel_id=1, source_target_pairs={{0,4},{1,5},{2,6},{3,7},{4,8},{5,9},{6,10},{7,11},{8,12},{9,13},{1... | collective-permute-start | bytes 1179656 | tf_op jit(solution)/shard_map/ppermute | solution.py:17
  71.2 8.3 %collective-permute-start.17 = (bf16[16,6144]{1,0:T(8,128)(2,1)S(1)}, bf16[16,6144]{1,0:T(8,128)(2,1)S(1)}, u32[]{:S(2)}, u32[]{:S(2)}) collective-permute-start(bf16[16,6144]{1,0:T(8,128)(2,1)S(1)} %pad_maximum_fusion.9), channel_id=1, source_target_pairs={{0,12},{1,13},{2,14},{3,15},{4,0},{5,1},{6,2},{7,3},{8,4},{9,5},{1... | collective-permute-start | bytes 589832 | tf_op jit(solution)/shard_map/ppermute | solution.py:17
  74.6 15.1 %collective-permute-start.21 = (bf16[32,6144]{1,0:T(8,128)(2,1)S(1)}, bf16[32,6144]{1,0:T(8,128)(2,1)S(1)}, u32[]{:S(2)}, u32[]{:S(2)}) collective-permute-start(bf16[32,6144]{1,0:T(8,128)(2,1)S(1)} %pad_maximum_fusion.2), channel_id=1, source_target_pairs={{0,12},{1,13},{2,14},{3,15},{4,0},{5,1},{6,2},{7,3},{8,4},{9,5},{1... | collective-permute-start | bytes 1179656 | tf_op jit(solution)/shard_map/ppermute | solution.py:17
  79.6 12.1 %collective-permute-start.22 = (bf16[16,3072]{1,0:T(8,128)(2,1)S(1)}, bf16[16,3072]{1,0:T(8,128)(2,1)S(1)}, u32[]{:S(2)}, u32[]{:S(2)}) collective-permute-start(bf16[16,3072]{1,0:T(8,128)(2,1)S(1)} %get-tuple-element.57), channel_id=1, source_target_pairs={{0,1},{1,2},{2,3},{3,0},{4,5},{5,6},{6,7},{7,4},{8,9},{9,10},{10,1... | collective-permute-start | bytes 294920 | tf_op jit(solution)/shard_map/ppermute | solution.py:17
  82.4 9.3 %collective-permute-start.24 = (bf16[16,3072]{1,0:T(8,128)(2,1)S(1)}, bf16[16,3072]{1,0:T(8,128)(2,1)S(1)}, u32[]{:S(2)}, u32[]{:S(2)}) collective-permute-start(bf16[16,3072]{1,0:T(8,128)(2,1)S(1)} %get-tuple-element.58), channel_id=1, source_target_pairs={{0,3},{1,0},{2,1},{3,2},{4,7},{5,4},{6,5},{7,6},{8,11},{9,8},{10,9... | collective-permute-start | bytes 294920 | tf_op jit(solution)/shard_map/ppermute | solution.py:17
  86.4 8.8 %collective-permute-start.18 = (bf16[16,6144]{1,0:T(8,128)(2,1)S(1)}, bf16[16,6144]{1,0:T(8,128)(2,1)S(1)}, u32[]{:S(2)}, u32[]{:S(2)}) collective-permute-start(bf16[16,6144]{1,0:T(8,128)(2,1)S(1)} %get-tuple-element.39), channel_id=1, source_target_pairs={{0,4},{1,5},{2,6},{3,7},{4,8},{5,9},{6,10},{7,11},{8,12},{9,13},{1... | collective-permute-start | bytes 589832 | tf_op jit(solution)/shard_map/ppermute | solution.py:17
  88.9 6.4 %collective-permute-start.19 = (bf16[16,6144]{1,0:T(8,128)(2,1)S(1)}, bf16[16,6144]{1,0:T(8,128)(2,1)S(1)}, u32[]{:S(2)}, u32[]{:S(2)}) collective-permute-start(bf16[16,6144]{1,0:T(8,128)(2,1)S(1)} %get-tuple-element.40), channel_id=1, source_target_pairs={{0,12},{1,13},{2,14},{3,15},{4,0},{5,1},{6,2},{7,3},{8,4},{9,5},{1... | collective-permute-start | bytes 589832 | tf_op jit(solution)/shard_map/ppermute | solution.py:17
  91.8 8.7 %collective-permute-start.25 = (bf16[16,6144]{1,0:T(8,128)(2,1)S(1)}, bf16[16,6144]{1,0:T(8,128)(2,1)S(1)}, u32[]{:S(2)}, u32[]{:S(2)}) collective-permute-start(bf16[16,6144]{1,0:T(8,128)(2,1)S(1)} %pad_maximum_fusion.11), channel_id=1, source_target_pairs={{0,3},{1,0},{2,1},{3,2},{4,7},{5,4},{6,5},{7,6},{8,11},{9,8},{10,9... | collective-permute-start | bytes 589832 | tf_op jit(solution)/shard_map/ppermute | solution.py:17
  95.2 9.9 %collective-permute-start.23 = (bf16[16,6144]{1,0:T(8,128)(2,1)S(1)}, bf16[16,6144]{1,0:T(8,128)(2,1)S(1)}, u32[]{:S(2)}, u32[]{:S(2)}) collective-permute-start(bf16[16,6144]{1,0:T(8,128)(2,1)S(1)} %pad_maximum_fusion.10), channel_id=1, source_target_pairs={{0,1},{1,2},{2,3},{3,0},{4,5},{5,6},{6,7},{7,4},{8,9},{9,10},{10,1... | collective-permute-start | bytes 589832 | tf_op jit(solution)/shard_map/ppermute | solution.py:17

commit v3 on v2

--- a/solution.py
+++ b/solution.py
@@ -25,14 +25,24 @@
     return v.astype(jnp.float32)
 
 
-def rms_normed(rows_in, norm_gain):
-    rows = f32(rows_in)
-    scale = lax.rsqrt(jnp.mean(rows * rows, axis=1, keepdims=True) + 1e-05)
-    return b16(rows * scale * norm_gain)
+def rms_normed(rows, gain):
+    def kernel(rows_ref, gain_ref, out_ref):
+        held = f32(rows_ref[...])
+        scale = lax.rsqrt(jnp.mean(held * held, axis=1, keepdims=True) + 1e-05)
+        out_ref[...] = b16(held * scale * gain_ref[...])
+
+    vmem = pl.BlockSpec(memory_space=pltpu.VMEM)
+    return pl.pallas_call(
+        kernel,
+        out_shape=pltpu.VMEM(rows.shape, jnp.bfloat16),
+        in_specs=[vmem] * 2,
+        out_specs=vmem,
+        compiler_params=pltpu.CompilerParams(vmem_limit_bytes=4 * 1024 * 1024),
+    )(*[pltpu.with_memory_space_constraint(v, pltpu.HBM) for v in (rows, gain.reshape(1, -1))])
 
 
 def swiglu(n, *refs):
-    ins, (gate_w, up_w, down_w), outs, (rows, hidden) = refs[:15], refs[15:18], refs[18:-2], refs[-2:]
+    ins, (gate_w, up_w, up_w2, down_w), outs, (rows, hidden) = refs[:15], refs[15:19], refs[19:-2], refs[-2:]
     plain, (two_up, two_down, below_2, above_2, far_2up, far_2down) = ins[:9], ins[9:]
     own_here, own_left, own_right, near_here, near_left, near_right, far_here, far_left, far_right = outs[:9]
     out_up, out_down = outs[9:]
@@ -52,7 +62,8 @@
     def units(start, size):
         cut = pl.ds(start, size)
         gate = jnp.dot(rows[...], gate_w[:, cut], preferred_element_type=jnp.float32)
-        up = jnp.dot(rows[...], up_w[:, cut], preferred_element_type=jnp.float32)
+        up = jnp.dot(rows[:, :half], up_w[:, cut], preferred_element_type=jnp.float32)
+        up = up + jnp.dot(rows[:, half:], up_w2[:, cut], preferred_element_type=jnp.float32)
         hidden[:, cut] = b16(gate / (1.0 + jnp.exp(-gate)) * up)
 
     step = 1024
@@ -110,48 +121,51 @@
     )(*[pltpu.with_memory_space_constraint(b, pltpu.VMEM) for b in blocks])
 
 
-def fetched(weight):
+def fetched(weight, part=0, parts=1):
+    size = weight.shape[0] // parts
+
     def kernel(source, target, done):
-        copy = pltpu.make_async_copy(source, target, done)
+        copy = pltpu.make_async_copy(source.at[pl.ds(part * size, size), :], target, done)
         copy.start()
         copy.wait()
 
     return pl.pallas_call(
         kernel,
-        out_shape=pltpu.VMEM(weight.shape, weight.dtype),
+        out_shape=pltpu.VMEM((size, weight.shape[1]), weight.dtype),
         in_specs=[pl.BlockSpec(memory_space=pltpu.HBM)],
         out_specs=pl.BlockSpec(memory_space=pltpu.VMEM),
         scratch_shapes=[pltpu.SemaphoreType.DMA],
         compiler_params=pltpu.CompilerParams(vmem_limit_bytes=1024 * 1024),
-        cost_estimate=pl.CostEstimate(flops=0, bytes_accessed=2 * weight.size, transcendentals=0),
+        cost_estimate=pl.CostEstimate(flops=0, bytes_accessed=2 * size * weight.shape[1], transcendentals=0),
     )(pltpu.with_memory_space_constraint(weight, pltpu.HBM))
 
 
 def gathered(own, gate_weight, up_weight, down_weight):
     n, d = own.shape
     h = d // 2
-    below, above = shift(own, 0, 1), shift(own, 0, -1)
+    below, above = lax.optimization_barrier((shift(own, 0, 1), shift(own, 0, -1)))
     own_l, own_r = shift(own, 1, 0), shift(own, -1, 0)
-    gate_weight = fetched(gate_weight)
-    near, own_l, own_r, gate_weight = lax.optimization_barrier((jnp.concatenate([below, above], 0), own_l, own_r, gate_weight))
+    near = jnp.concatenate([below, above], 0)
+    gate_v, up_v = fetched(gate_weight), fetched(up_weight, 0, 2)
+    near, own_l, own_r, gate_v, up_v, up_weight = lax.optimization_barrier((near, own_l, own_r, gate_v, up_v, up_weight))
     below_2, above_2 = shift(below[:, :h], 0, 1), shift(above[:, h:], 0, -1)
-    near_l, near_r = shift(near, 1, 0), shift(near, -1, 0)
-    up_weight = fetched(up_weight)
-    far, up_weight = lax.optimization_barrier((jnp.concatenate([below_2, above_2], 1), up_weight))
-    far_l, far_r = shift(far, 1, 0), shift(far, -1, 0)
+    near_l, near_r = lax.optimization_barrier((shift(near, 1, 0), shift(near, -1, 0)))
+    far = jnp.concatenate([below_2, above_2], 1)
+    far, up_v2 = lax.optimization_barrier((far, fetched(up_weight, 1, 2)))
+    far_l, far_r = lax.optimization_barrier((shift(far, 1, 0), shift(far, -1, 0)))
     two_up = shift(jnp.concatenate([near_l[:n], own_l[:, :h]], 1), 1, 0)
     two_down = shift(jnp.concatenate([near_r[n:], own_r[:, h:]], 1), -1, 0)
     far_2up, far_2down = shift(far_l[:, :h], 1, 0), shift(far_r[:, h:], -1, 0)
     return [
         own, own_l, own_r, below, above, near_l, near_r, far_l, far_r,
-        two_up, two_down, below_2, above_2, far_2up, far_2down, gate_weight, up_weight, fetched(down_weight),
+        two_up, two_down, below_2, above_2, far_2up, far_2down, gate_v, up_v, up_v2, fetched(down_weight),
     ]
 
 
 def returned(own_here, own_left, own_right, near_here, near_left, near_right, far_here, far_left, far_right, two_up, two_down):
     n, d = own_here.shape
     h = d // 2
-    two_up, two_down = shift(two_up, 1, 0), shift(two_down, -1, 0)
+    two_up, two_down = lax.optimization_barrier((shift(two_up, 1, 0), shift(two_down, -1, 0)))
     far_up, far_down = two_up[:, d + h :], two_down[:, d + h :]
     far_right = jnp.concatenate([b16(far_right[:, :h] + f32(far_up)), b16(far_right[:, h:])], 1)
     far_left = jnp.concatenate([b16(far_left[:, :h]), b16(far_left[:, h:] + f32(far_down))], 1)
@@ -159,18 +173,14 @@
     near_right = jnp.concatenate([b16(near_right[:n] + f32(two_up[:, :d])), b16(near_right[n:])], 0)
     near_left = jnp.concatenate([b16(near_left[:n]), b16(near_left[n:] + f32(two_down[:, :d]))], 0)
     near_p, near_m = shift(near_right, 1, 0), shift(near_left, -1, 0)
+    far_sum = shift(b16(far_here + f32(far_p) + f32(far_m)), 0, 2)
     own_right = jnp.concatenate([b16(own_right[:, :h] + f32(two_up[:, d : d + h])), b16(own_right[:, h:])], 1)
     own_left = jnp.concatenate([b16(own_left[:, :h]), b16(own_left[:, h:] + f32(two_down[:, d : d + h]))], 1)
-    own_right, own_left, far_p, far_m = lax.optimization_barrier((own_right, own_left, far_p, far_m))
+    own_right, own_left, near_p, near_m = lax.optimization_barrier((own_right, own_left, near_p, near_m))
     own_p, own_m = shift(own_right, 1, 0), shift(own_left, -1, 0)
-    far_sum = b16(far_here + f32(far_p) + f32(far_m))
-    by_above, by_below = shift(far_sum[:, :h], 0, 1), shift(far_sum[:, h:], 0, -1)
-    near_sum = near_here + f32(near_p) + f32(near_m)
-    below_sum, above_sum = near_sum[:n], near_sum[n:]
-    above_sum = jnp.concatenate([b16(above_sum[:, :h] + f32(by_above)), b16(above_sum[:, h:])], 1)
-    below_sum = jnp.concatenate([b16(below_sum[:, :h]), b16(below_sum[:, h:] + f32(by_below))], 1)
-    from_below, from_above = shift(above_sum, 0, 1), shift(below_sum, 0, -1)
-    return own_here + f32(own_p) + f32(own_m) + f32(from_below) + f32(from_above)
+    near_sum = b16(near_here + f32(near_p) + f32(near_m))
+    from_below, from_above = shift(near_sum[n:], 0, 1), shift(near_sum[:n], 0, -1)
+    return own_here + f32(own_p) + f32(own_m) + f32(far_sum) + f32(from_below) + f32(from_above)
 
 
 def on_device(tokens, norm_gain, gate_weight, up_weight, down_weight):

time: 106 us -> 101 us (0.953)
  waiting for transfers between devices: 28 us -> 25.3 us
  starting transfers between devices: 50.4 us -> 47.8 us
  other arithmetic: 3.56 us -> 1.37 us
  Pallas kernels: 23.4 us -> 25.5 us
    ppermute x26 -> x25, waiting for transfers between devices: 28 us -> 25.3 us  [shift(): return lax.ppermute(block, 'tensor', pairs)]
    ppermute x26 -> x25, starting transfers between devices: 50.4 us -> 47.8 us  [shift(): return lax.ppermute(block, 'tensor', pairs)]
    pallas_call x3 -> x5, Pallas kernels: 12.4 us -> 14.5 us  [the longest x4 13.4 us: fetched(): pl.pallas_call(kernel, out_shape=pltpu.VMEM((size, weight.shape[1]), weig...]
    reduce_sum x1 -> x0, other arithmetic: 1.09 us -> none  [rms_normed(): scale = lax.rsqrt(jnp.mean(rows * rows, axis=1, keepdims=True) + 1e-05)]
  transfers between devices with their start and end apart: 26 -> 25, of which waited for: 10 -> 13; matrix products, arithmetic and copies ran while one was open for 1% -> 1% of each run, Pallas kernels for 12% -> 13%
where the time goes in v3:
time: 101 us; the launch traced here: 100 us
  starting transfers between devices  47.8 us (47%)
  Pallas kernels  25.5 us (25%)
  waiting for transfers between devices  25.3 us (25%)
  other arithmetic  1.37 us (1%)
    ppermute x25, starting transfers between devices, shift(): return lax.ppermute(block, 'tensor', pairs)  47.8 us
    ppermute x25, waiting for transfers between devices, shift(): return lax.ppermute(block, 'tensor', pairs)  25.3 us
    pallas_call x4, Pallas kernels, fetched(): pl.pallas_call(kernel, out_shape=pltpu.VMEM((size, weight.shape[1]), weig...  13.4 us
    pallas_call x1, Pallas kernels, block_terms(): pl.pallas_call(lambda *refs: swiglu(n, *refs), out_shape=[jax.ShapeDtypeS...  11 us
  transfers between devices with their start and end apart: 25, of which 13 were waited for; matrix products, arithmetic and copies ran while one was open for 1% of the time, Pallas kernels for 13%

profile of v3, /device:TPU:8, one launch (start us, length us, event | category | flops | bytes accessed | tf_op | source)
XLA Modules:
  0.0 100.5 jit_solution(8168875003012877386)
XLA Ops:
  0.0 1.1 %shard_map.55.refs_0_ = bf16[16,6144]{1,0:T(8,128)(2,1)S(1)} custom-call(bf16[16,6144]{1,0:T(8,128)(2,1)} %rows_ref.1, f32[1,6144]{1,0:T(1,128)} %bitcast.1), custom_call_target="tpu_custom_call" | custom-call | tf_op jit(solution)/shard_map/pallas_call | solution.py:35
  1.1 6.4 %collective-permute-start.1 = (bf16[16,6144]{1,0:T(8,128)(2,1)S(1)}, bf16[16,6144]{1,0:T(8,128)(2,1)S(1)}, u32[]{:S(2)}, u32[]{:S(2)}) collective-permute-start(bf16[16,6144]{1,0:T(8,128)(2,1)S(1)} %shard_map.55.refs_0_), channel_id=1, source_target_pairs={{0,3},{1,0},{2,1},{3,2},{4,7},{5,4},{6,5},{7,6},{8,11},{9,8},{10,9... | collective-permute-start | bytes 589832 | tf_op jit(solution)/shard_map/ppermute | solution.py:17
  7.5 2.8 %collective-permute-start.3 = (bf16[16,6144]{1,0:T(8,128)(2,1)S(1)}, bf16[16,6144]{1,0:T(8,128)(2,1)S(1)}, u32[]{:S(2)}, u32[]{:S(2)}) collective-permute-start(bf16[16,6144]{1,0:T(8,128)(2,1)S(1)} %shard_map.55.refs_0_), channel_id=1, source_target_pairs={{0,12},{1,13},{2,14},{3,15},{4,0},{5,1},{6,2},{7,3},{8,4},{9,5},{1... | collective-permute-start | bytes 589832 | tf_op jit(solution)/shard_map/ppermute | solution.py:17
  10.3 0.0 collective-permute-start.2
  10.3 2.6 %shard_map.57.refs_16_ = bf16[3072,896]{1,0:T(8,128)(2,1)S(1)} custom-call(bf16[6144,896]{1,0:T(8,128)(2,1)} %source.5), custom_call_target="tpu_custom_call" | custom-call | bytes 5505024 | tf_op jit(solution)/shard_map/pallas_call | solution.py:132
  12.8 4.1 %shard_map.56.refs_15_ = bf16[6144,896]{1,0:T(8,128)(2,1)S(1)} custom-call(bf16[6144,896]{1,0:T(8,128)(2,1)} %source.3), custom_call_target="tpu_custom_call" | custom-call | bytes 11010048 | tf_op jit(solution)/shard_map/pallas_call | solution.py:132
  17.0 0.0 collective-permute-done.1.refs_4_
  17.0 2.7 %collective-permute-done.refs_3_ = bf16[16,6144]{1,0:T(8,128)(2,1)S(1)} collective-permute-done((bf16[16,6144]{1,0:T(8,128)(2,1)S(1)}, bf16[16,6144]{1,0:T(8,128)(2,1)S(1)}, u32[]{:S(2)}, u32[]{:S(2)}) %collective-permute-start) | collective-permute-done | bytes 196640 | tf_op jit(solution)/shard_map/ppermute | solution.py:17
  19.8 1.5 %collective-permute-start.7 = (bf16[16,3072]{1,0:T(8,128)(2,1)S(1)}, bf16[16,3072]{1,0:T(8,128)(2,1)S(1)}, u32[]{:S(2)}, u32[]{:S(2)}) collective-permute-start(bf16[16,3072]{1,0:T(8,128)(2,1)S(1)} %slice.91), channel_id=1, source_target_pairs={{0,3},{1,0},{2,1},{3,2},{4,7},{5,4},{6,5},{7,6},{8,11},{9,8},{10,9... | collective-permute-start | bytes 294920 | tf_op jit(solution)/shard_map/ppermute | solution.py:17
  21.3 1.5 %collective-permute-start.6 = (bf16[16,3072]{1,0:T(8,128)(2,1)S(1)}, bf16[16,3072]{1,0:T(8,128)(2,1)S(1)}, u32[]{:S(2)}, u32[]{:S(2)}) collective-permute-start(bf16[16,3072]{1,0:T(8,128)(2,1)S(1)} %slice.90), channel_id=1, source_target_pairs={{0,1},{1,2},{2,3},{3,0},{4,5},{5,6},{6,7},{7,4},{8,9},{9,10},{10,1... | collective-permute-start | bytes 294920 | tf_op jit(solution)/shard_map/ppermute | solution.py:17
  22.8 0.0 collective-permute-done.3.refs_2_
  22.8 0.0 collective-permute-done.2.refs_1_
  22.8 2.8 %collective-permute-start.5 = (bf16[32,6144]{1,0:T(8,128)(2,1)S(1)}, bf16[32,6144]{1,0:T(8,128)(2,1)S(1)}, u32[]{:S(2)}, u32[]{:S(2)}) collective-permute-start(bf16[32,6144]{1,0:T(8,128)(2,1)S(1)} %pad_maximum_fusion), channel_id=1, source_target_pairs={{0,12},{1,13},{2,14},{3,15},{4,0},{5,1},{6,2},{7,3},{8,4},{9,5},{1... | collective-permute-start | bytes 1179656 | tf_op jit(solution)/shard_map/ppermute | solution.py:17
  25.7 0.0 collective-permute-start.4
  25.7 2.6 %shard_map.58.refs_17_ = bf16[3072,896]{1,0:T(8,128)(2,1)S(1)} custom-call(bf16[6144,896]{1,0:T(8,128)(2,1)} %source.5), custom_call_target="tpu_custom_call" | custom-call | bytes 5505024 | tf_op jit(solution)/shard_map/pallas_call | solution.py:132
  28.3 0.3 collective-permute-done.6.refs_11_
  28.6 3.1 %collective-permute-start.9 = (bf16[16,6144]{1,0:T(8,128)(2,1)S(1)}, bf16[16,6144]{1,0:T(8,128)(2,1)S(1)}, u32[]{:S(2)}, u32[]{:S(2)}) collective-permute-start(bf16[16,6144]{1,0:T(8,128)(2,1)S(1)} %pad_maximum_fusion.5), channel_id=1, source_target_pairs={{0,12},{1,13},{2,14},{3,15},{4,0},{5,1},{6,2},{7,3},{8,4},{9,5},{1... | collective-permute-start | bytes 589832 | tf_op jit(solution)/shard_map/ppermute | solution.py:17
  31.7 1.8 %collective-permute-done.5.refs_6_ = bf16[32,6144]{1,0:T(8,128)(2,1)S(1)} collective-permute-done((bf16[32,6144]{1,0:T(8,128)(2,1)S(1)}, bf16[32,6144]{1,0:T(8,128)(2,1)S(1)}, u32[]{:S(2)}, u32[]{:S(2)}) %collective-permute-start.5) | collective-permute-done | bytes 393248 | tf_op jit(solution)/shard_map/ppermute | solution.py:17
  33.5 3.4 %collective-permute-done.4.refs_5_ = bf16[32,6144]{1,0:T(8,128)(2,1)S(1)} collective-permute-done((bf16[32,6144]{1,0:T(8,128)(2,1)S(1)}, bf16[32,6144]{1,0:T(8,128)(2,1)S(1)}, u32[]{:S(2)}, u32[]{:S(2)}) %collective-permute-start.4) | collective-permute-done | bytes 393248 | tf_op jit(solution)/shard_map/ppermute | solution.py:17
  36.9 0.4 collective-permute-start.11
  37.3 1.8 %collective-permute-start.10 = (bf16[16,9216]{1,0:T(8,128)(2,1)S(1)}, bf16[16,9216]{1,0:T(8,128)(2,1)S(1)}, u32[]{:S(2)}, u32[]{:S(2)}) collective-permute-start(bf16[16,9216]{1,0:T(8,128)(2,1)S(1)} %pad_maximum_fusion.3), channel_id=1, source_target_pairs={{0,4},{1,5},{2,6},{3,7},{4,8},{5,9},{6,10},{7,11},{8,12},{9,13},{1... | collective-permute-start | bytes 884744 | tf_op jit(solution)/shard_map/ppermute | solution.py:17
  39.2 1.9 %collective-permute-done.8.refs_7_ = bf16[16,6144]{1,0:T(8,128)(2,1)S(1)} collective-permute-done((bf16[16,6144]{1,0:T(8,128)(2,1)S(1)}, bf16[16,6144]{1,0:T(8,128)(2,1)S(1)}, u32[]{:S(2)}, u32[]{:S(2)}) %collective-permute-start.8) | collective-permute-done | bytes 196640 | tf_op jit(solution)/shard_map/ppermute | solution.py:17
  41.1 0.4 collective-permute-start.13
  41.5 1.7 %collective-permute-start.12 = (bf16[16,3072]{1,0:T(8,128)(2,1)S(1)}, bf16[16,3072]{1,0:T(8,128)(2,1)S(1)}, u32[]{:S(2)}, u32[]{:S(2)}) collective-permute-start(bf16[16,3072]{1,0:T(8,128)(2,1)S(1)} %slice.96), channel_id=1, source_target_pairs={{0,4},{1,5},{2,6},{3,7},{4,8},{5,9},{6,10},{7,11},{8,12},{9,13},{1... | collective-permute-start | bytes 294920 | tf_op jit(solution)/shard_map/ppermute | solution.py:17
  43.2 4.1 %shard_map.59.refs_18_ = bf16[896,6144]{1,0:T(8,128)(2,1)S(1)} custom-call(bf16[896,6144]{1,0:T(8,128)(2,1)} %source.6), custom_call_target="tpu_custom_call" | custom-call | bytes 11010048 | tf_op jit(solution)/shard_map/pallas_call | solution.py:132
  47.4 0.3 collective-permute-done.12.refs_13_
  47.6 11.0 %shard_map.60 = (f32[16,6144]{1,0:T(8,128)S(1)}, f32[16,6144]{1,0:T(8,128)S(1)}, f32[16,6144]{1,0:T(8,128)S(1)}, f32[32,6144]{1,0:T(8,128)S(1)}, f32[32,6144]{1,...) custom-call(bf16[16,6144]{1,0:T(8,128)(2,1)S(1)} %shard_map.55.refs_, ...), custom_call_target="tpu_custom_call" | custom-call | flops 8455716864 | bytes 33030144 | tf_op jit(solution)/shard_map/pallas_call | solution.py:113
  58.6 0.0 copy-start
  58.6 0.3 collective-permute-start.14
  58.9 3.0 %collective-permute-start.15 = (bf16[16,12288]{1,0:T(8,128)(2,1)S(1)}, bf16[16,12288]{1,0:T(8,128)(2,1)S(1)}, u32[]{:S(2)}, u32[]{:S(2)}) collective-permute-start(bf16[16,12288]{1,0:T(8,128)(2,1)S(1)} %get-tuple-element.53), channel_id=1, source_target_pairs={{0,12},{1,13},{2,14},{3,15},{4,0},{5,1},{6,2},{7,3},{8,4},{9,5},{1... | collective-permute-start | bytes 1179656 | tf_op jit(solution)/shard_map/ppermute | solution.py:17
  62.1 5.9 %collective-permute-done.14 = bf16[16,12288]{1,0:T(8,128)(2,1)S(1)} collective-permute-done((bf16[16,12288]{1,0:T(8,128)(2,1)S(1)}, bf16[16,12288]{1,0:T(8,128)(2,1)S(1)}, u32[]{:S(2)}, u32[]{:S(2)}) %collective-permute-start.14) | collective-permute-done | bytes 393248 | tf_op jit(solution)/shard_map/ppermute | solution.py:17
  68.2 3.3 %collective-permute-start.21 = (bf16[16,6144]{1,0:T(8,128)(2,1)S(1)}, bf16[16,6144]{1,0:T(8,128)(2,1)S(1)}, u32[]{:S(2)}, u32[]{:S(2)}) collective-permute-start(bf16[16,6144]{1,0:T(8,128)(2,1)S(1)} %pad_maximum_fusion.9), channel_id=1, source_target_pairs={{0,12},{1,13},{2,14},{3,15},{4,0},{5,1},{6,2},{7,3},{8,4},{9,5},{1... | collective-permute-start | bytes 589832 | tf_op jit(solution)/shard_map/ppermute | solution.py:17
  71.5 0.1 collective-permute-start.20
  71.6 3.3 %collective-permute-start.17 = (bf16[32,6144]{1,0:T(8,128)(2,1)S(1)}, bf16[32,6144]{1,0:T(8,128)(2,1)S(1)}, u32[]{:S(2)}, u32[]{:S(2)}) collective-permute-start(bf16[32,6144]{1,0:T(8,128)(2,1)S(1)} %pad_maximum_fusion.2), channel_id=1, source_target_pairs={{0,12},{1,13},{2,14},{3,15},{4,0},{5,1},{6,2},{7,3},{8,4},{9,5},{1... | collective-permute-start | bytes 1179656 | tf_op jit(solution)/shard_map/ppermute | solution.py:17
  75.0 0.1 collective-permute-start.16
  75.1 1.1 %collective-permute-done.21 = bf16[16,6144]{1,0:T(8,128)(2,1)S(1)} collective-permute-done((bf16[16,6144]{1,0:T(8,128)(2,1)S(1)}, bf16[16,6144]{1,0:T(8,128)(2,1)S(1)}, u32[]{:S(2)}, u32[]{:S(2)}) %collective-permute-start.21) | collective-permute-done | bytes 196640 | tf_op jit(solution)/shard_map/ppermute | solution.py:17
  76.2 3.5 %collective-permute-done.20 = bf16[16,6144]{1,0:T(8,128)(2,1)S(1)} collective-permute-done((bf16[16,6144]{1,0:T(8,128)(2,1)S(1)}, bf16[16,6144]{1,0:T(8,128)(2,1)S(1)}, u32[]{:S(2)}, u32[]{:S(2)}) %collective-permute-start.20) | collective-permute-done | bytes 196640 | tf_op jit(solution)/shard_map/ppermute | solution.py:17
  79.7 0.1 add_convert_fusion.2
  79.7 3.6 %collective-permute-start.22 = (bf16[16,6144]{1,0:T(8,128)(2,1)S(1)}, bf16[16,6144]{1,0:T(8,128)(2,1)S(1)}, u32[]{:S(2)}, u32[]{:S(2)}) collective-permute-start(bf16[16,6144]{1,0:T(8,128)(2,1)S(1)} %add_convert_fusion.2), channel_id=1, source_target_pairs={{0,2},{1,3},{2,0},{3,1},{4,6},{5,7},{6,4},{7,5},{8,10},{9,11},{10,... | collective-permute-start | bytes 589832 | tf_op jit(solution)/shard_map/ppermute | solution.py:17
  83.4 0.7 collective-permute-done.16
  84.0 0.1 add_convert_fusion
  84.2 4.7 %collective-permute-start.23 = (bf16[16,6144]{1,0:T(8,128)(2,1)S(1)}, bf16[16,6144]{1,0:T(8,128)(2,1)S(1)}, u32[]{:S(2)}, u32[]{:S(2)}) collective-permute-start(bf16[16,6144]{1,0:T(8,128)(2,1)S(1)} %get-tuple-element.71), channel_id=1, source_target_pairs={{0,1},{1,2},{2,3},{3,0},{4,5},{5,6},{6,7},{7,4},{8,9},{9,10},{10,1... | collective-permute-start | bytes 589832 | tf_op jit(solution)/shard_map/ppermute | solution.py:17
  88.9 3.9 %collective-permute-start.24 = (bf16[16,6144]{1,0:T(8,128)(2,1)S(1)}, bf16[16,6144]{1,0:T(8,128)(2,1)S(1)}, u32[]{:S(2)}, u32[]{:S(2)}) collective-permute-start(bf16[16,6144]{1,0:T(8,128)(2,1)S(1)} %get-tuple-element.72), channel_id=1, source_target_pairs={{0,3},{1,0},{2,1},{3,2},{4,7},{5,4},{6,5},{7,6},{8,11},{9,8},{10,9... | collective-permute-start | bytes 589832 | tf_op jit(solution)/shard_map/ppermute | solution.py:17
  92.8 3.2 %collective-permute-start.19 = (bf16[16,6144]{1,0:T(8,128)(2,1)S(1)}, bf16[16,6144]{1,0:T(8,128)(2,1)S(1)}, u32[]{:S(2)}, u32[]{:S(2)}) collective-permute-start(bf16[16,6144]{1,0:T(8,128)(2,1)S(1)} %pad_maximum_fusion.7), channel_id=1, source_target_pairs={{0,12},{1,13},{2,14},{3,15},{4,0},{5,1},{6,2},{7,3},{8,4},{9,5},{1... | collective-permute-start | bytes 589832 | tf_op jit(solution)/shard_map/ppermute | solution.py:17
  96.0 0.4 collective-permute-done.23
  96.4 1.6 %collective-permute-done.24 = bf16[16,6144]{1,0:T(8,128)(2,1)S(1)} collective-permute-done((bf16[16,6144]{1,0:T(8,128)(2,1)S(1)}, bf16[16,6144]{1,0:T(8,128)(2,1)S(1)}, u32[]{:S(2)}, u32[]{:S(2)}) %collective-permute-start.24) | collective-permute-done | bytes 196640 | tf_op jit(solution)/shard_map/ppermute | solution.py:17
  98.0 1.6 %collective-permute-done.18 = bf16[16,6144]{1,0:T(8,128)(2,1)S(1)} collective-permute-done((bf16[16,6144]{1,0:T(8,128)(2,1)S(1)}, bf16[16,6144]{1,0:T(8,128)(2,1)S(1)}, u32[]{:S(2)}, u32[]{:S(2)}) %collective-permute-start.18) | collective-permute-done | bytes 196640 | tf_op jit(solution)/shard_map/ppermute | solution.py:17
  99.6 0.8 add_convert_fusion.1
  (42 shorter events, 0.6 us)
Async XLA Ops:
  1.1 15.9 %collective-permute-start.1 = (bf16[16,6144]{1,0:T(8,128)(2,1)S(1)}, bf16[16,6144]{1,0:T(8,128)(2,1)S(1)}, u32[]{:S(2)}, u32[]{:S(2)}) collective-permute-start(bf16[16,6144]{1,0:T(8,128)(2,1)S(1)} %shard_map.55.refs_0_), channel_id=1, source_target_pairs={{0,3},{1,0},{2,1},{3,2},{4,7},{5,4},{6,5},{7,6},{8,11},{9,8},{10,9... | collective-permute-start | bytes 589832 | tf_op jit(solution)/shard_map/ppermute | solution.py:17
  7.5 12.2 %collective-permute-start = (bf16[16,6144]{1,0:T(8,128)(2,1)S(1)}, bf16[16,6144]{1,0:T(8,128)(2,1)S(1)}, u32[]{:S(2)}, u32[]{:S(2)}) collective-permute-start(bf16[16,6144]{1,0:T(8,128)(2,1)S(1)} %shard_map.55.refs_0_), channel_id=1, source_target_pairs={{0,1},{1,2},{2,3},{3,0},{4,5},{5,6},{6,7},{7,4},{8,9},{9,10},{10,1... | collective-permute-start | bytes 589832 | tf_op jit(solution)/shard_map/ppermute | solution.py:17
  7.5 15.3 %collective-permute-start.3 = (bf16[16,6144]{1,0:T(8,128)(2,1)S(1)}, bf16[16,6144]{1,0:T(8,128)(2,1)S(1)}, u32[]{:S(2)}, u32[]{:S(2)}) collective-permute-start(bf16[16,6144]{1,0:T(8,128)(2,1)S(1)} %shard_map.55.refs_0_), channel_id=1, source_target_pairs={{0,12},{1,13},{2,14},{3,15},{4,0},{5,1},{6,2},{7,3},{8,4},{9,5},{1... | collective-permute-start | bytes 589832 | tf_op jit(solution)/shard_map/ppermute | solution.py:17
  10.3 12.5 %collective-permute-start.2 = (bf16[16,6144]{1,0:T(8,128)(2,1)S(1)}, bf16[16,6144]{1,0:T(8,128)(2,1)S(1)}, u32[]{:S(2)}, u32[]{:S(2)}) collective-permute-start(bf16[16,6144]{1,0:T(8,128)(2,1)S(1)} %shard_map.55.refs_0_), channel_id=1, source_target_pairs={{0,4},{1,5},{2,6},{3,7},{4,8},{5,9},{6,10},{7,11},{8,12},{9,13},{1... | collective-permute-start | bytes 589832 | tf_op jit(solution)/shard_map/ppermute | solution.py:17
  19.8 8.5 %collective-permute-start.7 = (bf16[16,3072]{1,0:T(8,128)(2,1)S(1)}, bf16[16,3072]{1,0:T(8,128)(2,1)S(1)}, u32[]{:S(2)}, u32[]{:S(2)}) collective-permute-start(bf16[16,3072]{1,0:T(8,128)(2,1)S(1)} %slice.91), channel_id=1, source_target_pairs={{0,3},{1,0},{2,1},{3,2},{4,7},{5,4},{6,5},{7,6},{8,11},{9,8},{10,9... | collective-permute-start | bytes 294920 | tf_op jit(solution)/shard_map/ppermute | solution.py:17
  21.3 7.3 %collective-permute-start.6 = (bf16[16,3072]{1,0:T(8,128)(2,1)S(1)}, bf16[16,3072]{1,0:T(8,128)(2,1)S(1)}, u32[]{:S(2)}, u32[]{:S(2)}) collective-permute-start(bf16[16,3072]{1,0:T(8,128)(2,1)S(1)} %slice.90), channel_id=1, source_target_pairs={{0,1},{1,2},{2,3},{3,0},{4,5},{5,6},{6,7},{7,4},{8,9},{9,10},{10,1... | collective-permute-start | bytes 294920 | tf_op jit(solution)/shard_map/ppermute | solution.py:17
  22.8 10.7 %collective-permute-start.5 = (bf16[32,6144]{1,0:T(8,128)(2,1)S(1)}, bf16[32,6144]{1,0:T(8,128)(2,1)S(1)}, u32[]{:S(2)}, u32[]{:S(2)}) collective-permute-start(bf16[32,6144]{1,0:T(8,128)(2,1)S(1)} %pad_maximum_fusion), channel_id=1, source_target_pairs={{0,12},{1,13},{2,14},{3,15},{4,0},{5,1},{6,2},{7,3},{8,4},{9,5},{1... | collective-permute-start | bytes 1179656 | tf_op jit(solution)/shard_map/ppermute | solution.py:17
  25.7 11.2 %collective-permute-start.4 = (bf16[32,6144]{1,0:T(8,128)(2,1)S(1)}, bf16[32,6144]{1,0:T(8,128)(2,1)S(1)}, u32[]{:S(2)}, u32[]{:S(2)}) collective-permute-start(bf16[32,6144]{1,0:T(8,128)(2,1)S(1)} %pad_maximum_fusion), channel_id=1, source_target_pairs={{0,4},{1,5},{2,6},{3,7},{4,8},{5,9},{6,10},{7,11},{8,12},{9,13},{1... | collective-permute-start | bytes 1179656 | tf_op jit(solution)/shard_map/ppermute | solution.py:17
  28.6 10.6 %collective-permute-start.9 = (bf16[16,6144]{1,0:T(8,128)(2,1)S(1)}, bf16[16,6144]{1,0:T(8,128)(2,1)S(1)}, u32[]{:S(2)}, u32[]{:S(2)}) collective-permute-start(bf16[16,6144]{1,0:T(8,128)(2,1)S(1)} %pad_maximum_fusion.5), channel_id=1, source_target_pairs={{0,12},{1,13},{2,14},{3,15},{4,0},{5,1},{6,2},{7,3},{8,4},{9,5},{1... | collective-permute-start | bytes 589832 | tf_op jit(solution)/shard_map/ppermute | solution.py:17
  31.7 9.4 %collective-permute-start.8 = (bf16[16,6144]{1,0:T(8,128)(2,1)S(1)}, bf16[16,6144]{1,0:T(8,128)(2,1)S(1)}, u32[]{:S(2)}, u32[]{:S(2)}) collective-permute-start(bf16[16,6144]{1,0:T(8,128)(2,1)S(1)} %pad_maximum_fusion.5), channel_id=1, source_target_pairs={{0,4},{1,5},{2,6},{3,7},{4,8},{5,9},{6,10},{7,11},{8,12},{9,13},{1... | collective-permute-start | bytes 589832 | tf_op jit(solution)/shard_map/ppermute | solution.py:17
  36.9 10.7 %collective-permute-start.11 = (bf16[16,9216]{1,0:T(8,128)(2,1)S(1)}, bf16[16,9216]{1,0:T(8,128)(2,1)S(1)}, u32[]{:S(2)}, u32[]{:S(2)}) collective-permute-start(bf16[16,9216]{1,0:T(8,128)(2,1)S(1)} %pad_maximum_fusion.4), channel_id=1, source_target_pairs={{0,12},{1,13},{2,14},{3,15},{4,0},{5,1},{6,2},{7,3},{8,4},{9,5},{1... | collective-permute-start | bytes 884744 | tf_op jit(solution)/shard_map/ppermute | solution.py:17
  37.3 10.3 %collective-permute-start.10 = (bf16[16,9216]{1,0:T(8,128)(2,1)S(1)}, bf16[16,9216]{1,0:T(8,128)(2,1)S(1)}, u32[]{:S(2)}, u32[]{:S(2)}) collective-permute-start(bf16[16,9216]{1,0:T(8,128)(2,1)S(1)} %pad_maximum_fusion.3), channel_id=1, source_target_pairs={{0,4},{1,5},{2,6},{3,7},{4,8},{5,9},{6,10},{7,11},{8,12},{9,13},{1... | collective-permute-start | bytes 884744 | tf_op jit(solution)/shard_map/ppermute | solution.py:17
  41.1 6.3 %collective-permute-start.13 = (bf16[16,3072]{1,0:T(8,128)(2,1)S(1)}, bf16[16,3072]{1,0:T(8,128)(2,1)S(1)}, u32[]{:S(2)}, u32[]{:S(2)}) collective-permute-start(bf16[16,3072]{1,0:T(8,128)(2,1)S(1)} %slice.97), channel_id=1, source_target_pairs={{0,12},{1,13},{2,14},{3,15},{4,0},{5,1},{6,2},{7,3},{8,4},{9,5},{1... | collective-permute-start | bytes 294920 | tf_op jit(solution)/shard_map/ppermute | solution.py:17
  41.5 6.2 %collective-permute-start.12 = (bf16[16,3072]{1,0:T(8,128)(2,1)S(1)}, bf16[16,3072]{1,0:T(8,128)(2,1)S(1)}, u32[]{:S(2)}, u32[]{:S(2)}) collective-permute-start(bf16[16,3072]{1,0:T(8,128)(2,1)S(1)} %slice.96), channel_id=1, source_target_pairs={{0,4},{1,5},{2,6},{3,7},{4,8},{5,9},{6,10},{7,11},{8,12},{9,13},{1... | collective-permute-start | bytes 294920 | tf_op jit(solution)/shard_map/ppermute | solution.py:17
  58.6 41.0 %copy-start = (bf16[16,6144]{1,0:T(8,128)(2,1)S(1)}, bf16[16,6144]{1,0:T(8,128)(2,1)}, u32[]{:S(2)}) copy-start(bf16[16,6144]{1,0:T(8,128)(2,1)} %rows_ref.1) | copy-start | bytes 589828
  58.6 9.4 %collective-permute-start.14 = (bf16[16,12288]{1,0:T(8,128)(2,1)S(1)}, bf16[16,12288]{1,0:T(8,128)(2,1)S(1)}, u32[]{:S(2)}, u32[]{:S(2)}) collective-permute-start(bf16[16,12288]{1,0:T(8,128)(2,1)S(1)} %get-tuple-element.52), channel_id=1, source_target_pairs={{0,4},{1,5},{2,6},{3,7},{4,8},{5,9},{6,10},{7,11},{8,12},{9,13},{1... | collective-permute-start | bytes 1179656 | tf_op jit(solution)/shard_map/ppermute | solution.py:17
  58.9 9.1 %collective-permute-start.15 = (bf16[16,12288]{1,0:T(8,128)(2,1)S(1)}, bf16[16,12288]{1,0:T(8,128)(2,1)S(1)}, u32[]{:S(2)}, u32[]{:S(2)}) collective-permute-start(bf16[16,12288]{1,0:T(8,128)(2,1)S(1)} %get-tuple-element.53), channel_id=1, source_target_pairs={{0,12},{1,13},{2,14},{3,15},{4,0},{5,1},{6,2},{7,3},{8,4},{9,5},{1... | collective-permute-start | bytes 1179656 | tf_op jit(solution)/shard_map/ppermute | solution.py:17
  68.2 7.9 %collective-permute-start.21 = (bf16[16,6144]{1,0:T(8,128)(2,1)S(1)}, bf16[16,6144]{1,0:T(8,128)(2,1)S(1)}, u32[]{:S(2)}, u32[]{:S(2)}) collective-permute-start(bf16[16,6144]{1,0:T(8,128)(2,1)S(1)} %pad_maximum_fusion.9), channel_id=1, source_target_pairs={{0,12},{1,13},{2,14},{3,15},{4,0},{5,1},{6,2},{7,3},{8,4},{9,5},{1... | collective-permute-start | bytes 589832 | tf_op jit(solution)/shard_map/ppermute | solution.py:17
  71.5 8.2 %collective-permute-start.20 = (bf16[16,6144]{1,0:T(8,128)(2,1)S(1)}, bf16[16,6144]{1,0:T(8,128)(2,1)S(1)}, u32[]{:S(2)}, u32[]{:S(2)}) collective-permute-start(bf16[16,6144]{1,0:T(8,128)(2,1)S(1)} %pad_maximum_fusion.8), channel_id=1, source_target_pairs={{0,4},{1,5},{2,6},{3,7},{4,8},{5,9},{6,10},{7,11},{8,12},{9,13},{1... | collective-permute-start | bytes 589832 | tf_op jit(solution)/shard_map/ppermute | solution.py:17
  71.6 11.7 %collective-permute-start.17 = (bf16[32,6144]{1,0:T(8,128)(2,1)S(1)}, bf16[32,6144]{1,0:T(8,128)(2,1)S(1)}, u32[]{:S(2)}, u32[]{:S(2)}) collective-permute-start(bf16[32,6144]{1,0:T(8,128)(2,1)S(1)} %pad_maximum_fusion.2), channel_id=1, source_target_pairs={{0,12},{1,13},{2,14},{3,15},{4,0},{5,1},{6,2},{7,3},{8,4},{9,5},{1... | collective-permute-start | bytes 1179656 | tf_op jit(solution)/shard_map/ppermute | solution.py:17
  75.0 9.1 %collective-permute-start.16 = (bf16[32,6144]{1,0:T(8,128)(2,1)S(1)}, bf16[32,6144]{1,0:T(8,128)(2,1)S(1)}, u32[]{:S(2)}, u32[]{:S(2)}) collective-permute-start(bf16[32,6144]{1,0:T(8,128)(2,1)S(1)} %pad_maximum_fusion.1), channel_id=1, source_target_pairs={{0,4},{1,5},{2,6},{3,7},{4,8},{5,9},{6,10},{7,11},{8,12},{9,13},{1... | collective-permute-start | bytes 1179656 | tf_op jit(solution)/shard_map/ppermute | solution.py:17
  79.7 16.2 %collective-permute-start.22 = (bf16[16,6144]{1,0:T(8,128)(2,1)S(1)}, bf16[16,6144]{1,0:T(8,128)(2,1)S(1)}, u32[]{:S(2)}, u32[]{:S(2)}) collective-permute-start(bf16[16,6144]{1,0:T(8,128)(2,1)S(1)} %add_convert_fusion.2), channel_id=1, source_target_pairs={{0,2},{1,3},{2,0},{3,1},{4,6},{5,7},{6,4},{7,5},{8,10},{9,11},{10,... | collective-permute-start | bytes 589832 | tf_op jit(solution)/shard_map/ppermute | solution.py:17
  84.2 12.2 %collective-permute-start.23 = (bf16[16,6144]{1,0:T(8,128)(2,1)S(1)}, bf16[16,6144]{1,0:T(8,128)(2,1)S(1)}, u32[]{:S(2)}, u32[]{:S(2)}) collective-permute-start(bf16[16,6144]{1,0:T(8,128)(2,1)S(1)} %get-tuple-element.71), channel_id=1, source_target_pairs={{0,1},{1,2},{2,3},{3,0},{4,5},{5,6},{6,7},{7,4},{8,9},{9,10},{10,1... | collective-permute-start | bytes 589832 | tf_op jit(solution)/shard_map/ppermute | solution.py:17
  88.9 9.1 %collective-permute-start.24 = (bf16[16,6144]{1,0:T(8,128)(2,1)S(1)}, bf16[16,6144]{1,0:T(8,128)(2,1)S(1)}, u32[]{:S(2)}, u32[]{:S(2)}) collective-permute-start(bf16[16,6144]{1,0:T(8,128)(2,1)S(1)} %get-tuple-element.72), channel_id=1, source_target_pairs={{0,3},{1,0},{2,1},{3,2},{4,7},{5,4},{6,5},{7,6},{8,11},{9,8},{10,9... | collective-permute-start | bytes 589832 | tf_op jit(solution)/shard_map/ppermute | solution.py:17
  92.8 6.9 %collective-permute-start.18 = (bf16[16,6144]{1,0:T(8,128)(2,1)S(1)}, bf16[16,6144]{1,0:T(8,128)(2,1)S(1)}, u32[]{:S(2)}, u32[]{:S(2)}) collective-permute-start(bf16[16,6144]{1,0:T(8,128)(2,1)S(1)} %pad_maximum_fusion.6), channel_id=1, source_target_pairs={{0,4},{1,5},{2,6},{3,7},{4,8},{5,9},{6,10},{7,11},{8,12},{9,13},{1... | collective-permute-start | bytes 589832 | tf_op jit(solution)/shard_map/ppermute | solution.py:17
  92.8 6.9 %collective-permute-start.19 = (bf16[16,6144]{1,0:T(8,128)(2,1)S(1)}, bf16[16,6144]{1,0:T(8,128)(2,1)S(1)}, u32[]{:S(2)}, u32[]{:S(2)}) collective-permute-start(bf16[16,6144]{1,0:T(8,128)(2,1)S(1)} %pad_maximum_fusion.7), channel_id=1, source_target_pairs={{0,12},{1,13},{2,14},{3,15},{4,0},{5,1},{6,2},{7,3},{8,4},{9,5},{1... | collective-permute-start | bytes 589832 | tf_op jit(solution)/shard_map/ppermute | solution.py:17

commit v4 on v0

v4 whole, which is shorter than its diff:
```python
import jax
import jax.numpy as jnp
from jax import lax
from jax.experimental import pallas as pl
from jax.experimental.pallas import tpu as pltpu
from jax.sharding import PartitionSpec as P

SIDE = 4


def shift(block, dx, dz):
    pairs = [
        (x * SIDE + z, (x + dx) % SIDE * SIDE + (z + dz) % SIDE)
        for x in range(SIDE)
        for z in range(SIDE)
    ]
    return lax.ppermute(block, "tensor", pairs)


def b16(v):
    return v.astype(jnp.bfloat16)


def f32(v):
    return v.astype(jnp.float32)


def rms_normed(rows, gain):
    def kernel(rows_ref, gain_ref, out_ref):
        held = f32(rows_ref[...])
        scale = lax.rsqrt(jnp.mean(held * held, axis=1, keepdims=True) + 1e-05)
        out_ref[...] = b16(held * scale * gain_ref[...])

    vmem = pl.BlockSpec(memory_space=pltpu.VMEM)
    return pl.pallas_call(
        kernel,
        out_shape=pltpu.VMEM(rows.shape, jnp.bfloat16),
        in_specs=[vmem] * 2,
        out_specs=vmem,
        compiler_params=pltpu.CompilerParams(vmem_limit_bytes=4 * 1024 * 1024),
    )(*[pltpu.with_memory_space_constraint(v, pltpu.HBM) for v in (rows, gain.reshape(1, -1))])


def placed(blocks):
    return [pltpu.with_memory_space_constraint(v, pltpu.VMEM) for v in blocks]


def hidden_of(rows, gate_w, up_w, up_w2):
    half = up_w.shape[0]
    gate = jnp.dot(rows[...], gate_w[...], preferred_element_type=jnp.float32)
    up = jnp.dot(rows[:, :half], up_w[...], preferred_element_type=jnp.float32)
    up = up + jnp.dot(rows[:, half:], up_w2[...], preferred_element_type=jnp.float32)
    return b16(gate / (1.0 + jnp.exp(-gate)) * up)


def early_hidden(own, own_l, own_r, own_2up, own_2down, below, above, far, weights):
    n, d = own.shape
    h, ff = d // 2, weights[0].shape[1]

    def kernel(own, own_l, own_r, own_2up, own_2down, below, above, far, gate_w, up_w, up_w2, out, rows):
        for i, ref in ((0, own), (1, own_l), (2, own_r), (4, below), (5, above), (6, far)):
            rows[i * n : (i + 1) * n, :] = ref[...]
        rows[3 * n : 4 * n, :h] = own_2up[...]
        rows[3 * n : 4 * n, h:] = own_2down[...]
        out[...] = hidden_of(rows, gate_w, up_w, up_w2)

    vmem = pl.BlockSpec(memory_space=pltpu.VMEM)
    return pl.pallas_call(
        kernel,
        out_shape=pltpu.VMEM((7 * n, ff), jnp.bfloat16),
        in_specs=[vmem] * 11,
        out_specs=vmem,
        scratch_shapes=[pltpu.VMEM((7 * n, d), jnp.bfloat16)],
        compiler_params=pltpu.CompilerParams(vmem_limit_bytes=8 * 1024 * 1024),
        cost_estimate=pl.CostEstimate(flops=4 * 7 * n * d * ff, bytes_accessed=0, transcendentals=7 * n * ff),
    )(*placed((own, own_l, own_r, own_2up, own_2down, below, above, far, *weights)))


def late_hidden(near_l, near_r, far_l, far_r, near_2up, near_2down, far_2up, far_2down, early, weights, down_weight):
    n, d = far_l.shape
    h, ff, step = d // 2, early.shape[1], 1024

    def kernel(
        near_l, near_r, far_l, far_r, near_2up, near_2down, far_2up, far_2down, early, gate_w, up_w, up_w2, source,
        out, out_up, out_down, down_w, rows, two, done,
    ):
        copy = pltpu.make_async_copy(source, down_w, done)
        copy.start()
        for i, ref in ((0, near_l), (2, near_r), (4, far_l), (5, far_r), (6, near_2up), (7, near_2down)):
            rows[i * n : i * n + ref.shape[0], :] = ref[...]
        rows[8 * n :, :h] = far_2up[...]
        rows[8 * n :, h:] = far_2down[...]
        out[...] = hidden_of(rows, gate_w, up_w, up_w2)
        two[:n, :] = early[3 * n : 4 * n, :]
        two[n:, :] = out[6 * n :, :]
        copy.wait()
        for second in (False, True):
            target = out_down if second else out_up

            @pl.loop(0, h // step)
            def _(i):
                start = pl.multiple_of(i * step, step)
                cut = pl.ds(start + second * h, step)
                terms = b16(jnp.dot(two[...], down_w[:, cut], preferred_element_type=jnp.float32))
                out_up[:, cut] = terms[n : 2 * n]
                out_down[:, cut] = terms[2 * n : 3 * n]
                target[:, pl.ds(start + d, step)] = terms[:n]
                target[:, pl.ds(start + d + h, step)] = terms[3 * n :]

    vmem, b = pl.BlockSpec(memory_space=pltpu.VMEM), jnp.bfloat16
    return pl.pallas_call(
        kernel,
        out_shape=[pltpu.VMEM(shape, b) for shape in ((9 * n, ff), (n, 2 * d), (n, 2 * d), (ff, d))],
        in_specs=[vmem] * 12 + [pl.BlockSpec(memory_space=pltpu.HBM)],
        out_specs=[vmem] * 4,
        scratch_shapes=[pltpu.VMEM((9 * n, d), b), pltpu.VMEM((4 * n, ff), b), pltpu.SemaphoreType.DMA],
        compiler_params=pltpu.CompilerParams(vmem_limit_bytes=10 * 1024 * 1024),
        cost_estimate=pl.CostEstimate(flops=4 * 11 * n * d * ff, bytes_accessed=2 * d * ff, transcendentals=9 * n * ff),
    )(
        *placed((near_l, near_r, far_l, far_r, near_2up, near_2down, far_2up, far_2down, early, *weights)),
        pltpu.with_memory_space_constraint(down_weight, pltpu.HBM),
    )


def other_terms(early, late, down_weight):
    n, (ff, d), step = early.shape[0] // 7, down_weight.shape, 1024
    tall = (1, 1, 1, 2, 1, 2, 2, 1, 1)

    def kernel(early, late, down_w, *rest):
        outs, held = rest[:-1], rest[-1]
        held[: 3 * n, :] = early[: 3 * n, :]
        held[3 * n : 6 * n, :] = early[4 * n :, :]
        held[6 * n :, :] = late[: 6 * n, :]

        @pl.loop(0, d // step)
        def _(i):
            cut = pl.ds(pl.multiple_of(i * step, step), step)
            terms = jnp.dot(held[...], down_w[:, cut], preferred_element_type=jnp.float32)
            at = 0
            for out, k in zip(outs, tall, strict=True):
                out[:, cut] = terms[at * n : (at + k) * n]
                at += k

    vmem = pl.BlockSpec(memory_space=pltpu.VMEM)
    return pl.pallas_call(
        kernel,
        out_shape=[pltpu.VMEM((k * n, d), jnp.float32) for k in tall],
        in_specs=[vmem] * 3,
        out_specs=[vmem] * 9,
        scratch_shapes=[pltpu.VMEM((12 * n, ff), jnp.bfloat16)],
        compiler_params=pltpu.CompilerParams(vmem_limit_bytes=8 * 1024 * 1024),
        cost_estimate=pl.CostEstimate(flops=2 * 12 * n * d * ff, bytes_accessed=0, transcendentals=0),
    )(*placed((early, late, down_weight)))


def fetched(weight, part=0, parts=1):
    size = weight.shape[0] // parts

    def kernel(source, target, done):
        copy = pltpu.make_async_copy(source.at[pl.ds(part * size, size), :], target, done)
        copy.start()
        copy.wait()

    return pl.pallas_call(
        kernel,
        out_shape=pltpu.VMEM((size, weight.shape[1]), weight.dtype),
        in_specs=[pl.BlockSpec(memory_space=pltpu.HBM)],
        out_specs=pl.BlockSpec(memory_space=pltpu.VMEM),
        scratch_shapes=[pltpu.SemaphoreType.DMA],
        compiler_params=pltpu.CompilerParams(vmem_limit_bytes=1024 * 1024),
        cost_estimate=pl.CostEstimate(flops=0, bytes_accessed=2 * size * weight.shape[1], transcendentals=0),
    )(pltpu.with_memory_space_constraint(weight, pltpu.HBM))


def terms_of(own, gate_weight, up_weight, down_weight):
    n, d = own.shape
    h = d // 2
    below, above = shift(own, 0, 1), shift(own, 0, -1)
    own_l, own_r, gate_v = lax.optimization_barrier((shift(own, 1, 0), shift(own, -1, 0), fetched(gate_weight)))
    own_2up, own_2down = shift(own_l[:, :h], 1, 0), shift(own_r[:, h:], -1, 0)
    below, above, own_2up, own_2down, up_v, up_weight = lax.optimization_barrier(
        (below, above, own_2up, own_2down, fetched(up_weight, 0, 2), up_weight)
    )
    near = jnp.concatenate([below, above], 0)
    below_2, above_2 = shift(below[:, :h], 0, 1), shift(above[:, h:], 0, -1)
    near_l, near_r = shift(near, 1, 0), shift(near, -1, 0)
    far, up_v2 = lax.optimization_barrier((jnp.concatenate([below_2, above_2], 1), fetched(up_weight, 1, 2)))
    weights = gate_v, up_v, up_v2
    early = early_hidden(own, own_l, own_r, own_2up, own_2down, below, above, far, weights)
    far_l, far_r = lax.optimization_barrier((shift(far, 1, 0), shift(far, -1, 0)))
    near_l, near_r, early = lax.optimization_barrier((near_l, near_r, early))
    near_2up, near_2down = shift(near_l[:n], 1, 0), shift(near_r[n:], -1, 0)
    far_2up, far_2down = shift(far_l[:, :h], 1, 0), shift(far_r[:, h:], -1, 0)
    late, two_up, two_down, down_v = late_hidden(
        near_l, near_r, far_l, far_r, near_2up, near_2down, far_2up, far_2down, early, weights, down_weight
    )
    return *other_terms(early, late, down_v), two_up, two_down


def returned(own_here, own_left, own_right, near_here, far_here, near_left, near_right, far_left, far_right, two_up, two_down):
    n, d = own_here.shape
    h = d // 2
    two_up, two_down = lax.optimization_barrier((shift(two_up, 1, 0), shift(two_down, -1, 0)))
    far_up, far_down = two_up[:, d + h :], two_down[:, d + h :]
    far_right = jnp.concatenate([b16(far_right[:, :h] + f32(far_up)), b16(far_right[:, h:])], 1)
    far_left = jnp.concatenate([b16(far_left[:, :h]), b16(far_left[:, h:] + f32(far_down))], 1)
    far_p, far_m = shift(far_right, 1, 0), shift(far_left, -1, 0)
    near_right = jnp.concatenate([b16(near_right[:n] + f32(two_up[:, :d])), b16(near_right[n:])], 0)
    near_left = jnp.concatenate([b16(near_left[:n]), b16(near_left[n:] + f32(two_down[:, :d]))], 0)
    near_p, near_m = shift(near_right, 1, 0), shift(near_left, -1, 0)
    far_sum = shift(b16(far_here + f32(far_p) + f32(far_m)), 0, 2)
    own_right = jnp.concatenate([b16(own_right[:, :h] + f32(two_up[:, d : d + h])), b16(own_right[:, h:])], 1)
    own_left = jnp.concatenate([b16(own_left[:, :h]), b16(own_left[:, h:] + f32(two_down[:, d : d + h]))], 1)
    own_right, own_left, near_p, near_m = lax.optimization_barrier((own_right, own_left, near_p, near_m))
    own_p, own_m = shift(own_right, 1, 0), shift(own_left, -1, 0)
    near_sum = b16(near_here + f32(near_p) + f32(near_m))
    from_below, from_above = shift(near_sum[n:], 0, 1), shift(near_sum[:n], 0, -1)
    return own_here + f32(own_p) + f32(own_m) + f32(far_sum) + f32(from_below) + f32(from_above)


def on_device(tokens, norm_gain, gate_weight, up_weight, down_weight):
    own = rms_normed(tokens, norm_gain)
    return b16(f32(tokens) + returned(*terms_of(own, gate_weight, up_weight, down_weight)))


def solution(mesh):
    return jax.shard_map(
        on_device,
        mesh=mesh,
        in_specs=(
            P(("dp", "tensor"), None),
            P(),
            P(None, "tensor"),
            P(None, "tensor"),
            P("tensor", None),
        ),
        out_specs=P(("dp", "tensor"), None),
        check_vma=False,
    )
```

time: 226 us -> 101 us (0.45)
  the two profiles are of different devices: /device:TPU:8 before, /device:TPU:38 now
where the time goes in v4:
time: 101 us
  starting transfers between devices  47.3 us (47%)
  waiting for transfers between devices  27 us (27%)
  Pallas kernels  24.4 us (24%)
  other arithmetic  1.37 us (1%)
    ppermute x27, starting transfers between devices, shift(): return lax.ppermute(block, 'tensor', pairs)  47.3 us
    ppermute x27, waiting for transfers between devices, shift(): return lax.ppermute(block, 'tensor', pairs)  27 us
    pallas_call x3, Pallas kernels, fetched(): pl.pallas_call(kernel, out_shape=pltpu.VMEM((size, weight.shape[1]), weig...  9.27 us
    pallas_call x1, Pallas kernels, late_hidden(): pl.pallas_call(kernel, out_shape=[pltpu.VMEM(shape, b) for shape in ((9 *...  6.81 us
    pallas_call x1, Pallas kernels, early_hidden(): pl.pallas_call(kernel, out_shape=pltpu.VMEM((7 * n, ff), jnp.bfloat16), i...  3.59 us
    pallas_call x1, Pallas kernels, other_terms(): pl.pallas_call(kernel, out_shape=[pltpu.VMEM((k * n, d), jnp.float32) for...  3.57 us
  transfers between devices with their start and end apart: 27, of which 11 were waited for; matrix products, arithmetic and copies ran while one was open for 1% of the time, Pallas kernels for 16%

profile of v4, /device:TPU:38, one launch (start us, length us, event | category | flops | bytes accessed | tf_op | source)
XLA Modules:
  0.0 100.6 jit_solution(3549485017293045998)
XLA Ops:
  0.0 1.1 %shard_map.55.own = bf16[16,6144]{1,0:T(8,128)(2,1)S(1)} custom-call(bf16[16,6144]{1,0:T(8,128)(2,1)} %rows_ref.1, f32[1,6144]{1,0:T(1,128)} %bitcast.1), custom_call_target="tpu_custom_call" | custom-call | tf_op jit(solution)/shard_map/pallas_call | solution.py:35
  1.1 0.9 collective-permute-start.3
  2.0 2.4 %collective-permute-start.2 = (bf16[16,6144]{1,0:T(8,128)(2,1)S(1)}, bf16[16,6144]{1,0:T(8,128)(2,1)S(1)}, u32[]{:S(2)}, u32[]{:S(2)}) collective-permute-start(bf16[16,6144]{1,0:T(8,128)(2,1)S(1)} %shard_map.55.own), channel_id=1, source_target_pairs={{0,4},{1,5},{2,6},{3,7},{4,8},{5,9},{6,10},{7,11},{8,12},{9,13},{1... | collective-permute-start | bytes 589832 | tf_op jit(solution)/shard_map/ppermute | solution.py:17
  4.4 5.4 %collective-permute-start.1 = (bf16[16,6144]{1,0:T(8,128)(2,1)S(1)}, bf16[16,6144]{1,0:T(8,128)(2,1)S(1)}, u32[]{:S(2)}, u32[]{:S(2)}) collective-permute-start(bf16[16,6144]{1,0:T(8,128)(2,1)S(1)} %shard_map.55.own), channel_id=1, source_target_pairs={{0,3},{1,0},{2,1},{3,2},{4,7},{5,4},{6,5},{7,6},{8,11},{9,8},{10,9... | collective-permute-start | bytes 589832 | tf_op jit(solution)/shard_map/ppermute | solution.py:17
  9.8 0.0 collective-permute-start
  9.8 4.1 %shard_map.56.gate_w = bf16[6144,896]{1,0:T(8,128)(2,1)S(1)} custom-call(bf16[6144,896]{1,0:T(8,128)(2,1)} %source.3), custom_call_target="tpu_custom_call" | custom-call | bytes 11010048 | tf_op jit(solution)/shard_map/pallas_call | solution.py:164
  14.0 0.0 collective-permute-done.3.own_r
  14.0 0.1 collective-permute-start.5
  14.1 3.2 %collective-permute-start.4 = (bf16[16,3072]{1,0:T(8,128)(2,1)S(1)}, bf16[16,3072]{1,0:T(8,128)(2,1)S(1)}, u32[]{:S(2)}, u32[]{:S(2)}) collective-permute-start(bf16[16,3072]{1,0:T(8,128)(2,1)S(1)} %slice.90), channel_id=1, source_target_pairs={{0,4},{1,5},{2,6},{3,7},{4,8},{5,9},{6,10},{7,11},{8,12},{9,13},{1... | collective-permute-start | bytes 294920 | tf_op jit(solution)/shard_map/ppermute | solution.py:17
  17.4 2.6 %shard_map.57.up_w = bf16[3072,896]{1,0:T(8,128)(2,1)S(1)} custom-call(bf16[6144,896]{1,0:T(8,128)(2,1)} %source.5), custom_call_target="tpu_custom_call" | custom-call | bytes 5505024 | tf_op jit(solution)/shard_map/pallas_call | solution.py:164
  19.9 1.8 %collective-permute-done.below = bf16[16,6144]{1,0:T(8,128)(2,1)S(1)} collective-permute-done((bf16[16,6144]{1,0:T(8,128)(2,1)S(1)}, bf16[16,6144]{1,0:T(8,128)(2,1)S(1)}, u32[]{:S(2)}, u32[]{:S(2)}) %collective-permute-start) | collective-permute-done | bytes 196640 | tf_op jit(solution)/shard_map/ppermute | solution.py:17
  21.8 2.4 %collective-permute-start.9 = (bf16[16,3072]{1,0:T(8,128)(2,1)S(1)}, bf16[16,3072]{1,0:T(8,128)(2,1)S(1)}, u32[]{:S(2)}, u32[]{:S(2)}) collective-permute-start(bf16[16,3072]{1,0:T(8,128)(2,1)S(1)} %slice.93), channel_id=1, source_target_pairs={{0,3},{1,0},{2,1},{3,2},{4,7},{5,4},{6,5},{7,6},{8,11},{9,8},{10,9... | collective-permute-start | bytes 294920 | tf_op jit(solution)/shard_map/ppermute | solution.py:17
  24.2 0.6 collective-permute-start.8
  24.8 0.1 collective-permute-start.7
  24.9 3.2 %collective-permute-start.6 = (bf16[32,6144]{1,0:T(8,128)(2,1)S(1)}, bf16[32,6144]{1,0:T(8,128)(2,1)S(1)}, u32[]{:S(2)}, u32[]{:S(2)}) collective-permute-start(bf16[32,6144]{1,0:T(8,128)(2,1)S(1)} %constant_dynamic-update-slice_fusion), channel_id=1, source_target_pairs={{0,4},{1,5},{2,6},{3,7},{4,8},{5,9},{6,10},{7,11},{8,12},{9,13},{1... | collective-permute-start | bytes 1179656 | tf_op jit(solution)/shard_map/ppermute | solution.py:17
  28.2 2.6 %shard_map.58.up_w2 = bf16[3072,896]{1,0:T(8,128)(2,1)S(1)} custom-call(bf16[6144,896]{1,0:T(8,128)(2,1)} %source.5), custom_call_target="tpu_custom_call" | custom-call | bytes 5505024 | tf_op jit(solution)/shard_map/pallas_call | solution.py:164
  30.7 1.4 %collective-permute-done.8 = bf16[16,3072]{1,0:T(8,128)(2,1)S(1)} collective-permute-done((bf16[16,3072]{1,0:T(8,128)(2,1)S(1)}, bf16[16,3072]{1,0:T(8,128)(2,1)S(1)}, u32[]{:S(2)}, u32[]{:S(2)}) %collective-permute-start.8) | collective-permute-done | bytes 98336 | tf_op jit(solution)/shard_map/ppermute | solution.py:17
  32.2 0.1 collective-permute-start.11
  32.3 3.3 %collective-permute-start.10 = (bf16[16,6144]{1,0:T(8,128)(2,1)S(1)}, bf16[16,6144]{1,0:T(8,128)(2,1)S(1)}, u32[]{:S(2)}, u32[]{:S(2)}) collective-permute-start(bf16[16,6144]{1,0:T(8,128)(2,1)S(1)} %pad_maximum_fusion.2.far), channel_id=1, source_target_pairs={{0,4},{1,5},{2,6},{3,7},{4,8},{5,9},{6,10},{7,11},{8,12},{9,13},{1... | collective-permute-start | bytes 589832 | tf_op jit(solution)/shard_map/ppermute | solution.py:17
  35.6 3.6 %shard_map.59.early = bf16[112,896]{1,0:T(8,128)(2,1)S(1)} custom-call(bf16[16,6144]{1,0:T(8,128)(2,1)S(1)} %shard_map.55.own, bf16[16,6144]{1,0:T(8,128)(2,1)S(1)} %collective-permute-done.2.own_l, bf16[16,6144]{1,0:T(8,128)(2,1)S(1)} %collective-permute-done.3.own_r, bf16[16,3072]{1,0:T(8,128)(2,1)S(1)} %collective-permute-done.4.own_2up, ...), custom_call_target="tpu_custom_call" | custom-call | flops 2466250752 | tf_op jit(solution)/shard_map/pallas_call | solution.py:68
  39.2 0.1 collective-permute-start.13
  39.3 3.2 %collective-permute-start.12 = (bf16[16,6144]{1,0:T(8,128)(2,1)S(1)}, bf16[16,6144]{1,0:T(8,128)(2,1)S(1)}, u32[]{:S(2)}, u32[]{:S(2)}) collective-permute-start(bf16[16,6144]{1,0:T(8,128)(2,1)S(1)} %slice.94), channel_id=1, source_target_pairs={{0,4},{1,5},{2,6},{3,7},{4,8},{5,9},{6,10},{7,11},{8,12},{9,13},{1... | collective-permute-start | bytes 589832 | tf_op jit(solution)/shard_map/ppermute | solution.py:17
  42.6 0.1 collective-permute-start.15
  42.7 3.2 %collective-permute-start.14 = (bf16[16,3072]{1,0:T(8,128)(2,1)S(1)}, bf16[16,3072]{1,0:T(8,128)(2,1)S(1)}, u32[]{:S(2)}, u32[]{:S(2)}) collective-permute-start(bf16[16,3072]{1,0:T(8,128)(2,1)S(1)} %slice.96), channel_id=1, source_target_pairs={{0,4},{1,5},{2,6},{3,7},{4,8},{5,9},{6,10},{7,11},{8,12},{9,13},{1... | collective-permute-start | bytes 294920 | tf_op jit(solution)/shard_map/ppermute | solution.py:17
  45.9 2.6 %collective-permute-done.15.far_2down = bf16[16,3072]{1,0:T(8,128)(2,1)S(1)} collective-permute-done((bf16[16,3072]{1,0:T(8,128)(2,1)S(1)}, bf16[16,3072]{1,0:T(8,128)(2,1)S(1)}, u32[]{:S(2)}, u32[]{:S(2)}) %collective-permute-start.15) | collective-permute-done | bytes 98336 | tf_op jit(solution)/shard_map/ppermute | solution.py:17
  48.5 6.8 %shard_map.60 = (bf16[144,896]{1,0:T(8,128)(2,1)S(1)}, bf16[16,12288]{1,0:T(8,128)(2,1)S(1)}, bf16[16,12288]{1,0:T(8,128)(2,1)S(1)}, bf16[896,6144]{1,0:T(8,128)(2,1)S(1)}) custom-call(bf16[32,6144]{1,0:T(8,128)(2,1)S(1)} %collective-permute-done.6.near_l, bf16[32,6144]{1,0:T(8,128)(2,1)S(1)} %collective-permute-done.7.near_r, ...), custom_call_target="tpu_custom_call" | custom-call | flops 3875536896 | bytes 11010048 | tf_op jit(solution)/shard_map/pallas_call | solution.py:111
  55.3 3.3 %collective-permute-start.16 = (bf16[16,12288]{1,0:T(8,128)(2,1)S(1)}, bf16[16,12288]{1,0:T(8,128)(2,1)S(1)}, u32[]{:S(2)}, u32[]{:S(2)}) collective-permute-start(bf16[16,12288]{1,0:T(8,128)(2,1)S(1)} %get-tuple-element.60), channel_id=1, source_target_pairs={{0,4},{1,5},{2,6},{3,7},{4,8},{5,9},{6,10},{7,11},{8,12},{9,13},{1... | collective-permute-start | bytes 1179656 | tf_op jit(solution)/shard_map/ppermute | solution.py:17
  58.6 0.0 collective-permute-start.17
  58.7 3.6 %shard_map.61 = (f32[16,6144]{1,0:T(8,128)S(1)}, f32[16,6144]{1,0:T(8,128)S(1)}, f32[16,6144]{1,0:T(8,128)S(1)}, f32[32,6144]{1,0:T(8,128)S(1)}, f32[16,6144]{1,...) custom-call(bf16[112,896]{1,0:T(8,128)(2,1)S(1)} %shard_map.59.early, ...), custom_call_target="tpu_custom_call" | custom-call | flops 2113929216 | tf_op jit(solution)/shard_map/pallas_call | solution.py:145
  62.4 1.6 %collective-permute-done.16 = bf16[16,12288]{1,0:T(8,128)(2,1)S(1)} collective-permute-done((bf16[16,12288]{1,0:T(8,128)(2,1)S(1)}, bf16[16,12288]{1,0:T(8,128)(2,1)S(1)}, u32[]{:S(2)}, u32[]{:S(2)}) %collective-permute-start.16) | collective-permute-done | bytes 393248 | tf_op jit(solution)/shard_map/ppermute | solution.py:17
  63.9 6.7 %collective-permute-done.17 = bf16[16,12288]{1,0:T(8,128)(2,1)S(1)} collective-permute-done((bf16[16,12288]{1,0:T(8,128)(2,1)S(1)}, bf16[16,12288]{1,0:T(8,128)(2,1)S(1)}, u32[]{:S(2)}, u32[]{:S(2)}) %collective-permute-start.17) | collective-permute-done | bytes 393248 | tf_op jit(solution)/shard_map/ppermute | solution.py:17
  70.9 0.1 collective-permute-start.23
  71.0 3.3 %collective-permute-start.22 = (bf16[16,6144]{1,0:T(8,128)(2,1)S(1)}, bf16[16,6144]{1,0:T(8,128)(2,1)S(1)}, u32[]{:S(2)}, u32[]{:S(2)}) collective-permute-start(bf16[16,6144]{1,0:T(8,128)(2,1)S(1)} %pad_maximum_fusion.5), channel_id=1, source_target_pairs={{0,4},{1,5},{2,6},{3,7},{4,8},{5,9},{6,10},{7,11},{8,12},{9,13},{1... | collective-permute-start | bytes 589832 | tf_op jit(solution)/shard_map/ppermute | solution.py:17
  74.3 0.1 collective-permute-start.19
  74.5 3.3 %collective-permute-start.18 = (bf16[32,6144]{1,0:T(8,128)(2,1)S(1)}, bf16[32,6144]{1,0:T(8,128)(2,1)S(1)}, u32[]{:S(2)}, u32[]{:S(2)}) collective-permute-start(bf16[32,6144]{1,0:T(8,128)(2,1)S(1)} %pad_maximum_fusion), channel_id=1, source_target_pairs={{0,4},{1,5},{2,6},{3,7},{4,8},{5,9},{6,10},{7,11},{8,12},{9,13},{1... | collective-permute-start | bytes 1179656 | tf_op jit(solution)/shard_map/ppermute | solution.py:17
  77.8 0.1 collective-permute-done.23
  77.9 0.1 add_convert_fusion.2
  77.9 1.0 %collective-permute-start.24 = (bf16[16,6144]{1,0:T(8,128)(2,1)S(1)}, bf16[16,6144]{1,0:T(8,128)(2,1)S(1)}, u32[]{:S(2)}, u32[]{:S(2)}) collective-permute-start(bf16[16,6144]{1,0:T(8,128)(2,1)S(1)} %add_convert_fusion.2), channel_id=1, source_target_pairs={{0,2},{1,3},{2,0},{3,1},{4,6},{5,7},{6,4},{7,5},{8,10},{9,11},{10,... | collective-permute-start | bytes 589832 | tf_op jit(solution)/shard_map/ppermute | solution.py:17
  78.9 5.9 %collective-permute-done.19 = bf16[32,6144]{1,0:T(8,128)(2,1)S(1)} collective-permute-done((bf16[32,6144]{1,0:T(8,128)(2,1)S(1)}, bf16[32,6144]{1,0:T(8,128)(2,1)S(1)}, u32[]{:S(2)}, u32[]{:S(2)}) %collective-permute-start.19) | collective-permute-done | bytes 393248 | tf_op jit(solution)/shard_map/ppermute | solution.py:17
  84.8 0.1 add_convert_fusion
  85.0 0.1 collective-permute-start.25
  85.1 4.1 %collective-permute-start.26 = (bf16[16,6144]{1,0:T(8,128)(2,1)S(1)}, bf16[16,6144]{1,0:T(8,128)(2,1)S(1)}, u32[]{:S(2)}, u32[]{:S(2)}) collective-permute-start(bf16[16,6144]{1,0:T(8,128)(2,1)S(1)} %get-tuple-element.80), channel_id=1, source_target_pairs={{0,3},{1,0},{2,1},{3,2},{4,7},{5,4},{6,5},{7,6},{8,11},{9,8},{10,9... | collective-permute-start | bytes 589832 | tf_op jit(solution)/shard_map/ppermute | solution.py:17
  89.2 3.7 %collective-permute-start.20 = (bf16[16,6144]{1,0:T(8,128)(2,1)S(1)}, bf16[16,6144]{1,0:T(8,128)(2,1)S(1)}, u32[]{:S(2)}, u32[]{:S(2)}) collective-permute-start(bf16[16,6144]{1,0:T(8,128)(2,1)S(1)} %pad_maximum_fusion.3), channel_id=1, source_target_pairs={{0,4},{1,5},{2,6},{3,7},{4,8},{5,9},{6,10},{7,11},{8,12},{9,13},{1... | collective-permute-start | bytes 589832 | tf_op jit(solution)/shard_map/ppermute | solution.py:17
  92.9 0.6 collective-permute-done.25
  93.5 0.5 collective-permute-done.26
  94.0 2.1 %collective-permute-done.20 = bf16[16,6144]{1,0:T(8,128)(2,1)S(1)} collective-permute-done((bf16[16,6144]{1,0:T(8,128)(2,1)S(1)}, bf16[16,6144]{1,0:T(8,128)(2,1)S(1)}, u32[]{:S(2)}, u32[]{:S(2)}) %collective-permute-start.20) | collective-permute-done | bytes 196640 | tf_op jit(solution)/shard_map/ppermute | solution.py:17
  96.1 3.7 %collective-permute-done.21 = bf16[16,6144]{1,0:T(8,128)(2,1)S(1)} collective-permute-done((bf16[16,6144]{1,0:T(8,128)(2,1)S(1)}, bf16[16,6144]{1,0:T(8,128)(2,1)S(1)}, u32[]{:S(2)}, u32[]{:S(2)}) %collective-permute-start.21) | collective-permute-done | bytes 196640 | tf_op jit(solution)/shard_map/ppermute | solution.py:17
  99.8 0.9 add_convert_fusion.1
  (46 shorter events, 0.6 us)
Async XLA Ops:
  1.1 12.9 %collective-permute-start.3 = (bf16[16,6144]{1,0:T(8,128)(2,1)S(1)}, bf16[16,6144]{1,0:T(8,128)(2,1)S(1)}, u32[]{:S(2)}, u32[]{:S(2)}) collective-permute-start(bf16[16,6144]{1,0:T(8,128)(2,1)S(1)} %shard_map.55.own), channel_id=1, source_target_pairs={{0,12},{1,13},{2,14},{3,15},{4,0},{5,1},{6,2},{7,3},{8,4},{9,5},{1... | collective-permute-start | bytes 589832 | tf_op jit(solution)/shard_map/ppermute | solution.py:17
  2.0 12.0 %collective-permute-start.2 = (bf16[16,6144]{1,0:T(8,128)(2,1)S(1)}, bf16[16,6144]{1,0:T(8,128)(2,1)S(1)}, u32[]{:S(2)}, u32[]{:S(2)}) collective-permute-start(bf16[16,6144]{1,0:T(8,128)(2,1)S(1)} %shard_map.55.own), channel_id=1, source_target_pairs={{0,4},{1,5},{2,6},{3,7},{4,8},{5,9},{6,10},{7,11},{8,12},{9,13},{1... | collective-permute-start | bytes 589832 | tf_op jit(solution)/shard_map/ppermute | solution.py:17
  4.4 15.5 %collective-permute-start.1 = (bf16[16,6144]{1,0:T(8,128)(2,1)S(1)}, bf16[16,6144]{1,0:T(8,128)(2,1)S(1)}, u32[]{:S(2)}, u32[]{:S(2)}) collective-permute-start(bf16[16,6144]{1,0:T(8,128)(2,1)S(1)} %shard_map.55.own), channel_id=1, source_target_pairs={{0,3},{1,0},{2,1},{3,2},{4,7},{5,4},{6,5},{7,6},{8,11},{9,8},{10,9... | collective-permute-start | bytes 589832 | tf_op jit(solution)/shard_map/ppermute | solution.py:17
  9.8 11.9 %collective-permute-start = (bf16[16,6144]{1,0:T(8,128)(2,1)S(1)}, bf16[16,6144]{1,0:T(8,128)(2,1)S(1)}, u32[]{:S(2)}, u32[]{:S(2)}) collective-permute-start(bf16[16,6144]{1,0:T(8,128)(2,1)S(1)} %shard_map.55.own), channel_id=1, source_target_pairs={{0,1},{1,2},{2,3},{3,0},{4,5},{5,6},{6,7},{7,4},{8,9},{9,10},{10,1... | collective-permute-start | bytes 589832 | tf_op jit(solution)/shard_map/ppermute | solution.py:17
  14.0 7.7 %collective-permute-start.5 = (bf16[16,3072]{1,0:T(8,128)(2,1)S(1)}, bf16[16,3072]{1,0:T(8,128)(2,1)S(1)}, u32[]{:S(2)}, u32[]{:S(2)}) collective-permute-start(bf16[16,3072]{1,0:T(8,128)(2,1)S(1)} %slice.91), channel_id=1, source_target_pairs={{0,12},{1,13},{2,14},{3,15},{4,0},{5,1},{6,2},{7,3},{8,4},{9,5},{1... | collective-permute-start | bytes 294920 | tf_op jit(solution)/shard_map/ppermute | solution.py:17
  14.1 7.6 %collective-permute-start.4 = (bf16[16,3072]{1,0:T(8,128)(2,1)S(1)}, bf16[16,3072]{1,0:T(8,128)(2,1)S(1)}, u32[]{:S(2)}, u32[]{:S(2)}) collective-permute-start(bf16[16,3072]{1,0:T(8,128)(2,1)S(1)} %slice.90), channel_id=1, source_target_pairs={{0,4},{1,5},{2,6},{3,7},{4,8},{5,9},{6,10},{7,11},{8,12},{9,13},{1... | collective-permute-start | bytes 294920 | tf_op jit(solution)/shard_map/ppermute | solution.py:17
  21.8 8.9 %collective-permute-start.9 = (bf16[16,3072]{1,0:T(8,128)(2,1)S(1)}, bf16[16,3072]{1,0:T(8,128)(2,1)S(1)}, u32[]{:S(2)}, u32[]{:S(2)}) collective-permute-start(bf16[16,3072]{1,0:T(8,128)(2,1)S(1)} %slice.93), channel_id=1, source_target_pairs={{0,3},{1,0},{2,1},{3,2},{4,7},{5,4},{6,5},{7,6},{8,11},{9,8},{10,9... | collective-permute-start | bytes 294920 | tf_op jit(solution)/shard_map/ppermute | solution.py:17
  24.2 7.9 %collective-permute-start.8 = (bf16[16,3072]{1,0:T(8,128)(2,1)S(1)}, bf16[16,3072]{1,0:T(8,128)(2,1)S(1)}, u32[]{:S(2)}, u32[]{:S(2)}) collective-permute-start(bf16[16,3072]{1,0:T(8,128)(2,1)S(1)} %slice.92), channel_id=1, source_target_pairs={{0,1},{1,2},{2,3},{3,0},{4,5},{5,6},{6,7},{7,4},{8,9},{9,10},{10,1... | collective-permute-start | bytes 294920 | tf_op jit(solution)/shard_map/ppermute | solution.py:17
  24.8 14.3 %collective-permute-start.7 = (bf16[32,6144]{1,0:T(8,128)(2,1)S(1)}, bf16[32,6144]{1,0:T(8,128)(2,1)S(1)}, u32[]{:S(2)}, u32[]{:S(2)}) collective-permute-start(bf16[32,6144]{1,0:T(8,128)(2,1)S(1)} %constant_dynamic-update-slice_fusion), channel_id=1, source_target_pairs={{0,12},{1,13},{2,14},{3,15},{4,0},{5,1},{6,2},{7,3},{8,4},{9,5},{1... | collective-permute-start | bytes 1179656 | tf_op jit(solution)/shard_map/ppermute | solution.py:17
  24.9 14.3 %collective-permute-start.6 = (bf16[32,6144]{1,0:T(8,128)(2,1)S(1)}, bf16[32,6144]{1,0:T(8,128)(2,1)S(1)}, u32[]{:S(2)}, u32[]{:S(2)}) collective-permute-start(bf16[32,6144]{1,0:T(8,128)(2,1)S(1)} %constant_dynamic-update-slice_fusion), channel_id=1, source_target_pairs={{0,4},{1,5},{2,6},{3,7},{4,8},{5,9},{6,10},{7,11},{8,12},{9,13},{1... | collective-permute-start | bytes 1179656 | tf_op jit(solution)/shard_map/ppermute | solution.py:17
  32.2 10.4 %collective-permute-start.11 = (bf16[16,6144]{1,0:T(8,128)(2,1)S(1)}, bf16[16,6144]{1,0:T(8,128)(2,1)S(1)}, u32[]{:S(2)}, u32[]{:S(2)}) collective-permute-start(bf16[16,6144]{1,0:T(8,128)(2,1)S(1)} %pad_maximum_fusion.2.far), channel_id=1, source_target_pairs={{0,12},{1,13},{2,14},{3,15},{4,0},{5,1},{6,2},{7,3},{8,4},{9,5},{1... | collective-permute-start | bytes 589832 | tf_op jit(solution)/shard_map/ppermute | solution.py:17
  32.3 10.3 %collective-permute-start.10 = (bf16[16,6144]{1,0:T(8,128)(2,1)S(1)}, bf16[16,6144]{1,0:T(8,128)(2,1)S(1)}, u32[]{:S(2)}, u32[]{:S(2)}) collective-permute-start(bf16[16,6144]{1,0:T(8,128)(2,1)S(1)} %pad_maximum_fusion.2.far), channel_id=1, source_target_pairs={{0,4},{1,5},{2,6},{3,7},{4,8},{5,9},{6,10},{7,11},{8,12},{9,13},{1... | collective-permute-start | bytes 589832 | tf_op jit(solution)/shard_map/ppermute | solution.py:17
  39.2 9.3 %collective-permute-start.13 = (bf16[16,6144]{1,0:T(8,128)(2,1)S(1)}, bf16[16,6144]{1,0:T(8,128)(2,1)S(1)}, u32[]{:S(2)}, u32[]{:S(2)}) collective-permute-start(bf16[16,6144]{1,0:T(8,128)(2,1)S(1)} %slice.95), channel_id=1, source_target_pairs={{0,12},{1,13},{2,14},{3,15},{4,0},{5,1},{6,2},{7,3},{8,4},{9,5},{1... | collective-permute-start | bytes 589832 | tf_op jit(solution)/shard_map/ppermute | solution.py:17
  39.3 9.2 %collective-permute-start.12 = (bf16[16,6144]{1,0:T(8,128)(2,1)S(1)}, bf16[16,6144]{1,0:T(8,128)(2,1)S(1)}, u32[]{:S(2)}, u32[]{:S(2)}) collective-permute-start(bf16[16,6144]{1,0:T(8,128)(2,1)S(1)} %slice.94), channel_id=1, source_target_pairs={{0,4},{1,5},{2,6},{3,7},{4,8},{5,9},{6,10},{7,11},{8,12},{9,13},{1... | collective-permute-start | bytes 589832 | tf_op jit(solution)/shard_map/ppermute | solution.py:17
  42.6 5.9 %collective-permute-start.15 = (bf16[16,3072]{1,0:T(8,128)(2,1)S(1)}, bf16[16,3072]{1,0:T(8,128)(2,1)S(1)}, u32[]{:S(2)}, u32[]{:S(2)}) collective-permute-start(bf16[16,3072]{1,0:T(8,128)(2,1)S(1)} %slice.97), channel_id=1, source_target_pairs={{0,12},{1,13},{2,14},{3,15},{4,0},{5,1},{6,2},{7,3},{8,4},{9,5},{1... | collective-permute-start | bytes 294920 | tf_op jit(solution)/shard_map/ppermute | solution.py:17
  42.7 5.8 %collective-permute-start.14 = (bf16[16,3072]{1,0:T(8,128)(2,1)S(1)}, bf16[16,3072]{1,0:T(8,128)(2,1)S(1)}, u32[]{:S(2)}, u32[]{:S(2)}) collective-permute-start(bf16[16,3072]{1,0:T(8,128)(2,1)S(1)} %slice.96), channel_id=1, source_target_pairs={{0,4},{1,5},{2,6},{3,7},{4,8},{5,9},{6,10},{7,11},{8,12},{9,13},{1... | collective-permute-start | bytes 294920 | tf_op jit(solution)/shard_map/ppermute | solution.py:17
  55.3 8.6 %collective-permute-start.16 = (bf16[16,12288]{1,0:T(8,128)(2,1)S(1)}, bf16[16,12288]{1,0:T(8,128)(2,1)S(1)}, u32[]{:S(2)}, u32[]{:S(2)}) collective-permute-start(bf16[16,12288]{1,0:T(8,128)(2,1)S(1)} %get-tuple-element.60), channel_id=1, source_target_pairs={{0,4},{1,5},{2,6},{3,7},{4,8},{5,9},{6,10},{7,11},{8,12},{9,13},{1... | collective-permute-start | bytes 1179656 | tf_op jit(solution)/shard_map/ppermute | solution.py:17
  58.6 12.0 %collective-permute-start.17 = (bf16[16,12288]{1,0:T(8,128)(2,1)S(1)}, bf16[16,12288]{1,0:T(8,128)(2,1)S(1)}, u32[]{:S(2)}, u32[]{:S(2)}) collective-permute-start(bf16[16,12288]{1,0:T(8,128)(2,1)S(1)} %get-tuple-element.61), channel_id=1, source_target_pairs={{0,12},{1,13},{2,14},{3,15},{4,0},{5,1},{6,2},{7,3},{8,4},{9,5},{1... | collective-permute-start | bytes 1179656 | tf_op jit(solution)/shard_map/ppermute | solution.py:17
  58.6 41.1 %copy-start = (bf16[16,6144]{1,0:T(8,128)(2,1)S(1)}, bf16[16,6144]{1,0:T(8,128)(2,1)}, u32[]{:S(2)}) copy-start(bf16[16,6144]{1,0:T(8,128)(2,1)} %rows_ref.1) | copy-start | bytes 589828
  70.9 7.0 %collective-permute-start.23 = (bf16[16,6144]{1,0:T(8,128)(2,1)S(1)}, bf16[16,6144]{1,0:T(8,128)(2,1)S(1)}, u32[]{:S(2)}, u32[]{:S(2)}) collective-permute-start(bf16[16,6144]{1,0:T(8,128)(2,1)S(1)} %pad_maximum_fusion.6), channel_id=1, source_target_pairs={{0,12},{1,13},{2,14},{3,15},{4,0},{5,1},{6,2},{7,3},{8,4},{9,5},{1... | collective-permute-start | bytes 589832 | tf_op jit(solution)/shard_map/ppermute | solution.py:17
  71.0 6.8 %collective-permute-start.22 = (bf16[16,6144]{1,0:T(8,128)(2,1)S(1)}, bf16[16,6144]{1,0:T(8,128)(2,1)S(1)}, u32[]{:S(2)}, u32[]{:S(2)}) collective-permute-start(bf16[16,6144]{1,0:T(8,128)(2,1)S(1)} %pad_maximum_fusion.5), channel_id=1, source_target_pairs={{0,4},{1,5},{2,6},{3,7},{4,8},{5,9},{6,10},{7,11},{8,12},{9,13},{1... | collective-permute-start | bytes 589832 | tf_op jit(solution)/shard_map/ppermute | solution.py:17
  74.3 10.5 %collective-permute-start.19 = (bf16[32,6144]{1,0:T(8,128)(2,1)S(1)}, bf16[32,6144]{1,0:T(8,128)(2,1)S(1)}, u32[]{:S(2)}, u32[]{:S(2)}) collective-permute-start(bf16[32,6144]{1,0:T(8,128)(2,1)S(1)} %pad_maximum_fusion.1), channel_id=1, source_target_pairs={{0,12},{1,13},{2,14},{3,15},{4,0},{5,1},{6,2},{7,3},{8,4},{9,5},{1... | collective-permute-start | bytes 1179656 | tf_op jit(solution)/shard_map/ppermute | solution.py:17
  74.5 10.4 %collective-permute-start.18 = (bf16[32,6144]{1,0:T(8,128)(2,1)S(1)}, bf16[32,6144]{1,0:T(8,128)(2,1)S(1)}, u32[]{:S(2)}, u32[]{:S(2)}) collective-permute-start(bf16[32,6144]{1,0:T(8,128)(2,1)S(1)} %pad_maximum_fusion), channel_id=1, source_target_pairs={{0,4},{1,5},{2,6},{3,7},{4,8},{5,9},{6,10},{7,11},{8,12},{9,13},{1... | collective-permute-start | bytes 1179656 | tf_op jit(solution)/shard_map/ppermute | solution.py:17
  77.9 15.0 %collective-permute-start.24 = (bf16[16,6144]{1,0:T(8,128)(2,1)S(1)}, bf16[16,6144]{1,0:T(8,128)(2,1)S(1)}, u32[]{:S(2)}, u32[]{:S(2)}) collective-permute-start(bf16[16,6144]{1,0:T(8,128)(2,1)S(1)} %add_convert_fusion.2), channel_id=1, source_target_pairs={{0,2},{1,3},{2,0},{3,1},{4,6},{5,7},{6,4},{7,5},{8,10},{9,11},{10,... | collective-permute-start | bytes 589832 | tf_op jit(solution)/shard_map/ppermute | solution.py:17
  85.0 8.5 %collective-permute-start.25 = (bf16[16,6144]{1,0:T(8,128)(2,1)S(1)}, bf16[16,6144]{1,0:T(8,128)(2,1)S(1)}, u32[]{:S(2)}, u32[]{:S(2)}) collective-permute-start(bf16[16,6144]{1,0:T(8,128)(2,1)S(1)} %get-tuple-element.79), channel_id=1, source_target_pairs={{0,1},{1,2},{2,3},{3,0},{4,5},{5,6},{6,7},{7,4},{8,9},{9,10},{10,1... | collective-permute-start | bytes 589832 | tf_op jit(solution)/shard_map/ppermute | solution.py:17
  85.1 8.9 %collective-permute-start.26 = (bf16[16,6144]{1,0:T(8,128)(2,1)S(1)}, bf16[16,6144]{1,0:T(8,128)(2,1)S(1)}, u32[]{:S(2)}, u32[]{:S(2)}) collective-permute-start(bf16[16,6144]{1,0:T(8,128)(2,1)S(1)} %get-tuple-element.80), channel_id=1, source_target_pairs={{0,3},{1,0},{2,1},{3,2},{4,7},{5,4},{6,5},{7,6},{8,11},{9,8},{10,9... | collective-permute-start | bytes 589832 | tf_op jit(solution)/shard_map/ppermute | solution.py:17
  89.2 6.9 %collective-permute-start.20 = (bf16[16,6144]{1,0:T(8,128)(2,1)S(1)}, bf16[16,6144]{1,0:T(8,128)(2,1)S(1)}, u32[]{:S(2)}, u32[]{:S(2)}) collective-permute-start(bf16[16,6144]{1,0:T(8,128)(2,1)S(1)} %pad_maximum_fusion.3), channel_id=1, source_target_pairs={{0,4},{1,5},{2,6},{3,7},{4,8},{5,9},{6,10},{7,11},{8,12},{9,13},{1... | collective-permute-start | bytes 589832 | tf_op jit(solution)/shard_map/ppermute | solution.py:17
  92.9 6.9 %collective-permute-start.21 = (bf16[16,6144]{1,0:T(8,128)(2,1)S(1)}, bf16[16,6144]{1,0:T(8,128)(2,1)S(1)}, u32[]{:S(2)}, u32[]{:S(2)}) collective-permute-start(bf16[16,6144]{1,0:T(8,128)(2,1)S(1)} %pad_maximum_fusion.4), channel_id=1, source_target_pairs={{0,12},{1,13},{2,14},{3,15},{4,0},{5,1},{6,2},{7,3},{8,4},{9,5},{1... | collective-permute-start | bytes 589832 | tf_op jit(solution)/shard_map/ppermute | solution.py:17

commit v5 on v4

--- a/solution.py
+++ b/solution.py
@@ -53,46 +53,46 @@
     return b16(gate / (1.0 + jnp.exp(-gate)) * up)
 
 
-def early_hidden(own, own_l, own_r, own_2up, own_2down, below, above, far, weights):
-    n, d = own.shape
-    h, ff = d // 2, weights[0].shape[1]
-
-    def kernel(own, own_l, own_r, own_2up, own_2down, below, above, far, gate_w, up_w, up_w2, out, rows):
-        for i, ref in ((0, own), (1, own_l), (2, own_r), (4, below), (5, above), (6, far)):
+def early_hidden(blocks, weights):
+    (n, d), ff, sets = blocks[0].shape, weights[0].shape[1], len(blocks)
+
+    def kernel(*refs):
+        ins, ws, (out, rows) = refs[:sets], refs[sets:-2], refs[-2:]
+        for i, ref in enumerate(ins):
             rows[i * n : (i + 1) * n, :] = ref[...]
-        rows[3 * n : 4 * n, :h] = own_2up[...]
-        rows[3 * n : 4 * n, h:] = own_2down[...]
-        out[...] = hidden_of(rows, gate_w, up_w, up_w2)
+        out[...] = hidden_of(rows, *ws)
 
     vmem = pl.BlockSpec(memory_space=pltpu.VMEM)
     return pl.pallas_call(
         kernel,
-        out_shape=pltpu.VMEM((7 * n, ff), jnp.bfloat16),
-        in_specs=[vmem] * 11,
+        out_shape=pltpu.VMEM((sets * n, ff), jnp.bfloat16),
+        in_specs=[vmem] * (sets + len(weights)),
         out_specs=vmem,
-        scratch_shapes=[pltpu.VMEM((7 * n, d), jnp.bfloat16)],
+        scratch_shapes=[pltpu.VMEM((sets * n, d), jnp.bfloat16)],
         compiler_params=pltpu.CompilerParams(vmem_limit_bytes=8 * 1024 * 1024),
-        cost_estimate=pl.CostEstimate(flops=4 * 7 * n * d * ff, bytes_accessed=0, transcendentals=7 * n * ff),
-    )(*placed((own, own_l, own_r, own_2up, own_2down, below, above, far, *weights)))
-
-
-def late_hidden(near_l, near_r, far_l, far_r, near_2up, near_2down, far_2up, far_2down, early, weights, down_weight):
+        cost_estimate=pl.CostEstimate(flops=4 * sets * n * d * ff, bytes_accessed=0, transcendentals=sets * n * ff),
+    )(*placed((*blocks, *weights)))
+
+
+def late_hidden(near_l, near_r, far_l, far_r, two_up, two_down, far_2up, far_2down, weights, down_weight):
     n, d = far_l.shape
-    h, ff, step = d // 2, early.shape[1], 1024
+    (ff, _), h, step = down_weight.shape, d // 2, 1024
 
     def kernel(
-        near_l, near_r, far_l, far_r, near_2up, near_2down, far_2up, far_2down, early, gate_w, up_w, up_w2, source,
-        out, out_up, out_down, down_w, rows, two, done,
+        near_l, near_r, far_l, far_r, two_up, two_down, far_2up, far_2down, gate_w, up_w, up_w2, source,
+        out, out_up, out_down, down_w, rows, done,
     ):
         copy = pltpu.make_async_copy(source, down_w, done)
         copy.start()
-        for i, ref in ((0, near_l), (2, near_r), (4, far_l), (5, far_r), (6, near_2up), (7, near_2down)):
+        for i, ref in ((0, near_l), (2, near_r), (4, far_l), (5, far_r)):
             rows[i * n : i * n + ref.shape[0], :] = ref[...]
-        rows[8 * n :, :h] = far_2up[...]
-        rows[8 * n :, h:] = far_2down[...]
+        rows[6 * n : 7 * n, :] = two_up[:, :d]
+        rows[7 * n : 8 * n, :] = two_down[:, :d]
+        rows[8 * n : 9 * n, :h] = two_up[:, d:]
+        rows[8 * n : 9 * n, h:] = two_down[:, d:]
+        rows[9 * n :, :h] = far_2up[...]
+        rows[9 * n :, h:] = far_2down[...]
         out[...] = hidden_of(rows, gate_w, up_w, up_w2)
-        two[:n, :] = early[3 * n : 4 * n, :]
-        two[n:, :] = out[6 * n :, :]
         copy.wait()
         for second in (False, True):
             target = out_down if second else out_up
@@ -101,35 +101,34 @@
             def _(i):
                 start = pl.multiple_of(i * step, step)
                 cut = pl.ds(start + second * h, step)
-                terms = b16(jnp.dot(two[...], down_w[:, cut], preferred_element_type=jnp.float32))
-                out_up[:, cut] = terms[n : 2 * n]
-                out_down[:, cut] = terms[2 * n : 3 * n]
-                target[:, pl.ds(start + d, step)] = terms[:n]
+                terms = b16(jnp.dot(out[6 * n :, :], down_w[:, cut], preferred_element_type=jnp.float32))
+                out_up[:, cut] = terms[:n]
+                out_down[:, cut] = terms[n : 2 * n]
+                target[:, pl.ds(start + d, step)] = terms[2 * n : 3 * n]
                 target[:, pl.ds(start + d + h, step)] = terms[3 * n :]
 
     vmem, b = pl.BlockSpec(memory_space=pltpu.VMEM), jnp.bfloat16
     return pl.pallas_call(
         kernel,
-        out_shape=[pltpu.VMEM(shape, b) for shape in ((9 * n, ff), (n, 2 * d), (n, 2 * d), (ff, d))],
-        in_specs=[vmem] * 12 + [pl.BlockSpec(memory_space=pltpu.HBM)],
+        out_shape=[pltpu.VMEM(shape, b) for shape in ((10 * n, ff), (n, 2 * d), (n, 2 * d), (ff, d))],
+        in_specs=[vmem] * 11 + [pl.BlockSpec(memory_space=pltpu.HBM)],
         out_specs=[vmem] * 4,
-        scratch_shapes=[pltpu.VMEM((9 * n, d), b), pltpu.VMEM((4 * n, ff), b), pltpu.SemaphoreType.DMA],
+        scratch_shapes=[pltpu.VMEM((10 * n, d), b), pltpu.SemaphoreType.DMA],
         compiler_params=pltpu.CompilerParams(vmem_limit_bytes=10 * 1024 * 1024),
-        cost_estimate=pl.CostEstimate(flops=4 * 11 * n * d * ff, bytes_accessed=2 * d * ff, transcendentals=9 * n * ff),
+        cost_estimate=pl.CostEstimate(flops=4 * 12 * n * d * ff, bytes_accessed=2 * d * ff, transcendentals=10 * n * ff),
     )(
-        *placed((near_l, near_r, far_l, far_r, near_2up, near_2down, far_2up, far_2down, early, *weights)),
+        *placed((near_l, near_r, far_l, far_r, two_up, two_down, far_2up, far_2down, *weights)),
         pltpu.with_memory_space_constraint(down_weight, pltpu.HBM),
     )
 
 
 def other_terms(early, late, down_weight):
-    n, (ff, d), step = early.shape[0] // 7, down_weight.shape, 1024
+    n, (ff, d), step = early.shape[0] // 6, down_weight.shape, 1024
     tall = (1, 1, 1, 2, 1, 2, 2, 1, 1)
 
     def kernel(early, late, down_w, *rest):
         outs, held = rest[:-1], rest[-1]
-        held[: 3 * n, :] = early[: 3 * n, :]
-        held[3 * n : 6 * n, :] = early[4 * n :, :]
+        held[: 6 * n, :] = early[...]
         held[6 * n :, :] = late[: 6 * n, :]
 
         @pl.loop(0, d // step)
@@ -175,24 +174,23 @@
 def terms_of(own, gate_weight, up_weight, down_weight):
     n, d = own.shape
     h = d // 2
-    below, above = shift(own, 0, 1), shift(own, 0, -1)
-    own_l, own_r, gate_v = lax.optimization_barrier((shift(own, 1, 0), shift(own, -1, 0), fetched(gate_weight)))
-    own_2up, own_2down = shift(own_l[:, :h], 1, 0), shift(own_r[:, h:], -1, 0)
-    below, above, own_2up, own_2down, up_v, up_weight = lax.optimization_barrier(
-        (below, above, own_2up, own_2down, fetched(up_weight, 0, 2), up_weight)
-    )
-    near = jnp.concatenate([below, above], 0)
+    below, above = lax.optimization_barrier((shift(own, 0, 1), shift(own, 0, -1)))
+    own_l, own_r = shift(own, 1, 0), shift(own, -1, 0)
     below_2, above_2 = shift(below[:, :h], 0, 1), shift(above[:, h:], 0, -1)
+    near, own_l, own_r, gate_v, up_v, up_weight = lax.optimization_barrier(
+        (jnp.concatenate([below, above], 0), own_l, own_r, fetched(gate_weight), fetched(up_weight, 0, 2), up_weight)
+    )
     near_l, near_r = shift(near, 1, 0), shift(near, -1, 0)
     far, up_v2 = lax.optimization_barrier((jnp.concatenate([below_2, above_2], 1), fetched(up_weight, 1, 2)))
     weights = gate_v, up_v, up_v2
-    early = early_hidden(own, own_l, own_r, own_2up, own_2down, below, above, far, weights)
+    early = early_hidden((own, own_l, own_r, below, above, far), weights)
     far_l, far_r = lax.optimization_barrier((shift(far, 1, 0), shift(far, -1, 0)))
     near_l, near_r, early = lax.optimization_barrier((near_l, near_r, early))
-    near_2up, near_2down = shift(near_l[:n], 1, 0), shift(near_r[n:], -1, 0)
+    two_up = shift(jnp.concatenate([near_l[:n], own_l[:, :h]], 1), 1, 0)
+    two_down = shift(jnp.concatenate([near_r[n:], own_r[:, h:]], 1), -1, 0)
     far_2up, far_2down = shift(far_l[:, :h], 1, 0), shift(far_r[:, h:], -1, 0)
     late, two_up, two_down, down_v = late_hidden(
-        near_l, near_r, far_l, far_r, near_2up, near_2down, far_2up, far_2down, early, weights, down_weight
+        near_l, near_r, far_l, far_r, two_up, two_down, far_2up, far_2down, weights, down_weight
     )
     return *other_terms(early, late, down_v), two_up, two_down
 
@@ -208,10 +206,10 @@
     near_right = jnp.concatenate([b16(near_right[:n] + f32(two_up[:, :d])), b16(near_right[n:])], 0)
     near_left = jnp.concatenate([b16(near_left[:n]), b16(near_left[n:] + f32(two_down[:, :d]))], 0)
     near_p, near_m = shift(near_right, 1, 0), shift(near_left, -1, 0)
-    far_sum = shift(b16(far_here + f32(far_p) + f32(far_m)), 0, 2)
     own_right = jnp.concatenate([b16(own_right[:, :h] + f32(two_up[:, d : d + h])), b16(own_right[:, h:])], 1)
     own_left = jnp.concatenate([b16(own_left[:, :h]), b16(own_left[:, h:] + f32(two_down[:, d : d + h]))], 1)
     own_right, own_left, near_p, near_m = lax.optimization_barrier((own_right, own_left, near_p, near_m))
+    far_sum = shift(b16(far_here + f32(far_p) + f32(far_m)), 0, 2)
     own_p, own_m = shift(own_right, 1, 0), shift(own_left, -1, 0)
     near_sum = b16(near_here + f32(near_p) + f32(near_m))
     from_below, from_above = shift(near_sum[n:], 0, 1), shift(near_sum[:n], 0, -1)

time: 101 us -> 96.2 us (0.952)
  the two profiles are of different devices: /device:TPU:38 before, /device:TPU:8 now
where the time goes in v5:
time: 96.2 us; the launch traced here: 95.5 us
  starting transfers between devices  43.3 us (45%)
  Pallas kernels  25.7 us (27%)
  waiting for transfers between devices  24.5 us (25%)
  other arithmetic  1.45 us (2%)
    ppermute x25, starting transfers between devices, shift(): return lax.ppermute(block, 'tensor', pairs)  43.3 us
    ppermute x25, waiting for transfers between devices, shift(): return lax.ppermute(block, 'tensor', pairs)  24.5 us
    pallas_call x3, Pallas kernels, fetched(): pl.pallas_call(kernel, out_shape=pltpu.VMEM((size, weight.shape[1]), weig...  9.28 us
    pallas_call x1, Pallas kernels, late_hidden(): pl.pallas_call(kernel, out_shape=[pltpu.VMEM(shape, b) for shape in ((10...  7.94 us
    pallas_call x1, Pallas kernels, early_hidden(): pl.pallas_call(kernel, out_shape=pltpu.VMEM((sets * n, ff), jnp.bfloat16)...  3.72 us
    pallas_call x1, Pallas kernels, other_terms(): pl.pallas_call(kernel, out_shape=[pltpu.VMEM((k * n, d), jnp.float32) for...  3.61 us
  transfers between devices with their start and end apart: 25, of which 12 were waited for; matrix products, arithmetic and copies ran while one was open for 1% of the time, Pallas kernels for 17%

profile of v5, /device:TPU:8, one launch (start us, length us, event | category | flops | bytes accessed | tf_op | source)
XLA Modules:
  0.0 95.5 jit_solution(3721894883703419584)
XLA Ops:
  0.0 1.1 %shard_map.55.refs_0_ = bf16[16,6144]{1,0:T(8,128)(2,1)S(1)} custom-call(bf16[16,6144]{1,0:T(8,128)(2,1)} %rows_ref.1, f32[1,6144]{1,0:T(1,128)} %bitcast.1), custom_call_target="tpu_custom_call" | custom-call | tf_op jit(solution)/shard_map/pallas_call | solution.py:35
  1.1 6.4 %collective-permute-start.1 = (bf16[16,6144]{1,0:T(8,128)(2,1)S(1)}, bf16[16,6144]{1,0:T(8,128)(2,1)S(1)}, u32[]{:S(2)}, u32[]{:S(2)}) collective-permute-start(bf16[16,6144]{1,0:T(8,128)(2,1)S(1)} %shard_map.55.refs_0_), channel_id=1, source_target_pairs={{0,3},{1,0},{2,1},{3,2},{4,7},{5,4},{6,5},{7,6},{8,11},{9,8},{10,9... | collective-permute-start | bytes 589832 | tf_op jit(solution)/shard_map/ppermute | solution.py:17
  7.5 0.0 collective-permute-start
  7.5 2.8 %collective-permute-start.3 = (bf16[16,6144]{1,0:T(8,128)(2,1)S(1)}, bf16[16,6144]{1,0:T(8,128)(2,1)S(1)}, u32[]{:S(2)}, u32[]{:S(2)}) collective-permute-start(bf16[16,6144]{1,0:T(8,128)(2,1)S(1)} %shard_map.55.refs_0_), channel_id=1, source_target_pairs={{0,12},{1,13},{2,14},{3,15},{4,0},{5,1},{6,2},{7,3},{8,4},{9,5},{1... | collective-permute-start | bytes 589832 | tf_op jit(solution)/shard_map/ppermute | solution.py:17
  10.3 0.0 collective-permute-start.2
  10.3 2.6 %shard_map.57.refs_7_.up_w = bf16[3072,896]{1,0:T(8,128)(2,1)S(1)} custom-call(bf16[6144,896]{1,0:T(8,128)(2,1)} %source.5), custom_call_target="tpu_custom_call" | custom-call | bytes 5505024 | tf_op jit(solution)/shard_map/pallas_call | solution.py:163
  12.8 4.1 %shard_map.56.refs_6_.gate_w = bf16[6144,896]{1,0:T(8,128)(2,1)S(1)} custom-call(bf16[6144,896]{1,0:T(8,128)(2,1)} %source.3), custom_call_target="tpu_custom_call" | custom-call | bytes 11010048 | tf_op jit(solution)/shard_map/pallas_call | solution.py:163
  17.0 2.7 %collective-permute-done.refs_3_ = bf16[16,6144]{1,0:T(8,128)(2,1)S(1)} collective-permute-done((bf16[16,6144]{1,0:T(8,128)(2,1)S(1)}, bf16[16,6144]{1,0:T(8,128)(2,1)S(1)}, u32[]{:S(2)}, u32[]{:S(2)}) %collective-permute-start) | collective-permute-done | bytes 196640 | tf_op jit(solution)/shard_map/ppermute | solution.py:17
  19.8 1.5 %collective-permute-start.7 = (bf16[16,3072]{1,0:T(8,128)(2,1)S(1)}, bf16[16,3072]{1,0:T(8,128)(2,1)S(1)}, u32[]{:S(2)}, u32[]{:S(2)}) collective-permute-start(bf16[16,3072]{1,0:T(8,128)(2,1)S(1)} %slice.91), channel_id=1, source_target_pairs={{0,3},{1,0},{2,1},{3,2},{4,7},{5,4},{6,5},{7,6},{8,11},{9,8},{10,9... | collective-permute-start | bytes 294920 | tf_op jit(solution)/shard_map/ppermute | solution.py:17
  21.3 1.5 %collective-permute-start.6 = (bf16[16,3072]{1,0:T(8,128)(2,1)S(1)}, bf16[16,3072]{1,0:T(8,128)(2,1)S(1)}, u32[]{:S(2)}, u32[]{:S(2)}) collective-permute-start(bf16[16,3072]{1,0:T(8,128)(2,1)S(1)} %slice.90), channel_id=1, source_target_pairs={{0,1},{1,2},{2,3},{3,0},{4,5},{5,6},{6,7},{7,4},{8,9},{9,10},{10,1... | collective-permute-start | bytes 294920 | tf_op jit(solution)/shard_map/ppermute | solution.py:17
  22.8 0.0 collective-permute-done.3.refs_2_
  22.8 2.8 %collective-permute-start.5 = (bf16[32,6144]{1,0:T(8,128)(2,1)S(1)}, bf16[32,6144]{1,0:T(8,128)(2,1)S(1)}, u32[]{:S(2)}, u32[]{:S(2)}) collective-permute-start(bf16[32,6144]{1,0:T(8,128)(2,1)S(1)} %pad_maximum_fusion), channel_id=1, source_target_pairs={{0,12},{1,13},{2,14},{3,15},{4,0},{5,1},{6,2},{7,3},{8,4},{9,5},{1... | collective-permute-start | bytes 1179656 | tf_op jit(solution)/shard_map/ppermute | solution.py:17
  25.7 2.6 %shard_map.58.refs_8_.up_w2 = bf16[3072,896]{1,0:T(8,128)(2,1)S(1)} custom-call(bf16[6144,896]{1,0:T(8,128)(2,1)} %source.5), custom_call_target="tpu_custom_call" | custom-call | bytes 5505024 | tf_op jit(solution)/shard_map/pallas_call | solution.py:163
  28.3 0.0 collective-permute-done.7
  28.3 0.3 collective-permute-done.6
  28.6 3.1 %collective-permute-start.9 = (bf16[16,6144]{1,0:T(8,128)(2,1)S(1)}, bf16[16,6144]{1,0:T(8,128)(2,1)S(1)}, u32[]{:S(2)}, u32[]{:S(2)}) collective-permute-start(bf16[16,6144]{1,0:T(8,128)(2,1)S(1)} %pad_maximum_fusion.5.refs_5_), channel_id=1, source_target_pairs={{0,12},{1,13},{2,14},{3,15},{4,0},{5,1},{6,2},{7,3},{8,4},{9,5},{1... | collective-permute-start | bytes 589832 | tf_op jit(solution)/shard_map/ppermute | solution.py:17
  31.7 3.7 %shard_map.59.early = bf16[96,896]{1,0:T(8,128)(2,1)S(1)} custom-call(bf16[16,6144]{1,0:T(8,128)(2,1)S(1)} %shard_map.55.refs_0_, bf16[16,6144]{1,0:T(8,128)(2,1)S(1)} %collective-permute-done.2.refs_1_, bf16[16,6144]{1,0:T(8,128)(2,1)S(1)} %collective-permute-done.3.refs_2_, bf16[16,6144]{1,0:T(8,128)(2,1)S(1)} %collective-permute-done.refs_3_, ...), custom_call_target="tpu_custom_call" | custom-call | flops 2113929216 | tf_op jit(solution)/shard_map/pallas_call | solution.py:66
  35.4 1.5 %collective-permute-done.4.near_l = bf16[32,6144]{1,0:T(8,128)(2,1)S(1)} collective-permute-done((bf16[32,6144]{1,0:T(8,128)(2,1)S(1)}, bf16[32,6144]{1,0:T(8,128)(2,1)S(1)}, u32[]{:S(2)}, u32[]{:S(2)}) %collective-permute-start.4) | collective-permute-done | bytes 393248 | tf_op jit(solution)/shard_map/ppermute | solution.py:17
  37.0 1.9 %collective-permute-start.11 = (bf16[16,9216]{1,0:T(8,128)(2,1)S(1)}, bf16[16,9216]{1,0:T(8,128)(2,1)S(1)}, u32[]{:S(2)}, u32[]{:S(2)}) collective-permute-start(bf16[16,9216]{1,0:T(8,128)(2,1)S(1)} %pad_maximum_fusion.4), channel_id=1, source_target_pairs={{0,12},{1,13},{2,14},{3,15},{4,0},{5,1},{6,2},{7,3},{8,4},{9,5},{1... | collective-permute-start | bytes 884744 | tf_op jit(solution)/shard_map/ppermute | solution.py:17
  38.8 0.5 collective-permute-start.10
  39.4 3.1 %collective-permute-start.13 = (bf16[16,3072]{1,0:T(8,128)(2,1)S(1)}, bf16[16,3072]{1,0:T(8,128)(2,1)S(1)}, u32[]{:S(2)}, u32[]{:S(2)}) collective-permute-start(bf16[16,3072]{1,0:T(8,128)(2,1)S(1)} %slice.97), channel_id=1, source_target_pairs={{0,12},{1,13},{2,14},{3,15},{4,0},{5,1},{6,2},{7,3},{8,4},{9,5},{1... | collective-permute-start | bytes 294920 | tf_op jit(solution)/shard_map/ppermute | solution.py:17
  42.5 3.0 %collective-permute-done.13.far_2down = bf16[16,3072]{1,0:T(8,128)(2,1)S(1)} collective-permute-done((bf16[16,3072]{1,0:T(8,128)(2,1)S(1)}, bf16[16,3072]{1,0:T(8,128)(2,1)S(1)}, u32[]{:S(2)}, u32[]{:S(2)}) %collective-permute-start.13) | collective-permute-done | bytes 98336 | tf_op jit(solution)/shard_map/ppermute | solution.py:17
  45.4 2.9 %collective-permute-done.12.far_2up = bf16[16,3072]{1,0:T(8,128)(2,1)S(1)} collective-permute-done((bf16[16,3072]{1,0:T(8,128)(2,1)S(1)}, bf16[16,3072]{1,0:T(8,128)(2,1)S(1)}, u32[]{:S(2)}, u32[]{:S(2)}) %collective-permute-start.12) | collective-permute-done | bytes 98336 | tf_op jit(solution)/shard_map/ppermute | solution.py:17
  48.3 7.9 %shard_map.60 = (bf16[160,896]{1,0:T(8,128)(2,1)S(1)}, bf16[16,12288]{1,0:T(8,128)(2,1)S(1)}, bf16[16,12288]{1,0:T(8,128)(2,1)S(1)}, bf16[896,6144]{1,0:T(8,128)(2,1)S(1)}) custom-call(bf16[32,6144]{1,0:T(8,128)(2,1)S(1)} %collective-permute-done.4.near_l, bf16[32,6144]{1,0:T(8,128)(2,1)S(1)} %collective-permute-done.5.near_r, ...), custom_call_target="tpu_custom_call" | custom-call | flops 4227858432 | bytes 11010048 | tf_op jit(solution)/shard_map/pallas_call | solution.py:111
  56.3 0.1 collective-permute-start.14
  56.4 3.2 %collective-permute-start.15 = (bf16[16,12288]{1,0:T(8,128)(2,1)S(1)}, bf16[16,12288]{1,0:T(8,128)(2,1)S(1)}, u32[]{:S(2)}, u32[]{:S(2)}) collective-permute-start(bf16[16,12288]{1,0:T(8,128)(2,1)S(1)} %get-tuple-element.59), channel_id=1, source_target_pairs={{0,12},{1,13},{2,14},{3,15},{4,0},{5,1},{6,2},{7,3},{8,4},{9,5},{1... | collective-permute-start | bytes 1179656 | tf_op jit(solution)/shard_map/ppermute | solution.py:17
  59.6 3.6 %shard_map.61 = (f32[16,6144]{1,0:T(8,128)S(1)}, f32[16,6144]{1,0:T(8,128)S(1)}, f32[16,6144]{1,0:T(8,128)S(1)}, f32[32,6144]{1,0:T(8,128)S(1)}, f32[16,6144]{1,...) custom-call(bf16[96,896]{1,0:T(8,128)(2,1)S(1)} %shard_map.59.early,, ...), custom_call_target="tpu_custom_call" | custom-call | flops 2113929216 | tf_op jit(solution)/shard_map/pallas_call | solution.py:144
  63.4 2.0 %collective-permute-done.14 = bf16[16,12288]{1,0:T(8,128)(2,1)S(1)} collective-permute-done((bf16[16,12288]{1,0:T(8,128)(2,1)S(1)}, bf16[16,12288]{1,0:T(8,128)(2,1)S(1)}, u32[]{:S(2)}, u32[]{:S(2)}) %collective-permute-start.14) | collective-permute-done | bytes 393248 | tf_op jit(solution)/shard_map/ppermute | solution.py:17
  65.4 0.7 collective-permute-done.15
  66.1 0.1 add_convert_fusion.3
  66.2 0.1 add_convert_fusion.4
  66.2 0.1 add_convert_fusion.6
  66.3 3.8 %collective-permute-start.21 = (bf16[16,6144]{1,0:T(8,128)(2,1)S(1)}, bf16[16,6144]{1,0:T(8,128)(2,1)S(1)}, u32[]{:S(2)}, u32[]{:S(2)}) collective-permute-start(bf16[16,6144]{1,0:T(8,128)(2,1)S(1)} %pad_maximum_fusion.9), channel_id=1, source_target_pairs={{0,12},{1,13},{2,14},{3,15},{4,0},{5,1},{6,2},{7,3},{8,4},{9,5},{1... | collective-permute-start | bytes 589832 | tf_op jit(solution)/shard_map/ppermute | solution.py:17
  70.1 0.1 collective-permute-start.20
  70.2 3.3 %collective-permute-start.17 = (bf16[32,6144]{1,0:T(8,128)(2,1)S(1)}, bf16[32,6144]{1,0:T(8,128)(2,1)S(1)}, u32[]{:S(2)}, u32[]{:S(2)}) collective-permute-start(bf16[32,6144]{1,0:T(8,128)(2,1)S(1)} %pad_maximum_fusion.2), channel_id=1, source_target_pairs={{0,12},{1,13},{2,14},{3,15},{4,0},{5,1},{6,2},{7,3},{8,4},{9,5},{1... | collective-permute-start | bytes 1179656 | tf_op jit(solution)/shard_map/ppermute | solution.py:17
  73.5 0.1 collective-permute-start.16
  73.7 3.4 %collective-permute-done.20 = bf16[16,6144]{1,0:T(8,128)(2,1)S(1)} collective-permute-done((bf16[16,6144]{1,0:T(8,128)(2,1)S(1)}, bf16[16,6144]{1,0:T(8,128)(2,1)S(1)}, u32[]{:S(2)}, u32[]{:S(2)}) %collective-permute-start.20) | collective-permute-done | bytes 196640 | tf_op jit(solution)/shard_map/ppermute | solution.py:17
  77.0 0.1 add_convert_fusion.2
  77.1 1.8 %collective-permute-start.22 = (bf16[16,6144]{1,0:T(8,128)(2,1)S(1)}, bf16[16,6144]{1,0:T(8,128)(2,1)S(1)}, u32[]{:S(2)}, u32[]{:S(2)}) collective-permute-start(bf16[16,6144]{1,0:T(8,128)(2,1)S(1)} %add_convert_fusion.2), channel_id=1, source_target_pairs={{0,2},{1,3},{2,0},{3,1},{4,6},{5,7},{6,4},{7,5},{8,10},{9,11},{10,... | collective-permute-start | bytes 589832 | tf_op jit(solution)/shard_map/ppermute | solution.py:17
  79.0 4.4 %collective-permute-done.16 = bf16[32,6144]{1,0:T(8,128)(2,1)S(1)} collective-permute-done((bf16[32,6144]{1,0:T(8,128)(2,1)S(1)}, bf16[32,6144]{1,0:T(8,128)(2,1)S(1)}, u32[]{:S(2)}, u32[]{:S(2)}) %collective-permute-start.16) | collective-permute-done | bytes 393248 | tf_op jit(solution)/shard_map/ppermute | solution.py:17
  83.4 0.1 add_convert_fusion
  83.6 0.5 collective-permute-start.23
  84.0 3.8 %collective-permute-start.24 = (bf16[16,6144]{1,0:T(8,128)(2,1)S(1)}, bf16[16,6144]{1,0:T(8,128)(2,1)S(1)}, u32[]{:S(2)}, u32[]{:S(2)}) collective-permute-start(bf16[16,6144]{1,0:T(8,128)(2,1)S(1)} %get-tuple-element.78), channel_id=1, source_target_pairs={{0,3},{1,0},{2,1},{3,2},{4,7},{5,4},{6,5},{7,6},{8,11},{9,8},{10,9... | collective-permute-start | bytes 589832 | tf_op jit(solution)/shard_map/ppermute | solution.py:17
  87.8 3.2 %collective-permute-start.19 = (bf16[16,6144]{1,0:T(8,128)(2,1)S(1)}, bf16[16,6144]{1,0:T(8,128)(2,1)S(1)}, u32[]{:S(2)}, u32[]{:S(2)}) collective-permute-start(bf16[16,6144]{1,0:T(8,128)(2,1)S(1)} %pad_maximum_fusion.7), channel_id=1, source_target_pairs={{0,12},{1,13},{2,14},{3,15},{4,0},{5,1},{6,2},{7,3},{8,4},{9,5},{1... | collective-permute-start | bytes 589832 | tf_op jit(solution)/shard_map/ppermute | solution.py:17
  91.0 0.8 collective-permute-done.23
  91.9 2.3 %collective-permute-done.24 = bf16[16,6144]{1,0:T(8,128)(2,1)S(1)} collective-permute-done((bf16[16,6144]{1,0:T(8,128)(2,1)S(1)}, bf16[16,6144]{1,0:T(8,128)(2,1)S(1)}, u32[]{:S(2)}, u32[]{:S(2)}) %collective-permute-start.24) | collective-permute-done | bytes 196640 | tf_op jit(solution)/shard_map/ppermute | solution.py:17
  94.1 0.6 collective-permute-done.18
  94.7 0.8 add_convert_fusion.1
  (43 shorter events, 0.5 us)
Async XLA Ops:
  1.1 15.9 %collective-permute-start.1 = (bf16[16,6144]{1,0:T(8,128)(2,1)S(1)}, bf16[16,6144]{1,0:T(8,128)(2,1)S(1)}, u32[]{:S(2)}, u32[]{:S(2)}) collective-permute-start(bf16[16,6144]{1,0:T(8,128)(2,1)S(1)} %shard_map.55.refs_0_), channel_id=1, source_target_pairs={{0,3},{1,0},{2,1},{3,2},{4,7},{5,4},{6,5},{7,6},{8,11},{9,8},{10,9... | collective-permute-start | bytes 589832 | tf_op jit(solution)/shard_map/ppermute | solution.py:17
  7.5 12.2 %collective-permute-start = (bf16[16,6144]{1,0:T(8,128)(2,1)S(1)}, bf16[16,6144]{1,0:T(8,128)(2,1)S(1)}, u32[]{:S(2)}, u32[]{:S(2)}) collective-permute-start(bf16[16,6144]{1,0:T(8,128)(2,1)S(1)} %shard_map.55.refs_0_), channel_id=1, source_target_pairs={{0,1},{1,2},{2,3},{3,0},{4,5},{5,6},{6,7},{7,4},{8,9},{9,10},{10,1... | collective-permute-start | bytes 589832 | tf_op jit(solution)/shard_map/ppermute | solution.py:17
  7.5 15.3 %collective-permute-start.3 = (bf16[16,6144]{1,0:T(8,128)(2,1)S(1)}, bf16[16,6144]{1,0:T(8,128)(2,1)S(1)}, u32[]{:S(2)}, u32[]{:S(2)}) collective-permute-start(bf16[16,6144]{1,0:T(8,128)(2,1)S(1)} %shard_map.55.refs_0_), channel_id=1, source_target_pairs={{0,12},{1,13},{2,14},{3,15},{4,0},{5,1},{6,2},{7,3},{8,4},{9,5},{1... | collective-permute-start | bytes 589832 | tf_op jit(solution)/shard_map/ppermute | solution.py:17
  10.3 12.6 %collective-permute-start.2 = (bf16[16,6144]{1,0:T(8,128)(2,1)S(1)}, bf16[16,6144]{1,0:T(8,128)(2,1)S(1)}, u32[]{:S(2)}, u32[]{:S(2)}) collective-permute-start(bf16[16,6144]{1,0:T(8,128)(2,1)S(1)} %shard_map.55.refs_0_), channel_id=1, source_target_pairs={{0,4},{1,5},{2,6},{3,7},{4,8},{5,9},{6,10},{7,11},{8,12},{9,13},{1... | collective-permute-start | bytes 589832 | tf_op jit(solution)/shard_map/ppermute | solution.py:17
  19.8 8.5 %collective-permute-start.7 = (bf16[16,3072]{1,0:T(8,128)(2,1)S(1)}, bf16[16,3072]{1,0:T(8,128)(2,1)S(1)}, u32[]{:S(2)}, u32[]{:S(2)}) collective-permute-start(bf16[16,3072]{1,0:T(8,128)(2,1)S(1)} %slice.91), channel_id=1, source_target_pairs={{0,3},{1,0},{2,1},{3,2},{4,7},{5,4},{6,5},{7,6},{8,11},{9,8},{10,9... | collective-permute-start | bytes 294920 | tf_op jit(solution)/shard_map/ppermute | solution.py:17
  21.3 7.3 %collective-permute-start.6 = (bf16[16,3072]{1,0:T(8,128)(2,1)S(1)}, bf16[16,3072]{1,0:T(8,128)(2,1)S(1)}, u32[]{:S(2)}, u32[]{:S(2)}) collective-permute-start(bf16[16,3072]{1,0:T(8,128)(2,1)S(1)} %slice.90), channel_id=1, source_target_pairs={{0,1},{1,2},{2,3},{3,0},{4,5},{5,6},{6,7},{7,4},{8,9},{9,10},{10,1... | collective-permute-start | bytes 294920 | tf_op jit(solution)/shard_map/ppermute | solution.py:17
  22.8 12.6 %collective-permute-start.5 = (bf16[32,6144]{1,0:T(8,128)(2,1)S(1)}, bf16[32,6144]{1,0:T(8,128)(2,1)S(1)}, u32[]{:S(2)}, u32[]{:S(2)}) collective-permute-start(bf16[32,6144]{1,0:T(8,128)(2,1)S(1)} %pad_maximum_fusion), channel_id=1, source_target_pairs={{0,12},{1,13},{2,14},{3,15},{4,0},{5,1},{6,2},{7,3},{8,4},{9,5},{1... | collective-permute-start | bytes 1179656 | tf_op jit(solution)/shard_map/ppermute | solution.py:17
  25.7 11.2 %collective-permute-start.4 = (bf16[32,6144]{1,0:T(8,128)(2,1)S(1)}, bf16[32,6144]{1,0:T(8,128)(2,1)S(1)}, u32[]{:S(2)}, u32[]{:S(2)}) collective-permute-start(bf16[32,6144]{1,0:T(8,128)(2,1)S(1)} %pad_maximum_fusion), channel_id=1, source_target_pairs={{0,4},{1,5},{2,6},{3,7},{4,8},{5,9},{6,10},{7,11},{8,12},{9,13},{1... | collective-permute-start | bytes 1179656 | tf_op jit(solution)/shard_map/ppermute | solution.py:17
  28.6 10.8 %collective-permute-start.9 = (bf16[16,6144]{1,0:T(8,128)(2,1)S(1)}, bf16[16,6144]{1,0:T(8,128)(2,1)S(1)}, u32[]{:S(2)}, u32[]{:S(2)}) collective-permute-start(bf16[16,6144]{1,0:T(8,128)(2,1)S(1)} %pad_maximum_fusion.5.refs_5_), channel_id=1, source_target_pairs={{0,12},{1,13},{2,14},{3,15},{4,0},{5,1},{6,2},{7,3},{8,4},{9,5},{1... | collective-permute-start | bytes 589832 | tf_op jit(solution)/shard_map/ppermute | solution.py:17
  31.7 7.7 %collective-permute-start.8 = (bf16[16,6144]{1,0:T(8,128)(2,1)S(1)}, bf16[16,6144]{1,0:T(8,128)(2,1)S(1)}, u32[]{:S(2)}, u32[]{:S(2)}) collective-permute-start(bf16[16,6144]{1,0:T(8,128)(2,1)S(1)} %pad_maximum_fusion.5.refs_5_), channel_id=1, source_target_pairs={{0,4},{1,5},{2,6},{3,7},{4,8},{5,9},{6,10},{7,11},{8,12},{9,13},{1... | collective-permute-start | bytes 589832 | tf_op jit(solution)/shard_map/ppermute | solution.py:17
  37.0 11.4 %collective-permute-start.11 = (bf16[16,9216]{1,0:T(8,128)(2,1)S(1)}, bf16[16,9216]{1,0:T(8,128)(2,1)S(1)}, u32[]{:S(2)}, u32[]{:S(2)}) collective-permute-start(bf16[16,9216]{1,0:T(8,128)(2,1)S(1)} %pad_maximum_fusion.4), channel_id=1, source_target_pairs={{0,12},{1,13},{2,14},{3,15},{4,0},{5,1},{6,2},{7,3},{8,4},{9,5},{1... | collective-permute-start | bytes 884744 | tf_op jit(solution)/shard_map/ppermute | solution.py:17
  38.8 9.5 %collective-permute-start.10 = (bf16[16,9216]{1,0:T(8,128)(2,1)S(1)}, bf16[16,9216]{1,0:T(8,128)(2,1)S(1)}, u32[]{:S(2)}, u32[]{:S(2)}) collective-permute-start(bf16[16,9216]{1,0:T(8,128)(2,1)S(1)} %pad_maximum_fusion.3), channel_id=1, source_target_pairs={{0,4},{1,5},{2,6},{3,7},{4,8},{5,9},{6,10},{7,11},{8,12},{9,13},{1... | collective-permute-start | bytes 884744 | tf_op jit(solution)/shard_map/ppermute | solution.py:17
  39.4 6.0 %collective-permute-start.13 = (bf16[16,3072]{1,0:T(8,128)(2,1)S(1)}, bf16[16,3072]{1,0:T(8,128)(2,1)S(1)}, u32[]{:S(2)}, u32[]{:S(2)}) collective-permute-start(bf16[16,3072]{1,0:T(8,128)(2,1)S(1)} %slice.97), channel_id=1, source_target_pairs={{0,12},{1,13},{2,14},{3,15},{4,0},{5,1},{6,2},{7,3},{8,4},{9,5},{1... | collective-permute-start | bytes 294920 | tf_op jit(solution)/shard_map/ppermute | solution.py:17
  42.4 5.9 %collective-permute-start.12 = (bf16[16,3072]{1,0:T(8,128)(2,1)S(1)}, bf16[16,3072]{1,0:T(8,128)(2,1)S(1)}, u32[]{:S(2)}, u32[]{:S(2)}) collective-permute-start(bf16[16,3072]{1,0:T(8,128)(2,1)S(1)} %slice.96), channel_id=1, source_target_pairs={{0,4},{1,5},{2,6},{3,7},{4,8},{5,9},{6,10},{7,11},{8,12},{9,13},{1... | collective-permute-start | bytes 294920 | tf_op jit(solution)/shard_map/ppermute | solution.py:17
  56.3 9.1 %collective-permute-start.14 = (bf16[16,12288]{1,0:T(8,128)(2,1)S(1)}, bf16[16,12288]{1,0:T(8,128)(2,1)S(1)}, u32[]{:S(2)}, u32[]{:S(2)}) collective-permute-start(bf16[16,12288]{1,0:T(8,128)(2,1)S(1)} %get-tuple-element.58), channel_id=1, source_target_pairs={{0,4},{1,5},{2,6},{3,7},{4,8},{5,9},{6,10},{7,11},{8,12},{9,13},{1... | collective-permute-start | bytes 1179656 | tf_op jit(solution)/shard_map/ppermute | solution.py:17
  56.4 9.7 %collective-permute-start.15 = (bf16[16,12288]{1,0:T(8,128)(2,1)S(1)}, bf16[16,12288]{1,0:T(8,128)(2,1)S(1)}, u32[]{:S(2)}, u32[]{:S(2)}) collective-permute-start(bf16[16,12288]{1,0:T(8,128)(2,1)S(1)} %get-tuple-element.59), channel_id=1, source_target_pairs={{0,12},{1,13},{2,14},{3,15},{4,0},{5,1},{6,2},{7,3},{8,4},{9,5},{1... | collective-permute-start | bytes 1179656 | tf_op jit(solution)/shard_map/ppermute | solution.py:17
  59.6 35.1 %copy-start = (bf16[16,6144]{1,0:T(8,128)(2,1)S(1)}, bf16[16,6144]{1,0:T(8,128)(2,1)}, u32[]{:S(2)}) copy-start(bf16[16,6144]{1,0:T(8,128)(2,1)} %rows_ref.1) | copy-start | bytes 589828
  66.3 7.4 %collective-permute-start.21 = (bf16[16,6144]{1,0:T(8,128)(2,1)S(1)}, bf16[16,6144]{1,0:T(8,128)(2,1)S(1)}, u32[]{:S(2)}, u32[]{:S(2)}) collective-permute-start(bf16[16,6144]{1,0:T(8,128)(2,1)S(1)} %pad_maximum_fusion.9), channel_id=1, source_target_pairs={{0,12},{1,13},{2,14},{3,15},{4,0},{5,1},{6,2},{7,3},{8,4},{9,5},{1... | collective-permute-start | bytes 589832 | tf_op jit(solution)/shard_map/ppermute | solution.py:17
  70.1 7.0 %collective-permute-start.20 = (bf16[16,6144]{1,0:T(8,128)(2,1)S(1)}, bf16[16,6144]{1,0:T(8,128)(2,1)S(1)}, u32[]{:S(2)}, u32[]{:S(2)}) collective-permute-start(bf16[16,6144]{1,0:T(8,128)(2,1)S(1)} %pad_maximum_fusion.8), channel_id=1, source_target_pairs={{0,4},{1,5},{2,6},{3,7},{4,8},{5,9},{6,10},{7,11},{8,12},{9,13},{1... | collective-permute-start | bytes 589832 | tf_op jit(solution)/shard_map/ppermute | solution.py:17
  70.2 8.7 %collective-permute-start.17 = (bf16[32,6144]{1,0:T(8,128)(2,1)S(1)}, bf16[32,6144]{1,0:T(8,128)(2,1)S(1)}, u32[]{:S(2)}, u32[]{:S(2)}) collective-permute-start(bf16[32,6144]{1,0:T(8,128)(2,1)S(1)} %pad_maximum_fusion.2), channel_id=1, source_target_pairs={{0,12},{1,13},{2,14},{3,15},{4,0},{5,1},{6,2},{7,3},{8,4},{9,5},{1... | collective-permute-start | bytes 1179656 | tf_op jit(solution)/shard_map/ppermute | solution.py:17
  73.5 9.9 %collective-permute-start.16 = (bf16[32,6144]{1,0:T(8,128)(2,1)S(1)}, bf16[32,6144]{1,0:T(8,128)(2,1)S(1)}, u32[]{:S(2)}, u32[]{:S(2)}) collective-permute-start(bf16[32,6144]{1,0:T(8,128)(2,1)S(1)} %pad_maximum_fusion.1), channel_id=1, source_target_pairs={{0,4},{1,5},{2,6},{3,7},{4,8},{5,9},{6,10},{7,11},{8,12},{9,13},{1... | collective-permute-start | bytes 1179656 | tf_op jit(solution)/shard_map/ppermute | solution.py:17
  77.1 13.9 %collective-permute-start.22 = (bf16[16,6144]{1,0:T(8,128)(2,1)S(1)}, bf16[16,6144]{1,0:T(8,128)(2,1)S(1)}, u32[]{:S(2)}, u32[]{:S(2)}) collective-permute-start(bf16[16,6144]{1,0:T(8,128)(2,1)S(1)} %add_convert_fusion.2), channel_id=1, source_target_pairs={{0,2},{1,3},{2,0},{3,1},{4,6},{5,7},{6,4},{7,5},{8,10},{9,11},{10,... | collective-permute-start | bytes 589832 | tf_op jit(solution)/shard_map/ppermute | solution.py:17
  83.6 8.3 %collective-permute-start.23 = (bf16[16,6144]{1,0:T(8,128)(2,1)S(1)}, bf16[16,6144]{1,0:T(8,128)(2,1)S(1)}, u32[]{:S(2)}, u32[]{:S(2)}) collective-permute-start(bf16[16,6144]{1,0:T(8,128)(2,1)S(1)} %get-tuple-element.77), channel_id=1, source_target_pairs={{0,1},{1,2},{2,3},{3,0},{4,5},{5,6},{6,7},{7,4},{8,9},{9,10},{10,1... | collective-permute-start | bytes 589832 | tf_op jit(solution)/shard_map/ppermute | solution.py:17
  84.0 10.1 %collective-permute-start.24 = (bf16[16,6144]{1,0:T(8,128)(2,1)S(1)}, bf16[16,6144]{1,0:T(8,128)(2,1)S(1)}, u32[]{:S(2)}, u32[]{:S(2)}) collective-permute-start(bf16[16,6144]{1,0:T(8,128)(2,1)S(1)} %get-tuple-element.78), channel_id=1, source_target_pairs={{0,3},{1,0},{2,1},{3,2},{4,7},{5,4},{6,5},{7,6},{8,11},{9,8},{10,9... | collective-permute-start | bytes 589832 | tf_op jit(solution)/shard_map/ppermute | solution.py:17
  87.8 6.9 %collective-permute-start.18 = (bf16[16,6144]{1,0:T(8,128)(2,1)S(1)}, bf16[16,6144]{1,0:T(8,128)(2,1)S(1)}, u32[]{:S(2)}, u32[]{:S(2)}) collective-permute-start(bf16[16,6144]{1,0:T(8,128)(2,1)S(1)} %pad_maximum_fusion.6), channel_id=1, source_target_pairs={{0,4},{1,5},{2,6},{3,7},{4,8},{5,9},{6,10},{7,11},{8,12},{9,13},{1... | collective-permute-start | bytes 589832 | tf_op jit(solution)/shard_map/ppermute | solution.py:17
  87.8 6.9 %collective-permute-start.19 = (bf16[16,6144]{1,0:T(8,128)(2,1)S(1)}, bf16[16,6144]{1,0:T(8,128)(2,1)S(1)}, u32[]{:S(2)}, u32[]{:S(2)}) collective-permute-start(bf16[16,6144]{1,0:T(8,128)(2,1)S(1)} %pad_maximum_fusion.7), channel_id=1, source_target_pairs={{0,12},{1,13},{2,14},{3,15},{4,0},{5,1},{6,2},{7,3},{8,4},{9,5},{1... | collective-permute-start | bytes 589832 | tf_op jit(solution)/shard_map/ppermute | solution.py:17

commit v6 on v5

--- a/solution.py
+++ b/solution.py
@@ -53,47 +53,50 @@
     return b16(gate / (1.0 + jnp.exp(-gate)) * up)
 
 
-def early_hidden(blocks, weights):
-    (n, d), ff, sets = blocks[0].shape, weights[0].shape[1], len(blocks)
+def hidden_units(blocks, weights, down_weight=None):
+    (n, d), ff = blocks[0].shape, weights[0].shape[1]
+    tall, held = sum(v.shape[0] for v in blocks), len(blocks)
+    also = () if down_weight is None else (pltpu.with_memory_space_constraint(down_weight, pltpu.HBM),)
 
     def kernel(*refs):
-        ins, ws, (out, rows) = refs[:sets], refs[sets:-2], refs[-2:]
-        for i, ref in enumerate(ins):
-            rows[i * n : (i + 1) * n, :] = ref[...]
+        ins, ws, rest = refs[:held], refs[held : held + len(weights)], refs[held + len(weights) :]
+        if also:
+            source, out, target, rows, done = rest
+            copy = pltpu.make_async_copy(source, target, done)
+            copy.start()
+        else:
+            out, rows = rest
+        at = 0
+        for ref in ins:
+            rows[at : at + ref.shape[0], :] = ref[...]
+            at += ref.shape[0]
         out[...] = hidden_of(rows, *ws)
-
-    vmem = pl.BlockSpec(memory_space=pltpu.VMEM)
-    return pl.pallas_call(
-        kernel,
-        out_shape=pltpu.VMEM((sets * n, ff), jnp.bfloat16),
-        in_specs=[vmem] * (sets + len(weights)),
-        out_specs=vmem,
-        scratch_shapes=[pltpu.VMEM((sets * n, d), jnp.bfloat16)],
+        if also:
+            copy.wait()
+
+    vmem, b = pl.BlockSpec(memory_space=pltpu.VMEM), jnp.bfloat16
+    return pl.pallas_call(
+        kernel,
+        out_shape=[pltpu.VMEM((tall, ff), b)] + [pltpu.VMEM((ff, d), b) for _ in also],
+        in_specs=[vmem] * (held + len(weights)) + [pl.BlockSpec(memory_space=pltpu.HBM) for _ in also],
+        out_specs=[vmem] * (1 + len(also)),
+        scratch_shapes=[pltpu.VMEM((tall, d), b)] + [pltpu.SemaphoreType.DMA for _ in also],
         compiler_params=pltpu.CompilerParams(vmem_limit_bytes=8 * 1024 * 1024),
-        cost_estimate=pl.CostEstimate(flops=4 * sets * n * d * ff, bytes_accessed=0, transcendentals=sets * n * ff),
-    )(*placed((*blocks, *weights)))
-
-
-def late_hidden(near_l, near_r, far_l, far_r, two_up, two_down, far_2up, far_2down, weights, down_weight):
-    n, d = far_l.shape
-    (ff, _), h, step = down_weight.shape, d // 2, 1024
-
-    def kernel(
-        near_l, near_r, far_l, far_r, two_up, two_down, far_2up, far_2down, gate_w, up_w, up_w2, source,
-        out, out_up, out_down, down_w, rows, done,
-    ):
-        copy = pltpu.make_async_copy(source, down_w, done)
-        copy.start()
-        for i, ref in ((0, near_l), (2, near_r), (4, far_l), (5, far_r)):
-            rows[i * n : i * n + ref.shape[0], :] = ref[...]
-        rows[6 * n : 7 * n, :] = two_up[:, :d]
-        rows[7 * n : 8 * n, :] = two_down[:, :d]
-        rows[8 * n : 9 * n, :h] = two_up[:, d:]
-        rows[8 * n : 9 * n, h:] = two_down[:, d:]
-        rows[9 * n :, :h] = far_2up[...]
-        rows[9 * n :, h:] = far_2down[...]
-        out[...] = hidden_of(rows, gate_w, up_w, up_w2)
-        copy.wait()
+        cost_estimate=pl.CostEstimate(flops=4 * tall * d * ff, bytes_accessed=2 * d * ff * len(also), transcendentals=tall * ff),
+    )(*placed((*blocks, *weights)), *also)
+
+
+def two_hops(two_up, two_down, far_up, far_down, weights, down_w):
+    (n, h), (ff, d), step = far_up.shape, down_w.shape, 1024
+
+    def kernel(two_up, two_down, far_up, far_down, gate_w, up_w, up_w2, down_w, out_up, out_down, rows, hidden):
+        rows[:n, :] = two_up[:, :d]
+        rows[n : 2 * n, :] = two_down[:, :d]
+        rows[2 * n : 3 * n, :h] = two_up[:, d:]
+        rows[2 * n : 3 * n, h:] = two_down[:, d:]
+        rows[3 * n :, :h] = far_up[...]
+        rows[3 * n :, h:] = far_down[...]
+        hidden[...] = hidden_of(rows, gate_w, up_w, up_w2)
         for second in (False, True):
             target = out_down if second else out_up
 
@@ -101,7 +104,7 @@
             def _(i):
                 start = pl.multiple_of(i * step, step)
                 cut = pl.ds(start + second * h, step)
-                terms = b16(jnp.dot(out[6 * n :, :], down_w[:, cut], preferred_element_type=jnp.float32))
+                terms = b16(jnp.dot(hidden[...], down_w[:, cut], preferred_element_type=jnp.float32))
                 out_up[:, cut] = terms[:n]
                 out_down[:, cut] = terms[n : 2 * n]
                 target[:, pl.ds(start + d, step)] = terms[2 * n : 3 * n]
@@ -110,16 +113,13 @@
     vmem, b = pl.BlockSpec(memory_space=pltpu.VMEM), jnp.bfloat16
     return pl.pallas_call(
         kernel,
-        out_shape=[pltpu.VMEM(shape, b) for shape in ((10 * n, ff), (n, 2 * d), (n, 2 * d), (ff, d))],
-        in_specs=[vmem] * 11 + [pl.BlockSpec(memory_space=pltpu.HBM)],
-        out_specs=[vmem] * 4,
-        scratch_shapes=[pltpu.VMEM((10 * n, d), b), pltpu.SemaphoreType.DMA],
-        compiler_params=pltpu.CompilerParams(vmem_limit_bytes=10 * 1024 * 1024),
-        cost_estimate=pl.CostEstimate(flops=4 * 12 * n * d * ff, bytes_accessed=2 * d * ff, transcendentals=10 * n * ff),
-    )(
-        *placed((near_l, near_r, far_l, far_r, two_up, two_down, far_2up, far_2down, *weights)),
-        pltpu.with_memory_space_constraint(down_weight, pltpu.HBM),
-    )
+        out_shape=[pltpu.VMEM((n, 2 * d), b)] * 2,
+        in_specs=[vmem] * 8,
+        out_specs=[vmem] * 2,
+        scratch_shapes=[pltpu.VMEM((4 * n, d), b), pltpu.VMEM((4 * n, ff), b)],
+        compiler_params=pltpu.CompilerParams(vmem_limit_bytes=8 * 1024 * 1024),
+        cost_estimate=pl.CostEstimate(flops=6 * 4 * n * d * ff, bytes_accessed=0, transcendentals=4 * n * ff),
+    )(*placed((two_up, two_down, far_up, far_down, *weights, down_w)))
 
 
 def other_terms(early, late, down_weight):
@@ -129,7 +129,7 @@
     def kernel(early, late, down_w, *rest):
         outs, held = rest[:-1], rest[-1]
         held[: 6 * n, :] = early[...]
-        held[6 * n :, :] = late[: 6 * n, :]
+        held[6 * n :, :] = late[...]
 
         @pl.loop(0, d // step)
         def _(i):
@@ -183,15 +183,14 @@
     near_l, near_r = shift(near, 1, 0), shift(near, -1, 0)
     far, up_v2 = lax.optimization_barrier((jnp.concatenate([below_2, above_2], 1), fetched(up_weight, 1, 2)))
     weights = gate_v, up_v, up_v2
-    early = early_hidden((own, own_l, own_r, below, above, far), weights)
+    (early,) = hidden_units((own, own_l, own_r, below, above, far), weights)
     far_l, far_r = lax.optimization_barrier((shift(far, 1, 0), shift(far, -1, 0)))
     near_l, near_r, early = lax.optimization_barrier((near_l, near_r, early))
     two_up = shift(jnp.concatenate([near_l[:n], own_l[:, :h]], 1), 1, 0)
     two_down = shift(jnp.concatenate([near_r[n:], own_r[:, h:]], 1), -1, 0)
     far_2up, far_2down = shift(far_l[:, :h], 1, 0), shift(far_r[:, h:], -1, 0)
-    late, two_up, two_down, down_v = late_hidden(
-        near_l, near_r, far_l, far_r, two_up, two_down, far_2up, far_2down, weights, down_weight
-    )
+    late, down_v = hidden_units((near_l, near_r, far_l, far_r), weights, down_weight)
+    two_up, two_down = two_hops(two_up, two_down, far_2up, far_2down, weights, down_v)
     return *other_terms(early, late, down_v), two_up, two_down
 
 

time: 96.2 us -> 96.5 us (level)
  waiting for transfers between devices: 24.5 us -> 16 us
  starting transfers between devices: 43.3 us -> 49.3 us
  Pallas kernels: 25.7 us -> 28.2 us
    ppermute x25, waiting for transfers between devices: 24.5 us -> 16 us  [shift(): return lax.ppermute(block, 'tensor', pairs)]
    ppermute x25, starting transfers between devices: 43.3 us -> 49.3 us  [shift(): return lax.ppermute(block, 'tensor', pairs)]
    pallas_call x2 -> x3, Pallas kernels: 11.7 us -> 14.3 us  [the longest x2 7.79 us: hidden_units(): pl.pallas_call(kernel, out_shape=[pltpu.VMEM((tall, ff), b)] + [pltpu.VME...]
  transfers between devices with their start and end apart: 25 -> 25, of which waited for: 12 -> 11; matrix products, arithmetic and copies ran while one was open for 1% -> 1% of each run, Pallas kernels for 17% -> 22%
where the time goes in v6:
time: 96.5 us; the launch traced here: 95.5 us
  starting transfers between devices  49.3 us (51%)
  Pallas kernels  28.2 us (29%)
  waiting for transfers between devices  16 us (17%)
  other arithmetic  1.4 us (1%)
    ppermute x25, starting transfers between devices, shift(): return lax.ppermute(block, 'tensor', pairs)  49.3 us
    ppermute x25, waiting for transfers between devices, shift(): return lax.ppermute(block, 'tensor', pairs)  16 us
    pallas_call x3, Pallas kernels, fetched(): pl.pallas_call(kernel, out_shape=pltpu.VMEM((size, weight.shape[1]), weig...  9.28 us
    pallas_call x2, Pallas kernels, hidden_units(): pl.pallas_call(kernel, out_shape=[pltpu.VMEM((tall, ff), b)] + [pltpu.VME...  7.79 us
    pallas_call x1, Pallas kernels, two_hops(): pl.pallas_call(kernel, out_shape=[pltpu.VMEM((n, 2 * d), b)] * 2, in_spec...  6.51 us
    pallas_call x1, Pallas kernels, other_terms(): pl.pallas_call(kernel, out_shape=[pltpu.VMEM((k * n, d), jnp.float32) for...  3.56 us
  transfers between devices with their start and end apart: 25, of which 11 were waited for; matrix products, arithmetic and copies ran while one was open for 1% of the time, Pallas kernels for 22%

profile of v6, /device:TPU:8, one launch (start us, length us, event | category | flops | bytes accessed | tf_op | source)
XLA Modules:
  0.0 95.5 jit_solution(857554400022868635)
XLA Ops:
  0.0 1.1 %shard_map.55.refs_0_ = bf16[16,6144]{1,0:T(8,128)(2,1)S(1)} custom-call(bf16[16,6144]{1,0:T(8,128)(2,1)} %rows_ref.1, f32[1,6144]{1,0:T(1,128)} %bitcast.1), custom_call_target="tpu_custom_call" | custom-call | tf_op jit(solution)/shard_map/pallas_call | solution.py:35
  1.1 3.3 %collective-permute-start = (bf16[16,6144]{1,0:T(8,128)(2,1)S(1)}, bf16[16,6144]{1,0:T(8,128)(2,1)S(1)}, u32[]{:S(2)}, u32[]{:S(2)}) collective-permute-start(bf16[16,6144]{1,0:T(8,128)(2,1)S(1)} %shard_map.55.refs_0_), channel_id=1, source_target_pairs={{0,1},{1,2},{2,3},{3,0},{4,5},{5,6},{6,7},{7,4},{8,9},{9,10},{10,1... | collective-permute-start | bytes 589832 | tf_op jit(solution)/shard_map/ppermute | solution.py:17
  4.5 3.1 %collective-permute-start.1 = (bf16[16,6144]{1,0:T(8,128)(2,1)S(1)}, bf16[16,6144]{1,0:T(8,128)(2,1)S(1)}, u32[]{:S(2)}, u32[]{:S(2)}) collective-permute-start(bf16[16,6144]{1,0:T(8,128)(2,1)S(1)} %shard_map.55.refs_0_), channel_id=1, source_target_pairs={{0,3},{1,0},{2,1},{3,2},{4,7},{5,4},{6,5},{7,6},{8,11},{9,8},{10,9... | collective-permute-start | bytes 589832 | tf_op jit(solution)/shard_map/ppermute | solution.py:17
  7.6 1.5 %collective-permute-start.2 = (bf16[16,6144]{1,0:T(8,128)(2,1)S(1)}, bf16[16,6144]{1,0:T(8,128)(2,1)S(1)}, u32[]{:S(2)}, u32[]{:S(2)}) collective-permute-start(bf16[16,6144]{1,0:T(8,128)(2,1)S(1)} %shard_map.55.refs_0_), channel_id=1, source_target_pairs={{0,4},{1,5},{2,6},{3,7},{4,8},{5,9},{6,10},{7,11},{8,12},{9,13},{1... | collective-permute-start | bytes 589832 | tf_op jit(solution)/shard_map/ppermute | solution.py:17
  9.1 1.7 %collective-permute-start.3 = (bf16[16,6144]{1,0:T(8,128)(2,1)S(1)}, bf16[16,6144]{1,0:T(8,128)(2,1)S(1)}, u32[]{:S(2)}, u32[]{:S(2)}) collective-permute-start(bf16[16,6144]{1,0:T(8,128)(2,1)S(1)} %shard_map.55.refs_0_), channel_id=1, source_target_pairs={{0,12},{1,13},{2,14},{3,15},{4,0},{5,1},{6,2},{7,3},{8,4},{9,5},{1... | collective-permute-start | bytes 589832 | tf_op jit(solution)/shard_map/ppermute | solution.py:17
  10.8 4.1 %shard_map.56.refs_6_.refs_4_.gate_w = bf16[6144,896]{1,0:T(8,128)(2,1)S(1)} custom-call(bf16[6144,896]{1,0:T(8,128)(2,1)} %source.2), custom_call_target="tpu_custom_call" | custom-call | bytes 11010048 | tf_op jit(solution)/shard_map/pallas_call | solution.py:163
  15.0 2.6 %shard_map.57.refs_7_.refs_5_.up_w = bf16[3072,896]{1,0:T(8,128)(2,1)S(1)} custom-call(bf16[6144,896]{1,0:T(8,128)(2,1)} %source.4), custom_call_target="tpu_custom_call" | custom-call | bytes 5505024 | tf_op jit(solution)/shard_map/pallas_call | solution.py:163
  17.6 0.0 collective-permute-done.refs_3_
  17.6 0.2 collective-permute-done.1.refs_4_
  17.8 3.7 %collective-permute-start.6 = (bf16[16,3072]{1,0:T(8,128)(2,1)S(1)}, bf16[16,3072]{1,0:T(8,128)(2,1)S(1)}, u32[]{:S(2)}, u32[]{:S(2)}) collective-permute-start(bf16[16,3072]{1,0:T(8,128)(2,1)S(1)} %slice.90), channel_id=1, source_target_pairs={{0,1},{1,2},{2,3},{3,0},{4,5},{5,6},{6,7},{7,4},{8,9},{9,10},{10,1... | collective-permute-start | bytes 294920 | tf_op jit(solution)/shard_map/ppermute | solution.py:17
  21.5 0.5 collective-permute-start.7
  22.1 1.6 %collective-permute-start.4 = (bf16[32,6144]{1,0:T(8,128)(2,1)S(1)}, bf16[32,6144]{1,0:T(8,128)(2,1)S(1)}, u32[]{:S(2)}, u32[]{:S(2)}) collective-permute-start(bf16[32,6144]{1,0:T(8,128)(2,1)S(1)} %pad_maximum_fusion), channel_id=1, source_target_pairs={{0,4},{1,5},{2,6},{3,7},{4,8},{5,9},{6,10},{7,11},{8,12},{9,13},{1... | collective-permute-start | bytes 1179656 | tf_op jit(solution)/shard_map/ppermute | solution.py:17
  23.7 1.7 %collective-permute-start.5 = (bf16[32,6144]{1,0:T(8,128)(2,1)S(1)}, bf16[32,6144]{1,0:T(8,128)(2,1)S(1)}, u32[]{:S(2)}, u32[]{:S(2)}) collective-permute-start(bf16[32,6144]{1,0:T(8,128)(2,1)S(1)} %pad_maximum_fusion), channel_id=1, source_target_pairs={{0,12},{1,13},{2,14},{3,15},{4,0},{5,1},{6,2},{7,3},{8,4},{9,5},{1... | collective-permute-start | bytes 1179656 | tf_op jit(solution)/shard_map/ppermute | solution.py:17
  25.5 2.6 %shard_map.58.refs_8_.refs_6_.up_w2 = bf16[3072,896]{1,0:T(8,128)(2,1)S(1)} custom-call(bf16[6144,896]{1,0:T(8,128)(2,1)} %source.4), custom_call_target="tpu_custom_call" | custom-call | bytes 5505024 | tf_op jit(solution)/shard_map/pallas_call | solution.py:163
  28.1 0.0 collective-permute-done.6
  28.1 0.1 collective-permute-done.7
  28.2 1.5 %collective-permute-start.8 = (bf16[16,6144]{1,0:T(8,128)(2,1)S(1)}, bf16[16,6144]{1,0:T(8,128)(2,1)S(1)}, u32[]{:S(2)}, u32[]{:S(2)}) collective-permute-start(bf16[16,6144]{1,0:T(8,128)(2,1)S(1)} %pad_maximum_fusion.5.refs_5_), channel_id=1, source_target_pairs={{0,4},{1,5},{2,6},{3,7},{4,8},{5,9},{6,10},{7,11},{8,12},{9,13},{1... | collective-permute-start | bytes 589832 | tf_op jit(solution)/shard_map/ppermute | solution.py:17
  29.7 1.8 %collective-permute-start.9 = (bf16[16,6144]{1,0:T(8,128)(2,1)S(1)}, bf16[16,6144]{1,0:T(8,128)(2,1)S(1)}, u32[]{:S(2)}, u32[]{:S(2)}) collective-permute-start(bf16[16,6144]{1,0:T(8,128)(2,1)S(1)} %pad_maximum_fusion.5.refs_5_), channel_id=1, source_target_pairs={{0,12},{1,13},{2,14},{3,15},{4,0},{5,1},{6,2},{7,3},{8,4},{9,5},{1... | collective-permute-start | bytes 589832 | tf_op jit(solution)/shard_map/ppermute | solution.py:17
  31.5 3.6 %shard_map.59.early = bf16[96,896]{1,0:T(8,128)(2,1)S(1)} custom-call(bf16[16,6144]{1,0:T(8,128)(2,1)S(1)} %shard_map.55.refs_0_, bf16[16,6144]{1,0:T(8,128)(2,1)S(1)} %collective-permute-done.2.refs_1_, bf16[16,6144]{1,0:T(8,128)(2,1)S(1)} %collective-permute-done.3.refs_2_, bf16[16,6144]{1,0:T(8,128)(2,1)S(1)} %collective-permute-done.refs_3_, ...), custom_call_target="tpu_custom_call" | custom-call | flops 2113929216 | tf_op jit(solution)/shard_map/pallas_call | solution.py:78
  35.2 0.3 collective-permute-done.4.refs_0_
  35.5 0.1 collective-permute-done.5.refs_1_
  35.6 3.3 %collective-permute-start.11 = (bf16[16,9216]{1,0:T(8,128)(2,1)S(1)}, bf16[16,9216]{1,0:T(8,128)(2,1)S(1)}, u32[]{:S(2)}, u32[]{:S(2)}) collective-permute-start(bf16[16,9216]{1,0:T(8,128)(2,1)S(1)} %pad_maximum_fusion.4), channel_id=1, source_target_pairs={{0,12},{1,13},{2,14},{3,15},{4,0},{5,1},{6,2},{7,3},{8,4},{9,5},{1... | collective-permute-start | bytes 884744 | tf_op jit(solution)/shard_map/ppermute | solution.py:17
  38.9 0.3 collective-permute-start.10
  39.2 0.0 collective-permute-done.8.refs_2_
  39.2 0.4 collective-permute-done.9.refs_3_
  39.6 2.0 %collective-permute-start.12 = (bf16[16,3072]{1,0:T(8,128)(2,1)S(1)}, bf16[16,3072]{1,0:T(8,128)(2,1)S(1)}, u32[]{:S(2)}, u32[]{:S(2)}) collective-permute-start(bf16[16,3072]{1,0:T(8,128)(2,1)S(1)} %slice.97), channel_id=1, source_target_pairs={{0,4},{1,5},{2,6},{3,7},{4,8},{5,9},{6,10},{7,11},{8,12},{9,13},{1... | collective-permute-start | bytes 294920 | tf_op jit(solution)/shard_map/ppermute | solution.py:17
  41.6 1.6 %collective-permute-start.13 = (bf16[16,3072]{1,0:T(8,128)(2,1)S(1)}, bf16[16,3072]{1,0:T(8,128)(2,1)S(1)}, u32[]{:S(2)}, u32[]{:S(2)}) collective-permute-start(bf16[16,3072]{1,0:T(8,128)(2,1)S(1)} %slice.98), channel_id=1, source_target_pairs={{0,12},{1,13},{2,14},{3,15},{4,0},{5,1},{6,2},{7,3},{8,4},{9,5},{1... | collective-permute-start | bytes 294920 | tf_op jit(solution)/shard_map/ppermute | solution.py:17
  43.1 4.1 %shard_map.60 = (bf16[96,896]{1,0:T(8,128)(2,1)S(1)}, bf16[896,6144]{1,0:T(8,128)(2,1)S(1)}) custom-call(bf16[32,6144]{1,0:T(8,128)(2,1)S(1)} %collective-permute-done.4.refs_0_, bf16[32,6144]{1,0:T(8,128)(2,1)S(1)} %collective-permute-done.5.refs_1_, bf16[16,6144]{1,0:T(8,128)(2,1)S(1)} %collective-permute-done.8.refs_2_, ...), custom_call_target="tpu_custom_call" | custom-call | flops 2113929216 | bytes 11010048 | tf_op jit(solution)/shard_map/pallas_call | solution.py:78
  47.3 0.9 collective-permute-done.12.far_up
  48.1 6.5 %shard_map.62 = (bf16[16,12288]{1,0:T(8,128)(2,1)S(1)}, bf16[16,12288]{1,0:T(8,128)(2,1)S(1)}) custom-call(bf16[16,9216]{1,0:T(8,128)(2,1)S(1)} %collective-permute-done.10.two_up, bf16[16,9216]{1,0:T(8,128)(2,1)S(1)} %collective-permute-done.11.two_down, bf16[16,3072]{1,0:T(8,128)(2,1)S(1)} %collective-permute-done.12.far_up, ...), custom_call_target="tpu_custom_call" | custom-call | flops 2113929216 | tf_op jit(solution)/shard_map/pallas_call | solution.py:114
  54.7 0.1 collective-permute-start.14
  54.8 3.2 %collective-permute-start.15 = (bf16[16,12288]{1,0:T(8,128)(2,1)S(1)}, bf16[16,12288]{1,0:T(8,128)(2,1)S(1)}, u32[]{:S(2)}, u32[]{:S(2)}) collective-permute-start(bf16[16,12288]{1,0:T(8,128)(2,1)S(1)} %get-tuple-element.59), channel_id=1, source_target_pairs={{0,12},{1,13},{2,14},{3,15},{4,0},{5,1},{6,2},{7,3},{8,4},{9,5},{1... | collective-permute-start | bytes 1179656 | tf_op jit(solution)/shard_map/ppermute | solution.py:17
  58.0 3.6 %shard_map.61 = (f32[16,6144]{1,0:T(8,128)S(1)}, f32[16,6144]{1,0:T(8,128)S(1)}, f32[16,6144]{1,0:T(8,128)S(1)}, f32[32,6144]{1,0:T(8,128)S(1)}, f32[16,6144]{1,...) custom-call(bf16[96,896]{1,0:T(8,128)(2,1)S(1)} %shard_map.59.early,, ...), custom_call_target="tpu_custom_call" | custom-call | flops 2113929216 | tf_op jit(solution)/shard_map/pallas_call | solution.py:144
  61.7 2.9 %collective-permute-done.14 = bf16[16,12288]{1,0:T(8,128)(2,1)S(1)} collective-permute-done((bf16[16,12288]{1,0:T(8,128)(2,1)S(1)}, bf16[16,12288]{1,0:T(8,128)(2,1)S(1)}, u32[]{:S(2)}, u32[]{:S(2)}) %collective-permute-start.14) | collective-permute-done | bytes 393248 | tf_op jit(solution)/shard_map/ppermute | solution.py:17
  64.8 0.1 collective-permute-start.20
  64.9 3.5 %collective-permute-start.21 = (bf16[16,6144]{1,0:T(8,128)(2,1)S(1)}, bf16[16,6144]{1,0:T(8,128)(2,1)S(1)}, u32[]{:S(2)}, u32[]{:S(2)}) collective-permute-start(bf16[16,6144]{1,0:T(8,128)(2,1)S(1)} %pad_maximum_fusion.9), channel_id=1, source_target_pairs={{0,12},{1,13},{2,14},{3,15},{4,0},{5,1},{6,2},{7,3},{8,4},{9,5},{1... | collective-permute-start | bytes 589832 | tf_op jit(solution)/shard_map/ppermute | solution.py:17
  68.4 2.3 %collective-permute-start.17 = (bf16[32,6144]{1,0:T(8,128)(2,1)S(1)}, bf16[32,6144]{1,0:T(8,128)(2,1)S(1)}, u32[]{:S(2)}, u32[]{:S(2)}) collective-permute-start(bf16[32,6144]{1,0:T(8,128)(2,1)S(1)} %pad_maximum_fusion.2), channel_id=1, source_target_pairs={{0,12},{1,13},{2,14},{3,15},{4,0},{5,1},{6,2},{7,3},{8,4},{9,5},{1... | collective-permute-start | bytes 1179656 | tf_op jit(solution)/shard_map/ppermute | solution.py:17
  70.7 0.1 collective-permute-start.16
  70.9 3.0 %collective-permute-done.20 = bf16[16,6144]{1,0:T(8,128)(2,1)S(1)} collective-permute-done((bf16[16,6144]{1,0:T(8,128)(2,1)S(1)}, bf16[16,6144]{1,0:T(8,128)(2,1)S(1)}, u32[]{:S(2)}, u32[]{:S(2)}) %collective-permute-start.20) | collective-permute-done | bytes 196640 | tf_op jit(solution)/shard_map/ppermute | solution.py:17
  73.8 0.1 add_convert_fusion.2
  73.9 4.3 %collective-permute-start.22 = (bf16[16,6144]{1,0:T(8,128)(2,1)S(1)}, bf16[16,6144]{1,0:T(8,128)(2,1)S(1)}, u32[]{:S(2)}, u32[]{:S(2)}) collective-permute-start(bf16[16,6144]{1,0:T(8,128)(2,1)S(1)} %add_convert_fusion.2), channel_id=1, source_target_pairs={{0,2},{1,3},{2,0},{3,1},{4,6},{5,7},{6,4},{7,5},{8,10},{9,11},{10,... | collective-permute-start | bytes 589832 | tf_op jit(solution)/shard_map/ppermute | solution.py:17
  78.2 1.6 %collective-permute-done.16 = bf16[32,6144]{1,0:T(8,128)(2,1)S(1)} collective-permute-done((bf16[32,6144]{1,0:T(8,128)(2,1)S(1)}, bf16[32,6144]{1,0:T(8,128)(2,1)S(1)}, u32[]{:S(2)}, u32[]{:S(2)}) %collective-permute-start.16) | collective-permute-done | bytes 393248 | tf_op jit(solution)/shard_map/ppermute | solution.py:17
  79.8 0.1 add_convert_fusion
  79.9 4.9 %collective-permute-start.23 = (bf16[16,6144]{1,0:T(8,128)(2,1)S(1)}, bf16[16,6144]{1,0:T(8,128)(2,1)S(1)}, u32[]{:S(2)}, u32[]{:S(2)}) collective-permute-start(bf16[16,6144]{1,0:T(8,128)(2,1)S(1)} %get-tuple-element.77), channel_id=1, source_target_pairs={{0,1},{1,2},{2,3},{3,0},{4,5},{5,6},{6,7},{7,4},{8,9},{9,10},{10,1... | collective-permute-start | bytes 589832 | tf_op jit(solution)/shard_map/ppermute | solution.py:17
  84.8 3.2 %collective-permute-start.19 = (bf16[16,6144]{1,0:T(8,128)(2,1)S(1)}, bf16[16,6144]{1,0:T(8,128)(2,1)S(1)}, u32[]{:S(2)}, u32[]{:S(2)}) collective-permute-start(bf16[16,6144]{1,0:T(8,128)(2,1)S(1)} %pad_maximum_fusion.7), channel_id=1, source_target_pairs={{0,12},{1,13},{2,14},{3,15},{4,0},{5,1},{6,2},{7,3},{8,4},{9,5},{1... | collective-permute-start | bytes 589832 | tf_op jit(solution)/shard_map/ppermute | solution.py:17
  88.1 0.9 collective-permute-done.23
  89.0 5.7 %collective-permute-done.24 = bf16[16,6144]{1,0:T(8,128)(2,1)S(1)} collective-permute-done((bf16[16,6144]{1,0:T(8,128)(2,1)S(1)}, bf16[16,6144]{1,0:T(8,128)(2,1)S(1)}, u32[]{:S(2)}, u32[]{:S(2)}) %collective-permute-start.24) | collective-permute-done | bytes 196640 | tf_op jit(solution)/shard_map/ppermute | solution.py:17
  94.6 0.8 add_convert_fusion.1
  (44 shorter events, 0.6 us)
Async XLA Ops:
  1.1 16.4 %collective-permute-start = (bf16[16,6144]{1,0:T(8,128)(2,1)S(1)}, bf16[16,6144]{1,0:T(8,128)(2,1)S(1)}, u32[]{:S(2)}, u32[]{:S(2)}) collective-permute-start(bf16[16,6144]{1,0:T(8,128)(2,1)S(1)} %shard_map.55.refs_0_), channel_id=1, source_target_pairs={{0,1},{1,2},{2,3},{3,0},{4,5},{5,6},{6,7},{7,4},{8,9},{9,10},{10,1... | collective-permute-start | bytes 589832 | tf_op jit(solution)/shard_map/ppermute | solution.py:17
  4.5 13.3 %collective-permute-start.1 = (bf16[16,6144]{1,0:T(8,128)(2,1)S(1)}, bf16[16,6144]{1,0:T(8,128)(2,1)S(1)}, u32[]{:S(2)}, u32[]{:S(2)}) collective-permute-start(bf16[16,6144]{1,0:T(8,128)(2,1)S(1)} %shard_map.55.refs_0_), channel_id=1, source_target_pairs={{0,3},{1,0},{2,1},{3,2},{4,7},{5,4},{6,5},{7,6},{8,11},{9,8},{10,9... | collective-permute-start | bytes 589832 | tf_op jit(solution)/shard_map/ppermute | solution.py:17
  7.6 14.5 %collective-permute-start.2 = (bf16[16,6144]{1,0:T(8,128)(2,1)S(1)}, bf16[16,6144]{1,0:T(8,128)(2,1)S(1)}, u32[]{:S(2)}, u32[]{:S(2)}) collective-permute-start(bf16[16,6144]{1,0:T(8,128)(2,1)S(1)} %shard_map.55.refs_0_), channel_id=1, source_target_pairs={{0,4},{1,5},{2,6},{3,7},{4,8},{5,9},{6,10},{7,11},{8,12},{9,13},{1... | collective-permute-start | bytes 589832 | tf_op jit(solution)/shard_map/ppermute | solution.py:17
  9.1 13.1 %collective-permute-start.3 = (bf16[16,6144]{1,0:T(8,128)(2,1)S(1)}, bf16[16,6144]{1,0:T(8,128)(2,1)S(1)}, u32[]{:S(2)}, u32[]{:S(2)}) collective-permute-start(bf16[16,6144]{1,0:T(8,128)(2,1)S(1)} %shard_map.55.refs_0_), channel_id=1, source_target_pairs={{0,12},{1,13},{2,14},{3,15},{4,0},{5,1},{6,2},{7,3},{8,4},{9,5},{1... | collective-permute-start | bytes 589832 | tf_op jit(solution)/shard_map/ppermute | solution.py:17
  17.8 10.3 %collective-permute-start.6 = (bf16[16,3072]{1,0:T(8,128)(2,1)S(1)}, bf16[16,3072]{1,0:T(8,128)(2,1)S(1)}, u32[]{:S(2)}, u32[]{:S(2)}) collective-permute-start(bf16[16,3072]{1,0:T(8,128)(2,1)S(1)} %slice.90), channel_id=1, source_target_pairs={{0,1},{1,2},{2,3},{3,0},{4,5},{5,6},{6,7},{7,4},{8,9},{9,10},{10,1... | collective-permute-start | bytes 294920 | tf_op jit(solution)/shard_map/ppermute | solution.py:17
  21.5 6.6 %collective-permute-start.7 = (bf16[16,3072]{1,0:T(8,128)(2,1)S(1)}, bf16[16,3072]{1,0:T(8,128)(2,1)S(1)}, u32[]{:S(2)}, u32[]{:S(2)}) collective-permute-start(bf16[16,3072]{1,0:T(8,128)(2,1)S(1)} %slice.91), channel_id=1, source_target_pairs={{0,3},{1,0},{2,1},{3,2},{4,7},{5,4},{6,5},{7,6},{8,11},{9,8},{10,9... | collective-permute-start | bytes 294920 | tf_op jit(solution)/shard_map/ppermute | solution.py:17
  22.1 13.3 %collective-permute-start.4 = (bf16[32,6144]{1,0:T(8,128)(2,1)S(1)}, bf16[32,6144]{1,0:T(8,128)(2,1)S(1)}, u32[]{:S(2)}, u32[]{:S(2)}) collective-permute-start(bf16[32,6144]{1,0:T(8,128)(2,1)S(1)} %pad_maximum_fusion), channel_id=1, source_target_pairs={{0,4},{1,5},{2,6},{3,7},{4,8},{5,9},{6,10},{7,11},{8,12},{9,13},{1... | collective-permute-start | bytes 1179656 | tf_op jit(solution)/shard_map/ppermute | solution.py:17
  23.7 11.8 %collective-permute-start.5 = (bf16[32,6144]{1,0:T(8,128)(2,1)S(1)}, bf16[32,6144]{1,0:T(8,128)(2,1)S(1)}, u32[]{:S(2)}, u32[]{:S(2)}) collective-permute-start(bf16[32,6144]{1,0:T(8,128)(2,1)S(1)} %pad_maximum_fusion), channel_id=1, source_target_pairs={{0,12},{1,13},{2,14},{3,15},{4,0},{5,1},{6,2},{7,3},{8,4},{9,5},{1... | collective-permute-start | bytes 1179656 | tf_op jit(solution)/shard_map/ppermute | solution.py:17
  28.2 11.0 %collective-permute-start.8 = (bf16[16,6144]{1,0:T(8,128)(2,1)S(1)}, bf16[16,6144]{1,0:T(8,128)(2,1)S(1)}, u32[]{:S(2)}, u32[]{:S(2)}) collective-permute-start(bf16[16,6144]{1,0:T(8,128)(2,1)S(1)} %pad_maximum_fusion.5.refs_5_), channel_id=1, source_target_pairs={{0,4},{1,5},{2,6},{3,7},{4,8},{5,9},{6,10},{7,11},{8,12},{9,13},{1... | collective-permute-start | bytes 589832 | tf_op jit(solution)/shard_map/ppermute | solution.py:17
  29.7 9.9 %collective-permute-start.9 = (bf16[16,6144]{1,0:T(8,128)(2,1)S(1)}, bf16[16,6144]{1,0:T(8,128)(2,1)S(1)}, u32[]{:S(2)}, u32[]{:S(2)}) collective-permute-start(bf16[16,6144]{1,0:T(8,128)(2,1)S(1)} %pad_maximum_fusion.5.refs_5_), channel_id=1, source_target_pairs={{0,12},{1,13},{2,14},{3,15},{4,0},{5,1},{6,2},{7,3},{8,4},{9,5},{1... | collective-permute-start | bytes 589832 | tf_op jit(solution)/shard_map/ppermute | solution.py:17
  35.6 12.6 %collective-permute-start.11 = (bf16[16,9216]{1,0:T(8,128)(2,1)S(1)}, bf16[16,9216]{1,0:T(8,128)(2,1)S(1)}, u32[]{:S(2)}, u32[]{:S(2)}) collective-permute-start(bf16[16,9216]{1,0:T(8,128)(2,1)S(1)} %pad_maximum_fusion.4), channel_id=1, source_target_pairs={{0,12},{1,13},{2,14},{3,15},{4,0},{5,1},{6,2},{7,3},{8,4},{9,5},{1... | collective-permute-start | bytes 884744 | tf_op jit(solution)/shard_map/ppermute | solution.py:17
  38.9 9.3 %collective-permute-start.10 = (bf16[16,9216]{1,0:T(8,128)(2,1)S(1)}, bf16[16,9216]{1,0:T(8,128)(2,1)S(1)}, u32[]{:S(2)}, u32[]{:S(2)}) collective-permute-start(bf16[16,9216]{1,0:T(8,128)(2,1)S(1)} %pad_maximum_fusion.3), channel_id=1, source_target_pairs={{0,4},{1,5},{2,6},{3,7},{4,8},{5,9},{6,10},{7,11},{8,12},{9,13},{1... | collective-permute-start | bytes 884744 | tf_op jit(solution)/shard_map/ppermute | solution.py:17
  39.6 8.6 %collective-permute-start.12 = (bf16[16,3072]{1,0:T(8,128)(2,1)S(1)}, bf16[16,3072]{1,0:T(8,128)(2,1)S(1)}, u32[]{:S(2)}, u32[]{:S(2)}) collective-permute-start(bf16[16,3072]{1,0:T(8,128)(2,1)S(1)} %slice.97), channel_id=1, source_target_pairs={{0,4},{1,5},{2,6},{3,7},{4,8},{5,9},{6,10},{7,11},{8,12},{9,13},{1... | collective-permute-start | bytes 294920 | tf_op jit(solution)/shard_map/ppermute | solution.py:17
  41.6 6.6 %collective-permute-start.13 = (bf16[16,3072]{1,0:T(8,128)(2,1)S(1)}, bf16[16,3072]{1,0:T(8,128)(2,1)S(1)}, u32[]{:S(2)}, u32[]{:S(2)}) collective-permute-start(bf16[16,3072]{1,0:T(8,128)(2,1)S(1)} %slice.98), channel_id=1, source_target_pairs={{0,12},{1,13},{2,14},{3,15},{4,0},{5,1},{6,2},{7,3},{8,4},{9,5},{1... | collective-permute-start | bytes 294920 | tf_op jit(solution)/shard_map/ppermute | solution.py:17
  54.7 9.9 %collective-permute-start.14 = (bf16[16,12288]{1,0:T(8,128)(2,1)S(1)}, bf16[16,12288]{1,0:T(8,128)(2,1)S(1)}, u32[]{:S(2)}, u32[]{:S(2)}) collective-permute-start(bf16[16,12288]{1,0:T(8,128)(2,1)S(1)} %get-tuple-element.58), channel_id=1, source_target_pairs={{0,4},{1,5},{2,6},{3,7},{4,8},{5,9},{6,10},{7,11},{8,12},{9,13},{1... | collective-permute-start | bytes 1179656 | tf_op jit(solution)/shard_map/ppermute | solution.py:17
  54.8 9.8 %collective-permute-start.15 = (bf16[16,12288]{1,0:T(8,128)(2,1)S(1)}, bf16[16,12288]{1,0:T(8,128)(2,1)S(1)}, u32[]{:S(2)}, u32[]{:S(2)}) collective-permute-start(bf16[16,12288]{1,0:T(8,128)(2,1)S(1)} %get-tuple-element.59), channel_id=1, source_target_pairs={{0,12},{1,13},{2,14},{3,15},{4,0},{5,1},{6,2},{7,3},{8,4},{9,5},{1... | collective-permute-start | bytes 1179656 | tf_op jit(solution)/shard_map/ppermute | solution.py:17
  58.0 36.6 %copy-start = (bf16[16,6144]{1,0:T(8,128)(2,1)S(1)}, bf16[16,6144]{1,0:T(8,128)(2,1)}, u32[]{:S(2)}) copy-start(bf16[16,6144]{1,0:T(8,128)(2,1)} %rows_ref.1) | copy-start | bytes 589828
  64.8 9.1 %collective-permute-start.20 = (bf16[16,6144]{1,0:T(8,128)(2,1)S(1)}, bf16[16,6144]{1,0:T(8,128)(2,1)S(1)}, u32[]{:S(2)}, u32[]{:S(2)}) collective-permute-start(bf16[16,6144]{1,0:T(8,128)(2,1)S(1)} %pad_maximum_fusion.8), channel_id=1, source_target_pairs={{0,4},{1,5},{2,6},{3,7},{4,8},{5,9},{6,10},{7,11},{8,12},{9,13},{1... | collective-permute-start | bytes 589832 | tf_op jit(solution)/shard_map/ppermute | solution.py:17
  64.9 8.9 %collective-permute-start.21 = (bf16[16,6144]{1,0:T(8,128)(2,1)S(1)}, bf16[16,6144]{1,0:T(8,128)(2,1)S(1)}, u32[]{:S(2)}, u32[]{:S(2)}) collective-permute-start(bf16[16,6144]{1,0:T(8,128)(2,1)S(1)} %pad_maximum_fusion.9), channel_id=1, source_target_pairs={{0,12},{1,13},{2,14},{3,15},{4,0},{5,1},{6,2},{7,3},{8,4},{9,5},{1... | collective-permute-start | bytes 589832 | tf_op jit(solution)/shard_map/ppermute | solution.py:17
  68.4 9.8 %collective-permute-start.17 = (bf16[32,6144]{1,0:T(8,128)(2,1)S(1)}, bf16[32,6144]{1,0:T(8,128)(2,1)S(1)}, u32[]{:S(2)}, u32[]{:S(2)}) collective-permute-start(bf16[32,6144]{1,0:T(8,128)(2,1)S(1)} %pad_maximum_fusion.2), channel_id=1, source_target_pairs={{0,12},{1,13},{2,14},{3,15},{4,0},{5,1},{6,2},{7,3},{8,4},{9,5},{1... | collective-permute-start | bytes 1179656 | tf_op jit(solution)/shard_map/ppermute | solution.py:17
  70.7 9.1 %collective-permute-start.16 = (bf16[32,6144]{1,0:T(8,128)(2,1)S(1)}, bf16[32,6144]{1,0:T(8,128)(2,1)S(1)}, u32[]{:S(2)}, u32[]{:S(2)}) collective-permute-start(bf16[32,6144]{1,0:T(8,128)(2,1)S(1)} %pad_maximum_fusion.1), channel_id=1, source_target_pairs={{0,4},{1,5},{2,6},{3,7},{4,8},{5,9},{6,10},{7,11},{8,12},{9,13},{1... | collective-permute-start | bytes 1179656 | tf_op jit(solution)/shard_map/ppermute | solution.py:17
  73.9 14.2 %collective-permute-start.22 = (bf16[16,6144]{1,0:T(8,128)(2,1)S(1)}, bf16[16,6144]{1,0:T(8,128)(2,1)S(1)}, u32[]{:S(2)}, u32[]{:S(2)}) collective-permute-start(bf16[16,6144]{1,0:T(8,128)(2,1)S(1)} %add_convert_fusion.2), channel_id=1, source_target_pairs={{0,2},{1,3},{2,0},{3,1},{4,6},{5,7},{6,4},{7,5},{8,10},{9,11},{10,... | collective-permute-start | bytes 589832 | tf_op jit(solution)/shard_map/ppermute | solution.py:17
  79.9 9.0 %collective-permute-start.23 = (bf16[16,6144]{1,0:T(8,128)(2,1)S(1)}, bf16[16,6144]{1,0:T(8,128)(2,1)S(1)}, u32[]{:S(2)}, u32[]{:S(2)}) collective-permute-start(bf16[16,6144]{1,0:T(8,128)(2,1)S(1)} %get-tuple-element.77), channel_id=1, source_target_pairs={{0,1},{1,2},{2,3},{3,0},{4,5},{5,6},{6,7},{7,4},{8,9},{9,10},{10,1... | collective-permute-start | bytes 589832 | tf_op jit(solution)/shard_map/ppermute | solution.py:17
  84.8 9.8 %collective-permute-start.24 = (bf16[16,6144]{1,0:T(8,128)(2,1)S(1)}, bf16[16,6144]{1,0:T(8,128)(2,1)S(1)}, u32[]{:S(2)}, u32[]{:S(2)}) collective-permute-start(bf16[16,6144]{1,0:T(8,128)(2,1)S(1)} %get-tuple-element.78), channel_id=1, source_target_pairs={{0,3},{1,0},{2,1},{3,2},{4,7},{5,4},{6,5},{7,6},{8,11},{9,8},{10,9... | collective-permute-start | bytes 589832 | tf_op jit(solution)/shard_map/ppermute | solution.py:17
  84.8 9.8 %collective-permute-start.18 = (bf16[16,6144]{1,0:T(8,128)(2,1)S(1)}, bf16[16,6144]{1,0:T(8,128)(2,1)S(1)}, u32[]{:S(2)}, u32[]{:S(2)}) collective-permute-start(bf16[16,6144]{1,0:T(8,128)(2,1)S(1)} %pad_maximum_fusion.6), channel_id=1, source_target_pairs={{0,4},{1,5},{2,6},{3,7},{4,8},{5,9},{6,10},{7,11},{8,12},{9,13},{1... | collective-permute-start | bytes 589832 | tf_op jit(solution)/shard_map/ppermute | solution.py:17
  84.8 9.8 %collective-permute-start.19 = (bf16[16,6144]{1,0:T(8,128)(2,1)S(1)}, bf16[16,6144]{1,0:T(8,128)(2,1)S(1)}, u32[]{:S(2)}, u32[]{:S(2)}) collective-permute-start(bf16[16,6144]{1,0:T(8,128)(2,1)S(1)} %pad_maximum_fusion.7), channel_id=1, source_target_pairs={{0,12},{1,13},{2,14},{3,15},{4,0},{5,1},{6,2},{7,3},{8,4},{9,5},{1... | collective-permute-start | bytes 589832 | tf_op jit(solution)/shard_map/ppermute | solution.py:17

commit v7 on v6

v7 whole, which is shorter than its diff:
```python
import jax
import jax.numpy as jnp
from jax import lax
from jax.experimental import pallas as pl
from jax.experimental.pallas import tpu as pltpu
from jax.sharding import PartitionSpec as P

SIDE = 4


def shift(block, dx, dz):
    pairs = []
    for part in range(lax.axis_size("dp")):
        way = 1 - 2 * (part % 2)
        for x in range(SIDE):
            for z in range(SIDE):
                there = (x + way * dx) % SIDE * SIDE + (z + way * dz) % SIDE
                pairs.append((part * SIDE**2 + x * SIDE + z, part * SIDE**2 + there))
    return lax.ppermute(block, ("dp", "tensor"), pairs)


def b16(v):
    return v.astype(jnp.bfloat16)


def f32(v):
    return v.astype(jnp.float32)


def rms_normed(rows, gain):
    def kernel(rows_ref, gain_ref, out_ref):
        held = f32(rows_ref[...])
        scale = lax.rsqrt(jnp.mean(held * held, axis=1, keepdims=True) + 1e-05)
        out_ref[...] = b16(held * scale * gain_ref[...])

    vmem = pl.BlockSpec(memory_space=pltpu.VMEM)
    return pl.pallas_call(
        kernel,
        out_shape=pltpu.VMEM(rows.shape, jnp.bfloat16),
        in_specs=[vmem] * 2,
        out_specs=vmem,
        compiler_params=pltpu.CompilerParams(vmem_limit_bytes=4 * 1024 * 1024),
    )(*[pltpu.with_memory_space_constraint(v, pltpu.HBM) for v in (rows, gain.reshape(1, -1))])


def placed(blocks):
    return [pltpu.with_memory_space_constraint(v, pltpu.VMEM) for v in blocks]


def hidden_of(rows, gate_w, up_w, up_w2):
    half = up_w.shape[0]
    gate = jnp.dot(rows[...], gate_w[...], preferred_element_type=jnp.float32)
    up = jnp.dot(rows[:, :half], up_w[...], preferred_element_type=jnp.float32)
    up = up + jnp.dot(rows[:, half:], up_w2[...], preferred_element_type=jnp.float32)
    return b16(gate / (1.0 + jnp.exp(-gate)) * up)


def hidden_units(blocks, weights, down_weight=None):
    (n, d), ff = blocks[0].shape, weights[0].shape[1]
    tall, held = sum(v.shape[0] for v in blocks), len(blocks)
    also = () if down_weight is None else (pltpu.with_memory_space_constraint(down_weight, pltpu.HBM),)

    def kernel(*refs):
        ins, ws, rest = refs[:held], refs[held : held + len(weights)], refs[held + len(weights) :]
        if also:
            source, out, target, rows, done = rest
            copy = pltpu.make_async_copy(source, target, done)
            copy.start()
        else:
            out, rows = rest
        at = 0
        for ref in ins:
            rows[at : at + ref.shape[0], :] = ref[...]
            at += ref.shape[0]
        out[...] = hidden_of(rows, *ws)
        if also:
            copy.wait()

    vmem, b = pl.BlockSpec(memory_space=pltpu.VMEM), jnp.bfloat16
    return pl.pallas_call(
        kernel,
        out_shape=[pltpu.VMEM((tall, ff), b)] + [pltpu.VMEM((ff, d), b) for _ in also],
        in_specs=[vmem] * (held + len(weights)) + [pl.BlockSpec(memory_space=pltpu.HBM) for _ in also],
        out_specs=[vmem] * (1 + len(also)),
        scratch_shapes=[pltpu.VMEM((tall, d), b)] + [pltpu.SemaphoreType.DMA for _ in also],
        compiler_params=pltpu.CompilerParams(vmem_limit_bytes=8 * 1024 * 1024),
        cost_estimate=pl.CostEstimate(flops=4 * tall * d * ff, bytes_accessed=2 * d * ff * len(also), transcendentals=tall * ff),
    )(*placed((*blocks, *weights)), *also)


def two_hops(two, weights, down_w):
    rows, (ff, d), step = two.shape[0], down_w.shape, 1024

    def kernel(two, gate_w, up_w, up_w2, down_w, out, hidden):
        hidden[...] = hidden_of(two, gate_w, up_w, up_w2)

        @pl.loop(0, d // step)
        def _(i):
            cut = pl.ds(pl.multiple_of(i * step, step), step)
            out[:, cut] = b16(jnp.dot(hidden[...], down_w[:, cut], preferred_element_type=jnp.float32))

    vmem, b = pl.BlockSpec(memory_space=pltpu.VMEM), jnp.bfloat16
    return pl.pallas_call(
        kernel,
        out_shape=pltpu.VMEM((rows, d), b),
        in_specs=[vmem] * 5,
        out_specs=vmem,
        scratch_shapes=[pltpu.VMEM((rows, ff), b)],
        compiler_params=pltpu.CompilerParams(vmem_limit_bytes=8 * 1024 * 1024),
        cost_estimate=pl.CostEstimate(flops=6 * rows * d * ff, bytes_accessed=0, transcendentals=rows * ff),
    )(*placed((two, *weights, down_w)))


def other_terms(early, late, down_weight):
    n, (ff, d), step = early.shape[0] // 6, down_weight.shape, 1024
    b, f = jnp.bfloat16, jnp.float32
    made = ((1, f), (1, f), (1, b), (2, f), (1, f), (2, f), (2, b), (1, f), (1, b))

    def kernel(early, late, down_w, *rest):
        outs, held = rest[:-1], rest[-1]
        held[: 6 * n, :] = early[...]
        held[6 * n :, :] = late[...]

        @pl.loop(0, d // step)
        def _(i):
            cut = pl.ds(pl.multiple_of(i * step, step), step)
            terms = jnp.dot(held[...], down_w[:, cut], preferred_element_type=jnp.float32)
            at = 0
            for out, (k, kind) in zip(outs, made, strict=True):
                out[:, cut] = terms[at * n : (at + k) * n].astype(kind)
                at += k

    vmem = pl.BlockSpec(memory_space=pltpu.VMEM)
    return pl.pallas_call(
        kernel,
        out_shape=[pltpu.VMEM((k * n, d), kind) for k, kind in made],
        in_specs=[vmem] * 3,
        out_specs=[vmem] * 9,
        scratch_shapes=[pltpu.VMEM((12 * n, ff), jnp.bfloat16)],
        compiler_params=pltpu.CompilerParams(vmem_limit_bytes=8 * 1024 * 1024),
        cost_estimate=pl.CostEstimate(flops=2 * 12 * n * d * ff, bytes_accessed=0, transcendentals=0),
    )(*placed((early, late, down_weight)))


def fetched(weight, part=0, parts=1):
    size = weight.shape[0] // parts

    def kernel(source, target, done):
        copy = pltpu.make_async_copy(source.at[pl.ds(part * size, size), :], target, done)
        copy.start()
        copy.wait()

    return pl.pallas_call(
        kernel,
        out_shape=pltpu.VMEM((size, weight.shape[1]), weight.dtype),
        in_specs=[pl.BlockSpec(memory_space=pltpu.HBM)],
        out_specs=pl.BlockSpec(memory_space=pltpu.VMEM),
        scratch_shapes=[pltpu.SemaphoreType.DMA],
        compiler_params=pltpu.CompilerParams(vmem_limit_bytes=1024 * 1024),
        cost_estimate=pl.CostEstimate(flops=0, bytes_accessed=2 * size * weight.shape[1], transcendentals=0),
    )(pltpu.with_memory_space_constraint(weight, pltpu.HBM))


def terms_of(own, gate_weight, up_weight, down_weight):
    below, above = lax.optimization_barrier((shift(own, 0, 1), shift(own, 0, -1)))
    own_p, own_m = shift(own, 1, 0), shift(own, -1, 0)
    far = shift(below, 0, 1)
    near, own_p, own_m, gate_v, up_v, up_weight = lax.optimization_barrier(
        (jnp.concatenate([below, above], 0), own_p, own_m, fetched(gate_weight), fetched(up_weight, 0, 2), up_weight)
    )
    near_p, near_m = shift(near, 1, 0), shift(near, -1, 0)
    far, up_v2 = lax.optimization_barrier((far, fetched(up_weight, 1, 2)))
    weights = gate_v, up_v, up_v2
    (early,) = hidden_units((own, own_p, own_m, below, above, far), weights)
    far_p, far_m = shift(far, 1, 0), shift(far, -1, 0)
    near_p, near_m, far_p, far_m, early = lax.optimization_barrier((near_p, near_m, far_p, far_m, early))
    two = shift(jnp.concatenate([near_p, own_p, far_p], 0), 1, 0)
    late, down_v = hidden_units((near_p, near_m, far_p, far_m), weights, down_weight)
    back = two_hops(two, weights, down_v)
    return *other_terms(early, late, down_v), back


def returned(own_here, own_p, own_m, near_here, far_here, near_p, near_m, far_p, far_m, two):
    n = own_here.shape[0]
    two = shift(two, -1, 0)
    far_m, near_m = shift(far_m, 1, 0), shift(near_m, 1, 0)
    far_p = shift(b16(far_p + f32(two[3 * n :])), -1, 0)
    near_p = shift(b16(near_p + f32(two[: 2 * n])), -1, 0)
    far_sum = shift(b16(far_here + f32(far_p) + f32(far_m)), 0, 2)
    own_p, own_m, near_p, near_m = lax.optimization_barrier((b16(own_p + f32(two[2 * n : 3 * n])), own_m, near_p, near_m))
    own_p, own_m = shift(own_p, -1, 0), shift(own_m, 1, 0)
    near_sum = b16(near_here + f32(near_p) + f32(near_m))
    from_above, from_below = shift(near_sum[:n], 0, -1), shift(near_sum[n:], 0, 1)
    return own_here + f32(own_p) + f32(own_m) + f32(far_sum) + f32(from_below) + f32(from_above)


def on_device(tokens, norm_gain, gate_weight, up_weight, down_weight):
    own = rms_normed(tokens, norm_gain)
    return b16(f32(tokens) + returned(*terms_of(own, gate_weight, up_weight, down_weight)))


def solution(mesh):
    return jax.shard_map(
        on_device,
        mesh=mesh,
        in_specs=(
            P(("dp", "tensor"), None),
            P(),
            P(None, "tensor"),
            P(None, "tensor"),
            P("tensor", None),
        ),
        out_specs=P(("dp", "tensor"), None),
        check_vma=False,
    )
```

time: 96.5 us -> 105 us (1.088)
  starting transfers between devices: 49.3 us -> 32.4 us
  waiting for transfers between devices: 16 us -> 29 us
  local copies, waits for them, and re-layouts: 0.2 us -> 12.5 us
    ppermute x25 -> x20, starting transfers between devices: 49.3 us -> 32.4 us  [shift(): return lax.ppermute(block, ('dp', 'tensor'), pairs)]
    ppermute x25 -> x20, waiting for transfers between devices: 16 us -> 29 us  [shift(): return lax.ppermute(block, ('dp', 'tensor'), pairs)]
    unnamed x2 -> x8, local copies, waits for them, and re-layouts: 0.01 us -> 12.5 us
  transfers between devices with their start and end apart: 25 -> 20, of which waited for: 11 -> 12; matrix products, arithmetic and copies ran while one was open for 1% -> 0% of each run, Pallas kernels for 22% -> 20%
where the time goes in v7:
time: 105 us; the launch traced here: 104 us
  starting transfers between devices  32.4 us (31%)
  waiting for transfers between devices  29 us (28%)
  Pallas kernels  28.3 us (27%)
  local copies, waits for them, and re-layouts  12.5 us (12%)
  other arithmetic  1.25 us (1%)
    ppermute x20, starting transfers between devices, shift(): return lax.ppermute(block, ('dp', 'tensor'), pairs)  32.4 us
    ppermute x20, waiting for transfers between devices, shift(): return lax.ppermute(block, ('dp', 'tensor'), pairs)  29 us
    unnamed x8, local copies, waits for them, and re-layouts  12.5 us
    pallas_call x3, Pallas kernels, fetched(): pl.pallas_call(kernel, out_shape=pltpu.VMEM((size, weight.shape[1]), weig...  9.28 us
    pallas_call x2, Pallas kernels, hidden_units(): pl.pallas_call(kernel, out_shape=[pltpu.VMEM((tall, ff), b)] + [pltpu.VME...  7.76 us
    pallas_call x1, Pallas kernels, two_hops(): pl.pallas_call(kernel, out_shape=pltpu.VMEM((rows, d), b), in_specs=[vmem...  6.52 us
    pallas_call x1, Pallas kernels, other_terms(): pl.pallas_call(kernel, out_shape=[pltpu.VMEM((k * n, d), kind) for k, kin...  3.59 us
  transfers between devices with their start and end apart: 20, of which 12 were waited for; matrix products, arithmetic and copies ran while one was open for 0% of the time, Pallas kernels for 20%

profile of v7, /device:TPU:8, one launch (start us, length us, event | category | flops | bytes accessed | tf_op | source)
XLA Modules:
  0.0 103.6 jit_solution(16295857076645903229)
XLA Ops:
  0.0 1.1 %shard_map.55.refs_0_ = bf16[16,6144]{1,0:T(8,128)(2,1)S(1)} custom-call(bf16[16,6144]{1,0:T(8,128)(2,1)} %rows_ref.1, f32[1,6144]{1,0:T(1,128)} %bitcast.1), custom_call_target="tpu_custom_call" | custom-call | tf_op jit(solution)/shard_map/pallas_call | solution.py:37
  1.1 6.4 %collective-permute-start.1 = (bf16[16,6144]{1,0:T(8,128)(2,1)S(1)}, bf16[16,6144]{1,0:T(8,128)(2,1)S(1)}, u32[]{:S(2)}, u32[]{:S(2)}) collective-permute-start(bf16[16,6144]{1,0:T(8,128)(2,1)S(1)} %shard_map.55.refs_0_), channel_id=1, source_target_pairs={{0,3},{1,0},{2,1},{3,2},{4,7},{5,4},{6,5},{7,6},{8,11},{9,8},{10,9... | collective-permute-start | bytes 589832 | tf_op jit(solution)/shard_map/ppermute | solution.py:19
  7.5 0.0 collective-permute-start
  7.5 2.8 %collective-permute-start.3 = (bf16[16,6144]{1,0:T(8,128)(2,1)S(1)}, bf16[16,6144]{1,0:T(8,128)(2,1)S(1)}, u32[]{:S(2)}, u32[]{:S(2)}) collective-permute-start(bf16[16,6144]{1,0:T(8,128)(2,1)S(1)} %shard_map.55.refs_0_), channel_id=1, source_target_pairs={{0,12},{1,13},{2,14},{3,15},{4,0},{5,1},{6,2},{7,3},{8,4},{9,5},{1... | collective-permute-start | bytes 589832 | tf_op jit(solution)/shard_map/ppermute | solution.py:19
  10.3 2.6 %shard_map.57.refs_7_.refs_5_.up_w = bf16[3072,896]{1,0:T(8,128)(2,1)S(1)} custom-call(bf16[6144,896]{1,0:T(8,128)(2,1)} %source.4), custom_call_target="tpu_custom_call" | custom-call | bytes 5505024 | tf_op jit(solution)/shard_map/pallas_call | solution.py:153
  12.8 4.1 %shard_map.56.refs_6_.refs_4_.gate_w = bf16[6144,896]{1,0:T(8,128)(2,1)S(1)} custom-call(bf16[6144,896]{1,0:T(8,128)(2,1)} %source.2), custom_call_target="tpu_custom_call" | custom-call | bytes 11010048 | tf_op jit(solution)/shard_map/pallas_call | solution.py:153
  17.0 0.9 collective-permute-done.refs_3_
  17.9 0.7 collective-permute-start.6
  18.7 3.3 %collective-permute-start.5 = (bf16[32,6144]{1,0:T(8,128)(2,1)S(1)}, bf16[32,6144]{1,0:T(8,128)(2,1)S(1)}, u32[]{:S(2)}, u32[]{:S(2)}) collective-permute-start(bf16[32,6144]{1,0:T(8,128)(2,1)S(1)} %pad_maximum_fusion.1), channel_id=1, source_target_pairs={{0,12},{1,13},{2,14},{3,15},{4,0},{5,1},{6,2},{7,3},{8,4},{9,5},{1... | collective-permute-start | bytes 1179656 | tf_op jit(solution)/shard_map/ppermute | solution.py:19
  22.0 2.6 %shard_map.58.refs_8_.refs_6_.up_w2 = bf16[3072,896]{1,0:T(8,128)(2,1)S(1)} custom-call(bf16[6144,896]{1,0:T(8,128)(2,1)} %source.4), custom_call_target="tpu_custom_call" | custom-call | bytes 5505024 | tf_op jit(solution)/shard_map/pallas_call | solution.py:153
  24.6 2.6 %collective-permute-done.6.refs_5_ = bf16[16,6144]{1,0:T(8,128)(2,1)S(1)} collective-permute-done((bf16[16,6144]{1,0:T(8,128)(2,1)S(1)}, bf16[16,6144]{1,0:T(8,128)(2,1)S(1)}, u32[]{:S(2)}, u32[]{:S(2)}) %collective-permute-start.6) | collective-permute-done | bytes 196640 | tf_op jit(solution)/shard_map/ppermute | solution.py:19
  27.2 1.9 %collective-permute-start.8 = (bf16[16,6144]{1,0:T(8,128)(2,1)S(1)}, bf16[16,6144]{1,0:T(8,128)(2,1)S(1)}, u32[]{:S(2)}, u32[]{:S(2)}) collective-permute-start(bf16[16,6144]{1,0:T(8,128)(2,1)S(1)} %collective-permute-done.6.refs_5_), channel_id=1, source_target_pairs={{0,12},{1,13},{2,14},{3,15},{4,0},{5,1},{6,2},{7,3},{8,4},{9,5},{1... | collective-permute-start | bytes 589832 | tf_op jit(solution)/shard_map/ppermute | solution.py:19
  29.1 0.2 collective-permute-start.7
  29.3 3.6 %shard_map.59.early = bf16[96,896]{1,0:T(8,128)(2,1)S(1)} custom-call(bf16[16,6144]{1,0:T(8,128)(2,1)S(1)} %shard_map.55.refs_0_, bf16[16,6144]{1,0:T(8,128)(2,1)S(1)} %collective-permute-done.2.refs_1_, bf16[16,6144]{1,0:T(8,128)(2,1)S(1)} %collective-permute-done.3.refs_2_, bf16[16,6144]{1,0:T(8,128)(2,1)S(1)} %collective-permute-done.refs_3_, ...), custom_call_target="tpu_custom_call" | custom-call | flops 2113929216 | tf_op jit(solution)/shard_map/pallas_call | solution.py:80
  32.9 1.4 %collective-permute-done.4.refs_0_ = bf16[32,6144]{1,0:T(8,128)(2,1)S(1)} collective-permute-done((bf16[32,6144]{1,0:T(8,128)(2,1)S(1)}, bf16[32,6144]{1,0:T(8,128)(2,1)S(1)}, u32[]{:S(2)}, u32[]{:S(2)}) %collective-permute-start.4) | collective-permute-done | bytes 393248 | tf_op jit(solution)/shard_map/ppermute | solution.py:19
  34.3 1.4 %collective-permute-done.8.refs_3_ = bf16[16,6144]{1,0:T(8,128)(2,1)S(1)} collective-permute-done((bf16[16,6144]{1,0:T(8,128)(2,1)S(1)}, bf16[16,6144]{1,0:T(8,128)(2,1)S(1)}, u32[]{:S(2)}, u32[]{:S(2)}) %collective-permute-start.8) | collective-permute-done | bytes 196640 | tf_op jit(solution)/shard_map/ppermute | solution.py:19
  35.7 0.7 collective-permute-done.7.refs_2_
  36.4 0.1 pad_maximum_fusion
  36.5 0.5 collective-permute-start.9
  37.0 4.1 %shard_map.60 = (bf16[96,896]{1,0:T(8,128)(2,1)S(1)}, bf16[896,6144]{1,0:T(8,128)(2,1)S(1)}) custom-call(bf16[32,6144]{1,0:T(8,128)(2,1)S(1)} %collective-permute-done.4.refs_0_, bf16[32,6144]{1,0:T(8,128)(2,1)S(1)} %collective-permute-done.5.refs_1_, bf16[16,6144]{1,0:T(8,128)(2,1)S(1)} %collective-permute-done.7.refs_2_, ...), custom_call_target="tpu_custom_call" | custom-call | flops 2113929216 | bytes 11010048 | tf_op jit(solution)/shard_map/pallas_call | solution.py:80
  41.2 4.2 %copy-done = bf16[896,6144]{1,0:T(8,128)(2,1)} copy-done((bf16[896,6144]{1,0:T(8,128)(2,1)}, bf16[896,6144]{1,0:T(8,128)(2,1)S(1)}, u32[]{:S(2)}) %copy-start) | copy-done | bytes 11010072
  45.4 4.6 %collective-permute-done.9.two = bf16[64,6144]{1,0:T(8,128)(2,1)S(1)} collective-permute-done((bf16[64,6144]{1,0:T(8,128)(2,1)S(1)}, bf16[64,6144]{1,0:T(8,128)(2,1)S(1)}, u32[]{:S(2)}, u32[]{:S(2)}) %collective-permute-start.9) | collective-permute-done | bytes 786464 | tf_op jit(solution)/shard_map/ppermute | solution.py:19
  49.9 4.1 %copy-done.1 = bf16[896,6144]{1,0:T(8,128)(2,1)S(1)} copy-done((bf16[896,6144]{1,0:T(8,128)(2,1)S(1)}, bf16[896,6144]{1,0:T(8,128)(2,1)}, u32[]{:S(2)}) %copy-start.1) | copy-done | bytes 11010072
  54.1 6.5 %shard_map.62 = bf16[64,6144]{1,0:T(8,128)(2,1)S(1)} custom-call(bf16[64,6144]{1,0:T(8,128)(2,1)S(1)} %collective-permute-done.9.two, bf16[6144,896]{1,0:T(8,128)(2,1)S(1)} %shard_map.56.refs_6_.refs_4_.gate_w, bf16[3072,896]{1,0:T(8,128)(2,1)S(1)} %shard_map.57.refs_7_.refs_5_.up_w, bf16[3072,896]{1,0:T(8,128)(2,1)S(1)} %shard_map.58.refs_8_.refs_6_.up_w2, ...), custom_call_target="tpu_custom_call" | custom-call | flops 2113929216 | tf_op jit(solution)/shard_map/pallas_call | solution.py:103
  60.6 1.8 %collective-permute-start.10 = (bf16[64,6144]{1,0:T(8,128)(2,1)S(1)}, bf16[64,6144]{1,0:T(8,128)(2,1)S(1)}, u32[]{:S(2)}, u32[]{:S(2)}) collective-permute-start(bf16[64,6144]{1,0:T(8,128)(2,1)S(1)} %shard_map.62), channel_id=1, source_target_pairs={{0,12},{1,13},{2,14},{3,15},{4,0},{5,1},{6,2},{7,3},{8,4},{9,5},{1... | collective-permute-start | bytes 2359304 | tf_op jit(solution)/shard_map/ppermute | solution.py:19
  62.4 4.1 %copy-done.2 = bf16[896,6144]{1,0:T(8,128)(2,1)S(1)} copy-done((bf16[896,6144]{1,0:T(8,128)(2,1)S(1)}, bf16[896,6144]{1,0:T(8,128)(2,1)}, u32[]{:S(2)}) %copy-start.2) | copy-done | bytes 11010072
  66.5 3.6 %shard_map.61 = (f32[16,6144]{1,0:T(8,128)S(1)}, f32[16,6144]{1,0:T(8,128)S(1)}, bf16[16,6144]{1,0:T(8,128)(2,1)S(1)}, f32[32,6144]{1,0:T(8,128)S(1)}, f32[16,61...) custom-call(bf16[96,896]{1,0:T(8,128)(2,1)S(1)} %shard_map.59.early,, ...), custom_call_target="tpu_custom_call" | custom-call | flops 2113929216 | tf_op jit(solution)/shard_map/pallas_call | solution.py:134
  70.1 0.0 copy-start.3
  70.2 0.3 collective-permute-start.16
  70.5 0.1 collective-permute-start.12
  70.6 5.1 %collective-permute-done.10 = bf16[64,6144]{1,0:T(8,128)(2,1)S(1)} collective-permute-done((bf16[64,6144]{1,0:T(8,128)(2,1)S(1)}, bf16[64,6144]{1,0:T(8,128)(2,1)S(1)}, u32[]{:S(2)}, u32[]{:S(2)}) %collective-permute-start.10) | collective-permute-done | bytes 786464 | tf_op jit(solution)/shard_map/ppermute | solution.py:19
  75.7 0.1 add_convert_fusion.4
  75.8 1.4 %collective-permute-start.15 = (bf16[16,6144]{1,0:T(8,128)(2,1)S(1)}, bf16[16,6144]{1,0:T(8,128)(2,1)S(1)}, u32[]{:S(2)}, u32[]{:S(2)}) collective-permute-start(bf16[16,6144]{1,0:T(8,128)(2,1)S(1)} %get-tuple-element.65), channel_id=1, source_target_pairs={{0,12},{1,13},{2,14},{3,15},{4,0},{5,1},{6,2},{7,3},{8,4},{9,5},{1... | collective-permute-start | bytes 589832 | tf_op jit(solution)/shard_map/ppermute | solution.py:19
  77.2 0.1 add_convert_fusion.1
  77.2 0.1 collective-permute-start.11
  77.3 1.4 %collective-permute-done.16 = bf16[16,6144]{1,0:T(8,128)(2,1)S(1)} collective-permute-done((bf16[16,6144]{1,0:T(8,128)(2,1)S(1)}, bf16[16,6144]{1,0:T(8,128)(2,1)S(1)}, u32[]{:S(2)}, u32[]{:S(2)}) %collective-permute-start.16) | collective-permute-done | bytes 196640 | tf_op jit(solution)/shard_map/ppermute | solution.py:19
  78.7 2.8 %collective-permute-done.15 = bf16[16,6144]{1,0:T(8,128)(2,1)S(1)} collective-permute-done((bf16[16,6144]{1,0:T(8,128)(2,1)S(1)}, bf16[16,6144]{1,0:T(8,128)(2,1)S(1)}, u32[]{:S(2)}, u32[]{:S(2)}) %collective-permute-start.15) | collective-permute-done | bytes 196640 | tf_op jit(solution)/shard_map/ppermute | solution.py:19
  81.5 0.1 add_convert_fusion.3
  81.6 6.6 %collective-permute-start.17 = (bf16[16,6144]{1,0:T(8,128)(2,1)S(1)}, bf16[16,6144]{1,0:T(8,128)(2,1)S(1)}, u32[]{:S(2)}, u32[]{:S(2)}) collective-permute-start(bf16[16,6144]{1,0:T(8,128)(2,1)S(1)} %add_convert_fusion.3), channel_id=1, source_target_pairs={{0,2},{1,3},{2,0},{3,1},{4,6},{5,7},{6,4},{7,5},{8,10},{9,11},{10,... | collective-permute-start | bytes 589832 | tf_op jit(solution)/shard_map/ppermute | solution.py:19
  88.2 0.1 add_convert_fusion
  88.4 1.3 %collective-permute-start.18 = (bf16[16,6144]{1,0:T(8,128)(2,1)S(1)}, bf16[16,6144]{1,0:T(8,128)(2,1)S(1)}, u32[]{:S(2)}, u32[]{:S(2)}) collective-permute-start(bf16[16,6144]{1,0:T(8,128)(2,1)S(1)} %get-tuple-element.67), channel_id=1, source_target_pairs={{0,1},{1,2},{2,3},{3,0},{4,5},{5,6},{6,7},{7,4},{8,9},{9,10},{10,1... | collective-permute-start | bytes 589832 | tf_op jit(solution)/shard_map/ppermute | solution.py:19
  89.6 2.9 %collective-permute-start.19 = (bf16[16,6144]{1,0:T(8,128)(2,1)S(1)}, bf16[16,6144]{1,0:T(8,128)(2,1)S(1)}, u32[]{:S(2)}, u32[]{:S(2)}) collective-permute-start(bf16[16,6144]{1,0:T(8,128)(2,1)S(1)} %get-tuple-element.68), channel_id=1, source_target_pairs={{0,3},{1,0},{2,1},{3,2},{4,7},{5,4},{6,5},{7,6},{8,11},{9,8},{10,9... | collective-permute-start | bytes 589832 | tf_op jit(solution)/shard_map/ppermute | solution.py:19
  92.6 1.2 %collective-permute-start.13 = (bf16[16,6144]{1,0:T(8,128)(2,1)S(1)}, bf16[16,6144]{1,0:T(8,128)(2,1)S(1)}, u32[]{:S(2)}, u32[]{:S(2)}) collective-permute-start(bf16[16,6144]{1,0:T(8,128)(2,1)S(1)} %get-tuple-element.57), channel_id=1, source_target_pairs={{0,12},{1,13},{2,14},{3,15},{4,0},{5,1},{6,2},{7,3},{8,4},{9,5},{1... | collective-permute-start | bytes 589832 | tf_op jit(solution)/shard_map/ppermute | solution.py:19
  93.8 0.8 collective-permute-start.14
  94.6 2.7 %collective-permute-done.17 = bf16[16,6144]{1,0:T(8,128)(2,1)S(1)} collective-permute-done((bf16[16,6144]{1,0:T(8,128)(2,1)S(1)}, bf16[16,6144]{1,0:T(8,128)(2,1)S(1)}, u32[]{:S(2)}, u32[]{:S(2)}) %collective-permute-start.17) | collective-permute-done | bytes 196640 | tf_op jit(solution)/shard_map/ppermute | solution.py:19
  97.3 4.8 %collective-permute-done.18 = bf16[16,6144]{1,0:T(8,128)(2,1)S(1)} collective-permute-done((bf16[16,6144]{1,0:T(8,128)(2,1)S(1)}, bf16[16,6144]{1,0:T(8,128)(2,1)S(1)}, u32[]{:S(2)}, u32[]{:S(2)}) %collective-permute-start.18) | collective-permute-done | bytes 196640 | tf_op jit(solution)/shard_map/ppermute | solution.py:19
  102.1 0.6 collective-permute-done.19
  102.7 0.8 add_convert_fusion.2
  (16 shorter events, 0.1 us)
Async XLA Ops:
  1.1 15.9 %collective-permute-start.1 = (bf16[16,6144]{1,0:T(8,128)(2,1)S(1)}, bf16[16,6144]{1,0:T(8,128)(2,1)S(1)}, u32[]{:S(2)}, u32[]{:S(2)}) collective-permute-start(bf16[16,6144]{1,0:T(8,128)(2,1)S(1)} %shard_map.55.refs_0_), channel_id=1, source_target_pairs={{0,3},{1,0},{2,1},{3,2},{4,7},{5,4},{6,5},{7,6},{8,11},{9,8},{10,9... | collective-permute-start | bytes 589832 | tf_op jit(solution)/shard_map/ppermute | solution.py:19
  7.5 10.4 %collective-permute-start = (bf16[16,6144]{1,0:T(8,128)(2,1)S(1)}, bf16[16,6144]{1,0:T(8,128)(2,1)S(1)}, u32[]{:S(2)}, u32[]{:S(2)}) collective-permute-start(bf16[16,6144]{1,0:T(8,128)(2,1)S(1)} %shard_map.55.refs_0_), channel_id=1, source_target_pairs={{0,1},{1,2},{2,3},{3,0},{4,5},{5,6},{6,7},{7,4},{8,9},{9,10},{10,1... | collective-permute-start | bytes 589832 | tf_op jit(solution)/shard_map/ppermute | solution.py:19
  7.5 11.2 %collective-permute-start.3 = (bf16[16,6144]{1,0:T(8,128)(2,1)S(1)}, bf16[16,6144]{1,0:T(8,128)(2,1)S(1)}, u32[]{:S(2)}, u32[]{:S(2)}) collective-permute-start(bf16[16,6144]{1,0:T(8,128)(2,1)S(1)} %shard_map.55.refs_0_), channel_id=1, source_target_pairs={{0,12},{1,13},{2,14},{3,15},{4,0},{5,1},{6,2},{7,3},{8,4},{9,5},{1... | collective-permute-start | bytes 589832 | tf_op jit(solution)/shard_map/ppermute | solution.py:19
  10.3 8.4 %collective-permute-start.2 = (bf16[16,6144]{1,0:T(8,128)(2,1)S(1)}, bf16[16,6144]{1,0:T(8,128)(2,1)S(1)}, u32[]{:S(2)}, u32[]{:S(2)}) collective-permute-start(bf16[16,6144]{1,0:T(8,128)(2,1)S(1)} %shard_map.55.refs_0_), channel_id=1, source_target_pairs={{0,4},{1,5},{2,6},{3,7},{4,8},{5,9},{6,10},{7,11},{8,12},{9,13},{1... | collective-permute-start | bytes 589832 | tf_op jit(solution)/shard_map/ppermute | solution.py:19
  17.9 9.3 %collective-permute-start.6 = (bf16[16,6144]{1,0:T(8,128)(2,1)S(1)}, bf16[16,6144]{1,0:T(8,128)(2,1)S(1)}, u32[]{:S(2)}, u32[]{:S(2)}) collective-permute-start(bf16[16,6144]{1,0:T(8,128)(2,1)S(1)} %collective-permute-done.refs_3_), channel_id=1, source_target_pairs={{0,1},{1,2},{2,3},{3,0},{4,5},{5,6},{6,7},{7,4},{8,9},{9,10},{10,1... | collective-permute-start | bytes 589832 | tf_op jit(solution)/shard_map/ppermute | solution.py:19
  18.7 14.3 %collective-permute-start.5 = (bf16[32,6144]{1,0:T(8,128)(2,1)S(1)}, bf16[32,6144]{1,0:T(8,128)(2,1)S(1)}, u32[]{:S(2)}, u32[]{:S(2)}) collective-permute-start(bf16[32,6144]{1,0:T(8,128)(2,1)S(1)} %pad_maximum_fusion.1), channel_id=1, source_target_pairs={{0,12},{1,13},{2,14},{3,15},{4,0},{5,1},{6,2},{7,3},{8,4},{9,5},{1... | collective-permute-start | bytes 1179656 | tf_op jit(solution)/shard_map/ppermute | solution.py:19
  22.0 12.3 %collective-permute-start.4 = (bf16[32,6144]{1,0:T(8,128)(2,1)S(1)}, bf16[32,6144]{1,0:T(8,128)(2,1)S(1)}, u32[]{:S(2)}, u32[]{:S(2)}) collective-permute-start(bf16[32,6144]{1,0:T(8,128)(2,1)S(1)} %pad_maximum_fusion.1), channel_id=1, source_target_pairs={{0,4},{1,5},{2,6},{3,7},{4,8},{5,9},{6,10},{7,11},{8,12},{9,13},{1... | collective-permute-start | bytes 1179656 | tf_op jit(solution)/shard_map/ppermute | solution.py:19
  27.2 8.5 %collective-permute-start.8 = (bf16[16,6144]{1,0:T(8,128)(2,1)S(1)}, bf16[16,6144]{1,0:T(8,128)(2,1)S(1)}, u32[]{:S(2)}, u32[]{:S(2)}) collective-permute-start(bf16[16,6144]{1,0:T(8,128)(2,1)S(1)} %collective-permute-done.6.refs_5_), channel_id=1, source_target_pairs={{0,12},{1,13},{2,14},{3,15},{4,0},{5,1},{6,2},{7,3},{8,4},{9,5},{1... | collective-permute-start | bytes 589832 | tf_op jit(solution)/shard_map/ppermute | solution.py:19
  29.1 7.3 %collective-permute-start.7 = (bf16[16,6144]{1,0:T(8,128)(2,1)S(1)}, bf16[16,6144]{1,0:T(8,128)(2,1)S(1)}, u32[]{:S(2)}, u32[]{:S(2)}) collective-permute-start(bf16[16,6144]{1,0:T(8,128)(2,1)S(1)} %collective-permute-done.6.refs_5_), channel_id=1, source_target_pairs={{0,4},{1,5},{2,6},{3,7},{4,8},{5,9},{6,10},{7,11},{8,12},{9,13},{1... | collective-permute-start | bytes 589832 | tf_op jit(solution)/shard_map/ppermute | solution.py:19
  36.5 13.5 %collective-permute-start.9 = (bf16[64,6144]{1,0:T(8,128)(2,1)S(1)}, bf16[64,6144]{1,0:T(8,128)(2,1)S(1)}, u32[]{:S(2)}, u32[]{:S(2)}) collective-permute-start(bf16[64,6144]{1,0:T(8,128)(2,1)S(1)} %pad_maximum_fusion), channel_id=1, source_target_pairs={{0,4},{1,5},{2,6},{3,7},{4,8},{5,9},{6,10},{7,11},{8,12},{9,13},{1... | collective-permute-start | bytes 2359304 | tf_op jit(solution)/shard_map/ppermute | solution.py:19
  41.2 4.2 %copy-start = (bf16[896,6144]{1,0:T(8,128)(2,1)}, bf16[896,6144]{1,0:T(8,128)(2,1)S(1)}, u32[]{:S(2)}) copy-start(bf16[896,6144]{1,0:T(8,128)(2,1)S(1)} %get-tuple-element.51.down_w) | copy-start | bytes 33030148
  49.9 4.1 %copy-start.1 = (bf16[896,6144]{1,0:T(8,128)(2,1)S(1)}, bf16[896,6144]{1,0:T(8,128)(2,1)}, u32[]{:S(2)}) copy-start(bf16[896,6144]{1,0:T(8,128)(2,1)} %copy-done) | copy-start | bytes 33030148
  60.6 15.1 %collective-permute-start.10 = (bf16[64,6144]{1,0:T(8,128)(2,1)S(1)}, bf16[64,6144]{1,0:T(8,128)(2,1)S(1)}, u32[]{:S(2)}, u32[]{:S(2)}) collective-permute-start(bf16[64,6144]{1,0:T(8,128)(2,1)S(1)} %shard_map.62), channel_id=1, source_target_pairs={{0,12},{1,13},{2,14},{3,15},{4,0},{5,1},{6,2},{7,3},{8,4},{9,5},{1... | collective-permute-start | bytes 2359304 | tf_op jit(solution)/shard_map/ppermute | solution.py:19
  62.4 4.1 %copy-start.2 = (bf16[896,6144]{1,0:T(8,128)(2,1)S(1)}, bf16[896,6144]{1,0:T(8,128)(2,1)}, u32[]{:S(2)}) copy-start(bf16[896,6144]{1,0:T(8,128)(2,1)} %copy-done) | copy-start | bytes 33030148
  70.1 32.6 %copy-start.3 = (bf16[16,6144]{1,0:T(8,128)(2,1)S(1)}, bf16[16,6144]{1,0:T(8,128)(2,1)}, u32[]{:S(2)}) copy-start(bf16[16,6144]{1,0:T(8,128)(2,1)} %rows_ref.1) | copy-start | bytes 589828
  70.2 8.5 %collective-permute-start.16 = (bf16[16,6144]{1,0:T(8,128)(2,1)S(1)}, bf16[16,6144]{1,0:T(8,128)(2,1)S(1)}, u32[]{:S(2)}, u32[]{:S(2)}) collective-permute-start(bf16[16,6144]{1,0:T(8,128)(2,1)S(1)} %get-tuple-element.61), channel_id=1, source_target_pairs={{0,4},{1,5},{2,6},{3,7},{4,8},{5,9},{6,10},{7,11},{8,12},{9,13},{1... | collective-permute-start | bytes 589832 | tf_op jit(solution)/shard_map/ppermute | solution.py:19
  70.5 17.7 %collective-permute-start.12 = (bf16[32,6144]{1,0:T(8,128)(2,1)S(1)}, bf16[32,6144]{1,0:T(8,128)(2,1)S(1)}, u32[]{:S(2)}, u32[]{:S(2)}) collective-permute-start(bf16[32,6144]{1,0:T(8,128)(2,1)S(1)} %get-tuple-element.56), channel_id=1, source_target_pairs={{0,4},{1,5},{2,6},{3,7},{4,8},{5,9},{6,10},{7,11},{8,12},{9,13},{1... | collective-permute-start | bytes 1179656 | tf_op jit(solution)/shard_map/ppermute | solution.py:19
  75.8 5.7 %collective-permute-start.15 = (bf16[16,6144]{1,0:T(8,128)(2,1)S(1)}, bf16[16,6144]{1,0:T(8,128)(2,1)S(1)}, u32[]{:S(2)}, u32[]{:S(2)}) collective-permute-start(bf16[16,6144]{1,0:T(8,128)(2,1)S(1)} %get-tuple-element.65), channel_id=1, source_target_pairs={{0,12},{1,13},{2,14},{3,15},{4,0},{5,1},{6,2},{7,3},{8,4},{9,5},{1... | collective-permute-start | bytes 589832 | tf_op jit(solution)/shard_map/ppermute | solution.py:19
  77.2 11.0 %collective-permute-start.11 = (bf16[32,6144]{1,0:T(8,128)(2,1)S(1)}, bf16[32,6144]{1,0:T(8,128)(2,1)S(1)}, u32[]{:S(2)}, u32[]{:S(2)}) collective-permute-start(bf16[32,6144]{1,0:T(8,128)(2,1)S(1)} %add_convert_fusion.1), channel_id=1, source_target_pairs={{0,12},{1,13},{2,14},{3,15},{4,0},{5,1},{6,2},{7,3},{8,4},{9,5},{1... | collective-permute-start | bytes 1179656 | tf_op jit(solution)/shard_map/ppermute | solution.py:19
  81.6 15.7 %collective-permute-start.17 = (bf16[16,6144]{1,0:T(8,128)(2,1)S(1)}, bf16[16,6144]{1,0:T(8,128)(2,1)S(1)}, u32[]{:S(2)}, u32[]{:S(2)}) collective-permute-start(bf16[16,6144]{1,0:T(8,128)(2,1)S(1)} %add_convert_fusion.3), channel_id=1, source_target_pairs={{0,2},{1,3},{2,0},{3,1},{4,6},{5,7},{6,4},{7,5},{8,10},{9,11},{10,... | collective-permute-start | bytes 589832 | tf_op jit(solution)/shard_map/ppermute | solution.py:19
  88.4 13.8 %collective-permute-start.18 = (bf16[16,6144]{1,0:T(8,128)(2,1)S(1)}, bf16[16,6144]{1,0:T(8,128)(2,1)S(1)}, u32[]{:S(2)}, u32[]{:S(2)}) collective-permute-start(bf16[16,6144]{1,0:T(8,128)(2,1)S(1)} %get-tuple-element.67), channel_id=1, source_target_pairs={{0,1},{1,2},{2,3},{3,0},{4,5},{5,6},{6,7},{7,4},{8,9},{9,10},{10,1... | collective-permute-start | bytes 589832 | tf_op jit(solution)/shard_map/ppermute | solution.py:19
  89.6 13.1 %collective-permute-start.19 = (bf16[16,6144]{1,0:T(8,128)(2,1)S(1)}, bf16[16,6144]{1,0:T(8,128)(2,1)S(1)}, u32[]{:S(2)}, u32[]{:S(2)}) collective-permute-start(bf16[16,6144]{1,0:T(8,128)(2,1)S(1)} %get-tuple-element.68), channel_id=1, source_target_pairs={{0,3},{1,0},{2,1},{3,2},{4,7},{5,4},{6,5},{7,6},{8,11},{9,8},{10,9... | collective-permute-start | bytes 589832 | tf_op jit(solution)/shard_map/ppermute | solution.py:19
  92.6 10.2 %collective-permute-start.13 = (bf16[16,6144]{1,0:T(8,128)(2,1)S(1)}, bf16[16,6144]{1,0:T(8,128)(2,1)S(1)}, u32[]{:S(2)}, u32[]{:S(2)}) collective-permute-start(bf16[16,6144]{1,0:T(8,128)(2,1)S(1)} %get-tuple-element.57), channel_id=1, source_target_pairs={{0,12},{1,13},{2,14},{3,15},{4,0},{5,1},{6,2},{7,3},{8,4},{9,5},{1... | collective-permute-start | bytes 589832 | tf_op jit(solution)/shard_map/ppermute | solution.py:19
  93.8 8.9 %collective-permute-start.14 = (bf16[16,6144]{1,0:T(8,128)(2,1)S(1)}, bf16[16,6144]{1,0:T(8,128)(2,1)S(1)}, u32[]{:S(2)}, u32[]{:S(2)}) collective-permute-start(bf16[16,6144]{1,0:T(8,128)(2,1)S(1)} %get-tuple-element.58), channel_id=1, source_target_pairs={{0,4},{1,5},{2,6},{3,7},{4,8},{5,9},{6,10},{7,11},{8,12},{9,13},{1... | collective-permute-start | bytes 589832 | tf_op jit(solution)/shard_map/ppermute | solution.py:19

commit v8 on v6

--- a/solution.py
+++ b/solution.py
@@ -9,12 +9,14 @@
 
 
 def shift(block, dx, dz):
-    pairs = [
-        (x * SIDE + z, (x + dx) % SIDE * SIDE + (z + dz) % SIDE)
-        for x in range(SIDE)
-        for z in range(SIDE)
-    ]
-    return lax.ppermute(block, "tensor", pairs)
+    pairs = []
+    for part in range(lax.axis_size("dp")):
+        way = 1 - 2 * (part % 2)
+        for x in range(SIDE):
+            for z in range(SIDE):
+                there = (x + dx) % SIDE * SIDE + (z + way * dz) % SIDE
+                pairs.append((part * SIDE**2 + x * SIDE + z, part * SIDE**2 + there))
+    return lax.ppermute(block, ("dp", "tensor"), pairs)
 
 
 def b16(v):
@@ -176,12 +178,12 @@
     h = d // 2
     below, above = lax.optimization_barrier((shift(own, 0, 1), shift(own, 0, -1)))
     own_l, own_r = shift(own, 1, 0), shift(own, -1, 0)
-    below_2, above_2 = shift(below[:, :h], 0, 1), shift(above[:, h:], 0, -1)
+    far = shift(below, 0, 1)
     near, own_l, own_r, gate_v, up_v, up_weight = lax.optimization_barrier(
         (jnp.concatenate([below, above], 0), own_l, own_r, fetched(gate_weight), fetched(up_weight, 0, 2), up_weight)
     )
     near_l, near_r = shift(near, 1, 0), shift(near, -1, 0)
-    far, up_v2 = lax.optimization_barrier((jnp.concatenate([below_2, above_2], 1), fetched(up_weight, 1, 2)))
+    far, up_v2 = lax.optimization_barrier((far, fetched(up_weight, 1, 2)))
     weights = gate_v, up_v, up_v2
     (early,) = hidden_units((own, own_l, own_r, below, above, far), weights)
     far_l, far_r = lax.optimization_barrier((shift(far, 1, 0), shift(far, -1, 0)))

time: 96.5 us -> 94.1 us (0.975)
  starting transfers between devices: 49.3 us -> 41 us
  waiting for transfers between devices: 16 us -> 22.2 us
    ppermute x25 -> x24, starting transfers between devices: 49.3 us -> 41 us  [shift(): return lax.ppermute(block, ('dp', 'tensor'), pairs)]
    ppermute x25 -> x24, waiting for transfers between devices: 16 us -> 22.2 us  [shift(): return lax.ppermute(block, ('dp', 'tensor'), pairs)]
  transfers between devices with their start and end apart: 25 -> 24, of which waited for: 11 -> 9; matrix products, arithmetic and copies ran while one was open for 1% -> 1% of each run, Pallas kernels for 22% -> 22%
where the time goes in v8:
time: 94.1 us; the launch traced here: 93.4 us
  starting transfers between devices  41 us (44%)
  Pallas kernels  28.3 us (30%)
  waiting for transfers between devices  22.2 us (24%)
  other arithmetic  1.38 us (1%)
    ppermute x24, starting transfers between devices, shift(): return lax.ppermute(block, ('dp', 'tensor'), pairs)  41 us
    ppermute x24, waiting for transfers between devices, shift(): return lax.ppermute(block, ('dp', 'tensor'), pairs)  22.2 us
    pallas_call x3, Pallas kernels, fetched(): pl.pallas_call(kernel, out_shape=pltpu.VMEM((size, weight.shape[1]), weig...  9.28 us
    pallas_call x2, Pallas kernels, hidden_units(): pl.pallas_call(kernel, out_shape=[pltpu.VMEM((tall, ff), b)] + [pltpu.VME...  7.79 us
    pallas_call x1, Pallas kernels, two_hops(): pl.pallas_call(kernel, out_shape=[pltpu.VMEM((n, 2 * d), b)] * 2, in_spec...  6.52 us
    pallas_call x1, Pallas kernels, other_terms(): pl.pallas_call(kernel, out_shape=[pltpu.VMEM((k * n, d), jnp.float32) for...  3.56 us
  transfers between devices with their start and end apart: 24, of which 9 were waited for; matrix products, arithmetic and copies ran while one was open for 1% of the time, Pallas kernels for 22%

profile of v8, /device:TPU:8, one launch (start us, length us, event | category | flops | bytes accessed | tf_op | source)
XLA Modules:
  0.0 93.4 jit_solution(14416160609597582224)
XLA Ops:
  0.0 1.1 %shard_map.55.refs_0_ = bf16[16,6144]{1,0:T(8,128)(2,1)S(1)} custom-call(bf16[16,6144]{1,0:T(8,128)(2,1)} %rows_ref.1, f32[1,6144]{1,0:T(1,128)} %bitcast.1), custom_call_target="tpu_custom_call" | custom-call | tf_op jit(solution)/shard_map/pallas_call | solution.py:37
  1.1 3.3 %collective-permute-start = (bf16[16,6144]{1,0:T(8,128)(2,1)S(1)}, bf16[16,6144]{1,0:T(8,128)(2,1)S(1)}, u32[]{:S(2)}, u32[]{:S(2)}) collective-permute-start(bf16[16,6144]{1,0:T(8,128)(2,1)S(1)} %shard_map.55.refs_0_), channel_id=1, source_target_pairs={{0,1},{1,2},{2,3},{3,0},{4,5},{5,6},{6,7},{7,4},{8,9},{9,10},{10,1... | collective-permute-start | bytes 589832 | tf_op jit(solution)/shard_map/ppermute | solution.py:19
  4.5 3.1 %collective-permute-start.1 = (bf16[16,6144]{1,0:T(8,128)(2,1)S(1)}, bf16[16,6144]{1,0:T(8,128)(2,1)S(1)}, u32[]{:S(2)}, u32[]{:S(2)}) collective-permute-start(bf16[16,6144]{1,0:T(8,128)(2,1)S(1)} %shard_map.55.refs_0_), channel_id=1, source_target_pairs={{0,3},{1,0},{2,1},{3,2},{4,7},{5,4},{6,5},{7,6},{8,11},{9,8},{10,9... | collective-permute-start | bytes 589832 | tf_op jit(solution)/shard_map/ppermute | solution.py:19
  7.6 1.5 %collective-permute-start.2 = (bf16[16,6144]{1,0:T(8,128)(2,1)S(1)}, bf16[16,6144]{1,0:T(8,128)(2,1)S(1)}, u32[]{:S(2)}, u32[]{:S(2)}) collective-permute-start(bf16[16,6144]{1,0:T(8,128)(2,1)S(1)} %shard_map.55.refs_0_), channel_id=1, source_target_pairs={{0,4},{1,5},{2,6},{3,7},{4,8},{5,9},{6,10},{7,11},{8,12},{9,13},{1... | collective-permute-start | bytes 589832 | tf_op jit(solution)/shard_map/ppermute | solution.py:19
  9.1 1.7 %collective-permute-start.3 = (bf16[16,6144]{1,0:T(8,128)(2,1)S(1)}, bf16[16,6144]{1,0:T(8,128)(2,1)S(1)}, u32[]{:S(2)}, u32[]{:S(2)}) collective-permute-start(bf16[16,6144]{1,0:T(8,128)(2,1)S(1)} %shard_map.55.refs_0_), channel_id=1, source_target_pairs={{0,12},{1,13},{2,14},{3,15},{4,0},{5,1},{6,2},{7,3},{8,4},{9,5},{1... | collective-permute-start | bytes 589832 | tf_op jit(solution)/shard_map/ppermute | solution.py:19
  10.8 4.1 %shard_map.56.refs_6_.refs_4_.gate_w = bf16[6144,896]{1,0:T(8,128)(2,1)S(1)} custom-call(bf16[6144,896]{1,0:T(8,128)(2,1)} %source.2), custom_call_target="tpu_custom_call" | custom-call | bytes 11010048 | tf_op jit(solution)/shard_map/pallas_call | solution.py:165
  15.0 2.6 %shard_map.57.refs_7_.refs_5_.up_w = bf16[3072,896]{1,0:T(8,128)(2,1)S(1)} custom-call(bf16[6144,896]{1,0:T(8,128)(2,1)} %source.4), custom_call_target="tpu_custom_call" | custom-call | bytes 5505024 | tf_op jit(solution)/shard_map/pallas_call | solution.py:165
  17.6 0.0 collective-permute-done.1.refs_4_
  17.6 1.4 %collective-permute-start.6 = (bf16[16,6144]{1,0:T(8,128)(2,1)S(1)}, bf16[16,6144]{1,0:T(8,128)(2,1)S(1)}, u32[]{:S(2)}, u32[]{:S(2)}) collective-permute-start(bf16[16,6144]{1,0:T(8,128)(2,1)S(1)} %collective-permute-done.refs_3_), channel_id=1, source_target_pairs={{0,1},{1,2},{2,3},{3,0},{4,5},{5,6},{6,7},{7,4},{8,9},{9,10},{10,1... | collective-permute-start | bytes 589832 | tf_op jit(solution)/shard_map/ppermute | solution.py:19
  19.0 0.0 collective-permute-done.2.refs_1_
  19.1 0.0 collective-permute-done.3.refs_2_
  19.1 1.3 %collective-permute-start.4 = (bf16[32,6144]{1,0:T(8,128)(2,1)S(1)}, bf16[32,6144]{1,0:T(8,128)(2,1)S(1)}, u32[]{:S(2)}, u32[]{:S(2)}) collective-permute-start(bf16[32,6144]{1,0:T(8,128)(2,1)S(1)} %pad_maximum_fusion), channel_id=1, source_target_pairs={{0,4},{1,5},{2,6},{3,7},{4,8},{5,9},{6,10},{7,11},{8,12},{9,13},{1... | collective-permute-start | bytes 1179656 | tf_op jit(solution)/shard_map/ppermute | solution.py:19
  20.4 2.0 %collective-permute-start.5 = (bf16[32,6144]{1,0:T(8,128)(2,1)S(1)}, bf16[32,6144]{1,0:T(8,128)(2,1)S(1)}, u32[]{:S(2)}, u32[]{:S(2)}) collective-permute-start(bf16[32,6144]{1,0:T(8,128)(2,1)S(1)} %pad_maximum_fusion), channel_id=1, source_target_pairs={{0,12},{1,13},{2,14},{3,15},{4,0},{5,1},{6,2},{7,3},{8,4},{9,5},{1... | collective-permute-start | bytes 1179656 | tf_op jit(solution)/shard_map/ppermute | solution.py:19
  22.4 2.6 %shard_map.58.refs_8_.refs_6_.up_w2 = bf16[3072,896]{1,0:T(8,128)(2,1)S(1)} custom-call(bf16[6144,896]{1,0:T(8,128)(2,1)} %source.4), custom_call_target="tpu_custom_call" | custom-call | bytes 5505024 | tf_op jit(solution)/shard_map/pallas_call | solution.py:165
  25.0 1.0 %collective-permute-done.6.refs_5_ = bf16[16,6144]{1,0:T(8,128)(2,1)S(1)} collective-permute-done((bf16[16,6144]{1,0:T(8,128)(2,1)S(1)}, bf16[16,6144]{1,0:T(8,128)(2,1)S(1)}, u32[]{:S(2)}, u32[]{:S(2)}) %collective-permute-start.6) | collective-permute-done | bytes 196640 | tf_op jit(solution)/shard_map/ppermute | solution.py:19
  26.0 0.7 collective-permute-start.7
  26.7 2.5 %collective-permute-start.8 = (bf16[16,6144]{1,0:T(8,128)(2,1)S(1)}, bf16[16,6144]{1,0:T(8,128)(2,1)S(1)}, u32[]{:S(2)}, u32[]{:S(2)}) collective-permute-start(bf16[16,6144]{1,0:T(8,128)(2,1)S(1)} %collective-permute-done.6.refs_5_), channel_id=1, source_target_pairs={{0,12},{1,13},{2,14},{3,15},{4,0},{5,1},{6,2},{7,3},{8,4},{9,5},{1... | collective-permute-start | bytes 589832 | tf_op jit(solution)/shard_map/ppermute | solution.py:19
  29.2 3.6 %shard_map.59.early = bf16[96,896]{1,0:T(8,128)(2,1)S(1)} custom-call(bf16[16,6144]{1,0:T(8,128)(2,1)S(1)} %shard_map.55.refs_0_, bf16[16,6144]{1,0:T(8,128)(2,1)S(1)} %collective-permute-done.2.refs_1_, bf16[16,6144]{1,0:T(8,128)(2,1)S(1)} %collective-permute-done.3.refs_2_, bf16[16,6144]{1,0:T(8,128)(2,1)S(1)} %collective-permute-done.refs_3_, ...), custom_call_target="tpu_custom_call" | custom-call | flops 2113929216 | tf_op jit(solution)/shard_map/pallas_call | solution.py:80
  32.9 2.8 %collective-permute-start.10 = (bf16[16,9216]{1,0:T(8,128)(2,1)S(1)}, bf16[16,9216]{1,0:T(8,128)(2,1)S(1)}, u32[]{:S(2)}, u32[]{:S(2)}) collective-permute-start(bf16[16,9216]{1,0:T(8,128)(2,1)S(1)} %pad_maximum_fusion.4), channel_id=1, source_target_pairs={{0,12},{1,13},{2,14},{3,15},{4,0},{5,1},{6,2},{7,3},{8,4},{9,5},{1... | collective-permute-start | bytes 884744 | tf_op jit(solution)/shard_map/ppermute | solution.py:19
  35.7 0.1 collective-permute-start.9
  35.8 0.4 collective-permute-done.7.refs_2_
  36.3 0.0 collective-permute-done.8.refs_3_
  36.3 1.7 %collective-permute-start.11 = (bf16[16,3072]{1,0:T(8,128)(2,1)S(1)}, bf16[16,3072]{1,0:T(8,128)(2,1)S(1)}, u32[]{:S(2)}, u32[]{:S(2)}) collective-permute-start(bf16[16,3072]{1,0:T(8,128)(2,1)S(1)} %slice.89), channel_id=1, source_target_pairs={{0,4},{1,5},{2,6},{3,7},{4,8},{5,9},{6,10},{7,11},{8,12},{9,13},{1... | collective-permute-start | bytes 294920 | tf_op jit(solution)/shard_map/ppermute | solution.py:19
  38.1 2.1 %collective-permute-start.12 = (bf16[16,3072]{1,0:T(8,128)(2,1)S(1)}, bf16[16,3072]{1,0:T(8,128)(2,1)S(1)}, u32[]{:S(2)}, u32[]{:S(2)}) collective-permute-start(bf16[16,3072]{1,0:T(8,128)(2,1)S(1)} %slice.90), channel_id=1, source_target_pairs={{0,12},{1,13},{2,14},{3,15},{4,0},{5,1},{6,2},{7,3},{8,4},{9,5},{1... | collective-permute-start | bytes 294920 | tf_op jit(solution)/shard_map/ppermute | solution.py:19
  40.2 4.1 %shard_map.60 = (bf16[96,896]{1,0:T(8,128)(2,1)S(1)}, bf16[896,6144]{1,0:T(8,128)(2,1)S(1)}) custom-call(bf16[32,6144]{1,0:T(8,128)(2,1)S(1)} %collective-permute-done.4.refs_0_, bf16[32,6144]{1,0:T(8,128)(2,1)S(1)} %collective-permute-done.5.refs_1_, bf16[16,6144]{1,0:T(8,128)(2,1)S(1)} %collective-permute-done.7.refs_2_, ...), custom_call_target="tpu_custom_call" | custom-call | flops 2113929216 | bytes 11010048 | tf_op jit(solution)/shard_map/pallas_call | solution.py:80
  44.3 3.6 %collective-permute-done.11.far_up = bf16[16,3072]{1,0:T(8,128)(2,1)S(1)} collective-permute-done((bf16[16,3072]{1,0:T(8,128)(2,1)S(1)}, bf16[16,3072]{1,0:T(8,128)(2,1)S(1)}, u32[]{:S(2)}, u32[]{:S(2)}) %collective-permute-start.11) | collective-permute-done | bytes 98336 | tf_op jit(solution)/shard_map/ppermute | solution.py:19
  47.9 6.5 %shard_map.62 = (bf16[16,12288]{1,0:T(8,128)(2,1)S(1)}, bf16[16,12288]{1,0:T(8,128)(2,1)S(1)}) custom-call(bf16[16,9216]{1,0:T(8,128)(2,1)S(1)} %collective-permute-done.9.two_up, bf16[16,9216]{1,0:T(8,128)(2,1)S(1)} %collective-permute-done.10.two_down, bf16[16,3072]{1,0:T(8,128)(2,1)S(1)} %collective-permute-done.11.far_up, ...), custom_call_target="tpu_custom_call" | custom-call | flops 2113929216 | tf_op jit(solution)/shard_map/pallas_call | solution.py:116
  54.4 0.1 collective-permute-start.13
  54.5 3.2 %collective-permute-start.14 = (bf16[16,12288]{1,0:T(8,128)(2,1)S(1)}, bf16[16,12288]{1,0:T(8,128)(2,1)S(1)}, u32[]{:S(2)}, u32[]{:S(2)}) collective-permute-start(bf16[16,12288]{1,0:T(8,128)(2,1)S(1)} %get-tuple-element.59), channel_id=1, source_target_pairs={{0,12},{1,13},{2,14},{3,15},{4,0},{5,1},{6,2},{7,3},{8,4},{9,5},{1... | collective-permute-start | bytes 1179656 | tf_op jit(solution)/shard_map/ppermute | solution.py:19
  57.7 3.6 %shard_map.61 = (f32[16,6144]{1,0:T(8,128)S(1)}, f32[16,6144]{1,0:T(8,128)S(1)}, f32[16,6144]{1,0:T(8,128)S(1)}, f32[32,6144]{1,0:T(8,128)S(1)}, f32[16,6144]{1,...) custom-call(bf16[96,896]{1,0:T(8,128)(2,1)S(1)} %shard_map.59.early,, ...), custom_call_target="tpu_custom_call" | custom-call | flops 2113929216 | tf_op jit(solution)/shard_map/pallas_call | solution.py:146
  61.5 4.2 %collective-permute-done.13 = bf16[16,12288]{1,0:T(8,128)(2,1)S(1)} collective-permute-done((bf16[16,12288]{1,0:T(8,128)(2,1)S(1)}, bf16[16,12288]{1,0:T(8,128)(2,1)S(1)}, u32[]{:S(2)}, u32[]{:S(2)}) %collective-permute-start.13) | collective-permute-done | bytes 393248 | tf_op jit(solution)/shard_map/ppermute | solution.py:19
  65.9 0.1 collective-permute-start.19
  66.0 3.3 %collective-permute-start.20 = (bf16[16,6144]{1,0:T(8,128)(2,1)S(1)}, bf16[16,6144]{1,0:T(8,128)(2,1)S(1)}, u32[]{:S(2)}, u32[]{:S(2)}) collective-permute-start(bf16[16,6144]{1,0:T(8,128)(2,1)S(1)} %pad_maximum_fusion.8), channel_id=1, source_target_pairs={{0,12},{1,13},{2,14},{3,15},{4,0},{5,1},{6,2},{7,3},{8,4},{9,5},{1... | collective-permute-start | bytes 589832 | tf_op jit(solution)/shard_map/ppermute | solution.py:19
  69.3 1.8 %collective-permute-start.16 = (bf16[32,6144]{1,0:T(8,128)(2,1)S(1)}, bf16[32,6144]{1,0:T(8,128)(2,1)S(1)}, u32[]{:S(2)}, u32[]{:S(2)}) collective-permute-start(bf16[32,6144]{1,0:T(8,128)(2,1)S(1)} %pad_maximum_fusion.2), channel_id=1, source_target_pairs={{0,12},{1,13},{2,14},{3,15},{4,0},{5,1},{6,2},{7,3},{8,4},{9,5},{1... | collective-permute-start | bytes 1179656 | tf_op jit(solution)/shard_map/ppermute | solution.py:19
  71.2 0.6 collective-permute-start.15
  71.8 1.6 %collective-permute-done.19 = bf16[16,6144]{1,0:T(8,128)(2,1)S(1)} collective-permute-done((bf16[16,6144]{1,0:T(8,128)(2,1)S(1)}, bf16[16,6144]{1,0:T(8,128)(2,1)S(1)}, u32[]{:S(2)}, u32[]{:S(2)}) %collective-permute-start.19) | collective-permute-done | bytes 196640 | tf_op jit(solution)/shard_map/ppermute | solution.py:19
  73.5 1.2 %collective-permute-done.20 = bf16[16,6144]{1,0:T(8,128)(2,1)S(1)} collective-permute-done((bf16[16,6144]{1,0:T(8,128)(2,1)S(1)}, bf16[16,6144]{1,0:T(8,128)(2,1)S(1)}, u32[]{:S(2)}, u32[]{:S(2)}) %collective-permute-start.20) | collective-permute-done | bytes 196640 | tf_op jit(solution)/shard_map/ppermute | solution.py:19
  74.7 0.1 add_convert_fusion.2
  74.7 0.1 collective-permute-start.21
  74.8 5.2 %collective-permute-done.16 = bf16[32,6144]{1,0:T(8,128)(2,1)S(1)} collective-permute-done((bf16[32,6144]{1,0:T(8,128)(2,1)S(1)}, bf16[32,6144]{1,0:T(8,128)(2,1)S(1)}, u32[]{:S(2)}, u32[]{:S(2)}) %collective-permute-start.16) | collective-permute-done | bytes 393248 | tf_op jit(solution)/shard_map/ppermute | solution.py:19
  80.0 1.3 %collective-permute-done.15 = bf16[32,6144]{1,0:T(8,128)(2,1)S(1)} collective-permute-done((bf16[32,6144]{1,0:T(8,128)(2,1)S(1)}, bf16[32,6144]{1,0:T(8,128)(2,1)S(1)}, u32[]{:S(2)}, u32[]{:S(2)}) %collective-permute-start.15) | collective-permute-done | bytes 393248 | tf_op jit(solution)/shard_map/ppermute | solution.py:19
  81.3 0.1 add_convert_fusion
  81.5 0.1 collective-permute-start.22
  81.5 4.1 %collective-permute-start.23 = (bf16[16,6144]{1,0:T(8,128)(2,1)S(1)}, bf16[16,6144]{1,0:T(8,128)(2,1)S(1)}, u32[]{:S(2)}, u32[]{:S(2)}) collective-permute-start(bf16[16,6144]{1,0:T(8,128)(2,1)S(1)} %get-tuple-element.78), channel_id=1, source_target_pairs={{0,3},{1,0},{2,1},{3,2},{4,7},{5,4},{6,5},{7,6},{8,11},{9,8},{10,9... | collective-permute-start | bytes 589832 | tf_op jit(solution)/shard_map/ppermute | solution.py:19
  85.7 0.1 collective-permute-start.17
  85.8 3.1 %collective-permute-start.18 = (bf16[16,6144]{1,0:T(8,128)(2,1)S(1)}, bf16[16,6144]{1,0:T(8,128)(2,1)S(1)}, u32[]{:S(2)}, u32[]{:S(2)}) collective-permute-start(bf16[16,6144]{1,0:T(8,128)(2,1)S(1)} %pad_maximum_fusion.6), channel_id=1, source_target_pairs={{0,12},{1,13},{2,14},{3,15},{4,0},{5,1},{6,2},{7,3},{8,4},{9,5},{1... | collective-permute-start | bytes 589832 | tf_op jit(solution)/shard_map/ppermute | solution.py:19
  88.9 3.6 %collective-permute-done.22 = bf16[16,6144]{1,0:T(8,128)(2,1)S(1)} collective-permute-done((bf16[16,6144]{1,0:T(8,128)(2,1)S(1)}, bf16[16,6144]{1,0:T(8,128)(2,1)S(1)}, u32[]{:S(2)}, u32[]{:S(2)}) %collective-permute-start.22) | collective-permute-done | bytes 196640 | tf_op jit(solution)/shard_map/ppermute | solution.py:19
  92.6 0.8 add_convert_fusion.1
  (39 shorter events, 0.6 us)
Async XLA Ops:
  1.1 16.4 %collective-permute-start = (bf16[16,6144]{1,0:T(8,128)(2,1)S(1)}, bf16[16,6144]{1,0:T(8,128)(2,1)S(1)}, u32[]{:S(2)}, u32[]{:S(2)}) collective-permute-start(bf16[16,6144]{1,0:T(8,128)(2,1)S(1)} %shard_map.55.refs_0_), channel_id=1, source_target_pairs={{0,1},{1,2},{2,3},{3,0},{4,5},{5,6},{6,7},{7,4},{8,9},{9,10},{10,1... | collective-permute-start | bytes 589832 | tf_op jit(solution)/shard_map/ppermute | solution.py:19
  4.5 13.1 %collective-permute-start.1 = (bf16[16,6144]{1,0:T(8,128)(2,1)S(1)}, bf16[16,6144]{1,0:T(8,128)(2,1)S(1)}, u32[]{:S(2)}, u32[]{:S(2)}) collective-permute-start(bf16[16,6144]{1,0:T(8,128)(2,1)S(1)} %shard_map.55.refs_0_), channel_id=1, source_target_pairs={{0,3},{1,0},{2,1},{3,2},{4,7},{5,4},{6,5},{7,6},{8,11},{9,8},{10,9... | collective-permute-start | bytes 589832 | tf_op jit(solution)/shard_map/ppermute | solution.py:19
  7.6 11.5 %collective-permute-start.2 = (bf16[16,6144]{1,0:T(8,128)(2,1)S(1)}, bf16[16,6144]{1,0:T(8,128)(2,1)S(1)}, u32[]{:S(2)}, u32[]{:S(2)}) collective-permute-start(bf16[16,6144]{1,0:T(8,128)(2,1)S(1)} %shard_map.55.refs_0_), channel_id=1, source_target_pairs={{0,4},{1,5},{2,6},{3,7},{4,8},{5,9},{6,10},{7,11},{8,12},{9,13},{1... | collective-permute-start | bytes 589832 | tf_op jit(solution)/shard_map/ppermute | solution.py:19
  9.1 10.0 %collective-permute-start.3 = (bf16[16,6144]{1,0:T(8,128)(2,1)S(1)}, bf16[16,6144]{1,0:T(8,128)(2,1)S(1)}, u32[]{:S(2)}, u32[]{:S(2)}) collective-permute-start(bf16[16,6144]{1,0:T(8,128)(2,1)S(1)} %shard_map.55.refs_0_), channel_id=1, source_target_pairs={{0,12},{1,13},{2,14},{3,15},{4,0},{5,1},{6,2},{7,3},{8,4},{9,5},{1... | collective-permute-start | bytes 589832 | tf_op jit(solution)/shard_map/ppermute | solution.py:19
  17.6 8.4 %collective-permute-start.6 = (bf16[16,6144]{1,0:T(8,128)(2,1)S(1)}, bf16[16,6144]{1,0:T(8,128)(2,1)S(1)}, u32[]{:S(2)}, u32[]{:S(2)}) collective-permute-start(bf16[16,6144]{1,0:T(8,128)(2,1)S(1)} %collective-permute-done.refs_3_), channel_id=1, source_target_pairs={{0,1},{1,2},{2,3},{3,0},{4,5},{5,6},{6,7},{7,4},{8,9},{9,10},{10,1... | collective-permute-start | bytes 589832 | tf_op jit(solution)/shard_map/ppermute | solution.py:19
  19.1 13.8 %collective-permute-start.4 = (bf16[32,6144]{1,0:T(8,128)(2,1)S(1)}, bf16[32,6144]{1,0:T(8,128)(2,1)S(1)}, u32[]{:S(2)}, u32[]{:S(2)}) collective-permute-start(bf16[32,6144]{1,0:T(8,128)(2,1)S(1)} %pad_maximum_fusion), channel_id=1, source_target_pairs={{0,4},{1,5},{2,6},{3,7},{4,8},{5,9},{6,10},{7,11},{8,12},{9,13},{1... | collective-permute-start | bytes 1179656 | tf_op jit(solution)/shard_map/ppermute | solution.py:19
  20.4 12.5 %collective-permute-start.5 = (bf16[32,6144]{1,0:T(8,128)(2,1)S(1)}, bf16[32,6144]{1,0:T(8,128)(2,1)S(1)}, u32[]{:S(2)}, u32[]{:S(2)}) collective-permute-start(bf16[32,6144]{1,0:T(8,128)(2,1)S(1)} %pad_maximum_fusion), channel_id=1, source_target_pairs={{0,12},{1,13},{2,14},{3,15},{4,0},{5,1},{6,2},{7,3},{8,4},{9,5},{1... | collective-permute-start | bytes 1179656 | tf_op jit(solution)/shard_map/ppermute | solution.py:19
  26.0 10.3 %collective-permute-start.7 = (bf16[16,6144]{1,0:T(8,128)(2,1)S(1)}, bf16[16,6144]{1,0:T(8,128)(2,1)S(1)}, u32[]{:S(2)}, u32[]{:S(2)}) collective-permute-start(bf16[16,6144]{1,0:T(8,128)(2,1)S(1)} %collective-permute-done.6.refs_5_), channel_id=1, source_target_pairs={{0,4},{1,5},{2,6},{3,7},{4,8},{5,9},{6,10},{7,11},{8,12},{9,13},{1... | collective-permute-start | bytes 589832 | tf_op jit(solution)/shard_map/ppermute | solution.py:19
  26.7 9.6 %collective-permute-start.8 = (bf16[16,6144]{1,0:T(8,128)(2,1)S(1)}, bf16[16,6144]{1,0:T(8,128)(2,1)S(1)}, u32[]{:S(2)}, u32[]{:S(2)}) collective-permute-start(bf16[16,6144]{1,0:T(8,128)(2,1)S(1)} %collective-permute-done.6.refs_5_), channel_id=1, source_target_pairs={{0,12},{1,13},{2,14},{3,15},{4,0},{5,1},{6,2},{7,3},{8,4},{9,5},{1... | collective-permute-start | bytes 589832 | tf_op jit(solution)/shard_map/ppermute | solution.py:19
  32.9 15.0 %collective-permute-start.10 = (bf16[16,9216]{1,0:T(8,128)(2,1)S(1)}, bf16[16,9216]{1,0:T(8,128)(2,1)S(1)}, u32[]{:S(2)}, u32[]{:S(2)}) collective-permute-start(bf16[16,9216]{1,0:T(8,128)(2,1)S(1)} %pad_maximum_fusion.4), channel_id=1, source_target_pairs={{0,12},{1,13},{2,14},{3,15},{4,0},{5,1},{6,2},{7,3},{8,4},{9,5},{1... | collective-permute-start | bytes 884744 | tf_op jit(solution)/shard_map/ppermute | solution.py:19
  35.7 12.2 %collective-permute-start.9 = (bf16[16,9216]{1,0:T(8,128)(2,1)S(1)}, bf16[16,9216]{1,0:T(8,128)(2,1)S(1)}, u32[]{:S(2)}, u32[]{:S(2)}) collective-permute-start(bf16[16,9216]{1,0:T(8,128)(2,1)S(1)} %pad_maximum_fusion.3), channel_id=1, source_target_pairs={{0,4},{1,5},{2,6},{3,7},{4,8},{5,9},{6,10},{7,11},{8,12},{9,13},{1... | collective-permute-start | bytes 884744 | tf_op jit(solution)/shard_map/ppermute | solution.py:19
  36.3 11.6 %collective-permute-start.11 = (bf16[16,3072]{1,0:T(8,128)(2,1)S(1)}, bf16[16,3072]{1,0:T(8,128)(2,1)S(1)}, u32[]{:S(2)}, u32[]{:S(2)}) collective-permute-start(bf16[16,3072]{1,0:T(8,128)(2,1)S(1)} %slice.89), channel_id=1, source_target_pairs={{0,4},{1,5},{2,6},{3,7},{4,8},{5,9},{6,10},{7,11},{8,12},{9,13},{1... | collective-permute-start | bytes 294920 | tf_op jit(solution)/shard_map/ppermute | solution.py:19
  38.1 9.8 %collective-permute-start.12 = (bf16[16,3072]{1,0:T(8,128)(2,1)S(1)}, bf16[16,3072]{1,0:T(8,128)(2,1)S(1)}, u32[]{:S(2)}, u32[]{:S(2)}) collective-permute-start(bf16[16,3072]{1,0:T(8,128)(2,1)S(1)} %slice.90), channel_id=1, source_target_pairs={{0,12},{1,13},{2,14},{3,15},{4,0},{5,1},{6,2},{7,3},{8,4},{9,5},{1... | collective-permute-start | bytes 294920 | tf_op jit(solution)/shard_map/ppermute | solution.py:19
  54.4 11.3 %collective-permute-start.13 = (bf16[16,12288]{1,0:T(8,128)(2,1)S(1)}, bf16[16,12288]{1,0:T(8,128)(2,1)S(1)}, u32[]{:S(2)}, u32[]{:S(2)}) collective-permute-start(bf16[16,12288]{1,0:T(8,128)(2,1)S(1)} %get-tuple-element.58), channel_id=1, source_target_pairs={{0,4},{1,5},{2,6},{3,7},{4,8},{5,9},{6,10},{7,11},{8,12},{9,13},{1... | collective-permute-start | bytes 1179656 | tf_op jit(solution)/shard_map/ppermute | solution.py:19
  54.5 11.2 %collective-permute-start.14 = (bf16[16,12288]{1,0:T(8,128)(2,1)S(1)}, bf16[16,12288]{1,0:T(8,128)(2,1)S(1)}, u32[]{:S(2)}, u32[]{:S(2)}) collective-permute-start(bf16[16,12288]{1,0:T(8,128)(2,1)S(1)} %get-tuple-element.59), channel_id=1, source_target_pairs={{0,12},{1,13},{2,14},{3,15},{4,0},{5,1},{6,2},{7,3},{8,4},{9,5},{1... | collective-permute-start | bytes 1179656 | tf_op jit(solution)/shard_map/ppermute | solution.py:19
  57.7 34.8 %copy-start = (bf16[16,6144]{1,0:T(8,128)(2,1)S(1)}, bf16[16,6144]{1,0:T(8,128)(2,1)}, u32[]{:S(2)}) copy-start(bf16[16,6144]{1,0:T(8,128)(2,1)} %rows_ref.1) | copy-start | bytes 589828
  65.9 7.6 %collective-permute-start.19 = (bf16[16,6144]{1,0:T(8,128)(2,1)S(1)}, bf16[16,6144]{1,0:T(8,128)(2,1)S(1)}, u32[]{:S(2)}, u32[]{:S(2)}) collective-permute-start(bf16[16,6144]{1,0:T(8,128)(2,1)S(1)} %pad_maximum_fusion.7), channel_id=1, source_target_pairs={{0,4},{1,5},{2,6},{3,7},{4,8},{5,9},{6,10},{7,11},{8,12},{9,13},{1... | collective-permute-start | bytes 589832 | tf_op jit(solution)/shard_map/ppermute | solution.py:19
  66.0 8.7 %collective-permute-start.20 = (bf16[16,6144]{1,0:T(8,128)(2,1)S(1)}, bf16[16,6144]{1,0:T(8,128)(2,1)S(1)}, u32[]{:S(2)}, u32[]{:S(2)}) collective-permute-start(bf16[16,6144]{1,0:T(8,128)(2,1)S(1)} %pad_maximum_fusion.8), channel_id=1, source_target_pairs={{0,12},{1,13},{2,14},{3,15},{4,0},{5,1},{6,2},{7,3},{8,4},{9,5},{1... | collective-permute-start | bytes 589832 | tf_op jit(solution)/shard_map/ppermute | solution.py:19
  69.3 10.7 %collective-permute-start.16 = (bf16[32,6144]{1,0:T(8,128)(2,1)S(1)}, bf16[32,6144]{1,0:T(8,128)(2,1)S(1)}, u32[]{:S(2)}, u32[]{:S(2)}) collective-permute-start(bf16[32,6144]{1,0:T(8,128)(2,1)S(1)} %pad_maximum_fusion.2), channel_id=1, source_target_pairs={{0,12},{1,13},{2,14},{3,15},{4,0},{5,1},{6,2},{7,3},{8,4},{9,5},{1... | collective-permute-start | bytes 1179656 | tf_op jit(solution)/shard_map/ppermute | solution.py:19
  71.2 10.1 %collective-permute-start.15 = (bf16[32,6144]{1,0:T(8,128)(2,1)S(1)}, bf16[32,6144]{1,0:T(8,128)(2,1)S(1)}, u32[]{:S(2)}, u32[]{:S(2)}) collective-permute-start(bf16[32,6144]{1,0:T(8,128)(2,1)S(1)} %pad_maximum_fusion.1), channel_id=1, source_target_pairs={{0,4},{1,5},{2,6},{3,7},{4,8},{5,9},{6,10},{7,11},{8,12},{9,13},{1... | collective-permute-start | bytes 1179656 | tf_op jit(solution)/shard_map/ppermute | solution.py:19
  74.7 14.2 %collective-permute-start.21 = (bf16[16,6144]{1,0:T(8,128)(2,1)S(1)}, bf16[16,6144]{1,0:T(8,128)(2,1)S(1)}, u32[]{:S(2)}, u32[]{:S(2)}) collective-permute-start(bf16[16,6144]{1,0:T(8,128)(2,1)S(1)} %add_convert_fusion.2), channel_id=1, source_target_pairs={{0,2},{1,3},{2,0},{3,1},{4,6},{5,7},{6,4},{7,5},{8,10},{9,11},{10,... | collective-permute-start | bytes 589832 | tf_op jit(solution)/shard_map/ppermute | solution.py:19
  81.5 11.1 %collective-permute-start.22 = (bf16[16,6144]{1,0:T(8,128)(2,1)S(1)}, bf16[16,6144]{1,0:T(8,128)(2,1)S(1)}, u32[]{:S(2)}, u32[]{:S(2)}) collective-permute-start(bf16[16,6144]{1,0:T(8,128)(2,1)S(1)} %get-tuple-element.77), channel_id=1, source_target_pairs={{0,1},{1,2},{2,3},{3,0},{4,5},{5,6},{6,7},{7,4},{8,9},{9,10},{10,1... | collective-permute-start | bytes 589832 | tf_op jit(solution)/shard_map/ppermute | solution.py:19
  81.5 11.0 %collective-permute-start.23 = (bf16[16,6144]{1,0:T(8,128)(2,1)S(1)}, bf16[16,6144]{1,0:T(8,128)(2,1)S(1)}, u32[]{:S(2)}, u32[]{:S(2)}) collective-permute-start(bf16[16,6144]{1,0:T(8,128)(2,1)S(1)} %get-tuple-element.78), channel_id=1, source_target_pairs={{0,3},{1,0},{2,1},{3,2},{4,7},{5,4},{6,5},{7,6},{8,11},{9,8},{10,9... | collective-permute-start | bytes 589832 | tf_op jit(solution)/shard_map/ppermute | solution.py:19
  85.7 6.9 %collective-permute-start.17 = (bf16[16,6144]{1,0:T(8,128)(2,1)S(1)}, bf16[16,6144]{1,0:T(8,128)(2,1)S(1)}, u32[]{:S(2)}, u32[]{:S(2)}) collective-permute-start(bf16[16,6144]{1,0:T(8,128)(2,1)S(1)} %pad_maximum_fusion.5), channel_id=1, source_target_pairs={{0,4},{1,5},{2,6},{3,7},{4,8},{5,9},{6,10},{7,11},{8,12},{9,13},{1... | collective-permute-start | bytes 589832 | tf_op jit(solution)/shard_map/ppermute | solution.py:19
  85.8 6.8 %collective-permute-start.18 = (bf16[16,6144]{1,0:T(8,128)(2,1)S(1)}, bf16[16,6144]{1,0:T(8,128)(2,1)S(1)}, u32[]{:S(2)}, u32[]{:S(2)}) collective-permute-start(bf16[16,6144]{1,0:T(8,128)(2,1)S(1)} %pad_maximum_fusion.6), channel_id=1, source_target_pairs={{0,12},{1,13},{2,14},{3,15},{4,0},{5,1},{6,2},{7,3},{8,4},{9,5},{1... | collective-permute-start | bytes 589832 | tf_op jit(solution)/shard_map/ppermute | solution.py:19

commit v9 on v8

--- a/solution.py
+++ b/solution.py
@@ -210,11 +210,12 @@
     own_right = jnp.concatenate([b16(own_right[:, :h] + f32(two_up[:, d : d + h])), b16(own_right[:, h:])], 1)
     own_left = jnp.concatenate([b16(own_left[:, :h]), b16(own_left[:, h:] + f32(two_down[:, d : d + h]))], 1)
     own_right, own_left, near_p, near_m = lax.optimization_barrier((own_right, own_left, near_p, near_m))
-    far_sum = shift(b16(far_here + f32(far_p) + f32(far_m)), 0, 2)
+    far_sum = shift(b16(far_here + f32(far_p) + f32(far_m)), 0, -1)
     own_p, own_m = shift(own_right, 1, 0), shift(own_left, -1, 0)
-    near_sum = b16(near_here + f32(near_p) + f32(near_m))
-    from_below, from_above = shift(near_sum[n:], 0, 1), shift(near_sum[:n], 0, -1)
-    return own_here + f32(own_p) + f32(own_m) + f32(far_sum) + f32(from_below) + f32(from_above)
+    near_sum = near_here + f32(near_p) + f32(near_m)
+    from_below = shift(b16(near_sum[n:]), 0, 1)
+    from_above = shift(b16(near_sum[:n] + f32(far_sum)), 0, -1)
+    return own_here + f32(own_p) + f32(own_m) + f32(from_below) + f32(from_above)
 
 
 def on_device(tokens, norm_gain, gate_weight, up_weight, down_weight):

time: 94.1 us -> 102 us (1.084)
  starting transfers between devices: 41 us -> 45.1 us
  waiting for transfers between devices: 22.2 us -> 25.7 us
    ppermute x24, starting transfers between devices: 41 us -> 45.1 us  [shift(): return lax.ppermute(block, ('dp', 'tensor'), pairs)]
    ppermute x24, waiting for transfers between devices: 22.2 us -> 25.7 us  [shift(): return lax.ppermute(block, ('dp', 'tensor'), pairs)]
  transfers between devices with their start and end apart: 24 -> 24, of which waited for: 9 -> 10; matrix products, arithmetic and copies ran while one was open for 1% -> 1% of each run, Pallas kernels for 22% -> 20%
where the time goes in v9:
time: 102 us; the launch traced here: 101 us
  starting transfers between devices  45.1 us (44%)
  Pallas kernels  28.3 us (28%)
  waiting for transfers between devices  25.7 us (25%)
  other arithmetic  1.37 us (1%)
    ppermute x24, starting transfers between devices, shift(): return lax.ppermute(block, ('dp', 'tensor'), pairs)  45.1 us
    ppermute x24, waiting for transfers between devices, shift(): return lax.ppermute(block, ('dp', 'tensor'), pairs)  25.7 us
    pallas_call x3, Pallas kernels, fetched(): pl.pallas_call(kernel, out_shape=pltpu.VMEM((size, weight.shape[1]), weig...  9.28 us
    pallas_call x2, Pallas kernels, hidden_units(): pl.pallas_call(kernel, out_shape=[pltpu.VMEM((tall, ff), b)] + [pltpu.VME...  7.79 us
    pallas_call x1, Pallas kernels, two_hops(): pl.pallas_call(kernel, out_shape=[pltpu.VMEM((n, 2 * d), b)] * 2, in_spec...  6.52 us
    pallas_call x1, Pallas kernels, other_terms(): pl.pallas_call(kernel, out_shape=[pltpu.VMEM((k * n, d), jnp.float32) for...  3.56 us
  transfers between devices with their start and end apart: 24, of which 10 were waited for; matrix products, arithmetic and copies ran while one was open for 1% of the time, Pallas kernels for 20%

profile of v9, /device:TPU:8, one launch (start us, length us, event | category | flops | bytes accessed | tf_op | source)
XLA Modules:
  0.0 100.9 jit_solution(11920541341599486009)
XLA Ops:
  0.0 1.1 %shard_map.55.refs_0_ = bf16[16,6144]{1,0:T(8,128)(2,1)S(1)} custom-call(bf16[16,6144]{1,0:T(8,128)(2,1)} %rows_ref.1, f32[1,6144]{1,0:T(1,128)} %bitcast.1), custom_call_target="tpu_custom_call" | custom-call | tf_op jit(solution)/shard_map/pallas_call | solution.py:37
  1.1 3.3 %collective-permute-start = (bf16[16,6144]{1,0:T(8,128)(2,1)S(1)}, bf16[16,6144]{1,0:T(8,128)(2,1)S(1)}, u32[]{:S(2)}, u32[]{:S(2)}) collective-permute-start(bf16[16,6144]{1,0:T(8,128)(2,1)S(1)} %shard_map.55.refs_0_), channel_id=1, source_target_pairs={{0,1},{1,2},{2,3},{3,0},{4,5},{5,6},{6,7},{7,4},{8,9},{9,10},{10,1... | collective-permute-start | bytes 589832 | tf_op jit(solution)/shard_map/ppermute | solution.py:19
  4.5 3.1 %collective-permute-start.1 = (bf16[16,6144]{1,0:T(8,128)(2,1)S(1)}, bf16[16,6144]{1,0:T(8,128)(2,1)S(1)}, u32[]{:S(2)}, u32[]{:S(2)}) collective-permute-start(bf16[16,6144]{1,0:T(8,128)(2,1)S(1)} %shard_map.55.refs_0_), channel_id=1, source_target_pairs={{0,3},{1,0},{2,1},{3,2},{4,7},{5,4},{6,5},{7,6},{8,11},{9,8},{10,9... | collective-permute-start | bytes 589832 | tf_op jit(solution)/shard_map/ppermute | solution.py:19
  7.6 1.5 %collective-permute-start.2 = (bf16[16,6144]{1,0:T(8,128)(2,1)S(1)}, bf16[16,6144]{1,0:T(8,128)(2,1)S(1)}, u32[]{:S(2)}, u32[]{:S(2)}) collective-permute-start(bf16[16,6144]{1,0:T(8,128)(2,1)S(1)} %shard_map.55.refs_0_), channel_id=1, source_target_pairs={{0,4},{1,5},{2,6},{3,7},{4,8},{5,9},{6,10},{7,11},{8,12},{9,13},{1... | collective-permute-start | bytes 589832 | tf_op jit(solution)/shard_map/ppermute | solution.py:19
  9.1 1.7 %collective-permute-start.3 = (bf16[16,6144]{1,0:T(8,128)(2,1)S(1)}, bf16[16,6144]{1,0:T(8,128)(2,1)S(1)}, u32[]{:S(2)}, u32[]{:S(2)}) collective-permute-start(bf16[16,6144]{1,0:T(8,128)(2,1)S(1)} %shard_map.55.refs_0_), channel_id=1, source_target_pairs={{0,12},{1,13},{2,14},{3,15},{4,0},{5,1},{6,2},{7,3},{8,4},{9,5},{1... | collective-permute-start | bytes 589832 | tf_op jit(solution)/shard_map/ppermute | solution.py:19
  10.8 4.1 %shard_map.56.refs_6_.refs_4_.gate_w = bf16[6144,896]{1,0:T(8,128)(2,1)S(1)} custom-call(bf16[6144,896]{1,0:T(8,128)(2,1)} %source.2), custom_call_target="tpu_custom_call" | custom-call | bytes 11010048 | tf_op jit(solution)/shard_map/pallas_call | solution.py:165
  15.0 2.6 %shard_map.57.refs_7_.refs_5_.up_w = bf16[3072,896]{1,0:T(8,128)(2,1)S(1)} custom-call(bf16[6144,896]{1,0:T(8,128)(2,1)} %source.4), custom_call_target="tpu_custom_call" | custom-call | bytes 5505024 | tf_op jit(solution)/shard_map/pallas_call | solution.py:165
  17.6 0.0 collective-permute-done.refs_3_
  17.6 1.4 %collective-permute-start.6 = (bf16[16,6144]{1,0:T(8,128)(2,1)S(1)}, bf16[16,6144]{1,0:T(8,128)(2,1)S(1)}, u32[]{:S(2)}, u32[]{:S(2)}) collective-permute-start(bf16[16,6144]{1,0:T(8,128)(2,1)S(1)} %collective-permute-done.refs_3_), channel_id=1, source_target_pairs={{0,1},{1,2},{2,3},{3,0},{4,5},{5,6},{6,7},{7,4},{8,9},{9,10},{10,1... | collective-permute-start | bytes 589832 | tf_op jit(solution)/shard_map/ppermute | solution.py:19
  19.1 1.3 %collective-permute-start.4 = (bf16[32,6144]{1,0:T(8,128)(2,1)S(1)}, bf16[32,6144]{1,0:T(8,128)(2,1)S(1)}, u32[]{:S(2)}, u32[]{:S(2)}) collective-permute-start(bf16[32,6144]{1,0:T(8,128)(2,1)S(1)} %pad_maximum_fusion), channel_id=1, source_target_pairs={{0,4},{1,5},{2,6},{3,7},{4,8},{5,9},{6,10},{7,11},{8,12},{9,13},{1... | collective-permute-start | bytes 1179656 | tf_op jit(solution)/shard_map/ppermute | solution.py:19
  20.4 2.0 %collective-permute-start.5 = (bf16[32,6144]{1,0:T(8,128)(2,1)S(1)}, bf16[32,6144]{1,0:T(8,128)(2,1)S(1)}, u32[]{:S(2)}, u32[]{:S(2)}) collective-permute-start(bf16[32,6144]{1,0:T(8,128)(2,1)S(1)} %pad_maximum_fusion), channel_id=1, source_target_pairs={{0,12},{1,13},{2,14},{3,15},{4,0},{5,1},{6,2},{7,3},{8,4},{9,5},{1... | collective-permute-start | bytes 1179656 | tf_op jit(solution)/shard_map/ppermute | solution.py:19
  22.4 2.6 %shard_map.58.refs_8_.refs_6_.up_w2 = bf16[3072,896]{1,0:T(8,128)(2,1)S(1)} custom-call(bf16[6144,896]{1,0:T(8,128)(2,1)} %source.4), custom_call_target="tpu_custom_call" | custom-call | bytes 5505024 | tf_op jit(solution)/shard_map/pallas_call | solution.py:165
  25.0 1.0 collective-permute-done.6.refs_5_
  26.0 0.7 collective-permute-start.7
  26.7 2.5 %collective-permute-start.8 = (bf16[16,6144]{1,0:T(8,128)(2,1)S(1)}, bf16[16,6144]{1,0:T(8,128)(2,1)S(1)}, u32[]{:S(2)}, u32[]{:S(2)}) collective-permute-start(bf16[16,6144]{1,0:T(8,128)(2,1)S(1)} %collective-permute-done.6.refs_5_), channel_id=1, source_target_pairs={{0,12},{1,13},{2,14},{3,15},{4,0},{5,1},{6,2},{7,3},{8,4},{9,5},{1... | collective-permute-start | bytes 589832 | tf_op jit(solution)/shard_map/ppermute | solution.py:19
  29.2 3.6 %shard_map.59.early = bf16[96,896]{1,0:T(8,128)(2,1)S(1)} custom-call(bf16[16,6144]{1,0:T(8,128)(2,1)S(1)} %shard_map.55.refs_0_, bf16[16,6144]{1,0:T(8,128)(2,1)S(1)} %collective-permute-done.2.refs_1_, bf16[16,6144]{1,0:T(8,128)(2,1)S(1)} %collective-permute-done.3.refs_2_, bf16[16,6144]{1,0:T(8,128)(2,1)S(1)} %collective-permute-done.refs_3_, ...), custom_call_target="tpu_custom_call" | custom-call | flops 2113929216 | tf_op jit(solution)/shard_map/pallas_call | solution.py:80
  32.9 0.0 collective-permute-done.4.refs_0_
  32.9 2.8 %collective-permute-start.10 = (bf16[16,9216]{1,0:T(8,128)(2,1)S(1)}, bf16[16,9216]{1,0:T(8,128)(2,1)S(1)}, u32[]{:S(2)}, u32[]{:S(2)}) collective-permute-start(bf16[16,9216]{1,0:T(8,128)(2,1)S(1)} %pad_maximum_fusion.4), channel_id=1, source_target_pairs={{0,12},{1,13},{2,14},{3,15},{4,0},{5,1},{6,2},{7,3},{8,4},{9,5},{1... | collective-permute-start | bytes 884744 | tf_op jit(solution)/shard_map/ppermute | solution.py:19
  35.7 0.1 collective-permute-start.9
  35.8 0.4 collective-permute-done.7.refs_2_
  36.3 0.0 collective-permute-done.8.refs_3_
  36.3 1.7 %collective-permute-start.11 = (bf16[16,3072]{1,0:T(8,128)(2,1)S(1)}, bf16[16,3072]{1,0:T(8,128)(2,1)S(1)}, u32[]{:S(2)}, u32[]{:S(2)}) collective-permute-start(bf16[16,3072]{1,0:T(8,128)(2,1)S(1)} %slice.90), channel_id=1, source_target_pairs={{0,4},{1,5},{2,6},{3,7},{4,8},{5,9},{6,10},{7,11},{8,12},{9,13},{1... | collective-permute-start | bytes 294920 | tf_op jit(solution)/shard_map/ppermute | solution.py:19
  38.1 2.1 %collective-permute-start.12 = (bf16[16,3072]{1,0:T(8,128)(2,1)S(1)}, bf16[16,3072]{1,0:T(8,128)(2,1)S(1)}, u32[]{:S(2)}, u32[]{:S(2)}) collective-permute-start(bf16[16,3072]{1,0:T(8,128)(2,1)S(1)} %slice.91), channel_id=1, source_target_pairs={{0,12},{1,13},{2,14},{3,15},{4,0},{5,1},{6,2},{7,3},{8,4},{9,5},{1... | collective-permute-start | bytes 294920 | tf_op jit(solution)/shard_map/ppermute | solution.py:19
  40.2 4.1 %shard_map.60 = (bf16[96,896]{1,0:T(8,128)(2,1)S(1)}, bf16[896,6144]{1,0:T(8,128)(2,1)S(1)}) custom-call(bf16[32,6144]{1,0:T(8,128)(2,1)S(1)} %collective-permute-done.4.refs_0_, bf16[32,6144]{1,0:T(8,128)(2,1)S(1)} %collective-permute-done.5.refs_1_, bf16[16,6144]{1,0:T(8,128)(2,1)S(1)} %collective-permute-done.7.refs_2_, ...), custom_call_target="tpu_custom_call" | custom-call | flops 2113929216 | bytes 11010048 | tf_op jit(solution)/shard_map/pallas_call | solution.py:80
  44.3 3.6 %collective-permute-done.11.far_up = bf16[16,3072]{1,0:T(8,128)(2,1)S(1)} collective-permute-done((bf16[16,3072]{1,0:T(8,128)(2,1)S(1)}, bf16[16,3072]{1,0:T(8,128)(2,1)S(1)}, u32[]{:S(2)}, u32[]{:S(2)}) %collective-permute-start.11) | collective-permute-done | bytes 98336 | tf_op jit(solution)/shard_map/ppermute | solution.py:19
  47.9 6.5 %shard_map.62 = (bf16[16,12288]{1,0:T(8,128)(2,1)S(1)}, bf16[16,12288]{1,0:T(8,128)(2,1)S(1)}) custom-call(bf16[16,9216]{1,0:T(8,128)(2,1)S(1)} %collective-permute-done.9.two_up, bf16[16,9216]{1,0:T(8,128)(2,1)S(1)} %collective-permute-done.10.two_down, bf16[16,3072]{1,0:T(8,128)(2,1)S(1)} %collective-permute-done.11.far_up, ...), custom_call_target="tpu_custom_call" | custom-call | flops 2113929216 | tf_op jit(solution)/shard_map/pallas_call | solution.py:116
  54.4 0.1 collective-permute-start.13
  54.5 3.2 %collective-permute-start.14 = (bf16[16,12288]{1,0:T(8,128)(2,1)S(1)}, bf16[16,12288]{1,0:T(8,128)(2,1)S(1)}, u32[]{:S(2)}, u32[]{:S(2)}) collective-permute-start(bf16[16,12288]{1,0:T(8,128)(2,1)S(1)} %get-tuple-element.59), channel_id=1, source_target_pairs={{0,12},{1,13},{2,14},{3,15},{4,0},{5,1},{6,2},{7,3},{8,4},{9,5},{1... | collective-permute-start | bytes 1179656 | tf_op jit(solution)/shard_map/ppermute | solution.py:19
  57.7 3.6 %shard_map.61 = (f32[16,6144]{1,0:T(8,128)S(1)}, f32[16,6144]{1,0:T(8,128)S(1)}, f32[16,6144]{1,0:T(8,128)S(1)}, f32[32,6144]{1,0:T(8,128)S(1)}, f32[16,6144]{1,...) custom-call(bf16[96,896]{1,0:T(8,128)(2,1)S(1)} %shard_map.59.early,, ...), custom_call_target="tpu_custom_call" | custom-call | flops 2113929216 | tf_op jit(solution)/shard_map/pallas_call | solution.py:146
  61.5 4.2 %collective-permute-done.13 = bf16[16,12288]{1,0:T(8,128)(2,1)S(1)} collective-permute-done((bf16[16,12288]{1,0:T(8,128)(2,1)S(1)}, bf16[16,12288]{1,0:T(8,128)(2,1)S(1)}, u32[]{:S(2)}, u32[]{:S(2)}) %collective-permute-start.13) | collective-permute-done | bytes 393248 | tf_op jit(solution)/shard_map/ppermute | solution.py:19
  65.9 0.1 collective-permute-start.20
  66.0 3.3 %collective-permute-start.21 = (bf16[16,6144]{1,0:T(8,128)(2,1)S(1)}, bf16[16,6144]{1,0:T(8,128)(2,1)S(1)}, u32[]{:S(2)}, u32[]{:S(2)}) collective-permute-start(bf16[16,6144]{1,0:T(8,128)(2,1)S(1)} %pad_maximum_fusion.8), channel_id=1, source_target_pairs={{0,12},{1,13},{2,14},{3,15},{4,0},{5,1},{6,2},{7,3},{8,4},{9,5},{1... | collective-permute-start | bytes 589832 | tf_op jit(solution)/shard_map/ppermute | solution.py:19
  69.3 1.8 %collective-permute-start.16 = (bf16[32,6144]{1,0:T(8,128)(2,1)S(1)}, bf16[32,6144]{1,0:T(8,128)(2,1)S(1)}, u32[]{:S(2)}, u32[]{:S(2)}) collective-permute-start(bf16[32,6144]{1,0:T(8,128)(2,1)S(1)} %pad_maximum_fusion.2), channel_id=1, source_target_pairs={{0,12},{1,13},{2,14},{3,15},{4,0},{5,1},{6,2},{7,3},{8,4},{9,5},{1... | collective-permute-start | bytes 1179656 | tf_op jit(solution)/shard_map/ppermute | solution.py:19
  71.2 0.6 collective-permute-start.15
  71.8 1.6 %collective-permute-done.20 = bf16[16,6144]{1,0:T(8,128)(2,1)S(1)} collective-permute-done((bf16[16,6144]{1,0:T(8,128)(2,1)S(1)}, bf16[16,6144]{1,0:T(8,128)(2,1)S(1)}, u32[]{:S(2)}, u32[]{:S(2)}) %collective-permute-start.20) | collective-permute-done | bytes 196640 | tf_op jit(solution)/shard_map/ppermute | solution.py:19
  73.4 1.2 %collective-permute-done.21 = bf16[16,6144]{1,0:T(8,128)(2,1)S(1)} collective-permute-done((bf16[16,6144]{1,0:T(8,128)(2,1)S(1)}, bf16[16,6144]{1,0:T(8,128)(2,1)S(1)}, u32[]{:S(2)}, u32[]{:S(2)}) %collective-permute-start.21) | collective-permute-done | bytes 196640 | tf_op jit(solution)/shard_map/ppermute | solution.py:19
  74.7 0.1 add_convert_fusion.1
  74.7 2.4 %collective-permute-start.22 = (bf16[16,6144]{1,0:T(8,128)(2,1)S(1)}, bf16[16,6144]{1,0:T(8,128)(2,1)S(1)}, u32[]{:S(2)}, u32[]{:S(2)}) collective-permute-start(bf16[16,6144]{1,0:T(8,128)(2,1)S(1)} %add_convert_fusion.1), channel_id=1, source_target_pairs={{0,3},{1,0},{2,1},{3,2},{4,7},{5,4},{6,5},{7,6},{8,11},{9,8},{10,9... | collective-permute-start | bytes 589832 | tf_op jit(solution)/shard_map/ppermute | solution.py:19
  77.1 2.9 %collective-permute-done.16 = bf16[32,6144]{1,0:T(8,128)(2,1)S(1)} collective-permute-done((bf16[32,6144]{1,0:T(8,128)(2,1)S(1)}, bf16[32,6144]{1,0:T(8,128)(2,1)S(1)}, u32[]{:S(2)}, u32[]{:S(2)}) %collective-permute-start.16) | collective-permute-done | bytes 393248 | tf_op jit(solution)/shard_map/ppermute | solution.py:19
  80.0 1.3 %collective-permute-done.15 = bf16[32,6144]{1,0:T(8,128)(2,1)S(1)} collective-permute-done((bf16[32,6144]{1,0:T(8,128)(2,1)S(1)}, bf16[32,6144]{1,0:T(8,128)(2,1)S(1)}, u32[]{:S(2)}, u32[]{:S(2)}) %collective-permute-start.15) | collective-permute-done | bytes 393248 | tf_op jit(solution)/shard_map/ppermute | solution.py:19
  81.3 0.1 convert_add_fusion
  81.4 5.7 %collective-permute-done.22 = bf16[16,6144]{1,0:T(8,128)(2,1)S(1)} collective-permute-done((bf16[16,6144]{1,0:T(8,128)(2,1)S(1)}, bf16[16,6144]{1,0:T(8,128)(2,1)S(1)}, u32[]{:S(2)}, u32[]{:S(2)}) %collective-permute-start.22) | collective-permute-done | bytes 196640 | tf_op jit(solution)/shard_map/ppermute | solution.py:19
  87.2 0.1 collective-permute-start.23
  87.3 2.9 %collective-permute-start.19 = (bf16[16,6144]{1,0:T(8,128)(2,1)S(1)}, bf16[16,6144]{1,0:T(8,128)(2,1)S(1)}, u32[]{:S(2)}, u32[]{:S(2)}) collective-permute-start(bf16[16,6144]{1,0:T(8,128)(2,1)S(1)} %slice.141), channel_id=1, source_target_pairs={{0,1},{1,2},{2,3},{3,0},{4,5},{5,6},{6,7},{7,4},{8,9},{9,10},{10,1... | collective-permute-start | bytes 589832 | tf_op jit(solution)/shard_map/ppermute | solution.py:19
  90.2 4.2 %collective-permute-start.17 = (bf16[16,6144]{1,0:T(8,128)(2,1)S(1)}, bf16[16,6144]{1,0:T(8,128)(2,1)S(1)}, u32[]{:S(2)}, u32[]{:S(2)}) collective-permute-start(bf16[16,6144]{1,0:T(8,128)(2,1)S(1)} %pad_maximum_fusion.5), channel_id=1, source_target_pairs={{0,4},{1,5},{2,6},{3,7},{4,8},{5,9},{6,10},{7,11},{8,12},{9,13},{1... | collective-permute-start | bytes 589832 | tf_op jit(solution)/shard_map/ppermute | solution.py:19
  94.4 2.1 %collective-permute-start.18 = (bf16[16,6144]{1,0:T(8,128)(2,1)S(1)}, bf16[16,6144]{1,0:T(8,128)(2,1)S(1)}, u32[]{:S(2)}, u32[]{:S(2)}) collective-permute-start(bf16[16,6144]{1,0:T(8,128)(2,1)S(1)} %pad_maximum_fusion.6), channel_id=1, source_target_pairs={{0,12},{1,13},{2,14},{3,15},{4,0},{5,1},{6,2},{7,3},{8,4},{9,5},{1... | collective-permute-start | bytes 589832 | tf_op jit(solution)/shard_map/ppermute | solution.py:19
  96.5 3.6 %collective-permute-done.17 = bf16[16,6144]{1,0:T(8,128)(2,1)S(1)} collective-permute-done((bf16[16,6144]{1,0:T(8,128)(2,1)S(1)}, bf16[16,6144]{1,0:T(8,128)(2,1)S(1)}, u32[]{:S(2)}, u32[]{:S(2)}) %collective-permute-start.17) | collective-permute-done | bytes 196640 | tf_op jit(solution)/shard_map/ppermute | solution.py:19
  100.1 0.8 add_convert_fusion
  (40 shorter events, 0.6 us)
Async XLA Ops:
  1.1 16.4 %collective-permute-start = (bf16[16,6144]{1,0:T(8,128)(2,1)S(1)}, bf16[16,6144]{1,0:T(8,128)(2,1)S(1)}, u32[]{:S(2)}, u32[]{:S(2)}) collective-permute-start(bf16[16,6144]{1,0:T(8,128)(2,1)S(1)} %shard_map.55.refs_0_), channel_id=1, source_target_pairs={{0,1},{1,2},{2,3},{3,0},{4,5},{5,6},{6,7},{7,4},{8,9},{9,10},{10,1... | collective-permute-start | bytes 589832 | tf_op jit(solution)/shard_map/ppermute | solution.py:19
  4.5 13.1 %collective-permute-start.1 = (bf16[16,6144]{1,0:T(8,128)(2,1)S(1)}, bf16[16,6144]{1,0:T(8,128)(2,1)S(1)}, u32[]{:S(2)}, u32[]{:S(2)}) collective-permute-start(bf16[16,6144]{1,0:T(8,128)(2,1)S(1)} %shard_map.55.refs_0_), channel_id=1, source_target_pairs={{0,3},{1,0},{2,1},{3,2},{4,7},{5,4},{6,5},{7,6},{8,11},{9,8},{10,9... | collective-permute-start | bytes 589832 | tf_op jit(solution)/shard_map/ppermute | solution.py:19
  7.6 11.5 %collective-permute-start.2 = (bf16[16,6144]{1,0:T(8,128)(2,1)S(1)}, bf16[16,6144]{1,0:T(8,128)(2,1)S(1)}, u32[]{:S(2)}, u32[]{:S(2)}) collective-permute-start(bf16[16,6144]{1,0:T(8,128)(2,1)S(1)} %shard_map.55.refs_0_), channel_id=1, source_target_pairs={{0,4},{1,5},{2,6},{3,7},{4,8},{5,9},{6,10},{7,11},{8,12},{9,13},{1... | collective-permute-start | bytes 589832 | tf_op jit(solution)/shard_map/ppermute | solution.py:19
  9.1 10.0 %collective-permute-start.3 = (bf16[16,6144]{1,0:T(8,128)(2,1)S(1)}, bf16[16,6144]{1,0:T(8,128)(2,1)S(1)}, u32[]{:S(2)}, u32[]{:S(2)}) collective-permute-start(bf16[16,6144]{1,0:T(8,128)(2,1)S(1)} %shard_map.55.refs_0_), channel_id=1, source_target_pairs={{0,12},{1,13},{2,14},{3,15},{4,0},{5,1},{6,2},{7,3},{8,4},{9,5},{1... | collective-permute-start | bytes 589832 | tf_op jit(solution)/shard_map/ppermute | solution.py:19
  17.6 8.4 %collective-permute-start.6 = (bf16[16,6144]{1,0:T(8,128)(2,1)S(1)}, bf16[16,6144]{1,0:T(8,128)(2,1)S(1)}, u32[]{:S(2)}, u32[]{:S(2)}) collective-permute-start(bf16[16,6144]{1,0:T(8,128)(2,1)S(1)} %collective-permute-done.refs_3_), channel_id=1, source_target_pairs={{0,1},{1,2},{2,3},{3,0},{4,5},{5,6},{6,7},{7,4},{8,9},{9,10},{10,1... | collective-permute-start | bytes 589832 | tf_op jit(solution)/shard_map/ppermute | solution.py:19
  19.1 13.8 %collective-permute-start.4 = (bf16[32,6144]{1,0:T(8,128)(2,1)S(1)}, bf16[32,6144]{1,0:T(8,128)(2,1)S(1)}, u32[]{:S(2)}, u32[]{:S(2)}) collective-permute-start(bf16[32,6144]{1,0:T(8,128)(2,1)S(1)} %pad_maximum_fusion), channel_id=1, source_target_pairs={{0,4},{1,5},{2,6},{3,7},{4,8},{5,9},{6,10},{7,11},{8,12},{9,13},{1... | collective-permute-start | bytes 1179656 | tf_op jit(solution)/shard_map/ppermute | solution.py:19
  20.4 12.5 %collective-permute-start.5 = (bf16[32,6144]{1,0:T(8,128)(2,1)S(1)}, bf16[32,6144]{1,0:T(8,128)(2,1)S(1)}, u32[]{:S(2)}, u32[]{:S(2)}) collective-permute-start(bf16[32,6144]{1,0:T(8,128)(2,1)S(1)} %pad_maximum_fusion), channel_id=1, source_target_pairs={{0,12},{1,13},{2,14},{3,15},{4,0},{5,1},{6,2},{7,3},{8,4},{9,5},{1... | collective-permute-start | bytes 1179656 | tf_op jit(solution)/shard_map/ppermute | solution.py:19
  26.0 10.3 %collective-permute-start.7 = (bf16[16,6144]{1,0:T(8,128)(2,1)S(1)}, bf16[16,6144]{1,0:T(8,128)(2,1)S(1)}, u32[]{:S(2)}, u32[]{:S(2)}) collective-permute-start(bf16[16,6144]{1,0:T(8,128)(2,1)S(1)} %collective-permute-done.6.refs_5_), channel_id=1, source_target_pairs={{0,4},{1,5},{2,6},{3,7},{4,8},{5,9},{6,10},{7,11},{8,12},{9,13},{1... | collective-permute-start | bytes 589832 | tf_op jit(solution)/shard_map/ppermute | solution.py:19
  26.7 9.6 %collective-permute-start.8 = (bf16[16,6144]{1,0:T(8,128)(2,1)S(1)}, bf16[16,6144]{1,0:T(8,128)(2,1)S(1)}, u32[]{:S(2)}, u32[]{:S(2)}) collective-permute-start(bf16[16,6144]{1,0:T(8,128)(2,1)S(1)} %collective-permute-done.6.refs_5_), channel_id=1, source_target_pairs={{0,12},{1,13},{2,14},{3,15},{4,0},{5,1},{6,2},{7,3},{8,4},{9,5},{1... | collective-permute-start | bytes 589832 | tf_op jit(solution)/shard_map/ppermute | solution.py:19
  32.9 15.0 %collective-permute-start.10 = (bf16[16,9216]{1,0:T(8,128)(2,1)S(1)}, bf16[16,9216]{1,0:T(8,128)(2,1)S(1)}, u32[]{:S(2)}, u32[]{:S(2)}) collective-permute-start(bf16[16,9216]{1,0:T(8,128)(2,1)S(1)} %pad_maximum_fusion.4), channel_id=1, source_target_pairs={{0,12},{1,13},{2,14},{3,15},{4,0},{5,1},{6,2},{7,3},{8,4},{9,5},{1... | collective-permute-start | bytes 884744 | tf_op jit(solution)/shard_map/ppermute | solution.py:19
  35.7 12.2 %collective-permute-start.9 = (bf16[16,9216]{1,0:T(8,128)(2,1)S(1)}, bf16[16,9216]{1,0:T(8,128)(2,1)S(1)}, u32[]{:S(2)}, u32[]{:S(2)}) collective-permute-start(bf16[16,9216]{1,0:T(8,128)(2,1)S(1)} %pad_maximum_fusion.3), channel_id=1, source_target_pairs={{0,4},{1,5},{2,6},{3,7},{4,8},{5,9},{6,10},{7,11},{8,12},{9,13},{1... | collective-permute-start | bytes 884744 | tf_op jit(solution)/shard_map/ppermute | solution.py:19
  36.3 11.6 %collective-permute-start.11 = (bf16[16,3072]{1,0:T(8,128)(2,1)S(1)}, bf16[16,3072]{1,0:T(8,128)(2,1)S(1)}, u32[]{:S(2)}, u32[]{:S(2)}) collective-permute-start(bf16[16,3072]{1,0:T(8,128)(2,1)S(1)} %slice.90), channel_id=1, source_target_pairs={{0,4},{1,5},{2,6},{3,7},{4,8},{5,9},{6,10},{7,11},{8,12},{9,13},{1... | collective-permute-start | bytes 294920 | tf_op jit(solution)/shard_map/ppermute | solution.py:19
  38.1 9.8 %collective-permute-start.12 = (bf16[16,3072]{1,0:T(8,128)(2,1)S(1)}, bf16[16,3072]{1,0:T(8,128)(2,1)S(1)}, u32[]{:S(2)}, u32[]{:S(2)}) collective-permute-start(bf16[16,3072]{1,0:T(8,128)(2,1)S(1)} %slice.91), channel_id=1, source_target_pairs={{0,12},{1,13},{2,14},{3,15},{4,0},{5,1},{6,2},{7,3},{8,4},{9,5},{1... | collective-permute-start | bytes 294920 | tf_op jit(solution)/shard_map/ppermute | solution.py:19
  54.4 11.3 %collective-permute-start.13 = (bf16[16,12288]{1,0:T(8,128)(2,1)S(1)}, bf16[16,12288]{1,0:T(8,128)(2,1)S(1)}, u32[]{:S(2)}, u32[]{:S(2)}) collective-permute-start(bf16[16,12288]{1,0:T(8,128)(2,1)S(1)} %get-tuple-element.58), channel_id=1, source_target_pairs={{0,4},{1,5},{2,6},{3,7},{4,8},{5,9},{6,10},{7,11},{8,12},{9,13},{1... | collective-permute-start | bytes 1179656 | tf_op jit(solution)/shard_map/ppermute | solution.py:19
  54.5 11.2 %collective-permute-start.14 = (bf16[16,12288]{1,0:T(8,128)(2,1)S(1)}, bf16[16,12288]{1,0:T(8,128)(2,1)S(1)}, u32[]{:S(2)}, u32[]{:S(2)}) collective-permute-start(bf16[16,12288]{1,0:T(8,128)(2,1)S(1)} %get-tuple-element.59), channel_id=1, source_target_pairs={{0,12},{1,13},{2,14},{3,15},{4,0},{5,1},{6,2},{7,3},{8,4},{9,5},{1... | collective-permute-start | bytes 1179656 | tf_op jit(solution)/shard_map/ppermute | solution.py:19
  57.7 42.4 %copy-start = (bf16[16,6144]{1,0:T(8,128)(2,1)S(1)}, bf16[16,6144]{1,0:T(8,128)(2,1)}, u32[]{:S(2)}) copy-start(bf16[16,6144]{1,0:T(8,128)(2,1)} %rows_ref.1) | copy-start | bytes 589828
  65.9 7.6 %collective-permute-start.20 = (bf16[16,6144]{1,0:T(8,128)(2,1)S(1)}, bf16[16,6144]{1,0:T(8,128)(2,1)S(1)}, u32[]{:S(2)}, u32[]{:S(2)}) collective-permute-start(bf16[16,6144]{1,0:T(8,128)(2,1)S(1)} %pad_maximum_fusion.7), channel_id=1, source_target_pairs={{0,4},{1,5},{2,6},{3,7},{4,8},{5,9},{6,10},{7,11},{8,12},{9,13},{1... | collective-permute-start | bytes 589832 | tf_op jit(solution)/shard_map/ppermute | solution.py:19
  66.0 8.7 %collective-permute-start.21 = (bf16[16,6144]{1,0:T(8,128)(2,1)S(1)}, bf16[16,6144]{1,0:T(8,128)(2,1)S(1)}, u32[]{:S(2)}, u32[]{:S(2)}) collective-permute-start(bf16[16,6144]{1,0:T(8,128)(2,1)S(1)} %pad_maximum_fusion.8), channel_id=1, source_target_pairs={{0,12},{1,13},{2,14},{3,15},{4,0},{5,1},{6,2},{7,3},{8,4},{9,5},{1... | collective-permute-start | bytes 589832 | tf_op jit(solution)/shard_map/ppermute | solution.py:19
  69.3 10.7 %collective-permute-start.16 = (bf16[32,6144]{1,0:T(8,128)(2,1)S(1)}, bf16[32,6144]{1,0:T(8,128)(2,1)S(1)}, u32[]{:S(2)}, u32[]{:S(2)}) collective-permute-start(bf16[32,6144]{1,0:T(8,128)(2,1)S(1)} %pad_maximum_fusion.2), channel_id=1, source_target_pairs={{0,12},{1,13},{2,14},{3,15},{4,0},{5,1},{6,2},{7,3},{8,4},{9,5},{1... | collective-permute-start | bytes 1179656 | tf_op jit(solution)/shard_map/ppermute | solution.py:19
  71.2 10.1 %collective-permute-start.15 = (bf16[32,6144]{1,0:T(8,128)(2,1)S(1)}, bf16[32,6144]{1,0:T(8,128)(2,1)S(1)}, u32[]{:S(2)}, u32[]{:S(2)}) collective-permute-start(bf16[32,6144]{1,0:T(8,128)(2,1)S(1)} %pad_maximum_fusion.1), channel_id=1, source_target_pairs={{0,4},{1,5},{2,6},{3,7},{4,8},{5,9},{6,10},{7,11},{8,12},{9,13},{1... | collective-permute-start | bytes 1179656 | tf_op jit(solution)/shard_map/ppermute | solution.py:19
  74.7 12.4 %collective-permute-start.22 = (bf16[16,6144]{1,0:T(8,128)(2,1)S(1)}, bf16[16,6144]{1,0:T(8,128)(2,1)S(1)}, u32[]{:S(2)}, u32[]{:S(2)}) collective-permute-start(bf16[16,6144]{1,0:T(8,128)(2,1)S(1)} %add_convert_fusion.1), channel_id=1, source_target_pairs={{0,3},{1,0},{2,1},{3,2},{4,7},{5,4},{6,5},{7,6},{8,11},{9,8},{10,9... | collective-permute-start | bytes 589832 | tf_op jit(solution)/shard_map/ppermute | solution.py:19
  87.2 9.3 %collective-permute-start.23 = (bf16[16,6144]{1,0:T(8,128)(2,1)S(1)}, bf16[16,6144]{1,0:T(8,128)(2,1)S(1)}, u32[]{:S(2)}, u32[]{:S(2)}) collective-permute-start(bf16[16,6144]{1,0:T(8,128)(2,1)S(1)} %fusion), channel_id=1, source_target_pairs={{0,3},{1,0},{2,1},{3,2},{4,7},{5,4},{6,5},{7,6},{8,11},{9,8},{10,9... | collective-permute-start | bytes 589832 | tf_op jit(solution)/shard_map/ppermute | solution.py:19
  87.3 9.2 %collective-permute-start.19 = (bf16[16,6144]{1,0:T(8,128)(2,1)S(1)}, bf16[16,6144]{1,0:T(8,128)(2,1)S(1)}, u32[]{:S(2)}, u32[]{:S(2)}) collective-permute-start(bf16[16,6144]{1,0:T(8,128)(2,1)S(1)} %slice.141), channel_id=1, source_target_pairs={{0,1},{1,2},{2,3},{3,0},{4,5},{5,6},{6,7},{7,4},{8,9},{9,10},{10,1... | collective-permute-start | bytes 589832 | tf_op jit(solution)/shard_map/ppermute | solution.py:19
  90.2 9.9 %collective-permute-start.17 = (bf16[16,6144]{1,0:T(8,128)(2,1)S(1)}, bf16[16,6144]{1,0:T(8,128)(2,1)S(1)}, u32[]{:S(2)}, u32[]{:S(2)}) collective-permute-start(bf16[16,6144]{1,0:T(8,128)(2,1)S(1)} %pad_maximum_fusion.5), channel_id=1, source_target_pairs={{0,4},{1,5},{2,6},{3,7},{4,8},{5,9},{6,10},{7,11},{8,12},{9,13},{1... | collective-permute-start | bytes 589832 | tf_op jit(solution)/shard_map/ppermute | solution.py:19
  94.4 5.7 %collective-permute-start.18 = (bf16[16,6144]{1,0:T(8,128)(2,1)S(1)}, bf16[16,6144]{1,0:T(8,128)(2,1)S(1)}, u32[]{:S(2)}, u32[]{:S(2)}) collective-permute-start(bf16[16,6144]{1,0:T(8,128)(2,1)S(1)} %pad_maximum_fusion.6), channel_id=1, source_target_pairs={{0,12},{1,13},{2,14},{3,15},{4,0},{5,1},{6,2},{7,3},{8,4},{9,5},{1... | collective-permute-start | bytes 589832 | tf_op jit(solution)/shard_map/ppermute | solution.py:19

commit v10 on v8

--- a/solution.py
+++ b/solution.py
@@ -47,16 +47,17 @@
     return [pltpu.with_memory_space_constraint(v, pltpu.VMEM) for v in blocks]
 
 
-def hidden_of(rows, gate_w, up_w, up_w2):
-    half = up_w.shape[0]
-    gate = jnp.dot(rows[...], gate_w[...], preferred_element_type=jnp.float32)
-    up = jnp.dot(rows[:, :half], up_w[...], preferred_element_type=jnp.float32)
-    up = up + jnp.dot(rows[:, half:], up_w2[...], preferred_element_type=jnp.float32)
+def hidden_of(rows, *weights):
+    size, wide = weights[0].shape
+    both = jnp.dot(rows[:, :size], weights[0][...], preferred_element_type=jnp.float32)
+    for i, weight in enumerate(weights[1:], 1):
+        both = both + jnp.dot(rows[:, i * size : (i + 1) * size], weight[...], preferred_element_type=jnp.float32)
+    gate, up = both[:, : wide // 2], both[:, wide // 2 :]
     return b16(gate / (1.0 + jnp.exp(-gate)) * up)
 
 
 def hidden_units(blocks, weights, down_weight=None):
-    (n, d), ff = blocks[0].shape, weights[0].shape[1]
+    (n, d), ff = blocks[0].shape, weights[0].shape[1] // 2
     tall, held = sum(v.shape[0] for v in blocks), len(blocks)
     also = () if down_weight is None else (pltpu.with_memory_space_constraint(down_weight, pltpu.HBM),)
 
@@ -83,7 +84,7 @@
         in_specs=[vmem] * (held + len(weights)) + [pl.BlockSpec(memory_space=pltpu.HBM) for _ in also],
         out_specs=[vmem] * (1 + len(also)),
         scratch_shapes=[pltpu.VMEM((tall, d), b)] + [pltpu.SemaphoreType.DMA for _ in also],
-        compiler_params=pltpu.CompilerParams(vmem_limit_bytes=8 * 1024 * 1024),
+        compiler_params=pltpu.CompilerParams(vmem_limit_bytes=4 * 1024 * 1024),
         cost_estimate=pl.CostEstimate(flops=4 * tall * d * ff, bytes_accessed=2 * d * ff * len(also), transcendentals=tall * ff),
     )(*placed((*blocks, *weights)), *also)
 
@@ -91,14 +92,14 @@
 def two_hops(two_up, two_down, far_up, far_down, weights, down_w):
     (n, h), (ff, d), step = far_up.shape, down_w.shape, 1024
 
-    def kernel(two_up, two_down, far_up, far_down, gate_w, up_w, up_w2, down_w, out_up, out_down, rows, hidden):
+    def kernel(two_up, two_down, far_up, far_down, w_0, w_1, w_2, down_w, out_up, out_down, rows, hidden):
         rows[:n, :] = two_up[:, :d]
         rows[n : 2 * n, :] = two_down[:, :d]
         rows[2 * n : 3 * n, :h] = two_up[:, d:]
         rows[2 * n : 3 * n, h:] = two_down[:, d:]
         rows[3 * n :, :h] = far_up[...]
         rows[3 * n :, h:] = far_down[...]
-        hidden[...] = hidden_of(rows, gate_w, up_w, up_w2)
+        hidden[...] = hidden_of(rows, w_0, w_1, w_2)
         for second in (False, True):
             target = out_down if second else out_up
 
@@ -119,7 +120,7 @@
         in_specs=[vmem] * 8,
         out_specs=[vmem] * 2,
         scratch_shapes=[pltpu.VMEM((4 * n, d), b), pltpu.VMEM((4 * n, ff), b)],
-        compiler_params=pltpu.CompilerParams(vmem_limit_bytes=8 * 1024 * 1024),
+        compiler_params=pltpu.CompilerParams(vmem_limit_bytes=4 * 1024 * 1024),
         cost_estimate=pl.CostEstimate(flops=6 * 4 * n * d * ff, bytes_accessed=0, transcendentals=4 * n * ff),
     )(*placed((two_up, two_down, far_up, far_down, *weights, down_w)))
 
@@ -149,28 +150,34 @@
         in_specs=[vmem] * 3,
         out_specs=[vmem] * 9,
         scratch_shapes=[pltpu.VMEM((12 * n, ff), jnp.bfloat16)],
-        compiler_params=pltpu.CompilerParams(vmem_limit_bytes=8 * 1024 * 1024),
+        compiler_params=pltpu.CompilerParams(vmem_limit_bytes=4 * 1024 * 1024),
         cost_estimate=pl.CostEstimate(flops=2 * 12 * n * d * ff, bytes_accessed=0, transcendentals=0),
     )(*placed((early, late, down_weight)))
 
 
-def fetched(weight, part=0, parts=1):
-    size = weight.shape[0] // parts
-
-    def kernel(source, target, done):
-        copy = pltpu.make_async_copy(source.at[pl.ds(part * size, size), :], target, done)
-        copy.start()
-        copy.wait()
-
-    return pl.pallas_call(
-        kernel,
-        out_shape=pltpu.VMEM((size, weight.shape[1]), weight.dtype),
-        in_specs=[pl.BlockSpec(memory_space=pltpu.HBM)],
+def fetched(gate_weight, up_weight, part, parts=3):
+    (d, ff), size = gate_weight.shape, gate_weight.shape[0] // parts
+
+    def kernel(gate, up, target, done):
+        cut = pl.ds(part * size, size)
+        copies = [
+            pltpu.make_async_copy(gate.at[cut, :], target.at[:, pl.ds(0, ff)], done.at[0]),
+            pltpu.make_async_copy(up.at[cut, :], target.at[:, pl.ds(ff, ff)], done.at[1]),
+        ]
+        for copy in copies:
+            copy.start()
+        for copy in copies:
+            copy.wait()
+
+    return pl.pallas_call(
+        kernel,
+        out_shape=pltpu.VMEM((size, 2 * ff), gate_weight.dtype),
+        in_specs=[pl.BlockSpec(memory_space=pltpu.HBM)] * 2,
         out_specs=pl.BlockSpec(memory_space=pltpu.VMEM),
-        scratch_shapes=[pltpu.SemaphoreType.DMA],
+        scratch_shapes=[pltpu.SemaphoreType.DMA((2,))],
         compiler_params=pltpu.CompilerParams(vmem_limit_bytes=1024 * 1024),
-        cost_estimate=pl.CostEstimate(flops=0, bytes_accessed=2 * size * weight.shape[1], transcendentals=0),
-    )(pltpu.with_memory_space_constraint(weight, pltpu.HBM))
+        cost_estimate=pl.CostEstimate(flops=0, bytes_accessed=4 * size * ff, transcendentals=0),
+    )(*[pltpu.with_memory_space_constraint(w, pltpu.HBM) for w in (gate_weight, up_weight)])
 
 
 def terms_of(own, gate_weight, up_weight, down_weight):
@@ -179,12 +186,13 @@
     below, above = lax.optimization_barrier((shift(own, 0, 1), shift(own, 0, -1)))
     own_l, own_r = shift(own, 1, 0), shift(own, -1, 0)
     far = shift(below, 0, 1)
-    near, own_l, own_r, gate_v, up_v, up_weight = lax.optimization_barrier(
-        (jnp.concatenate([below, above], 0), own_l, own_r, fetched(gate_weight), fetched(up_weight, 0, 2), up_weight)
+    pieces = [fetched(gate_weight, up_weight, i) for i in range(2)]
+    near, own_l, own_r, gate_weight, *pieces = lax.optimization_barrier(
+        (jnp.concatenate([below, above], 0), own_l, own_r, gate_weight, *pieces)
     )
     near_l, near_r = shift(near, 1, 0), shift(near, -1, 0)
-    far, up_v2 = lax.optimization_barrier((far, fetched(up_weight, 1, 2)))
-    weights = gate_v, up_v, up_v2
+    far, last = lax.optimization_barrier((far, fetched(gate_weight, up_weight, 2)))
+    weights = *pieces, last
     (early,) = hidden_units((own, own_l, own_r, below, above, far), weights)
     far_l, far_r = lax.optimization_barrier((shift(far, 1, 0), shift(far, -1, 0)))
     near_l, near_r, early = lax.optimization_barrier((near_l, near_r, early))

time: 94.1 us -> 95.8 us (1.018)
  waiting for transfers between devices: 22.2 us -> 16.2 us
  local copies, waits for them, and re-layouts: 0.19 us -> 4.32 us
  Pallas kernels: 28.3 us -> 31 us
    ppermute x24, waiting for transfers between devices: 22.2 us -> 16.2 us  [shift(): return lax.ppermute(block, ('dp', 'tensor'), pairs)]
    unnamed x2 -> x6, local copies, waits for them, and re-layouts: 0.01 us -> 4.14 us
    pallas_call x2, Pallas kernels: 7.79 us -> 10.2 us  [hidden_units(): pl.pallas_call(kernel, out_shape=[pltpu.VMEM((tall, ff), b)] + [pltpu.VME...]
  transfers between devices with their start and end apart: 24 -> 24, of which waited for: 9 -> 11; matrix products, arithmetic and copies ran while one was open for 1% -> 1% of each run, Pallas kernels for 22% -> 25%
where the time goes in v10:
time: 95.8 us; the launch traced here: 94.9 us
  starting transfers between devices  41.7 us (44%)
  Pallas kernels  31 us (32%)
  waiting for transfers between devices  16.2 us (17%)
  local copies, waits for them, and re-layouts  4.32 us (5%)
  other arithmetic  1.37 us (1%)
    ppermute x24, starting transfers between devices, shift(): return lax.ppermute(block, ('dp', 'tensor'), pairs)  41.7 us
    ppermute x24, waiting for transfers between devices, shift(): return lax.ppermute(block, ('dp', 'tensor'), pairs)  16.2 us
    pallas_call x2, Pallas kernels, hidden_units(): pl.pallas_call(kernel, out_shape=[pltpu.VMEM((tall, ff), b)] + [pltpu.VME...  10.2 us
    pallas_call x3, Pallas kernels, fetched(): pl.pallas_call(kernel, out_shape=pltpu.VMEM((size, 2 * ff), gate_weight.d...  9.53 us
    pallas_call x1, Pallas kernels, two_hops(): pl.pallas_call(kernel, out_shape=[pltpu.VMEM((n, 2 * d), b)] * 2, in_spec...  6.58 us
    unnamed x6, local copies, waits for them, and re-layouts  4.14 us
    pallas_call x1, Pallas kernels, other_terms(): pl.pallas_call(kernel, out_shape=[pltpu.VMEM((k * n, d), jnp.float32) for...  3.56 us
  transfers between devices with their start and end apart: 24, of which 11 were waited for; matrix products, arithmetic and copies ran while one was open for 1% of the time, Pallas kernels for 25%

profile of v10, /device:TPU:8, one launch (start us, length us, event | category | flops | bytes accessed | tf_op | source)
XLA Modules:
  0.0 94.9 jit_solution(8907031504916694375)
XLA Ops:
  0.0 1.1 %shard_map.55.refs_0_ = bf16[16,6144]{1,0:T(8,128)(2,1)S(1)} custom-call(bf16[16,6144]{1,0:T(8,128)(2,1)} %rows_ref.1, f32[1,6144]{1,0:T(1,128)} %bitcast.1), custom_call_target="tpu_custom_call" | custom-call | tf_op jit(solution)/shard_map/pallas_call | solution.py:37
  1.1 3.3 %collective-permute-start = (bf16[16,6144]{1,0:T(8,128)(2,1)S(1)}, bf16[16,6144]{1,0:T(8,128)(2,1)S(1)}, u32[]{:S(2)}, u32[]{:S(2)}) collective-permute-start(bf16[16,6144]{1,0:T(8,128)(2,1)S(1)} %shard_map.55.refs_0_), channel_id=1, source_target_pairs={{0,1},{1,2},{2,3},{3,0},{4,5},{5,6},{6,7},{7,4},{8,9},{9,10},{10,1... | collective-permute-start | bytes 589832 | tf_op jit(solution)/shard_map/ppermute | solution.py:19
  4.5 3.1 %collective-permute-start.1 = (bf16[16,6144]{1,0:T(8,128)(2,1)S(1)}, bf16[16,6144]{1,0:T(8,128)(2,1)S(1)}, u32[]{:S(2)}, u32[]{:S(2)}) collective-permute-start(bf16[16,6144]{1,0:T(8,128)(2,1)S(1)} %shard_map.55.refs_0_), channel_id=1, source_target_pairs={{0,3},{1,0},{2,1},{3,2},{4,7},{5,4},{6,5},{7,6},{8,11},{9,8},{10,9... | collective-permute-start | bytes 589832 | tf_op jit(solution)/shard_map/ppermute | solution.py:19
  7.6 1.5 %collective-permute-start.2 = (bf16[16,6144]{1,0:T(8,128)(2,1)S(1)}, bf16[16,6144]{1,0:T(8,128)(2,1)S(1)}, u32[]{:S(2)}, u32[]{:S(2)}) collective-permute-start(bf16[16,6144]{1,0:T(8,128)(2,1)S(1)} %shard_map.55.refs_0_), channel_id=1, source_target_pairs={{0,4},{1,5},{2,6},{3,7},{4,8},{5,9},{6,10},{7,11},{8,12},{9,13},{1... | collective-permute-start | bytes 589832 | tf_op jit(solution)/shard_map/ppermute | solution.py:19
  9.1 1.7 %collective-permute-start.3 = (bf16[16,6144]{1,0:T(8,128)(2,1)S(1)}, bf16[16,6144]{1,0:T(8,128)(2,1)S(1)}, u32[]{:S(2)}, u32[]{:S(2)}) collective-permute-start(bf16[16,6144]{1,0:T(8,128)(2,1)S(1)} %shard_map.55.refs_0_), channel_id=1, source_target_pairs={{0,12},{1,13},{2,14},{3,15},{4,0},{5,1},{6,2},{7,3},{8,4},{9,5},{1... | collective-permute-start | bytes 589832 | tf_op jit(solution)/shard_map/ppermute | solution.py:19
  10.8 3.2 %shard_map.56.refs_6_.refs_4_.w_0 = bf16[2048,1792]{1,0:T(8,128)(2,1)S(1)} custom-call(bf16[6144,896]{1,0:T(8,128)(2,1)} %gate.4, bf16[6144,896]{1,0:T(8,128)(2,1)} %up.5), custom_call_target="tpu_custom_call" | custom-call | bytes 7340032 | tf_op jit(solution)/shard_map/pallas_call | solution.py:172
  14.0 3.2 %shard_map.57.refs_7_.refs_5_.w_1 = bf16[2048,1792]{1,0:T(8,128)(2,1)S(1)} custom-call(bf16[6144,896]{1,0:T(8,128)(2,1)} %gate.4, bf16[6144,896]{1,0:T(8,128)(2,1)} %up.5), custom_call_target="tpu_custom_call" | custom-call | bytes 7340032 | tf_op jit(solution)/shard_map/pallas_call | solution.py:172
  17.2 0.0 collective-permute-done.1.refs_4_
  17.2 1.5 %collective-permute-start.6 = (bf16[16,6144]{1,0:T(8,128)(2,1)S(1)}, bf16[16,6144]{1,0:T(8,128)(2,1)S(1)}, u32[]{:S(2)}, u32[]{:S(2)}) collective-permute-start(bf16[16,6144]{1,0:T(8,128)(2,1)S(1)} %collective-permute-done.refs_3_), channel_id=1, source_target_pairs={{0,1},{1,2},{2,3},{3,0},{4,5},{5,6},{6,7},{7,4},{8,9},{9,10},{10,1... | collective-permute-start | bytes 589832 | tf_op jit(solution)/shard_map/ppermute | solution.py:19
  18.8 1.6 %collective-permute-start.4 = (bf16[32,6144]{1,0:T(8,128)(2,1)S(1)}, bf16[32,6144]{1,0:T(8,128)(2,1)S(1)}, u32[]{:S(2)}, u32[]{:S(2)}) collective-permute-start(bf16[32,6144]{1,0:T(8,128)(2,1)S(1)} %pad_maximum_fusion), channel_id=1, source_target_pairs={{0,4},{1,5},{2,6},{3,7},{4,8},{5,9},{6,10},{7,11},{8,12},{9,13},{1... | collective-permute-start | bytes 1179656 | tf_op jit(solution)/shard_map/ppermute | solution.py:19
  20.4 1.7 %collective-permute-start.5 = (bf16[32,6144]{1,0:T(8,128)(2,1)S(1)}, bf16[32,6144]{1,0:T(8,128)(2,1)S(1)}, u32[]{:S(2)}, u32[]{:S(2)}) collective-permute-start(bf16[32,6144]{1,0:T(8,128)(2,1)S(1)} %pad_maximum_fusion), channel_id=1, source_target_pairs={{0,12},{1,13},{2,14},{3,15},{4,0},{5,1},{6,2},{7,3},{8,4},{9,5},{1... | collective-permute-start | bytes 1179656 | tf_op jit(solution)/shard_map/ppermute | solution.py:19
  22.1 3.2 %shard_map.58.refs_8_.refs_6_.w_2 = bf16[2048,1792]{1,0:T(8,128)(2,1)S(1)} custom-call(bf16[6144,896]{1,0:T(8,128)(2,1)} %gate.4, bf16[6144,896]{1,0:T(8,128)(2,1)} %up.5), custom_call_target="tpu_custom_call" | custom-call | bytes 7340032 | tf_op jit(solution)/shard_map/pallas_call | solution.py:172
  25.3 0.6 collective-permute-done.6.refs_5_
  26.0 0.6 collective-permute-start.7
  26.6 2.6 %collective-permute-start.8 = (bf16[16,6144]{1,0:T(8,128)(2,1)S(1)}, bf16[16,6144]{1,0:T(8,128)(2,1)S(1)}, u32[]{:S(2)}, u32[]{:S(2)}) collective-permute-start(bf16[16,6144]{1,0:T(8,128)(2,1)S(1)} %collective-permute-done.6.refs_5_), channel_id=1, source_target_pairs={{0,12},{1,13},{2,14},{3,15},{4,0},{5,1},{6,2},{7,3},{8,4},{9,5},{1... | collective-permute-start | bytes 589832 | tf_op jit(solution)/shard_map/ppermute | solution.py:19
  29.2 3.6 %shard_map.59.early = bf16[96,896]{1,0:T(8,128)(2,1)S(1)} custom-call(bf16[16,6144]{1,0:T(8,128)(2,1)S(1)} %shard_map.55.refs_0_, bf16[16,6144]{1,0:T(8,128)(2,1)S(1)} %collective-permute-done.2.refs_1_, bf16[16,6144]{1,0:T(8,128)(2,1)S(1)} %collective-permute-done.3.refs_2_, bf16[16,6144]{1,0:T(8,128)(2,1)S(1)} %collective-permute-done.refs_3_, ...), custom_call_target="tpu_custom_call" | custom-call | flops 2113929216 | tf_op jit(solution)/shard_map/pallas_call | solution.py:81
  32.9 2.3 %collective-permute-start.10 = (bf16[16,9216]{1,0:T(8,128)(2,1)S(1)}, bf16[16,9216]{1,0:T(8,128)(2,1)S(1)}, u32[]{:S(2)}, u32[]{:S(2)}) collective-permute-start(bf16[16,9216]{1,0:T(8,128)(2,1)S(1)} %pad_maximum_fusion.4), channel_id=1, source_target_pairs={{0,12},{1,13},{2,14},{3,15},{4,0},{5,1},{6,2},{7,3},{8,4},{9,5},{1... | collective-permute-start | bytes 884744 | tf_op jit(solution)/shard_map/ppermute | solution.py:19
  35.2 0.1 collective-permute-start.9
  35.3 0.5 collective-permute-done.7.refs_2_
  35.8 0.5 collective-permute-done.8.refs_3_
  36.3 1.6 %collective-permute-start.11 = (bf16[16,3072]{1,0:T(8,128)(2,1)S(1)}, bf16[16,3072]{1,0:T(8,128)(2,1)S(1)}, u32[]{:S(2)}, u32[]{:S(2)}) collective-permute-start(bf16[16,3072]{1,0:T(8,128)(2,1)S(1)} %slice.89), channel_id=1, source_target_pairs={{0,4},{1,5},{2,6},{3,7},{4,8},{5,9},{6,10},{7,11},{8,12},{9,13},{1... | collective-permute-start | bytes 294920 | tf_op jit(solution)/shard_map/ppermute | solution.py:19
  37.9 2.0 %collective-permute-start.12 = (bf16[16,3072]{1,0:T(8,128)(2,1)S(1)}, bf16[16,3072]{1,0:T(8,128)(2,1)S(1)}, u32[]{:S(2)}, u32[]{:S(2)}) collective-permute-start(bf16[16,3072]{1,0:T(8,128)(2,1)S(1)} %slice.90), channel_id=1, source_target_pairs={{0,12},{1,13},{2,14},{3,15},{4,0},{5,1},{6,2},{7,3},{8,4},{9,5},{1... | collective-permute-start | bytes 294920 | tf_op jit(solution)/shard_map/ppermute | solution.py:19
  39.9 6.6 %shard_map.60 = (bf16[96,896]{1,0:T(8,128)(2,1)S(1)}, bf16[896,6144]{1,0:T(8,128)(2,1)S(1)}) custom-call(bf16[32,6144]{1,0:T(8,128)(2,1)S(1)} %collective-permute-done.4.refs_0_, bf16[32,6144]{1,0:T(8,128)(2,1)S(1)} %collective-permute-done.5.refs_1_, bf16[16,6144]{1,0:T(8,128)(2,1)S(1)} %collective-permute-done.7.refs_2_, ...), custom_call_target="tpu_custom_call" | custom-call | flops 2113929216 | bytes 11010048 | tf_op jit(solution)/shard_map/pallas_call | solution.py:81
  46.5 1.4 %collective-permute-done.11.far_up = bf16[16,3072]{1,0:T(8,128)(2,1)S(1)} collective-permute-done((bf16[16,3072]{1,0:T(8,128)(2,1)S(1)}, bf16[16,3072]{1,0:T(8,128)(2,1)S(1)}, u32[]{:S(2)}, u32[]{:S(2)}) %collective-permute-start.11) | collective-permute-done | bytes 98336 | tf_op jit(solution)/shard_map/ppermute | solution.py:19
  47.9 6.6 %shard_map.62 = (bf16[16,12288]{1,0:T(8,128)(2,1)S(1)}, bf16[16,12288]{1,0:T(8,128)(2,1)S(1)}) custom-call(bf16[16,9216]{1,0:T(8,128)(2,1)S(1)} %collective-permute-done.9.two_up, bf16[16,9216]{1,0:T(8,128)(2,1)S(1)} %collective-permute-done.10.two_down, bf16[16,3072]{1,0:T(8,128)(2,1)S(1)} %collective-permute-done.11.far_up, ...), custom_call_target="tpu_custom_call" | custom-call | flops 2113929216 | tf_op jit(solution)/shard_map/pallas_call | solution.py:117
  54.5 0.1 collective-permute-start.13
  54.6 3.2 %collective-permute-start.14 = (bf16[16,12288]{1,0:T(8,128)(2,1)S(1)}, bf16[16,12288]{1,0:T(8,128)(2,1)S(1)}, u32[]{:S(2)}, u32[]{:S(2)}) collective-permute-start(bf16[16,12288]{1,0:T(8,128)(2,1)S(1)} %get-tuple-element.59), channel_id=1, source_target_pairs={{0,12},{1,13},{2,14},{3,15},{4,0},{5,1},{6,2},{7,3},{8,4},{9,5},{1... | collective-permute-start | bytes 1179656 | tf_op jit(solution)/shard_map/ppermute | solution.py:19
  57.8 4.1 %copy-done.1 = bf16[896,6144]{1,0:T(8,128)(2,1)S(1)} copy-done((bf16[896,6144]{1,0:T(8,128)(2,1)S(1)}, bf16[896,6144]{1,0:T(8,128)(2,1)}, u32[]{:S(2)}) %copy-start.1) | copy-done | bytes 11010072
  62.0 3.6 %shard_map.61 = (f32[16,6144]{1,0:T(8,128)S(1)}, f32[16,6144]{1,0:T(8,128)S(1)}, f32[16,6144]{1,0:T(8,128)S(1)}, f32[32,6144]{1,0:T(8,128)S(1)}, f32[16,6144]{1,...) custom-call(bf16[96,896]{1,0:T(8,128)(2,1)S(1)} %shard_map.59.early,, ...), custom_call_target="tpu_custom_call" | custom-call | flops 2113929216 | tf_op jit(solution)/shard_map/pallas_call | solution.py:147
  65.7 0.7 collective-permute-done.13
  66.6 0.1 collective-permute-start.19
  66.7 3.3 %collective-permute-start.20 = (bf16[16,6144]{1,0:T(8,128)(2,1)S(1)}, bf16[16,6144]{1,0:T(8,128)(2,1)S(1)}, u32[]{:S(2)}, u32[]{:S(2)}) collective-permute-start(bf16[16,6144]{1,0:T(8,128)(2,1)S(1)} %pad_maximum_fusion.8), channel_id=1, source_target_pairs={{0,12},{1,13},{2,14},{3,15},{4,0},{5,1},{6,2},{7,3},{8,4},{9,5},{1... | collective-permute-start | bytes 589832 | tf_op jit(solution)/shard_map/ppermute | solution.py:19
  70.0 1.8 %collective-permute-start.16 = (bf16[32,6144]{1,0:T(8,128)(2,1)S(1)}, bf16[32,6144]{1,0:T(8,128)(2,1)S(1)}, u32[]{:S(2)}, u32[]{:S(2)}) collective-permute-start(bf16[32,6144]{1,0:T(8,128)(2,1)S(1)} %pad_maximum_fusion.2), channel_id=1, source_target_pairs={{0,12},{1,13},{2,14},{3,15},{4,0},{5,1},{6,2},{7,3},{8,4},{9,5},{1... | collective-permute-start | bytes 1179656 | tf_op jit(solution)/shard_map/ppermute | solution.py:19
  71.9 0.4 collective-permute-start.15
  72.3 1.5 %collective-permute-done.19 = bf16[16,6144]{1,0:T(8,128)(2,1)S(1)} collective-permute-done((bf16[16,6144]{1,0:T(8,128)(2,1)S(1)}, bf16[16,6144]{1,0:T(8,128)(2,1)S(1)}, u32[]{:S(2)}, u32[]{:S(2)}) %collective-permute-start.19) | collective-permute-done | bytes 196640 | tf_op jit(solution)/shard_map/ppermute | solution.py:19
  73.7 1.6 %collective-permute-done.20 = bf16[16,6144]{1,0:T(8,128)(2,1)S(1)} collective-permute-done((bf16[16,6144]{1,0:T(8,128)(2,1)S(1)}, bf16[16,6144]{1,0:T(8,128)(2,1)S(1)}, u32[]{:S(2)}, u32[]{:S(2)}) %collective-permute-start.20) | collective-permute-done | bytes 196640 | tf_op jit(solution)/shard_map/ppermute | solution.py:19
  75.3 0.1 add_convert_fusion.2
  75.4 1.5 %collective-permute-start.21 = (bf16[16,6144]{1,0:T(8,128)(2,1)S(1)}, bf16[16,6144]{1,0:T(8,128)(2,1)S(1)}, u32[]{:S(2)}, u32[]{:S(2)}) collective-permute-start(bf16[16,6144]{1,0:T(8,128)(2,1)S(1)} %add_convert_fusion.2), channel_id=1, source_target_pairs={{0,2},{1,3},{2,0},{3,1},{4,6},{5,7},{6,4},{7,5},{8,10},{9,11},{10,... | collective-permute-start | bytes 589832 | tf_op jit(solution)/shard_map/ppermute | solution.py:19
  76.9 4.2 %collective-permute-done.16 = bf16[32,6144]{1,0:T(8,128)(2,1)S(1)} collective-permute-done((bf16[32,6144]{1,0:T(8,128)(2,1)S(1)}, bf16[32,6144]{1,0:T(8,128)(2,1)S(1)}, u32[]{:S(2)}, u32[]{:S(2)}) %collective-permute-start.16) | collective-permute-done | bytes 393248 | tf_op jit(solution)/shard_map/ppermute | solution.py:19
  81.1 0.9 collective-permute-done.15
  82.0 0.1 add_convert_fusion
  82.1 0.3 collective-permute-start.22
  82.4 4.1 %collective-permute-start.23 = (bf16[16,6144]{1,0:T(8,128)(2,1)S(1)}, bf16[16,6144]{1,0:T(8,128)(2,1)S(1)}, u32[]{:S(2)}, u32[]{:S(2)}) collective-permute-start(bf16[16,6144]{1,0:T(8,128)(2,1)S(1)} %get-tuple-element.78), channel_id=1, source_target_pairs={{0,3},{1,0},{2,1},{3,2},{4,7},{5,4},{6,5},{7,6},{8,11},{9,8},{10,9... | collective-permute-start | bytes 589832 | tf_op jit(solution)/shard_map/ppermute | solution.py:19
  86.6 0.7 collective-permute-start.17
  87.3 2.5 %collective-permute-start.18 = (bf16[16,6144]{1,0:T(8,128)(2,1)S(1)}, bf16[16,6144]{1,0:T(8,128)(2,1)S(1)}, u32[]{:S(2)}, u32[]{:S(2)}) collective-permute-start(bf16[16,6144]{1,0:T(8,128)(2,1)S(1)} %pad_maximum_fusion.6), channel_id=1, source_target_pairs={{0,12},{1,13},{2,14},{3,15},{4,0},{5,1},{6,2},{7,3},{8,4},{9,5},{1... | collective-permute-start | bytes 589832 | tf_op jit(solution)/shard_map/ppermute | solution.py:19
  89.8 4.2 %collective-permute-done.22 = bf16[16,6144]{1,0:T(8,128)(2,1)S(1)} collective-permute-done((bf16[16,6144]{1,0:T(8,128)(2,1)S(1)}, bf16[16,6144]{1,0:T(8,128)(2,1)S(1)}, u32[]{:S(2)}, u32[]{:S(2)}) %collective-permute-start.22) | collective-permute-done | bytes 196640 | tf_op jit(solution)/shard_map/ppermute | solution.py:19
  94.0 0.1 collective-permute-done.23
  94.1 0.8 add_convert_fusion.1
  (43 shorter events, 0.6 us)
Async XLA Ops:
  1.1 16.1 %collective-permute-start = (bf16[16,6144]{1,0:T(8,128)(2,1)S(1)}, bf16[16,6144]{1,0:T(8,128)(2,1)S(1)}, u32[]{:S(2)}, u32[]{:S(2)}) collective-permute-start(bf16[16,6144]{1,0:T(8,128)(2,1)S(1)} %shard_map.55.refs_0_), channel_id=1, source_target_pairs={{0,1},{1,2},{2,3},{3,0},{4,5},{5,6},{6,7},{7,4},{8,9},{9,10},{10,1... | collective-permute-start | bytes 589832 | tf_op jit(solution)/shard_map/ppermute | solution.py:19
  4.5 12.7 %collective-permute-start.1 = (bf16[16,6144]{1,0:T(8,128)(2,1)S(1)}, bf16[16,6144]{1,0:T(8,128)(2,1)S(1)}, u32[]{:S(2)}, u32[]{:S(2)}) collective-permute-start(bf16[16,6144]{1,0:T(8,128)(2,1)S(1)} %shard_map.55.refs_0_), channel_id=1, source_target_pairs={{0,3},{1,0},{2,1},{3,2},{4,7},{5,4},{6,5},{7,6},{8,11},{9,8},{10,9... | collective-permute-start | bytes 589832 | tf_op jit(solution)/shard_map/ppermute | solution.py:19
  7.6 11.2 %collective-permute-start.2 = (bf16[16,6144]{1,0:T(8,128)(2,1)S(1)}, bf16[16,6144]{1,0:T(8,128)(2,1)S(1)}, u32[]{:S(2)}, u32[]{:S(2)}) collective-permute-start(bf16[16,6144]{1,0:T(8,128)(2,1)S(1)} %shard_map.55.refs_0_), channel_id=1, source_target_pairs={{0,4},{1,5},{2,6},{3,7},{4,8},{5,9},{6,10},{7,11},{8,12},{9,13},{1... | collective-permute-start | bytes 589832 | tf_op jit(solution)/shard_map/ppermute | solution.py:19
  9.1 9.7 %collective-permute-start.3 = (bf16[16,6144]{1,0:T(8,128)(2,1)S(1)}, bf16[16,6144]{1,0:T(8,128)(2,1)S(1)}, u32[]{:S(2)}, u32[]{:S(2)}) collective-permute-start(bf16[16,6144]{1,0:T(8,128)(2,1)S(1)} %shard_map.55.refs_0_), channel_id=1, source_target_pairs={{0,12},{1,13},{2,14},{3,15},{4,0},{5,1},{6,2},{7,3},{8,4},{9,5},{1... | collective-permute-start | bytes 589832 | tf_op jit(solution)/shard_map/ppermute | solution.py:19
  17.2 8.7 %collective-permute-start.6 = (bf16[16,6144]{1,0:T(8,128)(2,1)S(1)}, bf16[16,6144]{1,0:T(8,128)(2,1)S(1)}, u32[]{:S(2)}, u32[]{:S(2)}) collective-permute-start(bf16[16,6144]{1,0:T(8,128)(2,1)S(1)} %collective-permute-done.refs_3_), channel_id=1, source_target_pairs={{0,1},{1,2},{2,3},{3,0},{4,5},{5,6},{6,7},{7,4},{8,9},{9,10},{10,1... | collective-permute-start | bytes 589832 | tf_op jit(solution)/shard_map/ppermute | solution.py:19
  18.8 14.0 %collective-permute-start.4 = (bf16[32,6144]{1,0:T(8,128)(2,1)S(1)}, bf16[32,6144]{1,0:T(8,128)(2,1)S(1)}, u32[]{:S(2)}, u32[]{:S(2)}) collective-permute-start(bf16[32,6144]{1,0:T(8,128)(2,1)S(1)} %pad_maximum_fusion), channel_id=1, source_target_pairs={{0,4},{1,5},{2,6},{3,7},{4,8},{5,9},{6,10},{7,11},{8,12},{9,13},{1... | collective-permute-start | bytes 1179656 | tf_op jit(solution)/shard_map/ppermute | solution.py:19
  20.4 12.5 %collective-permute-start.5 = (bf16[32,6144]{1,0:T(8,128)(2,1)S(1)}, bf16[32,6144]{1,0:T(8,128)(2,1)S(1)}, u32[]{:S(2)}, u32[]{:S(2)}) collective-permute-start(bf16[32,6144]{1,0:T(8,128)(2,1)S(1)} %pad_maximum_fusion), channel_id=1, source_target_pairs={{0,12},{1,13},{2,14},{3,15},{4,0},{5,1},{6,2},{7,3},{8,4},{9,5},{1... | collective-permute-start | bytes 1179656 | tf_op jit(solution)/shard_map/ppermute | solution.py:19
  26.0 9.8 %collective-permute-start.7 = (bf16[16,6144]{1,0:T(8,128)(2,1)S(1)}, bf16[16,6144]{1,0:T(8,128)(2,1)S(1)}, u32[]{:S(2)}, u32[]{:S(2)}) collective-permute-start(bf16[16,6144]{1,0:T(8,128)(2,1)S(1)} %collective-permute-done.6.refs_5_), channel_id=1, source_target_pairs={{0,4},{1,5},{2,6},{3,7},{4,8},{5,9},{6,10},{7,11},{8,12},{9,13},{1... | collective-permute-start | bytes 589832 | tf_op jit(solution)/shard_map/ppermute | solution.py:19
  26.6 9.7 %collective-permute-start.8 = (bf16[16,6144]{1,0:T(8,128)(2,1)S(1)}, bf16[16,6144]{1,0:T(8,128)(2,1)S(1)}, u32[]{:S(2)}, u32[]{:S(2)}) collective-permute-start(bf16[16,6144]{1,0:T(8,128)(2,1)S(1)} %collective-permute-done.6.refs_5_), channel_id=1, source_target_pairs={{0,12},{1,13},{2,14},{3,15},{4,0},{5,1},{6,2},{7,3},{8,4},{9,5},{1... | collective-permute-start | bytes 589832 | tf_op jit(solution)/shard_map/ppermute | solution.py:19
  32.9 15.0 %collective-permute-start.10 = (bf16[16,9216]{1,0:T(8,128)(2,1)S(1)}, bf16[16,9216]{1,0:T(8,128)(2,1)S(1)}, u32[]{:S(2)}, u32[]{:S(2)}) collective-permute-start(bf16[16,9216]{1,0:T(8,128)(2,1)S(1)} %pad_maximum_fusion.4), channel_id=1, source_target_pairs={{0,12},{1,13},{2,14},{3,15},{4,0},{5,1},{6,2},{7,3},{8,4},{9,5},{1... | collective-permute-start | bytes 884744 | tf_op jit(solution)/shard_map/ppermute | solution.py:19
  35.2 12.7 %collective-permute-start.9 = (bf16[16,9216]{1,0:T(8,128)(2,1)S(1)}, bf16[16,9216]{1,0:T(8,128)(2,1)S(1)}, u32[]{:S(2)}, u32[]{:S(2)}) collective-permute-start(bf16[16,9216]{1,0:T(8,128)(2,1)S(1)} %pad_maximum_fusion.3), channel_id=1, source_target_pairs={{0,4},{1,5},{2,6},{3,7},{4,8},{5,9},{6,10},{7,11},{8,12},{9,13},{1... | collective-permute-start | bytes 884744 | tf_op jit(solution)/shard_map/ppermute | solution.py:19
  36.3 11.6 %collective-permute-start.11 = (bf16[16,3072]{1,0:T(8,128)(2,1)S(1)}, bf16[16,3072]{1,0:T(8,128)(2,1)S(1)}, u32[]{:S(2)}, u32[]{:S(2)}) collective-permute-start(bf16[16,3072]{1,0:T(8,128)(2,1)S(1)} %slice.89), channel_id=1, source_target_pairs={{0,4},{1,5},{2,6},{3,7},{4,8},{5,9},{6,10},{7,11},{8,12},{9,13},{1... | collective-permute-start | bytes 294920 | tf_op jit(solution)/shard_map/ppermute | solution.py:19
  37.9 10.0 %collective-permute-start.12 = (bf16[16,3072]{1,0:T(8,128)(2,1)S(1)}, bf16[16,3072]{1,0:T(8,128)(2,1)S(1)}, u32[]{:S(2)}, u32[]{:S(2)}) collective-permute-start(bf16[16,3072]{1,0:T(8,128)(2,1)S(1)} %slice.90), channel_id=1, source_target_pairs={{0,12},{1,13},{2,14},{3,15},{4,0},{5,1},{6,2},{7,3},{8,4},{9,5},{1... | collective-permute-start | bytes 294920 | tf_op jit(solution)/shard_map/ppermute | solution.py:19
  46.5 8.0 %copy-start = (bf16[896,6144]{1,0:T(8,128)(2,1)}, bf16[896,6144]{1,0:T(8,128)(2,1)S(1)}, u32[]{:S(2)}) copy-start(bf16[896,6144]{1,0:T(8,128)(2,1)S(1)} %get-tuple-element.55.down_w) | copy-start | bytes 33030148
  54.5 11.9 %collective-permute-start.13 = (bf16[16,12288]{1,0:T(8,128)(2,1)S(1)}, bf16[16,12288]{1,0:T(8,128)(2,1)S(1)}, u32[]{:S(2)}, u32[]{:S(2)}) collective-permute-start(bf16[16,12288]{1,0:T(8,128)(2,1)S(1)} %get-tuple-element.58), channel_id=1, source_target_pairs={{0,4},{1,5},{2,6},{3,7},{4,8},{5,9},{6,10},{7,11},{8,12},{9,13},{1... | collective-permute-start | bytes 1179656 | tf_op jit(solution)/shard_map/ppermute | solution.py:19
  54.6 11.8 %collective-permute-start.14 = (bf16[16,12288]{1,0:T(8,128)(2,1)S(1)}, bf16[16,12288]{1,0:T(8,128)(2,1)S(1)}, u32[]{:S(2)}, u32[]{:S(2)}) collective-permute-start(bf16[16,12288]{1,0:T(8,128)(2,1)S(1)} %get-tuple-element.59), channel_id=1, source_target_pairs={{0,12},{1,13},{2,14},{3,15},{4,0},{5,1},{6,2},{7,3},{8,4},{9,5},{1... | collective-permute-start | bytes 1179656 | tf_op jit(solution)/shard_map/ppermute | solution.py:19
  57.8 4.1 %copy-start.1 = (bf16[896,6144]{1,0:T(8,128)(2,1)S(1)}, bf16[896,6144]{1,0:T(8,128)(2,1)}, u32[]{:S(2)}) copy-start(bf16[896,6144]{1,0:T(8,128)(2,1)} %copy-done) | copy-start | bytes 33030148
  62.0 32.1 %copy-start.2 = (bf16[16,6144]{1,0:T(8,128)(2,1)S(1)}, bf16[16,6144]{1,0:T(8,128)(2,1)}, u32[]{:S(2)}) copy-start(bf16[16,6144]{1,0:T(8,128)(2,1)} %rows_ref.1) | copy-start | bytes 589828
  66.6 7.2 %collective-permute-start.19 = (bf16[16,6144]{1,0:T(8,128)(2,1)S(1)}, bf16[16,6144]{1,0:T(8,128)(2,1)S(1)}, u32[]{:S(2)}, u32[]{:S(2)}) collective-permute-start(bf16[16,6144]{1,0:T(8,128)(2,1)S(1)} %pad_maximum_fusion.7), channel_id=1, source_target_pairs={{0,4},{1,5},{2,6},{3,7},{4,8},{5,9},{6,10},{7,11},{8,12},{9,13},{1... | collective-permute-start | bytes 589832 | tf_op jit(solution)/shard_map/ppermute | solution.py:19
  66.7 8.7 %collective-permute-start.20 = (bf16[16,6144]{1,0:T(8,128)(2,1)S(1)}, bf16[16,6144]{1,0:T(8,128)(2,1)S(1)}, u32[]{:S(2)}, u32[]{:S(2)}) collective-permute-start(bf16[16,6144]{1,0:T(8,128)(2,1)S(1)} %pad_maximum_fusion.8), channel_id=1, source_target_pairs={{0,12},{1,13},{2,14},{3,15},{4,0},{5,1},{6,2},{7,3},{8,4},{9,5},{1... | collective-permute-start | bytes 589832 | tf_op jit(solution)/shard_map/ppermute | solution.py:19
  70.0 11.1 %collective-permute-start.16 = (bf16[32,6144]{1,0:T(8,128)(2,1)S(1)}, bf16[32,6144]{1,0:T(8,128)(2,1)S(1)}, u32[]{:S(2)}, u32[]{:S(2)}) collective-permute-start(bf16[32,6144]{1,0:T(8,128)(2,1)S(1)} %pad_maximum_fusion.2), channel_id=1, source_target_pairs={{0,12},{1,13},{2,14},{3,15},{4,0},{5,1},{6,2},{7,3},{8,4},{9,5},{1... | collective-permute-start | bytes 1179656 | tf_op jit(solution)/shard_map/ppermute | solution.py:19
  71.9 10.1 %collective-permute-start.15 = (bf16[32,6144]{1,0:T(8,128)(2,1)S(1)}, bf16[32,6144]{1,0:T(8,128)(2,1)S(1)}, u32[]{:S(2)}, u32[]{:S(2)}) collective-permute-start(bf16[32,6144]{1,0:T(8,128)(2,1)S(1)} %pad_maximum_fusion.1), channel_id=1, source_target_pairs={{0,4},{1,5},{2,6},{3,7},{4,8},{5,9},{6,10},{7,11},{8,12},{9,13},{1... | collective-permute-start | bytes 1179656 | tf_op jit(solution)/shard_map/ppermute | solution.py:19
  75.4 14.4 %collective-permute-start.21 = (bf16[16,6144]{1,0:T(8,128)(2,1)S(1)}, bf16[16,6144]{1,0:T(8,128)(2,1)S(1)}, u32[]{:S(2)}, u32[]{:S(2)}) collective-permute-start(bf16[16,6144]{1,0:T(8,128)(2,1)S(1)} %add_convert_fusion.2), channel_id=1, source_target_pairs={{0,2},{1,3},{2,0},{3,1},{4,6},{5,7},{6,4},{7,5},{8,10},{9,11},{10,... | collective-permute-start | bytes 589832 | tf_op jit(solution)/shard_map/ppermute | solution.py:19
  82.1 11.9 %collective-permute-start.22 = (bf16[16,6144]{1,0:T(8,128)(2,1)S(1)}, bf16[16,6144]{1,0:T(8,128)(2,1)S(1)}, u32[]{:S(2)}, u32[]{:S(2)}) collective-permute-start(bf16[16,6144]{1,0:T(8,128)(2,1)S(1)} %get-tuple-element.77), channel_id=1, source_target_pairs={{0,1},{1,2},{2,3},{3,0},{4,5},{5,6},{6,7},{7,4},{8,9},{9,10},{10,1... | collective-permute-start | bytes 589832 | tf_op jit(solution)/shard_map/ppermute | solution.py:19
  82.4 11.6 %collective-permute-start.23 = (bf16[16,6144]{1,0:T(8,128)(2,1)S(1)}, bf16[16,6144]{1,0:T(8,128)(2,1)S(1)}, u32[]{:S(2)}, u32[]{:S(2)}) collective-permute-start(bf16[16,6144]{1,0:T(8,128)(2,1)S(1)} %get-tuple-element.78), channel_id=1, source_target_pairs={{0,3},{1,0},{2,1},{3,2},{4,7},{5,4},{6,5},{7,6},{8,11},{9,8},{10,9... | collective-permute-start | bytes 589832 | tf_op jit(solution)/shard_map/ppermute | solution.py:19
  86.6 7.5 %collective-permute-start.17 = (bf16[16,6144]{1,0:T(8,128)(2,1)S(1)}, bf16[16,6144]{1,0:T(8,128)(2,1)S(1)}, u32[]{:S(2)}, u32[]{:S(2)}) collective-permute-start(bf16[16,6144]{1,0:T(8,128)(2,1)S(1)} %pad_maximum_fusion.5), channel_id=1, source_target_pairs={{0,4},{1,5},{2,6},{3,7},{4,8},{5,9},{6,10},{7,11},{8,12},{9,13},{1... | collective-permute-start | bytes 589832 | tf_op jit(solution)/shard_map/ppermute | solution.py:19
  87.3 6.8 %collective-permute-start.18 = (bf16[16,6144]{1,0:T(8,128)(2,1)S(1)}, bf16[16,6144]{1,0:T(8,128)(2,1)S(1)}, u32[]{:S(2)}, u32[]{:S(2)}) collective-permute-start(bf16[16,6144]{1,0:T(8,128)(2,1)S(1)} %pad_maximum_fusion.6), channel_id=1, source_target_pairs={{0,12},{1,13},{2,14},{3,15},{4,0},{5,1},{6,2},{7,3},{8,4},{9,5},{1... | collective-permute-start | bytes 589832 | tf_op jit(solution)/shard_map/ppermute | solution.py:19

commit v11 on v8

--- a/solution.py
+++ b/solution.py
@@ -209,12 +209,14 @@
     near_p, near_m = shift(near_right, 1, 0), shift(near_left, -1, 0)
     own_right = jnp.concatenate([b16(own_right[:, :h] + f32(two_up[:, d : d + h])), b16(own_right[:, h:])], 1)
     own_left = jnp.concatenate([b16(own_left[:, :h]), b16(own_left[:, h:] + f32(two_down[:, d : d + h]))], 1)
-    own_right, own_left, near_p, near_m = lax.optimization_barrier((own_right, own_left, near_p, near_m))
+    near_p, near_m = lax.optimization_barrier((near_p, near_m))
+    far_p, far_m, _, _ = lax.optimization_barrier((far_p, far_m, near_p, near_m))
     far_sum = shift(b16(far_here + f32(far_p) + f32(far_m)), 0, 2)
+    own_right, own_left, far_p, far_m = lax.optimization_barrier((own_right, own_left, far_p, far_m))
     own_p, own_m = shift(own_right, 1, 0), shift(own_left, -1, 0)
     near_sum = b16(near_here + f32(near_p) + f32(near_m))
     from_below, from_above = shift(near_sum[n:], 0, 1), shift(near_sum[:n], 0, -1)
-    return own_here + f32(own_p) + f32(own_m) + f32(far_sum) + f32(from_below) + f32(from_above)
+    return own_here + f32(from_below) + f32(from_above) + f32(far_sum) + f32(own_p) + f32(own_m)
 
 
 def on_device(tokens, norm_gain, gate_weight, up_weight, down_weight):

time: 94.1 us -> 99.7 us (1.060)
  the two profiles are of different devices: /device:TPU:8 before, /device:TPU:56 now
where the time goes in v11:
time: 99.7 us; the launch traced here: 99.5 us
  starting transfers between devices  41.1 us (41%)
  Pallas kernels  28.3 us (28%)
  waiting for transfers between devices  28.2 us (28%)
  other arithmetic  1.39 us (1%)
    ppermute x24, starting transfers between devices, shift(): return lax.ppermute(block, ('dp', 'tensor'), pairs)  41.1 us
    ppermute x24, waiting for transfers between devices, shift(): return lax.ppermute(block, ('dp', 'tensor'), pairs)  28.2 us
    pallas_call x3, Pallas kernels, fetched(): pl.pallas_call(kernel, out_shape=pltpu.VMEM((size, weight.shape[1]), weig...  9.28 us
    pallas_call x2, Pallas kernels, hidden_units(): pl.pallas_call(kernel, out_shape=[pltpu.VMEM((tall, ff), b)] + [pltpu.VME...  7.79 us
    pallas_call x1, Pallas kernels, two_hops(): pl.pallas_call(kernel, out_shape=[pltpu.VMEM((n, 2 * d), b)] * 2, in_spec...  6.5 us
    pallas_call x1, Pallas kernels, other_terms(): pl.pallas_call(kernel, out_shape=[pltpu.VMEM((k * n, d), jnp.float32) for...  3.58 us
  transfers between devices with their start and end apart: 24, of which 6 were waited for; matrix products, arithmetic and copies ran while one was open for 1% of the time, Pallas kernels for 21%

profile of v11, /device:TPU:56, one launch (start us, length us, event | category | flops | bytes accessed | tf_op | source)
XLA Modules:
  0.0 99.5 jit_solution(6178140057700871489)
XLA Ops:
  0.0 1.1 %shard_map.55.refs_0_ = bf16[16,6144]{1,0:T(8,128)(2,1)S(1)} custom-call(bf16[16,6144]{1,0:T(8,128)(2,1)} %rows_ref.1, f32[1,6144]{1,0:T(1,128)} %bitcast.1), custom_call_target="tpu_custom_call" | custom-call | tf_op jit(solution)/shard_map/pallas_call | solution.py:37
  1.1 3.3 %collective-permute-start = (bf16[16,6144]{1,0:T(8,128)(2,1)S(1)}, bf16[16,6144]{1,0:T(8,128)(2,1)S(1)}, u32[]{:S(2)}, u32[]{:S(2)}) collective-permute-start(bf16[16,6144]{1,0:T(8,128)(2,1)S(1)} %shard_map.55.refs_0_), channel_id=1, source_target_pairs={{0,1},{1,2},{2,3},{3,0},{4,5},{5,6},{6,7},{7,4},{8,9},{9,10},{10,1... | collective-permute-start | bytes 589832 | tf_op jit(solution)/shard_map/ppermute | solution.py:19
  4.5 2.2 %collective-permute-start.1 = (bf16[16,6144]{1,0:T(8,128)(2,1)S(1)}, bf16[16,6144]{1,0:T(8,128)(2,1)S(1)}, u32[]{:S(2)}, u32[]{:S(2)}) collective-permute-start(bf16[16,6144]{1,0:T(8,128)(2,1)S(1)} %shard_map.55.refs_0_), channel_id=1, source_target_pairs={{0,3},{1,0},{2,1},{3,2},{4,7},{5,4},{6,5},{7,6},{8,11},{9,8},{10,9... | collective-permute-start | bytes 589832 | tf_op jit(solution)/shard_map/ppermute | solution.py:19
  6.7 1.5 %collective-permute-start.2 = (bf16[16,6144]{1,0:T(8,128)(2,1)S(1)}, bf16[16,6144]{1,0:T(8,128)(2,1)S(1)}, u32[]{:S(2)}, u32[]{:S(2)}) collective-permute-start(bf16[16,6144]{1,0:T(8,128)(2,1)S(1)} %shard_map.55.refs_0_), channel_id=1, source_target_pairs={{0,4},{1,5},{2,6},{3,7},{4,8},{5,9},{6,10},{7,11},{8,12},{9,13},{1... | collective-permute-start | bytes 589832 | tf_op jit(solution)/shard_map/ppermute | solution.py:19
  8.2 1.7 %collective-permute-start.3 = (bf16[16,6144]{1,0:T(8,128)(2,1)S(1)}, bf16[16,6144]{1,0:T(8,128)(2,1)S(1)}, u32[]{:S(2)}, u32[]{:S(2)}) collective-permute-start(bf16[16,6144]{1,0:T(8,128)(2,1)S(1)} %shard_map.55.refs_0_), channel_id=1, source_target_pairs={{0,12},{1,13},{2,14},{3,15},{4,0},{5,1},{6,2},{7,3},{8,4},{9,5},{1... | collective-permute-start | bytes 589832 | tf_op jit(solution)/shard_map/ppermute | solution.py:19
  9.9 4.1 %shard_map.56.refs_6_.refs_4_.gate_w = bf16[6144,896]{1,0:T(8,128)(2,1)S(1)} custom-call(bf16[6144,896]{1,0:T(8,128)(2,1)} %source.2), custom_call_target="tpu_custom_call" | custom-call | bytes 11010048 | tf_op jit(solution)/shard_map/pallas_call | solution.py:165
  14.1 2.6 %shard_map.57.refs_7_.refs_5_.up_w = bf16[3072,896]{1,0:T(8,128)(2,1)S(1)} custom-call(bf16[6144,896]{1,0:T(8,128)(2,1)} %source.4), custom_call_target="tpu_custom_call" | custom-call | bytes 5505024 | tf_op jit(solution)/shard_map/pallas_call | solution.py:165
  16.7 0.0 collective-permute-done.1.refs_4_
  16.7 1.4 %collective-permute-start.6 = (bf16[16,6144]{1,0:T(8,128)(2,1)S(1)}, bf16[16,6144]{1,0:T(8,128)(2,1)S(1)}, u32[]{:S(2)}, u32[]{:S(2)}) collective-permute-start(bf16[16,6144]{1,0:T(8,128)(2,1)S(1)} %collective-permute-done.refs_3_), channel_id=1, source_target_pairs={{0,1},{1,2},{2,3},{3,0},{4,5},{5,6},{6,7},{7,4},{8,9},{9,10},{10,1... | collective-permute-start | bytes 589832 | tf_op jit(solution)/shard_map/ppermute | solution.py:19
  18.2 1.1 %collective-permute-start.4 = (bf16[32,6144]{1,0:T(8,128)(2,1)S(1)}, bf16[32,6144]{1,0:T(8,128)(2,1)S(1)}, u32[]{:S(2)}, u32[]{:S(2)}) collective-permute-start(bf16[32,6144]{1,0:T(8,128)(2,1)S(1)} %pad_maximum_fusion), channel_id=1, source_target_pairs={{0,4},{1,5},{2,6},{3,7},{4,8},{5,9},{6,10},{7,11},{8,12},{9,13},{1... | collective-permute-start | bytes 1179656 | tf_op jit(solution)/shard_map/ppermute | solution.py:19
  19.2 2.3 %collective-permute-start.5 = (bf16[32,6144]{1,0:T(8,128)(2,1)S(1)}, bf16[32,6144]{1,0:T(8,128)(2,1)S(1)}, u32[]{:S(2)}, u32[]{:S(2)}) collective-permute-start(bf16[32,6144]{1,0:T(8,128)(2,1)S(1)} %pad_maximum_fusion), channel_id=1, source_target_pairs={{0,12},{1,13},{2,14},{3,15},{4,0},{5,1},{6,2},{7,3},{8,4},{9,5},{1... | collective-permute-start | bytes 1179656 | tf_op jit(solution)/shard_map/ppermute | solution.py:19
  21.5 2.6 %shard_map.58.refs_8_.refs_6_.up_w2 = bf16[3072,896]{1,0:T(8,128)(2,1)S(1)} custom-call(bf16[6144,896]{1,0:T(8,128)(2,1)} %source.4), custom_call_target="tpu_custom_call" | custom-call | bytes 5505024 | tf_op jit(solution)/shard_map/pallas_call | solution.py:165
  24.1 2.5 %collective-permute-done.6.refs_5_ = bf16[16,6144]{1,0:T(8,128)(2,1)S(1)} collective-permute-done((bf16[16,6144]{1,0:T(8,128)(2,1)S(1)}, bf16[16,6144]{1,0:T(8,128)(2,1)S(1)}, u32[]{:S(2)}, u32[]{:S(2)}) %collective-permute-start.6) | collective-permute-done | bytes 196640 | tf_op jit(solution)/shard_map/ppermute | solution.py:19
  26.6 0.5 collective-permute-start.7
  27.1 2.7 %collective-permute-start.8 = (bf16[16,6144]{1,0:T(8,128)(2,1)S(1)}, bf16[16,6144]{1,0:T(8,128)(2,1)S(1)}, u32[]{:S(2)}, u32[]{:S(2)}) collective-permute-start(bf16[16,6144]{1,0:T(8,128)(2,1)S(1)} %collective-permute-done.6.refs_5_), channel_id=1, source_target_pairs={{0,12},{1,13},{2,14},{3,15},{4,0},{5,1},{6,2},{7,3},{8,4},{9,5},{1... | collective-permute-start | bytes 589832 | tf_op jit(solution)/shard_map/ppermute | solution.py:19
  29.9 3.6 %shard_map.59.early = bf16[96,896]{1,0:T(8,128)(2,1)S(1)} custom-call(bf16[16,6144]{1,0:T(8,128)(2,1)S(1)} %shard_map.55.refs_0_, bf16[16,6144]{1,0:T(8,128)(2,1)S(1)} %collective-permute-done.2.refs_1_, bf16[16,6144]{1,0:T(8,128)(2,1)S(1)} %collective-permute-done.3.refs_2_, bf16[16,6144]{1,0:T(8,128)(2,1)S(1)} %collective-permute-done.refs_3_, ...), custom_call_target="tpu_custom_call" | custom-call | flops 2113929216 | tf_op jit(solution)/shard_map/pallas_call | solution.py:80
  33.5 0.0 collective-permute-done.5.refs_1_
  33.6 1.2 %collective-permute-start.10 = (bf16[16,9216]{1,0:T(8,128)(2,1)S(1)}, bf16[16,9216]{1,0:T(8,128)(2,1)S(1)}, u32[]{:S(2)}, u32[]{:S(2)}) collective-permute-start(bf16[16,9216]{1,0:T(8,128)(2,1)S(1)} %pad_maximum_fusion.4), channel_id=1, source_target_pairs={{0,12},{1,13},{2,14},{3,15},{4,0},{5,1},{6,2},{7,3},{8,4},{9,5},{1... | collective-permute-start | bytes 884744 | tf_op jit(solution)/shard_map/ppermute | solution.py:19
  34.8 1.0 collective-permute-start.9
  35.8 1.2 %collective-permute-start.11 = (bf16[16,3072]{1,0:T(8,128)(2,1)S(1)}, bf16[16,3072]{1,0:T(8,128)(2,1)S(1)}, u32[]{:S(2)}, u32[]{:S(2)}) collective-permute-start(bf16[16,3072]{1,0:T(8,128)(2,1)S(1)} %slice.89), channel_id=1, source_target_pairs={{0,4},{1,5},{2,6},{3,7},{4,8},{5,9},{6,10},{7,11},{8,12},{9,13},{1... | collective-permute-start | bytes 294920 | tf_op jit(solution)/shard_map/ppermute | solution.py:19
  37.0 2.4 %collective-permute-start.12 = (bf16[16,3072]{1,0:T(8,128)(2,1)S(1)}, bf16[16,3072]{1,0:T(8,128)(2,1)S(1)}, u32[]{:S(2)}, u32[]{:S(2)}) collective-permute-start(bf16[16,3072]{1,0:T(8,128)(2,1)S(1)} %slice.90), channel_id=1, source_target_pairs={{0,12},{1,13},{2,14},{3,15},{4,0},{5,1},{6,2},{7,3},{8,4},{9,5},{1... | collective-permute-start | bytes 294920 | tf_op jit(solution)/shard_map/ppermute | solution.py:19
  39.4 4.1 %shard_map.60 = (bf16[96,896]{1,0:T(8,128)(2,1)S(1)}, bf16[896,6144]{1,0:T(8,128)(2,1)S(1)}) custom-call(bf16[32,6144]{1,0:T(8,128)(2,1)S(1)} %collective-permute-done.4.refs_0_, bf16[32,6144]{1,0:T(8,128)(2,1)S(1)} %collective-permute-done.5.refs_1_, bf16[16,6144]{1,0:T(8,128)(2,1)S(1)} %collective-permute-done.7.refs_2_, ...), custom_call_target="tpu_custom_call" | custom-call | flops 2113929216 | bytes 11010048 | tf_op jit(solution)/shard_map/pallas_call | solution.py:80
  43.6 3.2 %collective-permute-done.11.far_up = bf16[16,3072]{1,0:T(8,128)(2,1)S(1)} collective-permute-done((bf16[16,3072]{1,0:T(8,128)(2,1)S(1)}, bf16[16,3072]{1,0:T(8,128)(2,1)S(1)}, u32[]{:S(2)}, u32[]{:S(2)}) %collective-permute-start.11) | collective-permute-done | bytes 98336 | tf_op jit(solution)/shard_map/ppermute | solution.py:19
  46.7 0.0 collective-permute-done.9.two_up
  46.7 6.5 %shard_map.62 = (bf16[16,12288]{1,0:T(8,128)(2,1)S(1)}, bf16[16,12288]{1,0:T(8,128)(2,1)S(1)}) custom-call(bf16[16,9216]{1,0:T(8,128)(2,1)S(1)} %collective-permute-done.9.two_up, bf16[16,9216]{1,0:T(8,128)(2,1)S(1)} %collective-permute-done.10.two_down, bf16[16,3072]{1,0:T(8,128)(2,1)S(1)} %collective-permute-done.11.far_up, ...), custom_call_target="tpu_custom_call" | custom-call | flops 2113929216 | tf_op jit(solution)/shard_map/pallas_call | solution.py:116
  53.2 0.1 collective-permute-start.13
  53.3 3.2 %collective-permute-start.14 = (bf16[16,12288]{1,0:T(8,128)(2,1)S(1)}, bf16[16,12288]{1,0:T(8,128)(2,1)S(1)}, u32[]{:S(2)}, u32[]{:S(2)}) collective-permute-start(bf16[16,12288]{1,0:T(8,128)(2,1)S(1)} %get-tuple-element.62), channel_id=1, source_target_pairs={{0,12},{1,13},{2,14},{3,15},{4,0},{5,1},{6,2},{7,3},{8,4},{9,5},{1... | collective-permute-start | bytes 1179656 | tf_op jit(solution)/shard_map/ppermute | solution.py:19
  56.6 3.6 %shard_map.61 = (f32[16,6144]{1,0:T(8,128)S(1)}, f32[16,6144]{1,0:T(8,128)S(1)}, f32[16,6144]{1,0:T(8,128)S(1)}, f32[32,6144]{1,0:T(8,128)S(1)}, f32[16,6144]{1,...) custom-call(bf16[96,896]{1,0:T(8,128)(2,1)S(1)} %shard_map.59.early,, ...), custom_call_target="tpu_custom_call" | custom-call | flops 2113929216 | tf_op jit(solution)/shard_map/pallas_call | solution.py:146
  60.3 3.9 %collective-permute-done.13 = bf16[16,12288]{1,0:T(8,128)(2,1)S(1)} collective-permute-done((bf16[16,12288]{1,0:T(8,128)(2,1)S(1)}, bf16[16,12288]{1,0:T(8,128)(2,1)S(1)}, u32[]{:S(2)}, u32[]{:S(2)}) %collective-permute-start.13) | collective-permute-done | bytes 393248 | tf_op jit(solution)/shard_map/ppermute | solution.py:19
  64.2 0.0 collective-permute-done.14
  64.4 3.0 %collective-permute-start.16 = (bf16[32,6144]{1,0:T(8,128)(2,1)S(1)}, bf16[32,6144]{1,0:T(8,128)(2,1)S(1)}, u32[]{:S(2)}, u32[]{:S(2)}) collective-permute-start(bf16[32,6144]{1,0:T(8,128)(2,1)S(1)} %pad_maximum_fusion.2), channel_id=1, source_target_pairs={{0,12},{1,13},{2,14},{3,15},{4,0},{5,1},{6,2},{7,3},{8,4},{9,5},{1... | collective-permute-start | bytes 1179656 | tf_op jit(solution)/shard_map/ppermute | solution.py:19
  67.5 0.1 collective-permute-start.15
  67.6 3.3 %collective-permute-start.20 = (bf16[16,6144]{1,0:T(8,128)(2,1)S(1)}, bf16[16,6144]{1,0:T(8,128)(2,1)S(1)}, u32[]{:S(2)}, u32[]{:S(2)}) collective-permute-start(bf16[16,6144]{1,0:T(8,128)(2,1)S(1)} %pad_maximum_fusion.6), channel_id=1, source_target_pairs={{0,12},{1,13},{2,14},{3,15},{4,0},{5,1},{6,2},{7,3},{8,4},{9,5},{1... | collective-permute-start | bytes 589832 | tf_op jit(solution)/shard_map/ppermute | solution.py:19
  70.9 0.3 collective-permute-start.19
  71.3 4.3 %collective-permute-done.16 = bf16[32,6144]{1,0:T(8,128)(2,1)S(1)} collective-permute-done((bf16[32,6144]{1,0:T(8,128)(2,1)S(1)}, bf16[32,6144]{1,0:T(8,128)(2,1)S(1)}, u32[]{:S(2)}, u32[]{:S(2)}) %collective-permute-start.16) | collective-permute-done | bytes 393248 | tf_op jit(solution)/shard_map/ppermute | solution.py:19
  75.6 3.5 %collective-permute-done.15 = bf16[32,6144]{1,0:T(8,128)(2,1)S(1)} collective-permute-done((bf16[32,6144]{1,0:T(8,128)(2,1)S(1)}, bf16[32,6144]{1,0:T(8,128)(2,1)S(1)}, u32[]{:S(2)}, u32[]{:S(2)}) %collective-permute-start.15) | collective-permute-done | bytes 393248 | tf_op jit(solution)/shard_map/ppermute | solution.py:19
  79.1 0.1 add_convert_fusion
  79.2 0.1 collective-permute-start.17
  79.3 4.1 %collective-permute-start.18 = (bf16[16,6144]{1,0:T(8,128)(2,1)S(1)}, bf16[16,6144]{1,0:T(8,128)(2,1)S(1)}, u32[]{:S(2)}, u32[]{:S(2)}) collective-permute-start(bf16[16,6144]{1,0:T(8,128)(2,1)S(1)} %get-tuple-element.78), channel_id=1, source_target_pairs={{0,3},{1,0},{2,1},{3,2},{4,7},{5,4},{6,5},{7,6},{8,11},{9,8},{10,9... | collective-permute-start | bytes 589832 | tf_op jit(solution)/shard_map/ppermute | solution.py:19
  83.5 0.0 collective-permute-done.20
  83.5 0.0 collective-permute-done.19
  83.5 0.1 add_convert_fusion.2
  83.5 1.2 %collective-permute-start.21 = (bf16[16,6144]{1,0:T(8,128)(2,1)S(1)}, bf16[16,6144]{1,0:T(8,128)(2,1)S(1)}, u32[]{:S(2)}, u32[]{:S(2)}) collective-permute-start(bf16[16,6144]{1,0:T(8,128)(2,1)S(1)} %add_convert_fusion.2), channel_id=1, source_target_pairs={{0,2},{1,3},{2,0},{3,1},{4,6},{5,7},{6,4},{7,5},{8,10},{9,11},{10,... | collective-permute-start | bytes 589832 | tf_op jit(solution)/shard_map/ppermute | solution.py:19
  84.7 0.0 collective-permute-start.22
  84.7 3.2 %collective-permute-start.23 = (bf16[16,6144]{1,0:T(8,128)(2,1)S(1)}, bf16[16,6144]{1,0:T(8,128)(2,1)S(1)}, u32[]{:S(2)}, u32[]{:S(2)}) collective-permute-start(bf16[16,6144]{1,0:T(8,128)(2,1)S(1)} %pad_maximum_fusion.8), channel_id=1, source_target_pairs={{0,12},{1,13},{2,14},{3,15},{4,0},{5,1},{6,2},{7,3},{8,4},{9,5},{1... | collective-permute-start | bytes 589832 | tf_op jit(solution)/shard_map/ppermute | solution.py:19
  87.9 10.7 %collective-permute-done.17 = bf16[16,6144]{1,0:T(8,128)(2,1)S(1)} collective-permute-done((bf16[16,6144]{1,0:T(8,128)(2,1)S(1)}, bf16[16,6144]{1,0:T(8,128)(2,1)S(1)}, u32[]{:S(2)}, u32[]{:S(2)}) %collective-permute-start.17) | collective-permute-done | bytes 196640 | tf_op jit(solution)/shard_map/ppermute | solution.py:19
  98.6 0.0 collective-permute-done.22
  98.7 0.8 add_convert_fusion.1
  (39 shorter events, 0.6 us)
Async XLA Ops:
  1.1 15.5 %collective-permute-start = (bf16[16,6144]{1,0:T(8,128)(2,1)S(1)}, bf16[16,6144]{1,0:T(8,128)(2,1)S(1)}, u32[]{:S(2)}, u32[]{:S(2)}) collective-permute-start(bf16[16,6144]{1,0:T(8,128)(2,1)S(1)} %shard_map.55.refs_0_), channel_id=1, source_target_pairs={{0,1},{1,2},{2,3},{3,0},{4,5},{5,6},{6,7},{7,4},{8,9},{9,10},{10,1... | collective-permute-start | bytes 589832 | tf_op jit(solution)/shard_map/ppermute | solution.py:19
  4.5 12.2 %collective-permute-start.1 = (bf16[16,6144]{1,0:T(8,128)(2,1)S(1)}, bf16[16,6144]{1,0:T(8,128)(2,1)S(1)}, u32[]{:S(2)}, u32[]{:S(2)}) collective-permute-start(bf16[16,6144]{1,0:T(8,128)(2,1)S(1)} %shard_map.55.refs_0_), channel_id=1, source_target_pairs={{0,3},{1,0},{2,1},{3,2},{4,7},{5,4},{6,5},{7,6},{8,11},{9,8},{10,9... | collective-permute-start | bytes 589832 | tf_op jit(solution)/shard_map/ppermute | solution.py:19
  6.7 11.5 %collective-permute-start.2 = (bf16[16,6144]{1,0:T(8,128)(2,1)S(1)}, bf16[16,6144]{1,0:T(8,128)(2,1)S(1)}, u32[]{:S(2)}, u32[]{:S(2)}) collective-permute-start(bf16[16,6144]{1,0:T(8,128)(2,1)S(1)} %shard_map.55.refs_0_), channel_id=1, source_target_pairs={{0,4},{1,5},{2,6},{3,7},{4,8},{5,9},{6,10},{7,11},{8,12},{9,13},{1... | collective-permute-start | bytes 589832 | tf_op jit(solution)/shard_map/ppermute | solution.py:19
  8.2 10.0 %collective-permute-start.3 = (bf16[16,6144]{1,0:T(8,128)(2,1)S(1)}, bf16[16,6144]{1,0:T(8,128)(2,1)S(1)}, u32[]{:S(2)}, u32[]{:S(2)}) collective-permute-start(bf16[16,6144]{1,0:T(8,128)(2,1)S(1)} %shard_map.55.refs_0_), channel_id=1, source_target_pairs={{0,12},{1,13},{2,14},{3,15},{4,0},{5,1},{6,2},{7,3},{8,4},{9,5},{1... | collective-permute-start | bytes 589832 | tf_op jit(solution)/shard_map/ppermute | solution.py:19
  16.7 10.0 %collective-permute-start.6 = (bf16[16,6144]{1,0:T(8,128)(2,1)S(1)}, bf16[16,6144]{1,0:T(8,128)(2,1)S(1)}, u32[]{:S(2)}, u32[]{:S(2)}) collective-permute-start(bf16[16,6144]{1,0:T(8,128)(2,1)S(1)} %collective-permute-done.refs_3_), channel_id=1, source_target_pairs={{0,1},{1,2},{2,3},{3,0},{4,5},{5,6},{6,7},{7,4},{8,9},{9,10},{10,1... | collective-permute-start | bytes 589832 | tf_op jit(solution)/shard_map/ppermute | solution.py:19
  18.2 15.4 %collective-permute-start.4 = (bf16[32,6144]{1,0:T(8,128)(2,1)S(1)}, bf16[32,6144]{1,0:T(8,128)(2,1)S(1)}, u32[]{:S(2)}, u32[]{:S(2)}) collective-permute-start(bf16[32,6144]{1,0:T(8,128)(2,1)S(1)} %pad_maximum_fusion), channel_id=1, source_target_pairs={{0,4},{1,5},{2,6},{3,7},{4,8},{5,9},{6,10},{7,11},{8,12},{9,13},{1... | collective-permute-start | bytes 1179656 | tf_op jit(solution)/shard_map/ppermute | solution.py:19
  19.2 14.3 %collective-permute-start.5 = (bf16[32,6144]{1,0:T(8,128)(2,1)S(1)}, bf16[32,6144]{1,0:T(8,128)(2,1)S(1)}, u32[]{:S(2)}, u32[]{:S(2)}) collective-permute-start(bf16[32,6144]{1,0:T(8,128)(2,1)S(1)} %pad_maximum_fusion), channel_id=1, source_target_pairs={{0,12},{1,13},{2,14},{3,15},{4,0},{5,1},{6,2},{7,3},{8,4},{9,5},{1... | collective-permute-start | bytes 1179656 | tf_op jit(solution)/shard_map/ppermute | solution.py:19
  26.6 9.2 %collective-permute-start.7 = (bf16[16,6144]{1,0:T(8,128)(2,1)S(1)}, bf16[16,6144]{1,0:T(8,128)(2,1)S(1)}, u32[]{:S(2)}, u32[]{:S(2)}) collective-permute-start(bf16[16,6144]{1,0:T(8,128)(2,1)S(1)} %collective-permute-done.6.refs_5_), channel_id=1, source_target_pairs={{0,4},{1,5},{2,6},{3,7},{4,8},{5,9},{6,10},{7,11},{8,12},{9,13},{1... | collective-permute-start | bytes 589832 | tf_op jit(solution)/shard_map/ppermute | solution.py:19
  27.1 8.7 %collective-permute-start.8 = (bf16[16,6144]{1,0:T(8,128)(2,1)S(1)}, bf16[16,6144]{1,0:T(8,128)(2,1)S(1)}, u32[]{:S(2)}, u32[]{:S(2)}) collective-permute-start(bf16[16,6144]{1,0:T(8,128)(2,1)S(1)} %collective-permute-done.6.refs_5_), channel_id=1, source_target_pairs={{0,12},{1,13},{2,14},{3,15},{4,0},{5,1},{6,2},{7,3},{8,4},{9,5},{1... | collective-permute-start | bytes 589832 | tf_op jit(solution)/shard_map/ppermute | solution.py:19
  33.6 13.1 %collective-permute-start.10 = (bf16[16,9216]{1,0:T(8,128)(2,1)S(1)}, bf16[16,9216]{1,0:T(8,128)(2,1)S(1)}, u32[]{:S(2)}, u32[]{:S(2)}) collective-permute-start(bf16[16,9216]{1,0:T(8,128)(2,1)S(1)} %pad_maximum_fusion.4), channel_id=1, source_target_pairs={{0,12},{1,13},{2,14},{3,15},{4,0},{5,1},{6,2},{7,3},{8,4},{9,5},{1... | collective-permute-start | bytes 884744 | tf_op jit(solution)/shard_map/ppermute | solution.py:19
  34.8 11.9 %collective-permute-start.9 = (bf16[16,9216]{1,0:T(8,128)(2,1)S(1)}, bf16[16,9216]{1,0:T(8,128)(2,1)S(1)}, u32[]{:S(2)}, u32[]{:S(2)}) collective-permute-start(bf16[16,9216]{1,0:T(8,128)(2,1)S(1)} %pad_maximum_fusion.3), channel_id=1, source_target_pairs={{0,4},{1,5},{2,6},{3,7},{4,8},{5,9},{6,10},{7,11},{8,12},{9,13},{1... | collective-permute-start | bytes 884744 | tf_op jit(solution)/shard_map/ppermute | solution.py:19
  35.8 10.9 %collective-permute-start.11 = (bf16[16,3072]{1,0:T(8,128)(2,1)S(1)}, bf16[16,3072]{1,0:T(8,128)(2,1)S(1)}, u32[]{:S(2)}, u32[]{:S(2)}) collective-permute-start(bf16[16,3072]{1,0:T(8,128)(2,1)S(1)} %slice.89), channel_id=1, source_target_pairs={{0,4},{1,5},{2,6},{3,7},{4,8},{5,9},{6,10},{7,11},{8,12},{9,13},{1... | collective-permute-start | bytes 294920 | tf_op jit(solution)/shard_map/ppermute | solution.py:19
  37.0 9.7 %collective-permute-start.12 = (bf16[16,3072]{1,0:T(8,128)(2,1)S(1)}, bf16[16,3072]{1,0:T(8,128)(2,1)S(1)}, u32[]{:S(2)}, u32[]{:S(2)}) collective-permute-start(bf16[16,3072]{1,0:T(8,128)(2,1)S(1)} %slice.90), channel_id=1, source_target_pairs={{0,12},{1,13},{2,14},{3,15},{4,0},{5,1},{6,2},{7,3},{8,4},{9,5},{1... | collective-permute-start | bytes 294920 | tf_op jit(solution)/shard_map/ppermute | solution.py:19
  53.2 11.0 %collective-permute-start.13 = (bf16[16,12288]{1,0:T(8,128)(2,1)S(1)}, bf16[16,12288]{1,0:T(8,128)(2,1)S(1)}, u32[]{:S(2)}, u32[]{:S(2)}) collective-permute-start(bf16[16,12288]{1,0:T(8,128)(2,1)S(1)} %get-tuple-element.61), channel_id=1, source_target_pairs={{0,4},{1,5},{2,6},{3,7},{4,8},{5,9},{6,10},{7,11},{8,12},{9,13},{1... | collective-permute-start | bytes 1179656 | tf_op jit(solution)/shard_map/ppermute | solution.py:19
  53.3 10.9 %collective-permute-start.14 = (bf16[16,12288]{1,0:T(8,128)(2,1)S(1)}, bf16[16,12288]{1,0:T(8,128)(2,1)S(1)}, u32[]{:S(2)}, u32[]{:S(2)}) collective-permute-start(bf16[16,12288]{1,0:T(8,128)(2,1)S(1)} %get-tuple-element.62), channel_id=1, source_target_pairs={{0,12},{1,13},{2,14},{3,15},{4,0},{5,1},{6,2},{7,3},{8,4},{9,5},{1... | collective-permute-start | bytes 1179656 | tf_op jit(solution)/shard_map/ppermute | solution.py:19
  56.6 42.1 %copy-start = (bf16[16,6144]{1,0:T(8,128)(2,1)S(1)}, bf16[16,6144]{1,0:T(8,128)(2,1)}, u32[]{:S(2)}) copy-start(bf16[16,6144]{1,0:T(8,128)(2,1)} %rows_ref.1) | copy-start | bytes 589828
  64.4 11.1 %collective-permute-start.16 = (bf16[32,6144]{1,0:T(8,128)(2,1)S(1)}, bf16[32,6144]{1,0:T(8,128)(2,1)S(1)}, u32[]{:S(2)}, u32[]{:S(2)}) collective-permute-start(bf16[32,6144]{1,0:T(8,128)(2,1)S(1)} %pad_maximum_fusion.2), channel_id=1, source_target_pairs={{0,12},{1,13},{2,14},{3,15},{4,0},{5,1},{6,2},{7,3},{8,4},{9,5},{1... | collective-permute-start | bytes 1179656 | tf_op jit(solution)/shard_map/ppermute | solution.py:19
  67.5 11.6 %collective-permute-start.15 = (bf16[32,6144]{1,0:T(8,128)(2,1)S(1)}, bf16[32,6144]{1,0:T(8,128)(2,1)S(1)}, u32[]{:S(2)}, u32[]{:S(2)}) collective-permute-start(bf16[32,6144]{1,0:T(8,128)(2,1)S(1)} %pad_maximum_fusion.1), channel_id=1, source_target_pairs={{0,4},{1,5},{2,6},{3,7},{4,8},{5,9},{6,10},{7,11},{8,12},{9,13},{1... | collective-permute-start | bytes 1179656 | tf_op jit(solution)/shard_map/ppermute | solution.py:19
  67.6 15.8 %collective-permute-start.20 = (bf16[16,6144]{1,0:T(8,128)(2,1)S(1)}, bf16[16,6144]{1,0:T(8,128)(2,1)S(1)}, u32[]{:S(2)}, u32[]{:S(2)}) collective-permute-start(bf16[16,6144]{1,0:T(8,128)(2,1)S(1)} %pad_maximum_fusion.6), channel_id=1, source_target_pairs={{0,12},{1,13},{2,14},{3,15},{4,0},{5,1},{6,2},{7,3},{8,4},{9,5},{1... | collective-permute-start | bytes 589832 | tf_op jit(solution)/shard_map/ppermute | solution.py:19
  70.9 12.5 %collective-permute-start.19 = (bf16[16,6144]{1,0:T(8,128)(2,1)S(1)}, bf16[16,6144]{1,0:T(8,128)(2,1)S(1)}, u32[]{:S(2)}, u32[]{:S(2)}) collective-permute-start(bf16[16,6144]{1,0:T(8,128)(2,1)S(1)} %pad_maximum_fusion.5), channel_id=1, source_target_pairs={{0,4},{1,5},{2,6},{3,7},{4,8},{5,9},{6,10},{7,11},{8,12},{9,13},{1... | collective-permute-start | bytes 589832 | tf_op jit(solution)/shard_map/ppermute | solution.py:19
  79.2 19.4 %collective-permute-start.17 = (bf16[16,6144]{1,0:T(8,128)(2,1)S(1)}, bf16[16,6144]{1,0:T(8,128)(2,1)S(1)}, u32[]{:S(2)}, u32[]{:S(2)}) collective-permute-start(bf16[16,6144]{1,0:T(8,128)(2,1)S(1)} %get-tuple-element.77), channel_id=1, source_target_pairs={{0,1},{1,2},{2,3},{3,0},{4,5},{5,6},{6,7},{7,4},{8,9},{9,10},{10,1... | collective-permute-start | bytes 589832 | tf_op jit(solution)/shard_map/ppermute | solution.py:19
  79.3 19.3 %collective-permute-start.18 = (bf16[16,6144]{1,0:T(8,128)(2,1)S(1)}, bf16[16,6144]{1,0:T(8,128)(2,1)S(1)}, u32[]{:S(2)}, u32[]{:S(2)}) collective-permute-start(bf16[16,6144]{1,0:T(8,128)(2,1)S(1)} %get-tuple-element.78), channel_id=1, source_target_pairs={{0,3},{1,0},{2,1},{3,2},{4,7},{5,4},{6,5},{7,6},{8,11},{9,8},{10,9... | collective-permute-start | bytes 589832 | tf_op jit(solution)/shard_map/ppermute | solution.py:19
  83.5 15.1 %collective-permute-start.21 = (bf16[16,6144]{1,0:T(8,128)(2,1)S(1)}, bf16[16,6144]{1,0:T(8,128)(2,1)S(1)}, u32[]{:S(2)}, u32[]{:S(2)}) collective-permute-start(bf16[16,6144]{1,0:T(8,128)(2,1)S(1)} %add_convert_fusion.2), channel_id=1, source_target_pairs={{0,2},{1,3},{2,0},{3,1},{4,6},{5,7},{6,4},{7,5},{8,10},{9,11},{10,... | collective-permute-start | bytes 589832 | tf_op jit(solution)/shard_map/ppermute | solution.py:19
  84.7 13.9 %collective-permute-start.22 = (bf16[16,6144]{1,0:T(8,128)(2,1)S(1)}, bf16[16,6144]{1,0:T(8,128)(2,1)S(1)}, u32[]{:S(2)}, u32[]{:S(2)}) collective-permute-start(bf16[16,6144]{1,0:T(8,128)(2,1)S(1)} %pad_maximum_fusion.7), channel_id=1, source_target_pairs={{0,4},{1,5},{2,6},{3,7},{4,8},{5,9},{6,10},{7,11},{8,12},{9,13},{1... | collective-permute-start | bytes 589832 | tf_op jit(solution)/shard_map/ppermute | solution.py:19
  84.7 13.9 %collective-permute-start.23 = (bf16[16,6144]{1,0:T(8,128)(2,1)S(1)}, bf16[16,6144]{1,0:T(8,128)(2,1)S(1)}, u32[]{:S(2)}, u32[]{:S(2)}) collective-permute-start(bf16[16,6144]{1,0:T(8,128)(2,1)S(1)} %pad_maximum_fusion.8), channel_id=1, source_target_pairs={{0,12},{1,13},{2,14},{3,15},{4,0},{5,1},{6,2},{7,3},{8,4},{9,5},{1... | collective-permute-start | bytes 589832 | tf_op jit(solution)/shard_map/ppermute | solution.py:19

commit v12 on v8

--- a/solution.py
+++ b/solution.py
@@ -89,7 +89,7 @@
 
 
 def two_hops(two_up, two_down, far_up, far_down, weights, down_w):
-    (n, h), (ff, d), step = far_up.shape, down_w.shape, 1024
+    (n, h), (ff, d) = far_up.shape, down_w.shape
 
     def kernel(two_up, two_down, far_up, far_down, gate_w, up_w, up_w2, down_w, out_up, out_down, rows, hidden):
         rows[:n, :] = two_up[:, :d]
@@ -102,15 +102,12 @@
         for second in (False, True):
             target = out_down if second else out_up
 
-            @pl.loop(0, h // step)
-            def _(i):
-                start = pl.multiple_of(i * step, step)
-                cut = pl.ds(start + second * h, step)
-                terms = b16(jnp.dot(hidden[...], down_w[:, cut], preferred_element_type=jnp.float32))
-                out_up[:, cut] = terms[:n]
-                out_down[:, cut] = terms[n : 2 * n]
-                target[:, pl.ds(start + d, step)] = terms[2 * n : 3 * n]
-                target[:, pl.ds(start + d + h, step)] = terms[3 * n :]
+            cut = pl.ds(second * h, h)
+            terms = b16(jnp.dot(hidden[...], down_w[:, cut], preferred_element_type=jnp.float32))
+            out_up[:, cut] = terms[:n]
+            out_down[:, cut] = terms[n : 2 * n]
+            target[:, pl.ds(d, h)] = terms[2 * n : 3 * n]
+            target[:, pl.ds(d + h, h)] = terms[3 * n :]
 
     vmem, b = pl.BlockSpec(memory_space=pltpu.VMEM), jnp.bfloat16
     return pl.pallas_call(

time: 94.1 us -> 93.6 us (level)
  no operation moved by 1% of the time
where the time goes in v12:
time: 93.6 us; the launch traced here: 93 us
  starting transfers between devices  41 us (44%)
  Pallas kernels  27.7 us (30%)
  waiting for transfers between devices  22.4 us (24%)
  other arithmetic  1.38 us (1%)
    ppermute x24, starting transfers between devices, shift(): return lax.ppermute(block, ('dp', 'tensor'), pairs)  41 us
    ppermute x24, waiting for transfers between devices, shift(): return lax.ppermute(block, ('dp', 'tensor'), pairs)  22.4 us
    pallas_call x3, Pallas kernels, fetched(): pl.pallas_call(kernel, out_shape=pltpu.VMEM((size, weight.shape[1]), weig...  9.28 us
    pallas_call x2, Pallas kernels, hidden_units(): pl.pallas_call(kernel, out_shape=[pltpu.VMEM((tall, ff), b)] + [pltpu.VME...  7.79 us
    pallas_call x1, Pallas kernels, two_hops(): pl.pallas_call(kernel, out_shape=[pltpu.VMEM((n, 2 * d), b)] * 2, in_spec...  6 us
    pallas_call x1, Pallas kernels, other_terms(): pl.pallas_call(kernel, out_shape=[pltpu.VMEM((k * n, d), jnp.float32) for...  3.57 us
  transfers between devices with their start and end apart: 24, of which 9 were waited for; matrix products, arithmetic and copies ran while one was open for 1% of the time, Pallas kernels for 22%

profile of v12, /device:TPU:8, one launch (start us, length us, event | category | flops | bytes accessed | tf_op | source)
XLA Modules:
  0.0 93.0 jit_solution(6076043521617009179)
XLA Ops:
  0.0 1.1 %shard_map.55.refs_0_ = bf16[16,6144]{1,0:T(8,128)(2,1)S(1)} custom-call(bf16[16,6144]{1,0:T(8,128)(2,1)} %rows_ref.1, f32[1,6144]{1,0:T(1,128)} %bitcast.1), custom_call_target="tpu_custom_call" | custom-call | tf_op jit(solution)/shard_map/pallas_call | solution.py:37
  1.1 3.3 %collective-permute-start = (bf16[16,6144]{1,0:T(8,128)(2,1)S(1)}, bf16[16,6144]{1,0:T(8,128)(2,1)S(1)}, u32[]{:S(2)}, u32[]{:S(2)}) collective-permute-start(bf16[16,6144]{1,0:T(8,128)(2,1)S(1)} %shard_map.55.refs_0_), channel_id=1, source_target_pairs={{0,1},{1,2},{2,3},{3,0},{4,5},{5,6},{6,7},{7,4},{8,9},{9,10},{10,1... | collective-permute-start | bytes 589832 | tf_op jit(solution)/shard_map/ppermute | solution.py:19
  4.5 3.1 %collective-permute-start.1 = (bf16[16,6144]{1,0:T(8,128)(2,1)S(1)}, bf16[16,6144]{1,0:T(8,128)(2,1)S(1)}, u32[]{:S(2)}, u32[]{:S(2)}) collective-permute-start(bf16[16,6144]{1,0:T(8,128)(2,1)S(1)} %shard_map.55.refs_0_), channel_id=1, source_target_pairs={{0,3},{1,0},{2,1},{3,2},{4,7},{5,4},{6,5},{7,6},{8,11},{9,8},{10,9... | collective-permute-start | bytes 589832 | tf_op jit(solution)/shard_map/ppermute | solution.py:19
  7.6 1.5 %collective-permute-start.2 = (bf16[16,6144]{1,0:T(8,128)(2,1)S(1)}, bf16[16,6144]{1,0:T(8,128)(2,1)S(1)}, u32[]{:S(2)}, u32[]{:S(2)}) collective-permute-start(bf16[16,6144]{1,0:T(8,128)(2,1)S(1)} %shard_map.55.refs_0_), channel_id=1, source_target_pairs={{0,4},{1,5},{2,6},{3,7},{4,8},{5,9},{6,10},{7,11},{8,12},{9,13},{1... | collective-permute-start | bytes 589832 | tf_op jit(solution)/shard_map/ppermute | solution.py:19
  9.1 1.7 %collective-permute-start.3 = (bf16[16,6144]{1,0:T(8,128)(2,1)S(1)}, bf16[16,6144]{1,0:T(8,128)(2,1)S(1)}, u32[]{:S(2)}, u32[]{:S(2)}) collective-permute-start(bf16[16,6144]{1,0:T(8,128)(2,1)S(1)} %shard_map.55.refs_0_), channel_id=1, source_target_pairs={{0,12},{1,13},{2,14},{3,15},{4,0},{5,1},{6,2},{7,3},{8,4},{9,5},{1... | collective-permute-start | bytes 589832 | tf_op jit(solution)/shard_map/ppermute | solution.py:19
  10.8 4.1 %shard_map.56.refs_6_.refs_4_.gate_w = bf16[6144,896]{1,0:T(8,128)(2,1)S(1)} custom-call(bf16[6144,896]{1,0:T(8,128)(2,1)} %source.2), custom_call_target="tpu_custom_call" | custom-call | bytes 11010048 | tf_op jit(solution)/shard_map/pallas_call | solution.py:162
  15.0 2.6 %shard_map.57.refs_7_.refs_5_.up_w = bf16[3072,896]{1,0:T(8,128)(2,1)S(1)} custom-call(bf16[6144,896]{1,0:T(8,128)(2,1)} %source.4), custom_call_target="tpu_custom_call" | custom-call | bytes 5505024 | tf_op jit(solution)/shard_map/pallas_call | solution.py:162
  17.6 0.0 collective-permute-done.refs_3_
  17.6 1.4 %collective-permute-start.6 = (bf16[16,6144]{1,0:T(8,128)(2,1)S(1)}, bf16[16,6144]{1,0:T(8,128)(2,1)S(1)}, u32[]{:S(2)}, u32[]{:S(2)}) collective-permute-start(bf16[16,6144]{1,0:T(8,128)(2,1)S(1)} %collective-permute-done.refs_3_), channel_id=1, source_target_pairs={{0,1},{1,2},{2,3},{3,0},{4,5},{5,6},{6,7},{7,4},{8,9},{9,10},{10,1... | collective-permute-start | bytes 589832 | tf_op jit(solution)/shard_map/ppermute | solution.py:19
  19.0 0.0 collective-permute-done.2.refs_1_
  19.1 1.3 %collective-permute-start.4 = (bf16[32,6144]{1,0:T(8,128)(2,1)S(1)}, bf16[32,6144]{1,0:T(8,128)(2,1)S(1)}, u32[]{:S(2)}, u32[]{:S(2)}) collective-permute-start(bf16[32,6144]{1,0:T(8,128)(2,1)S(1)} %pad_maximum_fusion), channel_id=1, source_target_pairs={{0,4},{1,5},{2,6},{3,7},{4,8},{5,9},{6,10},{7,11},{8,12},{9,13},{1... | collective-permute-start | bytes 1179656 | tf_op jit(solution)/shard_map/ppermute | solution.py:19
  20.4 2.0 %collective-permute-start.5 = (bf16[32,6144]{1,0:T(8,128)(2,1)S(1)}, bf16[32,6144]{1,0:T(8,128)(2,1)S(1)}, u32[]{:S(2)}, u32[]{:S(2)}) collective-permute-start(bf16[32,6144]{1,0:T(8,128)(2,1)S(1)} %pad_maximum_fusion), channel_id=1, source_target_pairs={{0,12},{1,13},{2,14},{3,15},{4,0},{5,1},{6,2},{7,3},{8,4},{9,5},{1... | collective-permute-start | bytes 1179656 | tf_op jit(solution)/shard_map/ppermute | solution.py:19
  22.4 2.6 %shard_map.58.refs_8_.refs_6_.up_w2 = bf16[3072,896]{1,0:T(8,128)(2,1)S(1)} custom-call(bf16[6144,896]{1,0:T(8,128)(2,1)} %source.4), custom_call_target="tpu_custom_call" | custom-call | bytes 5505024 | tf_op jit(solution)/shard_map/pallas_call | solution.py:162
  25.0 1.0 %collective-permute-done.6.refs_5_ = bf16[16,6144]{1,0:T(8,128)(2,1)S(1)} collective-permute-done((bf16[16,6144]{1,0:T(8,128)(2,1)S(1)}, bf16[16,6144]{1,0:T(8,128)(2,1)S(1)}, u32[]{:S(2)}, u32[]{:S(2)}) %collective-permute-start.6) | collective-permute-done | bytes 196640 | tf_op jit(solution)/shard_map/ppermute | solution.py:19
  26.0 0.7 collective-permute-start.7
  26.7 2.5 %collective-permute-start.8 = (bf16[16,6144]{1,0:T(8,128)(2,1)S(1)}, bf16[16,6144]{1,0:T(8,128)(2,1)S(1)}, u32[]{:S(2)}, u32[]{:S(2)}) collective-permute-start(bf16[16,6144]{1,0:T(8,128)(2,1)S(1)} %collective-permute-done.6.refs_5_), channel_id=1, source_target_pairs={{0,12},{1,13},{2,14},{3,15},{4,0},{5,1},{6,2},{7,3},{8,4},{9,5},{1... | collective-permute-start | bytes 589832 | tf_op jit(solution)/shard_map/ppermute | solution.py:19
  29.2 3.6 %shard_map.59.early = bf16[96,896]{1,0:T(8,128)(2,1)S(1)} custom-call(bf16[16,6144]{1,0:T(8,128)(2,1)S(1)} %shard_map.55.refs_0_, bf16[16,6144]{1,0:T(8,128)(2,1)S(1)} %collective-permute-done.2.refs_1_, bf16[16,6144]{1,0:T(8,128)(2,1)S(1)} %collective-permute-done.3.refs_2_, bf16[16,6144]{1,0:T(8,128)(2,1)S(1)} %collective-permute-done.refs_3_, ...), custom_call_target="tpu_custom_call" | custom-call | flops 2113929216 | tf_op jit(solution)/shard_map/pallas_call | solution.py:80
  32.9 0.0 collective-permute-done.5.refs_1_
  32.9 2.8 %collective-permute-start.10 = (bf16[16,9216]{1,0:T(8,128)(2,1)S(1)}, bf16[16,9216]{1,0:T(8,128)(2,1)S(1)}, u32[]{:S(2)}, u32[]{:S(2)}) collective-permute-start(bf16[16,9216]{1,0:T(8,128)(2,1)S(1)} %pad_maximum_fusion.4), channel_id=1, source_target_pairs={{0,12},{1,13},{2,14},{3,15},{4,0},{5,1},{6,2},{7,3},{8,4},{9,5},{1... | collective-permute-start | bytes 884744 | tf_op jit(solution)/shard_map/ppermute | solution.py:19
  35.7 0.1 collective-permute-start.9
  35.8 0.4 collective-permute-done.7.refs_2_
  36.3 0.0 collective-permute-done.8.refs_3_
  36.3 1.7 %collective-permute-start.11 = (bf16[16,3072]{1,0:T(8,128)(2,1)S(1)}, bf16[16,3072]{1,0:T(8,128)(2,1)S(1)}, u32[]{:S(2)}, u32[]{:S(2)}) collective-permute-start(bf16[16,3072]{1,0:T(8,128)(2,1)S(1)} %slice.89), channel_id=1, source_target_pairs={{0,4},{1,5},{2,6},{3,7},{4,8},{5,9},{6,10},{7,11},{8,12},{9,13},{1... | collective-permute-start | bytes 294920 | tf_op jit(solution)/shard_map/ppermute | solution.py:19
  38.1 2.1 %collective-permute-start.12 = (bf16[16,3072]{1,0:T(8,128)(2,1)S(1)}, bf16[16,3072]{1,0:T(8,128)(2,1)S(1)}, u32[]{:S(2)}, u32[]{:S(2)}) collective-permute-start(bf16[16,3072]{1,0:T(8,128)(2,1)S(1)} %slice.90), channel_id=1, source_target_pairs={{0,12},{1,13},{2,14},{3,15},{4,0},{5,1},{6,2},{7,3},{8,4},{9,5},{1... | collective-permute-start | bytes 294920 | tf_op jit(solution)/shard_map/ppermute | solution.py:19
  40.2 4.1 %shard_map.60 = (bf16[96,896]{1,0:T(8,128)(2,1)S(1)}, bf16[896,6144]{1,0:T(8,128)(2,1)S(1)}) custom-call(bf16[32,6144]{1,0:T(8,128)(2,1)S(1)} %collective-permute-done.4.refs_0_, bf16[32,6144]{1,0:T(8,128)(2,1)S(1)} %collective-permute-done.5.refs_1_, bf16[16,6144]{1,0:T(8,128)(2,1)S(1)} %collective-permute-done.7.refs_2_, ...), custom_call_target="tpu_custom_call" | custom-call | flops 2113929216 | bytes 11010048 | tf_op jit(solution)/shard_map/pallas_call | solution.py:80
  44.3 3.6 %collective-permute-done.11.far_up = bf16[16,3072]{1,0:T(8,128)(2,1)S(1)} collective-permute-done((bf16[16,3072]{1,0:T(8,128)(2,1)S(1)}, bf16[16,3072]{1,0:T(8,128)(2,1)S(1)}, u32[]{:S(2)}, u32[]{:S(2)}) %collective-permute-start.11) | collective-permute-done | bytes 98336 | tf_op jit(solution)/shard_map/ppermute | solution.py:19
  47.9 6.0 %shard_map.62 = (bf16[16,12288]{1,0:T(8,128)(2,1)S(1)}, bf16[16,12288]{1,0:T(8,128)(2,1)S(1)}) custom-call(bf16[16,9216]{1,0:T(8,128)(2,1)S(1)} %collective-permute-done.9.two_up, bf16[16,9216]{1,0:T(8,128)(2,1)S(1)} %collective-permute-done.10.two_down, bf16[16,3072]{1,0:T(8,128)(2,1)S(1)} %collective-permute-done.11.far_up, ...), custom_call_target="tpu_custom_call" | custom-call | flops 2113929216 | tf_op jit(solution)/shard_map/pallas_call | solution.py:113
  53.9 0.1 collective-permute-start.13
  54.0 3.2 %collective-permute-start.14 = (bf16[16,12288]{1,0:T(8,128)(2,1)S(1)}, bf16[16,12288]{1,0:T(8,128)(2,1)S(1)}, u32[]{:S(2)}, u32[]{:S(2)}) collective-permute-start(bf16[16,12288]{1,0:T(8,128)(2,1)S(1)} %get-tuple-element.59), channel_id=1, source_target_pairs={{0,12},{1,13},{2,14},{3,15},{4,0},{5,1},{6,2},{7,3},{8,4},{9,5},{1... | collective-permute-start | bytes 1179656 | tf_op jit(solution)/shard_map/ppermute | solution.py:19
  57.2 3.6 %shard_map.61 = (f32[16,6144]{1,0:T(8,128)S(1)}, f32[16,6144]{1,0:T(8,128)S(1)}, f32[16,6144]{1,0:T(8,128)S(1)}, f32[32,6144]{1,0:T(8,128)S(1)}, f32[16,6144]{1,...) custom-call(bf16[96,896]{1,0:T(8,128)(2,1)S(1)} %shard_map.59.early,, ...), custom_call_target="tpu_custom_call" | custom-call | flops 2113929216 | tf_op jit(solution)/shard_map/pallas_call | solution.py:143
  60.9 4.2 %collective-permute-done.13 = bf16[16,12288]{1,0:T(8,128)(2,1)S(1)} collective-permute-done((bf16[16,12288]{1,0:T(8,128)(2,1)S(1)}, bf16[16,12288]{1,0:T(8,128)(2,1)S(1)}, u32[]{:S(2)}, u32[]{:S(2)}) %collective-permute-start.13) | collective-permute-done | bytes 393248 | tf_op jit(solution)/shard_map/ppermute | solution.py:19
  65.4 0.1 collective-permute-start.19
  65.5 3.3 %collective-permute-start.20 = (bf16[16,6144]{1,0:T(8,128)(2,1)S(1)}, bf16[16,6144]{1,0:T(8,128)(2,1)S(1)}, u32[]{:S(2)}, u32[]{:S(2)}) collective-permute-start(bf16[16,6144]{1,0:T(8,128)(2,1)S(1)} %pad_maximum_fusion.8), channel_id=1, source_target_pairs={{0,12},{1,13},{2,14},{3,15},{4,0},{5,1},{6,2},{7,3},{8,4},{9,5},{1... | collective-permute-start | bytes 589832 | tf_op jit(solution)/shard_map/ppermute | solution.py:19
  68.8 2.0 %collective-permute-start.16 = (bf16[32,6144]{1,0:T(8,128)(2,1)S(1)}, bf16[32,6144]{1,0:T(8,128)(2,1)S(1)}, u32[]{:S(2)}, u32[]{:S(2)}) collective-permute-start(bf16[32,6144]{1,0:T(8,128)(2,1)S(1)} %pad_maximum_fusion.2), channel_id=1, source_target_pairs={{0,12},{1,13},{2,14},{3,15},{4,0},{5,1},{6,2},{7,3},{8,4},{9,5},{1... | collective-permute-start | bytes 1179656 | tf_op jit(solution)/shard_map/ppermute | solution.py:19
  70.9 0.4 collective-permute-start.15
  71.3 1.6 %collective-permute-done.19 = bf16[16,6144]{1,0:T(8,128)(2,1)S(1)} collective-permute-done((bf16[16,6144]{1,0:T(8,128)(2,1)S(1)}, bf16[16,6144]{1,0:T(8,128)(2,1)S(1)}, u32[]{:S(2)}, u32[]{:S(2)}) %collective-permute-start.19) | collective-permute-done | bytes 196640 | tf_op jit(solution)/shard_map/ppermute | solution.py:19
  72.9 1.2 %collective-permute-done.20 = bf16[16,6144]{1,0:T(8,128)(2,1)S(1)} collective-permute-done((bf16[16,6144]{1,0:T(8,128)(2,1)S(1)}, bf16[16,6144]{1,0:T(8,128)(2,1)S(1)}, u32[]{:S(2)}, u32[]{:S(2)}) %collective-permute-start.20) | collective-permute-done | bytes 196640 | tf_op jit(solution)/shard_map/ppermute | solution.py:19
  74.2 0.1 add_convert_fusion.2
  74.2 0.1 collective-permute-start.21
  74.3 5.4 %collective-permute-done.16 = bf16[32,6144]{1,0:T(8,128)(2,1)S(1)} collective-permute-done((bf16[32,6144]{1,0:T(8,128)(2,1)S(1)}, bf16[32,6144]{1,0:T(8,128)(2,1)S(1)}, u32[]{:S(2)}, u32[]{:S(2)}) %collective-permute-start.16) | collective-permute-done | bytes 393248 | tf_op jit(solution)/shard_map/ppermute | solution.py:19
  79.7 1.1 %collective-permute-done.15 = bf16[32,6144]{1,0:T(8,128)(2,1)S(1)} collective-permute-done((bf16[32,6144]{1,0:T(8,128)(2,1)S(1)}, bf16[32,6144]{1,0:T(8,128)(2,1)S(1)}, u32[]{:S(2)}, u32[]{:S(2)}) %collective-permute-start.15) | collective-permute-done | bytes 393248 | tf_op jit(solution)/shard_map/ppermute | solution.py:19
  80.8 0.1 add_convert_fusion
  80.9 0.1 collective-permute-start.22
  81.0 4.1 %collective-permute-start.23 = (bf16[16,6144]{1,0:T(8,128)(2,1)S(1)}, bf16[16,6144]{1,0:T(8,128)(2,1)S(1)}, u32[]{:S(2)}, u32[]{:S(2)}) collective-permute-start(bf16[16,6144]{1,0:T(8,128)(2,1)S(1)} %get-tuple-element.78), channel_id=1, source_target_pairs={{0,3},{1,0},{2,1},{3,2},{4,7},{5,4},{6,5},{7,6},{8,11},{9,8},{10,9... | collective-permute-start | bytes 589832 | tf_op jit(solution)/shard_map/ppermute | solution.py:19
  85.2 0.1 collective-permute-start.17
  85.3 3.1 %collective-permute-start.18 = (bf16[16,6144]{1,0:T(8,128)(2,1)S(1)}, bf16[16,6144]{1,0:T(8,128)(2,1)S(1)}, u32[]{:S(2)}, u32[]{:S(2)}) collective-permute-start(bf16[16,6144]{1,0:T(8,128)(2,1)S(1)} %pad_maximum_fusion.6), channel_id=1, source_target_pairs={{0,12},{1,13},{2,14},{3,15},{4,0},{5,1},{6,2},{7,3},{8,4},{9,5},{1... | collective-permute-start | bytes 589832 | tf_op jit(solution)/shard_map/ppermute | solution.py:19
  88.4 3.8 %collective-permute-done.22 = bf16[16,6144]{1,0:T(8,128)(2,1)S(1)} collective-permute-done((bf16[16,6144]{1,0:T(8,128)(2,1)S(1)}, bf16[16,6144]{1,0:T(8,128)(2,1)S(1)}, u32[]{:S(2)}, u32[]{:S(2)}) %collective-permute-start.22) | collective-permute-done | bytes 196640 | tf_op jit(solution)/shard_map/ppermute | solution.py:19
  92.2 0.8 add_convert_fusion.1
  (39 shorter events, 0.6 us)
Async XLA Ops:
  1.1 16.4 %collective-permute-start = (bf16[16,6144]{1,0:T(8,128)(2,1)S(1)}, bf16[16,6144]{1,0:T(8,128)(2,1)S(1)}, u32[]{:S(2)}, u32[]{:S(2)}) collective-permute-start(bf16[16,6144]{1,0:T(8,128)(2,1)S(1)} %shard_map.55.refs_0_), channel_id=1, source_target_pairs={{0,1},{1,2},{2,3},{3,0},{4,5},{5,6},{6,7},{7,4},{8,9},{9,10},{10,1... | collective-permute-start | bytes 589832 | tf_op jit(solution)/shard_map/ppermute | solution.py:19
  4.5 13.1 %collective-permute-start.1 = (bf16[16,6144]{1,0:T(8,128)(2,1)S(1)}, bf16[16,6144]{1,0:T(8,128)(2,1)S(1)}, u32[]{:S(2)}, u32[]{:S(2)}) collective-permute-start(bf16[16,6144]{1,0:T(8,128)(2,1)S(1)} %shard_map.55.refs_0_), channel_id=1, source_target_pairs={{0,3},{1,0},{2,1},{3,2},{4,7},{5,4},{6,5},{7,6},{8,11},{9,8},{10,9... | collective-permute-start | bytes 589832 | tf_op jit(solution)/shard_map/ppermute | solution.py:19
  7.6 11.5 %collective-permute-start.2 = (bf16[16,6144]{1,0:T(8,128)(2,1)S(1)}, bf16[16,6144]{1,0:T(8,128)(2,1)S(1)}, u32[]{:S(2)}, u32[]{:S(2)}) collective-permute-start(bf16[16,6144]{1,0:T(8,128)(2,1)S(1)} %shard_map.55.refs_0_), channel_id=1, source_target_pairs={{0,4},{1,5},{2,6},{3,7},{4,8},{5,9},{6,10},{7,11},{8,12},{9,13},{1... | collective-permute-start | bytes 589832 | tf_op jit(solution)/shard_map/ppermute | solution.py:19
  9.1 10.0 %collective-permute-start.3 = (bf16[16,6144]{1,0:T(8,128)(2,1)S(1)}, bf16[16,6144]{1,0:T(8,128)(2,1)S(1)}, u32[]{:S(2)}, u32[]{:S(2)}) collective-permute-start(bf16[16,6144]{1,0:T(8,128)(2,1)S(1)} %shard_map.55.refs_0_), channel_id=1, source_target_pairs={{0,12},{1,13},{2,14},{3,15},{4,0},{5,1},{6,2},{7,3},{8,4},{9,5},{1... | collective-permute-start | bytes 589832 | tf_op jit(solution)/shard_map/ppermute | solution.py:19
  17.6 8.4 %collective-permute-start.6 = (bf16[16,6144]{1,0:T(8,128)(2,1)S(1)}, bf16[16,6144]{1,0:T(8,128)(2,1)S(1)}, u32[]{:S(2)}, u32[]{:S(2)}) collective-permute-start(bf16[16,6144]{1,0:T(8,128)(2,1)S(1)} %collective-permute-done.refs_3_), channel_id=1, source_target_pairs={{0,1},{1,2},{2,3},{3,0},{4,5},{5,6},{6,7},{7,4},{8,9},{9,10},{10,1... | collective-permute-start | bytes 589832 | tf_op jit(solution)/shard_map/ppermute | solution.py:19
  19.1 13.8 %collective-permute-start.4 = (bf16[32,6144]{1,0:T(8,128)(2,1)S(1)}, bf16[32,6144]{1,0:T(8,128)(2,1)S(1)}, u32[]{:S(2)}, u32[]{:S(2)}) collective-permute-start(bf16[32,6144]{1,0:T(8,128)(2,1)S(1)} %pad_maximum_fusion), channel_id=1, source_target_pairs={{0,4},{1,5},{2,6},{3,7},{4,8},{5,9},{6,10},{7,11},{8,12},{9,13},{1... | collective-permute-start | bytes 1179656 | tf_op jit(solution)/shard_map/ppermute | solution.py:19
  20.4 12.5 %collective-permute-start.5 = (bf16[32,6144]{1,0:T(8,128)(2,1)S(1)}, bf16[32,6144]{1,0:T(8,128)(2,1)S(1)}, u32[]{:S(2)}, u32[]{:S(2)}) collective-permute-start(bf16[32,6144]{1,0:T(8,128)(2,1)S(1)} %pad_maximum_fusion), channel_id=1, source_target_pairs={{0,12},{1,13},{2,14},{3,15},{4,0},{5,1},{6,2},{7,3},{8,4},{9,5},{1... | collective-permute-start | bytes 1179656 | tf_op jit(solution)/shard_map/ppermute | solution.py:19
  26.0 10.3 %collective-permute-start.7 = (bf16[16,6144]{1,0:T(8,128)(2,1)S(1)}, bf16[16,6144]{1,0:T(8,128)(2,1)S(1)}, u32[]{:S(2)}, u32[]{:S(2)}) collective-permute-start(bf16[16,6144]{1,0:T(8,128)(2,1)S(1)} %collective-permute-done.6.refs_5_), channel_id=1, source_target_pairs={{0,4},{1,5},{2,6},{3,7},{4,8},{5,9},{6,10},{7,11},{8,12},{9,13},{1... | collective-permute-start | bytes 589832 | tf_op jit(solution)/shard_map/ppermute | solution.py:19
  26.7 9.6 %collective-permute-start.8 = (bf16[16,6144]{1,0:T(8,128)(2,1)S(1)}, bf16[16,6144]{1,0:T(8,128)(2,1)S(1)}, u32[]{:S(2)}, u32[]{:S(2)}) collective-permute-start(bf16[16,6144]{1,0:T(8,128)(2,1)S(1)} %collective-permute-done.6.refs_5_), channel_id=1, source_target_pairs={{0,12},{1,13},{2,14},{3,15},{4,0},{5,1},{6,2},{7,3},{8,4},{9,5},{1... | collective-permute-start | bytes 589832 | tf_op jit(solution)/shard_map/ppermute | solution.py:19
  32.9 15.0 %collective-permute-start.10 = (bf16[16,9216]{1,0:T(8,128)(2,1)S(1)}, bf16[16,9216]{1,0:T(8,128)(2,1)S(1)}, u32[]{:S(2)}, u32[]{:S(2)}) collective-permute-start(bf16[16,9216]{1,0:T(8,128)(2,1)S(1)} %pad_maximum_fusion.4), channel_id=1, source_target_pairs={{0,12},{1,13},{2,14},{3,15},{4,0},{5,1},{6,2},{7,3},{8,4},{9,5},{1... | collective-permute-start | bytes 884744 | tf_op jit(solution)/shard_map/ppermute | solution.py:19
  35.7 12.2 %collective-permute-start.9 = (bf16[16,9216]{1,0:T(8,128)(2,1)S(1)}, bf16[16,9216]{1,0:T(8,128)(2,1)S(1)}, u32[]{:S(2)}, u32[]{:S(2)}) collective-permute-start(bf16[16,9216]{1,0:T(8,128)(2,1)S(1)} %pad_maximum_fusion.3), channel_id=1, source_target_pairs={{0,4},{1,5},{2,6},{3,7},{4,8},{5,9},{6,10},{7,11},{8,12},{9,13},{1... | collective-permute-start | bytes 884744 | tf_op jit(solution)/shard_map/ppermute | solution.py:19
  36.3 11.6 %collective-permute-start.11 = (bf16[16,3072]{1,0:T(8,128)(2,1)S(1)}, bf16[16,3072]{1,0:T(8,128)(2,1)S(1)}, u32[]{:S(2)}, u32[]{:S(2)}) collective-permute-start(bf16[16,3072]{1,0:T(8,128)(2,1)S(1)} %slice.89), channel_id=1, source_target_pairs={{0,4},{1,5},{2,6},{3,7},{4,8},{5,9},{6,10},{7,11},{8,12},{9,13},{1... | collective-permute-start | bytes 294920 | tf_op jit(solution)/shard_map/ppermute | solution.py:19
  38.1 9.8 %collective-permute-start.12 = (bf16[16,3072]{1,0:T(8,128)(2,1)S(1)}, bf16[16,3072]{1,0:T(8,128)(2,1)S(1)}, u32[]{:S(2)}, u32[]{:S(2)}) collective-permute-start(bf16[16,3072]{1,0:T(8,128)(2,1)S(1)} %slice.90), channel_id=1, source_target_pairs={{0,12},{1,13},{2,14},{3,15},{4,0},{5,1},{6,2},{7,3},{8,4},{9,5},{1... | collective-permute-start | bytes 294920 | tf_op jit(solution)/shard_map/ppermute | solution.py:19
  53.9 11.3 %collective-permute-start.13 = (bf16[16,12288]{1,0:T(8,128)(2,1)S(1)}, bf16[16,12288]{1,0:T(8,128)(2,1)S(1)}, u32[]{:S(2)}, u32[]{:S(2)}) collective-permute-start(bf16[16,12288]{1,0:T(8,128)(2,1)S(1)} %get-tuple-element.58), channel_id=1, source_target_pairs={{0,4},{1,5},{2,6},{3,7},{4,8},{5,9},{6,10},{7,11},{8,12},{9,13},{1... | collective-permute-start | bytes 1179656 | tf_op jit(solution)/shard_map/ppermute | solution.py:19
  54.0 11.2 %collective-permute-start.14 = (bf16[16,12288]{1,0:T(8,128)(2,1)S(1)}, bf16[16,12288]{1,0:T(8,128)(2,1)S(1)}, u32[]{:S(2)}, u32[]{:S(2)}) collective-permute-start(bf16[16,12288]{1,0:T(8,128)(2,1)S(1)} %get-tuple-element.59), channel_id=1, source_target_pairs={{0,12},{1,13},{2,14},{3,15},{4,0},{5,1},{6,2},{7,3},{8,4},{9,5},{1... | collective-permute-start | bytes 1179656 | tf_op jit(solution)/shard_map/ppermute | solution.py:19
  57.2 34.9 %copy-start = (bf16[16,6144]{1,0:T(8,128)(2,1)S(1)}, bf16[16,6144]{1,0:T(8,128)(2,1)}, u32[]{:S(2)}) copy-start(bf16[16,6144]{1,0:T(8,128)(2,1)} %rows_ref.1) | copy-start | bytes 589828
  65.4 7.5 %collective-permute-start.19 = (bf16[16,6144]{1,0:T(8,128)(2,1)S(1)}, bf16[16,6144]{1,0:T(8,128)(2,1)S(1)}, u32[]{:S(2)}, u32[]{:S(2)}) collective-permute-start(bf16[16,6144]{1,0:T(8,128)(2,1)S(1)} %pad_maximum_fusion.7), channel_id=1, source_target_pairs={{0,4},{1,5},{2,6},{3,7},{4,8},{5,9},{6,10},{7,11},{8,12},{9,13},{1... | collective-permute-start | bytes 589832 | tf_op jit(solution)/shard_map/ppermute | solution.py:19
  65.5 8.7 %collective-permute-start.20 = (bf16[16,6144]{1,0:T(8,128)(2,1)S(1)}, bf16[16,6144]{1,0:T(8,128)(2,1)S(1)}, u32[]{:S(2)}, u32[]{:S(2)}) collective-permute-start(bf16[16,6144]{1,0:T(8,128)(2,1)S(1)} %pad_maximum_fusion.8), channel_id=1, source_target_pairs={{0,12},{1,13},{2,14},{3,15},{4,0},{5,1},{6,2},{7,3},{8,4},{9,5},{1... | collective-permute-start | bytes 589832 | tf_op jit(solution)/shard_map/ppermute | solution.py:19
  68.8 10.8 %collective-permute-start.16 = (bf16[32,6144]{1,0:T(8,128)(2,1)S(1)}, bf16[32,6144]{1,0:T(8,128)(2,1)S(1)}, u32[]{:S(2)}, u32[]{:S(2)}) collective-permute-start(bf16[32,6144]{1,0:T(8,128)(2,1)S(1)} %pad_maximum_fusion.2), channel_id=1, source_target_pairs={{0,12},{1,13},{2,14},{3,15},{4,0},{5,1},{6,2},{7,3},{8,4},{9,5},{1... | collective-permute-start | bytes 1179656 | tf_op jit(solution)/shard_map/ppermute | solution.py:19
  70.9 9.9 %collective-permute-start.15 = (bf16[32,6144]{1,0:T(8,128)(2,1)S(1)}, bf16[32,6144]{1,0:T(8,128)(2,1)S(1)}, u32[]{:S(2)}, u32[]{:S(2)}) collective-permute-start(bf16[32,6144]{1,0:T(8,128)(2,1)S(1)} %pad_maximum_fusion.1), channel_id=1, source_target_pairs={{0,4},{1,5},{2,6},{3,7},{4,8},{5,9},{6,10},{7,11},{8,12},{9,13},{1... | collective-permute-start | bytes 1179656 | tf_op jit(solution)/shard_map/ppermute | solution.py:19
  74.2 14.2 %collective-permute-start.21 = (bf16[16,6144]{1,0:T(8,128)(2,1)S(1)}, bf16[16,6144]{1,0:T(8,128)(2,1)S(1)}, u32[]{:S(2)}, u32[]{:S(2)}) collective-permute-start(bf16[16,6144]{1,0:T(8,128)(2,1)S(1)} %add_convert_fusion.2), channel_id=1, source_target_pairs={{0,2},{1,3},{2,0},{3,1},{4,6},{5,7},{6,4},{7,5},{8,10},{9,11},{10,... | collective-permute-start | bytes 589832 | tf_op jit(solution)/shard_map/ppermute | solution.py:19
  80.9 11.2 %collective-permute-start.22 = (bf16[16,6144]{1,0:T(8,128)(2,1)S(1)}, bf16[16,6144]{1,0:T(8,128)(2,1)S(1)}, u32[]{:S(2)}, u32[]{:S(2)}) collective-permute-start(bf16[16,6144]{1,0:T(8,128)(2,1)S(1)} %get-tuple-element.77), channel_id=1, source_target_pairs={{0,1},{1,2},{2,3},{3,0},{4,5},{5,6},{6,7},{7,4},{8,9},{9,10},{10,1... | collective-permute-start | bytes 589832 | tf_op jit(solution)/shard_map/ppermute | solution.py:19
  81.0 11.1 %collective-permute-start.23 = (bf16[16,6144]{1,0:T(8,128)(2,1)S(1)}, bf16[16,6144]{1,0:T(8,128)(2,1)S(1)}, u32[]{:S(2)}, u32[]{:S(2)}) collective-permute-start(bf16[16,6144]{1,0:T(8,128)(2,1)S(1)} %get-tuple-element.78), channel_id=1, source_target_pairs={{0,3},{1,0},{2,1},{3,2},{4,7},{5,4},{6,5},{7,6},{8,11},{9,8},{10,9... | collective-permute-start | bytes 589832 | tf_op jit(solution)/shard_map/ppermute | solution.py:19
  85.2 7.0 %collective-permute-start.17 = (bf16[16,6144]{1,0:T(8,128)(2,1)S(1)}, bf16[16,6144]{1,0:T(8,128)(2,1)S(1)}, u32[]{:S(2)}, u32[]{:S(2)}) collective-permute-start(bf16[16,6144]{1,0:T(8,128)(2,1)S(1)} %pad_maximum_fusion.5), channel_id=1, source_target_pairs={{0,4},{1,5},{2,6},{3,7},{4,8},{5,9},{6,10},{7,11},{8,12},{9,13},{1... | collective-permute-start | bytes 589832 | tf_op jit(solution)/shard_map/ppermute | solution.py:19
  85.3 6.9 %collective-permute-start.18 = (bf16[16,6144]{1,0:T(8,128)(2,1)S(1)}, bf16[16,6144]{1,0:T(8,128)(2,1)S(1)}, u32[]{:S(2)}, u32[]{:S(2)}) collective-permute-start(bf16[16,6144]{1,0:T(8,128)(2,1)S(1)} %pad_maximum_fusion.6), channel_id=1, source_target_pairs={{0,12},{1,13},{2,14},{3,15},{4,0},{5,1},{6,2},{7,3},{8,4},{9,5},{1... | collective-permute-start | bytes 589832 | tf_op jit(solution)/shard_map/ppermute | solution.py:19

commit v13 on v12

--- a/solution.py
+++ b/solution.py
@@ -99,15 +99,12 @@
         rows[3 * n :, :h] = far_up[...]
         rows[3 * n :, h:] = far_down[...]
         hidden[...] = hidden_of(rows, gate_w, up_w, up_w2)
-        for second in (False, True):
-            target = out_down if second else out_up
-
-            cut = pl.ds(second * h, h)
-            terms = b16(jnp.dot(hidden[...], down_w[:, cut], preferred_element_type=jnp.float32))
-            out_up[:, cut] = terms[:n]
-            out_down[:, cut] = terms[n : 2 * n]
-            target[:, pl.ds(d, h)] = terms[2 * n : 3 * n]
-            target[:, pl.ds(d + h, h)] = terms[3 * n :]
+        terms = b16(jnp.dot(hidden[...], down_w[...], preferred_element_type=jnp.float32))
+        out_up[:, :d] = terms[:n]
+        out_down[:, :d] = terms[n : 2 * n]
+        for side, target in ((0, out_up), (h, out_down)):
+            target[:, d : d + h] = terms[2 * n : 3 * n, side : side + h]
+            target[:, d + h :] = terms[3 * n :, side : side + h]
 
     vmem, b = pl.BlockSpec(memory_space=pltpu.VMEM), jnp.bfloat16
     return pl.pallas_call(

time: 93.6 us -> 93.6 us (level)
  no operation moved by 1% of the time
where the time goes in v13:
time: 93.6 us; the launch traced here: 93 us
  starting transfers between devices  41 us (44%)
  Pallas kernels  27.7 us (30%)
  waiting for transfers between devices  22.4 us (24%)
  other arithmetic  1.38 us (1%)
    ppermute x24, starting transfers between devices, shift(): return lax.ppermute(block, ('dp', 'tensor'), pairs)  41 us
    ppermute x24, waiting for transfers between devices, shift(): return lax.ppermute(block, ('dp', 'tensor'), pairs)  22.4 us
    pallas_call x3, Pallas kernels, fetched(): pl.pallas_call(kernel, out_shape=pltpu.VMEM((size, weight.shape[1]), weig...  9.28 us
    pallas_call x2, Pallas kernels, hidden_units(): pl.pallas_call(kernel, out_shape=[pltpu.VMEM((tall, ff), b)] + [pltpu.VME...  7.79 us
    pallas_call x1, Pallas kernels, two_hops(): pl.pallas_call(kernel, out_shape=[pltpu.VMEM((n, 2 * d), b)] * 2, in_spec...  6 us
    pallas_call x1, Pallas kernels, other_terms(): pl.pallas_call(kernel, out_shape=[pltpu.VMEM((k * n, d), jnp.float32) for...  3.57 us
  transfers between devices with their start and end apart: 24, of which 9 were waited for; matrix products, arithmetic and copies ran while one was open for 1% of the time, Pallas kernels for 22%

profile of v13, /device:TPU:8, one launch (start us, length us, event | category | flops | bytes accessed | tf_op | source)
XLA Modules:
  0.0 93.0 jit_solution(6076043521617009179)
XLA Ops:
  0.0 1.1 %shard_map.55.refs_0_ = bf16[16,6144]{1,0:T(8,128)(2,1)S(1)} custom-call(bf16[16,6144]{1,0:T(8,128)(2,1)} %rows_ref.1, f32[1,6144]{1,0:T(1,128)} %bitcast.1), custom_call_target="tpu_custom_call" | custom-call | tf_op jit(solution)/shard_map/pallas_call | solution.py:37
  1.1 3.3 %collective-permute-start = (bf16[16,6144]{1,0:T(8,128)(2,1)S(1)}, bf16[16,6144]{1,0:T(8,128)(2,1)S(1)}, u32[]{:S(2)}, u32[]{:S(2)}) collective-permute-start(bf16[16,6144]{1,0:T(8,128)(2,1)S(1)} %shard_map.55.refs_0_), channel_id=1, source_target_pairs={{0,1},{1,2},{2,3},{3,0},{4,5},{5,6},{6,7},{7,4},{8,9},{9,10},{10,1... | collective-permute-start | bytes 589832 | tf_op jit(solution)/shard_map/ppermute | solution.py:19
  4.5 3.1 %collective-permute-start.1 = (bf16[16,6144]{1,0:T(8,128)(2,1)S(1)}, bf16[16,6144]{1,0:T(8,128)(2,1)S(1)}, u32[]{:S(2)}, u32[]{:S(2)}) collective-permute-start(bf16[16,6144]{1,0:T(8,128)(2,1)S(1)} %shard_map.55.refs_0_), channel_id=1, source_target_pairs={{0,3},{1,0},{2,1},{3,2},{4,7},{5,4},{6,5},{7,6},{8,11},{9,8},{10,9... | collective-permute-start | bytes 589832 | tf_op jit(solution)/shard_map/ppermute | solution.py:19
  7.6 1.5 %collective-permute-start.2 = (bf16[16,6144]{1,0:T(8,128)(2,1)S(1)}, bf16[16,6144]{1,0:T(8,128)(2,1)S(1)}, u32[]{:S(2)}, u32[]{:S(2)}) collective-permute-start(bf16[16,6144]{1,0:T(8,128)(2,1)S(1)} %shard_map.55.refs_0_), channel_id=1, source_target_pairs={{0,4},{1,5},{2,6},{3,7},{4,8},{5,9},{6,10},{7,11},{8,12},{9,13},{1... | collective-permute-start | bytes 589832 | tf_op jit(solution)/shard_map/ppermute | solution.py:19
  9.1 1.7 %collective-permute-start.3 = (bf16[16,6144]{1,0:T(8,128)(2,1)S(1)}, bf16[16,6144]{1,0:T(8,128)(2,1)S(1)}, u32[]{:S(2)}, u32[]{:S(2)}) collective-permute-start(bf16[16,6144]{1,0:T(8,128)(2,1)S(1)} %shard_map.55.refs_0_), channel_id=1, source_target_pairs={{0,12},{1,13},{2,14},{3,15},{4,0},{5,1},{6,2},{7,3},{8,4},{9,5},{1... | collective-permute-start | bytes 589832 | tf_op jit(solution)/shard_map/ppermute | solution.py:19
  10.8 4.1 %shard_map.56.refs_6_.refs_4_.gate_w = bf16[6144,896]{1,0:T(8,128)(2,1)S(1)} custom-call(bf16[6144,896]{1,0:T(8,128)(2,1)} %source.2), custom_call_target="tpu_custom_call" | custom-call | bytes 11010048 | tf_op jit(solution)/shard_map/pallas_call | solution.py:159
  15.0 2.6 %shard_map.57.refs_7_.refs_5_.up_w = bf16[3072,896]{1,0:T(8,128)(2,1)S(1)} custom-call(bf16[6144,896]{1,0:T(8,128)(2,1)} %source.4), custom_call_target="tpu_custom_call" | custom-call | bytes 5505024 | tf_op jit(solution)/shard_map/pallas_call | solution.py:159
  17.6 0.0 collective-permute-done.refs_3_
  17.6 1.4 %collective-permute-start.6 = (bf16[16,6144]{1,0:T(8,128)(2,1)S(1)}, bf16[16,6144]{1,0:T(8,128)(2,1)S(1)}, u32[]{:S(2)}, u32[]{:S(2)}) collective-permute-start(bf16[16,6144]{1,0:T(8,128)(2,1)S(1)} %collective-permute-done.refs_3_), channel_id=1, source_target_pairs={{0,1},{1,2},{2,3},{3,0},{4,5},{5,6},{6,7},{7,4},{8,9},{9,10},{10,1... | collective-permute-start | bytes 589832 | tf_op jit(solution)/shard_map/ppermute | solution.py:19
  19.0 0.0 collective-permute-done.2.refs_1_
  19.1 1.3 %collective-permute-start.4 = (bf16[32,6144]{1,0:T(8,128)(2,1)S(1)}, bf16[32,6144]{1,0:T(8,128)(2,1)S(1)}, u32[]{:S(2)}, u32[]{:S(2)}) collective-permute-start(bf16[32,6144]{1,0:T(8,128)(2,1)S(1)} %pad_maximum_fusion), channel_id=1, source_target_pairs={{0,4},{1,5},{2,6},{3,7},{4,8},{5,9},{6,10},{7,11},{8,12},{9,13},{1... | collective-permute-start | bytes 1179656 | tf_op jit(solution)/shard_map/ppermute | solution.py:19
  20.4 2.0 %collective-permute-start.5 = (bf16[32,6144]{1,0:T(8,128)(2,1)S(1)}, bf16[32,6144]{1,0:T(8,128)(2,1)S(1)}, u32[]{:S(2)}, u32[]{:S(2)}) collective-permute-start(bf16[32,6144]{1,0:T(8,128)(2,1)S(1)} %pad_maximum_fusion), channel_id=1, source_target_pairs={{0,12},{1,13},{2,14},{3,15},{4,0},{5,1},{6,2},{7,3},{8,4},{9,5},{1... | collective-permute-start | bytes 1179656 | tf_op jit(solution)/shard_map/ppermute | solution.py:19
  22.4 2.6 %shard_map.58.refs_8_.refs_6_.up_w2 = bf16[3072,896]{1,0:T(8,128)(2,1)S(1)} custom-call(bf16[6144,896]{1,0:T(8,128)(2,1)} %source.4), custom_call_target="tpu_custom_call" | custom-call | bytes 5505024 | tf_op jit(solution)/shard_map/pallas_call | solution.py:159
  25.0 1.0 %collective-permute-done.6.refs_5_ = bf16[16,6144]{1,0:T(8,128)(2,1)S(1)} collective-permute-done((bf16[16,6144]{1,0:T(8,128)(2,1)S(1)}, bf16[16,6144]{1,0:T(8,128)(2,1)S(1)}, u32[]{:S(2)}, u32[]{:S(2)}) %collective-permute-start.6) | collective-permute-done | bytes 196640 | tf_op jit(solution)/shard_map/ppermute | solution.py:19
  26.0 0.7 collective-permute-start.7
  26.7 2.5 %collective-permute-start.8 = (bf16[16,6144]{1,0:T(8,128)(2,1)S(1)}, bf16[16,6144]{1,0:T(8,128)(2,1)S(1)}, u32[]{:S(2)}, u32[]{:S(2)}) collective-permute-start(bf16[16,6144]{1,0:T(8,128)(2,1)S(1)} %collective-permute-done.6.refs_5_), channel_id=1, source_target_pairs={{0,12},{1,13},{2,14},{3,15},{4,0},{5,1},{6,2},{7,3},{8,4},{9,5},{1... | collective-permute-start | bytes 589832 | tf_op jit(solution)/shard_map/ppermute | solution.py:19
  29.2 3.6 %shard_map.59.early = bf16[96,896]{1,0:T(8,128)(2,1)S(1)} custom-call(bf16[16,6144]{1,0:T(8,128)(2,1)S(1)} %shard_map.55.refs_0_, bf16[16,6144]{1,0:T(8,128)(2,1)S(1)} %collective-permute-done.2.refs_1_, bf16[16,6144]{1,0:T(8,128)(2,1)S(1)} %collective-permute-done.3.refs_2_, bf16[16,6144]{1,0:T(8,128)(2,1)S(1)} %collective-permute-done.refs_3_, ...), custom_call_target="tpu_custom_call" | custom-call | flops 2113929216 | tf_op jit(solution)/shard_map/pallas_call | solution.py:80
  32.9 0.0 collective-permute-done.5.refs_1_
  32.9 2.8 %collective-permute-start.10 = (bf16[16,9216]{1,0:T(8,128)(2,1)S(1)}, bf16[16,9216]{1,0:T(8,128)(2,1)S(1)}, u32[]{:S(2)}, u32[]{:S(2)}) collective-permute-start(bf16[16,9216]{1,0:T(8,128)(2,1)S(1)} %pad_maximum_fusion.4), channel_id=1, source_target_pairs={{0,12},{1,13},{2,14},{3,15},{4,0},{5,1},{6,2},{7,3},{8,4},{9,5},{1... | collective-permute-start | bytes 884744 | tf_op jit(solution)/shard_map/ppermute | solution.py:19
  35.7 0.1 collective-permute-start.9
  35.8 0.4 collective-permute-done.7.refs_2_
  36.3 0.0 collective-permute-done.8.refs_3_
  36.3 1.7 %collective-permute-start.11 = (bf16[16,3072]{1,0:T(8,128)(2,1)S(1)}, bf16[16,3072]{1,0:T(8,128)(2,1)S(1)}, u32[]{:S(2)}, u32[]{:S(2)}) collective-permute-start(bf16[16,3072]{1,0:T(8,128)(2,1)S(1)} %slice.89), channel_id=1, source_target_pairs={{0,4},{1,5},{2,6},{3,7},{4,8},{5,9},{6,10},{7,11},{8,12},{9,13},{1... | collective-permute-start | bytes 294920 | tf_op jit(solution)/shard_map/ppermute | solution.py:19
  38.1 2.1 %collective-permute-start.12 = (bf16[16,3072]{1,0:T(8,128)(2,1)S(1)}, bf16[16,3072]{1,0:T(8,128)(2,1)S(1)}, u32[]{:S(2)}, u32[]{:S(2)}) collective-permute-start(bf16[16,3072]{1,0:T(8,128)(2,1)S(1)} %slice.90), channel_id=1, source_target_pairs={{0,12},{1,13},{2,14},{3,15},{4,0},{5,1},{6,2},{7,3},{8,4},{9,5},{1... | collective-permute-start | bytes 294920 | tf_op jit(solution)/shard_map/ppermute | solution.py:19
  40.2 4.1 %shard_map.60 = (bf16[96,896]{1,0:T(8,128)(2,1)S(1)}, bf16[896,6144]{1,0:T(8,128)(2,1)S(1)}) custom-call(bf16[32,6144]{1,0:T(8,128)(2,1)S(1)} %collective-permute-done.4.refs_0_, bf16[32,6144]{1,0:T(8,128)(2,1)S(1)} %collective-permute-done.5.refs_1_, bf16[16,6144]{1,0:T(8,128)(2,1)S(1)} %collective-permute-done.7.refs_2_, ...), custom_call_target="tpu_custom_call" | custom-call | flops 2113929216 | bytes 11010048 | tf_op jit(solution)/shard_map/pallas_call | solution.py:80
  44.3 3.6 %collective-permute-done.11.far_up = bf16[16,3072]{1,0:T(8,128)(2,1)S(1)} collective-permute-done((bf16[16,3072]{1,0:T(8,128)(2,1)S(1)}, bf16[16,3072]{1,0:T(8,128)(2,1)S(1)}, u32[]{:S(2)}, u32[]{:S(2)}) %collective-permute-start.11) | collective-permute-done | bytes 98336 | tf_op jit(solution)/shard_map/ppermute | solution.py:19
  47.9 6.0 %shard_map.62 = (bf16[16,12288]{1,0:T(8,128)(2,1)S(1)}, bf16[16,12288]{1,0:T(8,128)(2,1)S(1)}) custom-call(bf16[16,9216]{1,0:T(8,128)(2,1)S(1)} %collective-permute-done.9.two_up, bf16[16,9216]{1,0:T(8,128)(2,1)S(1)} %collective-permute-done.10.two_down, bf16[16,3072]{1,0:T(8,128)(2,1)S(1)} %collective-permute-done.11.far_up, ...), custom_call_target="tpu_custom_call" | custom-call | flops 2113929216 | tf_op jit(solution)/shard_map/pallas_call | solution.py:110
  53.9 0.1 collective-permute-start.13
  54.0 3.2 %collective-permute-start.14 = (bf16[16,12288]{1,0:T(8,128)(2,1)S(1)}, bf16[16,12288]{1,0:T(8,128)(2,1)S(1)}, u32[]{:S(2)}, u32[]{:S(2)}) collective-permute-start(bf16[16,12288]{1,0:T(8,128)(2,1)S(1)} %get-tuple-element.59), channel_id=1, source_target_pairs={{0,12},{1,13},{2,14},{3,15},{4,0},{5,1},{6,2},{7,3},{8,4},{9,5},{1... | collective-permute-start | bytes 1179656 | tf_op jit(solution)/shard_map/ppermute | solution.py:19
  57.2 3.6 %shard_map.61 = (f32[16,6144]{1,0:T(8,128)S(1)}, f32[16,6144]{1,0:T(8,128)S(1)}, f32[16,6144]{1,0:T(8,128)S(1)}, f32[32,6144]{1,0:T(8,128)S(1)}, f32[16,6144]{1,...) custom-call(bf16[96,896]{1,0:T(8,128)(2,1)S(1)} %shard_map.59.early,, ...), custom_call_target="tpu_custom_call" | custom-call | flops 2113929216 | tf_op jit(solution)/shard_map/pallas_call | solution.py:140
  60.9 4.2 %collective-permute-done.13 = bf16[16,12288]{1,0:T(8,128)(2,1)S(1)} collective-permute-done((bf16[16,12288]{1,0:T(8,128)(2,1)S(1)}, bf16[16,12288]{1,0:T(8,128)(2,1)S(1)}, u32[]{:S(2)}, u32[]{:S(2)}) %collective-permute-start.13) | collective-permute-done | bytes 393248 | tf_op jit(solution)/shard_map/ppermute | solution.py:19
  65.4 0.1 collective-permute-start.19
  65.5 3.3 %collective-permute-start.20 = (bf16[16,6144]{1,0:T(8,128)(2,1)S(1)}, bf16[16,6144]{1,0:T(8,128)(2,1)S(1)}, u32[]{:S(2)}, u32[]{:S(2)}) collective-permute-start(bf16[16,6144]{1,0:T(8,128)(2,1)S(1)} %pad_maximum_fusion.8), channel_id=1, source_target_pairs={{0,12},{1,13},{2,14},{3,15},{4,0},{5,1},{6,2},{7,3},{8,4},{9,5},{1... | collective-permute-start | bytes 589832 | tf_op jit(solution)/shard_map/ppermute | solution.py:19
  68.8 2.0 %collective-permute-start.16 = (bf16[32,6144]{1,0:T(8,128)(2,1)S(1)}, bf16[32,6144]{1,0:T(8,128)(2,1)S(1)}, u32[]{:S(2)}, u32[]{:S(2)}) collective-permute-start(bf16[32,6144]{1,0:T(8,128)(2,1)S(1)} %pad_maximum_fusion.2), channel_id=1, source_target_pairs={{0,12},{1,13},{2,14},{3,15},{4,0},{5,1},{6,2},{7,3},{8,4},{9,5},{1... | collective-permute-start | bytes 1179656 | tf_op jit(solution)/shard_map/ppermute | solution.py:19
  70.9 0.4 collective-permute-start.15
  71.3 1.6 %collective-permute-done.19 = bf16[16,6144]{1,0:T(8,128)(2,1)S(1)} collective-permute-done((bf16[16,6144]{1,0:T(8,128)(2,1)S(1)}, bf16[16,6144]{1,0:T(8,128)(2,1)S(1)}, u32[]{:S(2)}, u32[]{:S(2)}) %collective-permute-start.19) | collective-permute-done | bytes 196640 | tf_op jit(solution)/shard_map/ppermute | solution.py:19
  72.9 1.2 %collective-permute-done.20 = bf16[16,6144]{1,0:T(8,128)(2,1)S(1)} collective-permute-done((bf16[16,6144]{1,0:T(8,128)(2,1)S(1)}, bf16[16,6144]{1,0:T(8,128)(2,1)S(1)}, u32[]{:S(2)}, u32[]{:S(2)}) %collective-permute-start.20) | collective-permute-done | bytes 196640 | tf_op jit(solution)/shard_map/ppermute | solution.py:19
  74.2 0.1 add_convert_fusion.2
  74.2 0.1 collective-permute-start.21
  74.3 5.4 %collective-permute-done.16 = bf16[32,6144]{1,0:T(8,128)(2,1)S(1)} collective-permute-done((bf16[32,6144]{1,0:T(8,128)(2,1)S(1)}, bf16[32,6144]{1,0:T(8,128)(2,1)S(1)}, u32[]{:S(2)}, u32[]{:S(2)}) %collective-permute-start.16) | collective-permute-done | bytes 393248 | tf_op jit(solution)/shard_map/ppermute | solution.py:19
  79.7 1.1 %collective-permute-done.15 = bf16[32,6144]{1,0:T(8,128)(2,1)S(1)} collective-permute-done((bf16[32,6144]{1,0:T(8,128)(2,1)S(1)}, bf16[32,6144]{1,0:T(8,128)(2,1)S(1)}, u32[]{:S(2)}, u32[]{:S(2)}) %collective-permute-start.15) | collective-permute-done | bytes 393248 | tf_op jit(solution)/shard_map/ppermute | solution.py:19
  80.8 0.1 add_convert_fusion
  80.9 0.1 collective-permute-start.22
  81.0 4.1 %collective-permute-start.23 = (bf16[16,6144]{1,0:T(8,128)(2,1)S(1)}, bf16[16,6144]{1,0:T(8,128)(2,1)S(1)}, u32[]{:S(2)}, u32[]{:S(2)}) collective-permute-start(bf16[16,6144]{1,0:T(8,128)(2,1)S(1)} %get-tuple-element.78), channel_id=1, source_target_pairs={{0,3},{1,0},{2,1},{3,2},{4,7},{5,4},{6,5},{7,6},{8,11},{9,8},{10,9... | collective-permute-start | bytes 589832 | tf_op jit(solution)/shard_map/ppermute | solution.py:19
  85.2 0.1 collective-permute-start.17
  85.3 3.1 %collective-permute-start.18 = (bf16[16,6144]{1,0:T(8,128)(2,1)S(1)}, bf16[16,6144]{1,0:T(8,128)(2,1)S(1)}, u32[]{:S(2)}, u32[]{:S(2)}) collective-permute-start(bf16[16,6144]{1,0:T(8,128)(2,1)S(1)} %pad_maximum_fusion.6), channel_id=1, source_target_pairs={{0,12},{1,13},{2,14},{3,15},{4,0},{5,1},{6,2},{7,3},{8,4},{9,5},{1... | collective-permute-start | bytes 589832 | tf_op jit(solution)/shard_map/ppermute | solution.py:19
  88.4 3.8 %collective-permute-done.22 = bf16[16,6144]{1,0:T(8,128)(2,1)S(1)} collective-permute-done((bf16[16,6144]{1,0:T(8,128)(2,1)S(1)}, bf16[16,6144]{1,0:T(8,128)(2,1)S(1)}, u32[]{:S(2)}, u32[]{:S(2)}) %collective-permute-start.22) | collective-permute-done | bytes 196640 | tf_op jit(solution)/shard_map/ppermute | solution.py:19
  92.2 0.8 add_convert_fusion.1
  (39 shorter events, 0.6 us)
Async XLA Ops:
  1.1 16.4 %collective-permute-start = (bf16[16,6144]{1,0:T(8,128)(2,1)S(1)}, bf16[16,6144]{1,0:T(8,128)(2,1)S(1)}, u32[]{:S(2)}, u32[]{:S(2)}) collective-permute-start(bf16[16,6144]{1,0:T(8,128)(2,1)S(1)} %shard_map.55.refs_0_), channel_id=1, source_target_pairs={{0,1},{1,2},{2,3},{3,0},{4,5},{5,6},{6,7},{7,4},{8,9},{9,10},{10,1... | collective-permute-start | bytes 589832 | tf_op jit(solution)/shard_map/ppermute | solution.py:19
  4.5 13.1 %collective-permute-start.1 = (bf16[16,6144]{1,0:T(8,128)(2,1)S(1)}, bf16[16,6144]{1,0:T(8,128)(2,1)S(1)}, u32[]{:S(2)}, u32[]{:S(2)}) collective-permute-start(bf16[16,6144]{1,0:T(8,128)(2,1)S(1)} %shard_map.55.refs_0_), channel_id=1, source_target_pairs={{0,3},{1,0},{2,1},{3,2},{4,7},{5,4},{6,5},{7,6},{8,11},{9,8},{10,9... | collective-permute-start | bytes 589832 | tf_op jit(solution)/shard_map/ppermute | solution.py:19
  7.6 11.5 %collective-permute-start.2 = (bf16[16,6144]{1,0:T(8,128)(2,1)S(1)}, bf16[16,6144]{1,0:T(8,128)(2,1)S(1)}, u32[]{:S(2)}, u32[]{:S(2)}) collective-permute-start(bf16[16,6144]{1,0:T(8,128)(2,1)S(1)} %shard_map.55.refs_0_), channel_id=1, source_target_pairs={{0,4},{1,5},{2,6},{3,7},{4,8},{5,9},{6,10},{7,11},{8,12},{9,13},{1... | collective-permute-start | bytes 589832 | tf_op jit(solution)/shard_map/ppermute | solution.py:19
  9.1 10.0 %collective-permute-start.3 = (bf16[16,6144]{1,0:T(8,128)(2,1)S(1)}, bf16[16,6144]{1,0:T(8,128)(2,1)S(1)}, u32[]{:S(2)}, u32[]{:S(2)}) collective-permute-start(bf16[16,6144]{1,0:T(8,128)(2,1)S(1)} %shard_map.55.refs_0_), channel_id=1, source_target_pairs={{0,12},{1,13},{2,14},{3,15},{4,0},{5,1},{6,2},{7,3},{8,4},{9,5},{1... | collective-permute-start | bytes 589832 | tf_op jit(solution)/shard_map/ppermute | solution.py:19
  17.6 8.4 %collective-permute-start.6 = (bf16[16,6144]{1,0:T(8,128)(2,1)S(1)}, bf16[16,6144]{1,0:T(8,128)(2,1)S(1)}, u32[]{:S(2)}, u32[]{:S(2)}) collective-permute-start(bf16[16,6144]{1,0:T(8,128)(2,1)S(1)} %collective-permute-done.refs_3_), channel_id=1, source_target_pairs={{0,1},{1,2},{2,3},{3,0},{4,5},{5,6},{6,7},{7,4},{8,9},{9,10},{10,1... | collective-permute-start | bytes 589832 | tf_op jit(solution)/shard_map/ppermute | solution.py:19
  19.1 13.8 %collective-permute-start.4 = (bf16[32,6144]{1,0:T(8,128)(2,1)S(1)}, bf16[32,6144]{1,0:T(8,128)(2,1)S(1)}, u32[]{:S(2)}, u32[]{:S(2)}) collective-permute-start(bf16[32,6144]{1,0:T(8,128)(2,1)S(1)} %pad_maximum_fusion), channel_id=1, source_target_pairs={{0,4},{1,5},{2,6},{3,7},{4,8},{5,9},{6,10},{7,11},{8,12},{9,13},{1... | collective-permute-start | bytes 1179656 | tf_op jit(solution)/shard_map/ppermute | solution.py:19
  20.4 12.5 %collective-permute-start.5 = (bf16[32,6144]{1,0:T(8,128)(2,1)S(1)}, bf16[32,6144]{1,0:T(8,128)(2,1)S(1)}, u32[]{:S(2)}, u32[]{:S(2)}) collective-permute-start(bf16[32,6144]{1,0:T(8,128)(2,1)S(1)} %pad_maximum_fusion), channel_id=1, source_target_pairs={{0,12},{1,13},{2,14},{3,15},{4,0},{5,1},{6,2},{7,3},{8,4},{9,5},{1... | collective-permute-start | bytes 1179656 | tf_op jit(solution)/shard_map/ppermute | solution.py:19
  26.0 10.3 %collective-permute-start.7 = (bf16[16,6144]{1,0:T(8,128)(2,1)S(1)}, bf16[16,6144]{1,0:T(8,128)(2,1)S(1)}, u32[]{:S(2)}, u32[]{:S(2)}) collective-permute-start(bf16[16,6144]{1,0:T(8,128)(2,1)S(1)} %collective-permute-done.6.refs_5_), channel_id=1, source_target_pairs={{0,4},{1,5},{2,6},{3,7},{4,8},{5,9},{6,10},{7,11},{8,12},{9,13},{1... | collective-permute-start | bytes 589832 | tf_op jit(solution)/shard_map/ppermute | solution.py:19
  26.7 9.6 %collective-permute-start.8 = (bf16[16,6144]{1,0:T(8,128)(2,1)S(1)}, bf16[16,6144]{1,0:T(8,128)(2,1)S(1)}, u32[]{:S(2)}, u32[]{:S(2)}) collective-permute-start(bf16[16,6144]{1,0:T(8,128)(2,1)S(1)} %collective-permute-done.6.refs_5_), channel_id=1, source_target_pairs={{0,12},{1,13},{2,14},{3,15},{4,0},{5,1},{6,2},{7,3},{8,4},{9,5},{1... | collective-permute-start | bytes 589832 | tf_op jit(solution)/shard_map/ppermute | solution.py:19
  32.9 15.0 %collective-permute-start.10 = (bf16[16,9216]{1,0:T(8,128)(2,1)S(1)}, bf16[16,9216]{1,0:T(8,128)(2,1)S(1)}, u32[]{:S(2)}, u32[]{:S(2)}) collective-permute-start(bf16[16,9216]{1,0:T(8,128)(2,1)S(1)} %pad_maximum_fusion.4), channel_id=1, source_target_pairs={{0,12},{1,13},{2,14},{3,15},{4,0},{5,1},{6,2},{7,3},{8,4},{9,5},{1... | collective-permute-start | bytes 884744 | tf_op jit(solution)/shard_map/ppermute | solution.py:19
  35.7 12.2 %collective-permute-start.9 = (bf16[16,9216]{1,0:T(8,128)(2,1)S(1)}, bf16[16,9216]{1,0:T(8,128)(2,1)S(1)}, u32[]{:S(2)}, u32[]{:S(2)}) collective-permute-start(bf16[16,9216]{1,0:T(8,128)(2,1)S(1)} %pad_maximum_fusion.3), channel_id=1, source_target_pairs={{0,4},{1,5},{2,6},{3,7},{4,8},{5,9},{6,10},{7,11},{8,12},{9,13},{1... | collective-permute-start | bytes 884744 | tf_op jit(solution)/shard_map/ppermute | solution.py:19
  36.3 11.6 %collective-permute-start.11 = (bf16[16,3072]{1,0:T(8,128)(2,1)S(1)}, bf16[16,3072]{1,0:T(8,128)(2,1)S(1)}, u32[]{:S(2)}, u32[]{:S(2)}) collective-permute-start(bf16[16,3072]{1,0:T(8,128)(2,1)S(1)} %slice.89), channel_id=1, source_target_pairs={{0,4},{1,5},{2,6},{3,7},{4,8},{5,9},{6,10},{7,11},{8,12},{9,13},{1... | collective-permute-start | bytes 294920 | tf_op jit(solution)/shard_map/ppermute | solution.py:19
  38.1 9.8 %collective-permute-start.12 = (bf16[16,3072]{1,0:T(8,128)(2,1)S(1)}, bf16[16,3072]{1,0:T(8,128)(2,1)S(1)}, u32[]{:S(2)}, u32[]{:S(2)}) collective-permute-start(bf16[16,3072]{1,0:T(8,128)(2,1)S(1)} %slice.90), channel_id=1, source_target_pairs={{0,12},{1,13},{2,14},{3,15},{4,0},{5,1},{6,2},{7,3},{8,4},{9,5},{1... | collective-permute-start | bytes 294920 | tf_op jit(solution)/shard_map/ppermute | solution.py:19
  53.9 11.3 %collective-permute-start.13 = (bf16[16,12288]{1,0:T(8,128)(2,1)S(1)}, bf16[16,12288]{1,0:T(8,128)(2,1)S(1)}, u32[]{:S(2)}, u32[]{:S(2)}) collective-permute-start(bf16[16,12288]{1,0:T(8,128)(2,1)S(1)} %get-tuple-element.58), channel_id=1, source_target_pairs={{0,4},{1,5},{2,6},{3,7},{4,8},{5,9},{6,10},{7,11},{8,12},{9,13},{1... | collective-permute-start | bytes 1179656 | tf_op jit(solution)/shard_map/ppermute | solution.py:19
  54.0 11.2 %collective-permute-start.14 = (bf16[16,12288]{1,0:T(8,128)(2,1)S(1)}, bf16[16,12288]{1,0:T(8,128)(2,1)S(1)}, u32[]{:S(2)}, u32[]{:S(2)}) collective-permute-start(bf16[16,12288]{1,0:T(8,128)(2,1)S(1)} %get-tuple-element.59), channel_id=1, source_target_pairs={{0,12},{1,13},{2,14},{3,15},{4,0},{5,1},{6,2},{7,3},{8,4},{9,5},{1... | collective-permute-start | bytes 1179656 | tf_op jit(solution)/shard_map/ppermute | solution.py:19
  57.2 34.9 %copy-start = (bf16[16,6144]{1,0:T(8,128)(2,1)S(1)}, bf16[16,6144]{1,0:T(8,128)(2,1)}, u32[]{:S(2)}) copy-start(bf16[16,6144]{1,0:T(8,128)(2,1)} %rows_ref.1) | copy-start | bytes 589828
  65.4 7.5 %collective-permute-start.19 = (bf16[16,6144]{1,0:T(8,128)(2,1)S(1)}, bf16[16,6144]{1,0:T(8,128)(2,1)S(1)}, u32[]{:S(2)}, u32[]{:S(2)}) collective-permute-start(bf16[16,6144]{1,0:T(8,128)(2,1)S(1)} %pad_maximum_fusion.7), channel_id=1, source_target_pairs={{0,4},{1,5},{2,6},{3,7},{4,8},{5,9},{6,10},{7,11},{8,12},{9,13},{1... | collective-permute-start | bytes 589832 | tf_op jit(solution)/shard_map/ppermute | solution.py:19
  65.5 8.7 %collective-permute-start.20 = (bf16[16,6144]{1,0:T(8,128)(2,1)S(1)}, bf16[16,6144]{1,0:T(8,128)(2,1)S(1)}, u32[]{:S(2)}, u32[]{:S(2)}) collective-permute-start(bf16[16,6144]{1,0:T(8,128)(2,1)S(1)} %pad_maximum_fusion.8), channel_id=1, source_target_pairs={{0,12},{1,13},{2,14},{3,15},{4,0},{5,1},{6,2},{7,3},{8,4},{9,5},{1... | collective-permute-start | bytes 589832 | tf_op jit(solution)/shard_map/ppermute | solution.py:19
  68.8 10.8 %collective-permute-start.16 = (bf16[32,6144]{1,0:T(8,128)(2,1)S(1)}, bf16[32,6144]{1,0:T(8,128)(2,1)S(1)}, u32[]{:S(2)}, u32[]{:S(2)}) collective-permute-start(bf16[32,6144]{1,0:T(8,128)(2,1)S(1)} %pad_maximum_fusion.2), channel_id=1, source_target_pairs={{0,12},{1,13},{2,14},{3,15},{4,0},{5,1},{6,2},{7,3},{8,4},{9,5},{1... | collective-permute-start | bytes 1179656 | tf_op jit(solution)/shard_map/ppermute | solution.py:19
  70.9 9.9 %collective-permute-start.15 = (bf16[32,6144]{1,0:T(8,128)(2,1)S(1)}, bf16[32,6144]{1,0:T(8,128)(2,1)S(1)}, u32[]{:S(2)}, u32[]{:S(2)}) collective-permute-start(bf16[32,6144]{1,0:T(8,128)(2,1)S(1)} %pad_maximum_fusion.1), channel_id=1, source_target_pairs={{0,4},{1,5},{2,6},{3,7},{4,8},{5,9},{6,10},{7,11},{8,12},{9,13},{1... | collective-permute-start | bytes 1179656 | tf_op jit(solution)/shard_map/ppermute | solution.py:19
  74.2 14.2 %collective-permute-start.21 = (bf16[16,6144]{1,0:T(8,128)(2,1)S(1)}, bf16[16,6144]{1,0:T(8,128)(2,1)S(1)}, u32[]{:S(2)}, u32[]{:S(2)}) collective-permute-start(bf16[16,6144]{1,0:T(8,128)(2,1)S(1)} %add_convert_fusion.2), channel_id=1, source_target_pairs={{0,2},{1,3},{2,0},{3,1},{4,6},{5,7},{6,4},{7,5},{8,10},{9,11},{10,... | collective-permute-start | bytes 589832 | tf_op jit(solution)/shard_map/ppermute | solution.py:19
  80.9 11.2 %collective-permute-start.22 = (bf16[16,6144]{1,0:T(8,128)(2,1)S(1)}, bf16[16,6144]{1,0:T(8,128)(2,1)S(1)}, u32[]{:S(2)}, u32[]{:S(2)}) collective-permute-start(bf16[16,6144]{1,0:T(8,128)(2,1)S(1)} %get-tuple-element.77), channel_id=1, source_target_pairs={{0,1},{1,2},{2,3},{3,0},{4,5},{5,6},{6,7},{7,4},{8,9},{9,10},{10,1... | collective-permute-start | bytes 589832 | tf_op jit(solution)/shard_map/ppermute | solution.py:19
  81.0 11.1 %collective-permute-start.23 = (bf16[16,6144]{1,0:T(8,128)(2,1)S(1)}, bf16[16,6144]{1,0:T(8,128)(2,1)S(1)}, u32[]{:S(2)}, u32[]{:S(2)}) collective-permute-start(bf16[16,6144]{1,0:T(8,128)(2,1)S(1)} %get-tuple-element.78), channel_id=1, source_target_pairs={{0,3},{1,0},{2,1},{3,2},{4,7},{5,4},{6,5},{7,6},{8,11},{9,8},{10,9... | collective-permute-start | bytes 589832 | tf_op jit(solution)/shard_map/ppermute | solution.py:19
  85.2 7.0 %collective-permute-start.17 = (bf16[16,6144]{1,0:T(8,128)(2,1)S(1)}, bf16[16,6144]{1,0:T(8,128)(2,1)S(1)}, u32[]{:S(2)}, u32[]{:S(2)}) collective-permute-start(bf16[16,6144]{1,0:T(8,128)(2,1)S(1)} %pad_maximum_fusion.5), channel_id=1, source_target_pairs={{0,4},{1,5},{2,6},{3,7},{4,8},{5,9},{6,10},{7,11},{8,12},{9,13},{1... | collective-permute-start | bytes 589832 | tf_op jit(solution)/shard_map/ppermute | solution.py:19
  85.3 6.9 %collective-permute-start.18 = (bf16[16,6144]{1,0:T(8,128)(2,1)S(1)}, bf16[16,6144]{1,0:T(8,128)(2,1)S(1)}, u32[]{:S(2)}, u32[]{:S(2)}) collective-permute-start(bf16[16,6144]{1,0:T(8,128)(2,1)S(1)} %pad_maximum_fusion.6), channel_id=1, source_target_pairs={{0,12},{1,13},{2,14},{3,15},{4,0},{5,1},{6,2},{7,3},{8,4},{9,5},{1... | collective-permute-start | bytes 589832 | tf_op jit(solution)/shard_map/ppermute | solution.py:19
